TPU v7x, 32 devices: a whole 2x2x4 slice. The times are simulated.
32 devices in a mesh: segment: 2 (over core), row: 4 (over y, x), col: 4 (over z).
Axes of the slice: x: 2, y: 2, z: 4, core: 2. Of those that a mesh axis runs over, the one named last changes fastest.
Arguments:
- activations: bfloat16 [2, 96, 96, 128], P('segment', 'row', 'col'), may hold values from -6 to 6
- cotangent: bfloat16 [2, 96, 96, 128], P('segment', 'row', 'col'), may hold values from -6 to 6
- conv_weight: bfloat16 [2, 9, 128, 64], P('segment'), may hold values from -0.1875 to 0.1875
- conv_bias: bfloat16 [2, 64], P('segment'), may hold values from -3 to 3
- out_weight: bfloat16 [2, 64, 128], P('segment'), may hold values from -0.75 to 0.75
Outputs:
- input_gradient: bfloat16 [2, 96, 96, 128], P('segment', 'row', 'col')
- conv_gradient: float32 [2, 9, 128, 64], P('segment')
- bias_gradient: float32 [2, 64], P('segment')
- output_weight_gradient: float32 [2, 64, 128], P('segment')
All inputs are finite; a program needn't handle non-finite values.
Results may differ from a plain program's by a relative error of at most 0.022.
The roundings to bfloat16 on the way count: a program that leaves them out, or rounds other values in their place, can miss the bound.
Values may be sent and summed in bfloat16 or wider, within the bound.
No kernel may reach another device: no remote copies, remote signals or barrier semaphores. Data moves between devices by JAX's collectives and lax.ppermute only.
A program may use at most 64 MiB of HBM per device.

v0:
```python
import jax
import jax.numpy as jnp
from jax import lax
from jax.sharding import PartitionSpec as P

FIRST_DILATION = 2
SECOND_DILATION = 8


def extended(x, sides, width):
    for axis, dim in sides:
        count, length = (lax.axis_size(axis), x.shape[dim])
        up = [(i, (i + 1) % count) for i in range(count - 1)]
        down = [(j, i) for i, j in up]
        last = lax.slice_in_dim(x, length - width, length, axis=dim)
        first = lax.slice_in_dim(x, 0, width, axis=dim)
        before = lax.ppermute(last, axis, up)
        after = lax.ppermute(first, axis, down)
        x = jnp.concatenate([before, x, after], axis=dim)
    return x


def tap_window(padded, dilation, row_offset_tap, col_tap, side):
    row_start = dilation * (1 + row_offset_tap)
    col_start = dilation * (1 + col_tap)
    return padded[row_start : row_start + side, col_start : col_start + side]


def mirror(square):
    number = lax.axis_size("row")
    groups = square.reshape(square.shape[0], square.shape[1], number, square.shape[2] // number)
    groups = lax.all_to_all(groups, "col", split_axis=2, concat_axis=2, tiled=True)
    groups = lax.all_to_all(groups, "row", split_axis=2, concat_axis=2, tiled=True)
    groups = lax.all_to_all(groups, "col", split_axis=2, concat_axis=2, tiled=True)
    current = groups.reshape(square.shape)
    return jnp.swapaxes(current, 0, 1)


def forward_section(inputs, conv, bias, projection, dilation):
    side = inputs.shape[0]
    channels = inputs.shape[2]
    hidden = jnp.maximum(inputs, 0)
    padded = extended(hidden, (("row", 0), ("col", 1)), dilation)
    summed = jnp.zeros((side * side, conv.shape[2]), jnp.float32)
    for tap_index in range(9):
        window = tap_window(padded, dilation, tap_index // 3 - 1, tap_index % 3 - 1, side)
        summed = summed + jnp.dot(
            window.reshape(-1, channels), conv[tap_index], preferred_element_type=jnp.float32
        )
    pre_act = summed + bias.astype(jnp.float32)
    bottle = jnp.maximum(pre_act, 0.0).astype(jnp.bfloat16)
    branch_sum = (
        (
            inputs.reshape(-1, channels).astype(jnp.float32)
            + jnp.dot(bottle, projection, preferred_element_type=jnp.float32)
        )
        .astype(jnp.bfloat16)
        .reshape(side, side, channels)
    )
    mirrored = mirror(branch_sum)
    sym = ((branch_sum.astype(jnp.float32) + mirrored.astype(jnp.float32)) * 0.5).astype(
        jnp.bfloat16
    )
    return (sym, (inputs, padded, pre_act, bottle))


def backward_section(upstream, stored, conv, projection, dilation):
    inputs, padded, pre_act, bottle = stored
    side = inputs.shape[0]
    channels = inputs.shape[2]
    mirrored = mirror(upstream)
    grad_branch = (
        ((upstream.astype(jnp.float32) + mirrored.astype(jnp.float32)) * 0.5)
        .astype(jnp.bfloat16)
        .reshape(-1, channels)
    )
    grad_bottle = lax.dot_general(
        grad_branch, projection, (((1,), (1,)), ((), ())), preferred_element_type=jnp.float32
    )
    grad_pre = jnp.where(pre_act > 0, grad_bottle, 0.0).astype(jnp.bfloat16)
    grad_proj = lax.dot_general(
        bottle, grad_branch, (((0,), (0,)), ((), ())), preferred_element_type=jnp.float32
    )
    grad_bias = jnp.sum(grad_pre.astype(jnp.float32), axis=0)
    conv_terms = []
    for tap_index in range(9):
        window = tap_window(padded, dilation, tap_index // 3 - 1, tap_index % 3 - 1, side)
        conv_terms.append(
            lax.dot_general(
                window.reshape(-1, channels),
                grad_pre,
                (((0,), (0,)), ((), ())),
                preferred_element_type=jnp.float32,
            )
        )
    grad_conv = jnp.stack(conv_terms)
    grad_square = grad_pre.reshape(side, side, -1)
    grad_padded = extended(grad_square, (("row", 0), ("col", 1)), dilation)
    summed = jnp.zeros((side * side, channels), jnp.float32)
    for tap_index in range(9):
        window = tap_window(grad_padded, dilation, 1 - tap_index // 3, 1 - tap_index % 3, side)
        summed = summed + lax.dot_general(
            window.reshape(-1, window.shape[2]),
            conv[tap_index],
            (((1,), (1,)), ((), ())),
            preferred_element_type=jnp.float32,
        )
    masked = jnp.where(inputs.reshape(-1, channels) > 0, summed, 0.0)
    grad_inputs = (
        (grad_branch.astype(jnp.float32) + masked)
        .astype(jnp.bfloat16)
        .reshape(side, side, channels)
    )
    return (grad_inputs, (grad_conv, grad_bias, grad_proj))


def local(activations, cotangent, conv_weight, conv_bias, out_weight):
    every_convolution, all_bias, all_proj = (
        lax.all_gather(conv_weight, "segment", axis=0, tiled=True),
        lax.all_gather(conv_bias, "segment", axis=0, tiled=True),
        lax.all_gather(out_weight, "segment", axis=0, tiled=True),
    )
    dilation_list = (FIRST_DILATION, SECOND_DILATION)
    current = activations[0]
    stored_list = []
    for section in range(2):
        current, stored = forward_section(
            current,
            every_convolution[section],
            all_bias[section],
            all_proj[section],
            dilation_list[section],
        )
        stored_list.append(stored)
    upstream = cotangent[0]
    conv_list = [None, None]
    bias_list = [None, None]
    proj_list = [None, None]
    for section in (1, 0):
        upstream, section_grads = backward_section(
            upstream,
            stored_list[section],
            every_convolution[section],
            all_proj[section],
            dilation_list[section],
        )
        conv_list[section] = section_grads[0]
        bias_list[section] = section_grads[1]
        proj_list[section] = section_grads[2]
    conv_both = jnp.stack(conv_list)
    bias_both = jnp.stack(bias_list)
    proj_both = jnp.stack(proj_list)
    convolution_sum, bias_sum, projection_sum = lax.psum(
        (conv_both, bias_both, proj_both), ("segment", "row", "col")
    )
    own_segment = lax.axis_index("segment")
    convolution_sum = lax.dynamic_slice_in_dim(convolution_sum, own_segment, 1, 0)
    bias_sum = lax.dynamic_slice_in_dim(bias_sum, own_segment, 1, 0)
    projection_sum = lax.dynamic_slice_in_dim(projection_sum, own_segment, 1, 0)
    side = activations.shape[1]
    cells = lax.axis_size("segment") * (side * lax.axis_size("row")) * (side * lax.axis_size("col"))
    factor = 1.0 / jnp.sqrt(jnp.float32(cells))
    return (upstream[None], convolution_sum * factor, bias_sum * factor, projection_sum * factor)


def solution(mesh):
    in_specs = (
        P("segment", "row", "col", None),
        P("segment", "row", "col", None),
        P("segment", None, None, None),
        P("segment", None),
        P("segment", None, None),
    )
    out_specs = (
        P("segment", "row", "col", None),
        P("segment", None, None, None),
        P("segment", None),
        P("segment", None, None),
    )
    return jax.shard_map(local, mesh=mesh, in_specs=in_specs, out_specs=out_specs, check_vma=False)
```

profile of v0, /device:TPU:0, one launch (start us, length us, event | category | flops | bytes accessed | tf_op | source)
XLA Modules:
  0.0 358.3 jit_solution(7200110666693840404)
XLA Ops:
  8.1 4.8 %collective-permute-start = (bf16[2,24,128]{2,1,0:T(8,128)(2,1)S(1)}, bf16[2,24,128]{2,1,0:T(8,128)(2,1)S(1)}, u32[]{:S(2)}, u32[]{:S(2)}) collective-permute-start(bf16[2,24,128]{2,1,0:T(8,128)(2,1)S(1)} %get-tuple-element.58), channel_id=1, source_target_pairs={{0,4},{4,8},{8,12},{1,5},{5,9},{9,13},{2,6},{6,10},{10,14},{3,7},{... | collective-permute-start | bytes 36872 | tf_op jit(solution)/shard_map/ppermute | solution.py:17
  13.0 1.3 collective-permute-start.1
  15.6 1.2 reshape.270
  16.8 4.9 %all-to-all-start = ((bf16[4,2,9216]{2,1,0:T(2,128)(2,1)}), bf16[4,2,9216]{2,1,0:T(2,128)(2,1)S(1)}, u32[]{:S(2)}, u32[]{:S(2)}) async-start(bf16[4,2,9216]{2,1,0:T(2,128)(2,1)} %reshape.270), calls=%async_computation | async-start | bytes 294912 | tf_op jit(solution)/shard_map/all_to_all | solution.py:32
  22.4 1.8 all-gather
  24.6 2.0 all_gather.9
  26.6 1.8 all_gather.11
  28.5 3.9 %collective-permute-start.2 = (bf16[28,2,128]{2,1,0:T(2,128)(2,1)S(1)}, bf16[28,2,128]{2,1,0:T(2,128)(2,1)S(1)}, u32[]{:S(2)}, u32[]{:S(2)}) collective-permute-start(bf16[28,2,128]{2,1,0:T(2,128)(2,1)S(1)} %get-tuple-element.46), channel_id=1, source_target_pairs={{0,1},{1,2},{2,3},{4,5},{5,6},{6,7},{8,9},{9,10},{10,11},{12,13},{... | collective-permute-start | bytes 43016 | tf_op jit(solution)/shard_map/ppermute | solution.py:17
  32.4 1.3 collective-permute-start.3
  34.0 4.1 %collective-permute-done.3 = bf16[28,2,128]{2,1,0:T(2,128)(2,1)S(1)} collective-permute-done((bf16[28,2,128]{2,1,0:T(2,128)(2,1)S(1)}, bf16[28,2,128]{2,1,0:T(2,128)(2,1)S(1)}, u32[]{:S(2)}, u32[]{:S(2)}) %collective-permute-start.3) | collective-permute-done | bytes 14368 | tf_op jit(solution)/shard_map/ppermute | solution.py:18
  42.3 3.6 %all-to-all-start.3 = ((bf16[4,2,9216]{2,1,0:T(2,128)(2,1)}), bf16[4,2,9216]{2,1,0:T(2,128)(2,1)S(1)}, u32[]{:S(2)}, u32[]{:S(2)}) async-start(bf16[4,2,9216]{2,1,0:T(2,128)(2,1)} %reshape.264), calls=%async_computation.3 | async-start | bytes 294912 | tf_op jit(solution)/shard_map/all_to_all | solution.py:32
  46.3 1.2 reshape.272
  47.5 4.4 %all-to-all-done.3 = bf16[4,2,9216]{2,1,0:T(2,128)(2,1)S(1)} async-done(((bf16[4,2,9216]{2,1,0:T(2,128)(2,1)}), bf16[4,2,9216]{2,1,0:T(2,128)(2,1)S(1)}, u32[]{:S(2)}, u32[]{:S(2)}) %all-to-all-start.3) | async-done | bytes 147488 | tf_op jit(solution)/shard_map/all_to_all | solution.py:32
  51.9 4.9 %all-to-all-start.1 = ((bf16[4,2,9216]{2,1,0:T(2,128)(2,1)}), bf16[4,2,9216]{2,1,0:T(2,128)(2,1)S(1)}, u32[]{:S(2)}, u32[]{:S(2)}) async-start(bf16[4,2,9216]{2,1,0:T(2,128)(2,1)} %reshape.272), calls=%async_computation.1 | async-start | bytes 294912 | tf_op jit(solution)/shard_map/all_to_all | solution.py:33
  58.4 3.5 all-to-all-done.1
  61.8 3.3 all-to-all-start.4
  65.5 1.2 reshape.274
  66.8 3.5 all-to-all-done.4
  70.2 3.3 all-to-all-start.2
  75.1 4.4 %all-to-all-done.2 = bf16[4,2,9216]{2,1,0:T(2,128)(2,1)S(1)} async-done(((bf16[4,2,9216]{2,1,0:T(2,128)(2,1)}), bf16[4,2,9216]{2,1,0:T(2,128)(2,1)S(1)}, u32[]{:S(2)}, u32[]{:S(2)}) %all-to-all-start.2) | async-done | bytes 147488 | tf_op jit(solution)/shard_map/all_to_all | solution.py:34
  79.5 3.3 all-to-all-start.5
  84.6 4.2 %all-to-all-done.5 = bf16[4,2,9216]{2,1,0:T(2,128)(2,1)S(1)} async-done(((bf16[4,2,9216]{2,1,0:T(2,128)(2,1)}), bf16[4,2,9216]{2,1,0:T(2,128)(2,1)S(1)}, u32[]{:S(2)}, u32[]{:S(2)}) %all-to-all-start.5) | async-done | bytes 147488 | tf_op jit(solution)/shard_map/all_to_all | solution.py:34
  90.6 2.9 collective-permute-start.4
  93.5 1.3 collective-permute-start.5
  95.2 4.3 %collective-permute-done.5 = bf16[8,24,128]{2,0,1:T(8,128)(2,1)S(1)} collective-permute-done((bf16[8,24,128]{2,0,1:T(8,128)(2,1)S(1)}, bf16[8,24,128]{2,0,1:T(8,128)(2,1)S(1)}, u32[]{:S(2)}, u32[]{:S(2)}) %collective-permute-start.5) | collective-permute-done | bytes 49184 | tf_op jit(solution)/shard_map/ppermute | solution.py:18
  99.5 1.3 collective-permute-start.7
  100.8 4.7 %collective-permute-start.6 = (bf16[40,8,128]{2,0,1:T(8,128)(2,1)S(1)}, bf16[40,8,128]{2,0,1:T(8,128)(2,1)S(1)}, u32[]{:S(2)}, u32[]{:S(2)}) collective-permute-start(bf16[40,8,128]{2,0,1:T(8,128)(2,1)S(1)} %get-tuple-element.27), channel_id=1, source_target_pairs={{0,1},{1,2},{2,3},{4,5},{5,6},{6,7},{8,9},{9,10},{10,11},{12,13},{... | collective-permute-start | bytes 245768 | tf_op jit(solution)/shard_map/ppermute | solution.py:17
  105.8 1.6 collective-permute-done.6
  112.2 1.3 collective-permute-start.9
  113.4 4.9 %collective-permute-start.8 = (bf16[8,24,64]{2,1,0:T(8,128)(2,1)}, bf16[8,24,64]{2,1,0:T(8,128)(2,1)S(1)}, u32[]{:S(2)}, u32[]{:S(2)}) collective-permute-start(bf16[8,24,64]{2,1,0:T(8,128)(2,1)} %bitcast.441), channel_id=1, source_target_pairs={{0,4},{4,8},{8,12},{1,5},{5,9},{9,13},{2,6},{6,10},{10,14},{3,7},{... | collective-permute-start | bytes 73736 | tf_op jit(solution)/shard_map/ppermute | solution.py:17
  123.2 1.3 collective-permute-start.10
  124.5 4.9 %collective-permute-start.11 = (bf16[40,8,64]{2,1,0:T(8,128)(2,1)S(1)}, bf16[40,8,64]{2,1,0:T(8,128)(2,1)S(1)}, u32[]{:S(2)}, u32[]{:S(2)}) collective-permute-start(bf16[40,8,64]{2,1,0:T(8,128)(2,1)S(1)} %get-tuple-element.23), channel_id=1, source_target_pairs={{0,1},{1,2},{2,3},{4,5},{5,6},{6,7},{8,9},{9,10},{10,11},{12,13},{... | collective-permute-start | bytes 122888 | tf_op jit(solution)/shard_map/ppermute | solution.py:17
  129.9 1.6 collective-permute-done.11
  134.5 5.9 %all-to-all-start.6 = ((bf16[4,2,9216]{2,1,0:T(2,128)(2,1)}), bf16[4,2,9216]{2,1,0:T(2,128)(2,1)S(1)}, u32[]{:S(2)}, u32[]{:S(2)}) async-start(bf16[4,2,9216]{2,1,0:T(2,128)(2,1)} %reshape.276), calls=%async_computation.6 | async-start | bytes 294912 | tf_op jit(solution)/shard_map/all_to_all | solution.py:32
  140.4 1.7 fusion.17
  142.0 4.3 %all-to-all-done.6 = bf16[4,2,9216]{2,1,0:T(2,128)(2,1)S(1)} async-done(((bf16[4,2,9216]{2,1,0:T(2,128)(2,1)}), bf16[4,2,9216]{2,1,0:T(2,128)(2,1)S(1)}, u32[]{:S(2)}, u32[]{:S(2)}) %all-to-all-start.6) | async-done | bytes 147488 | tf_op jit(solution)/shard_map/all_to_all | solution.py:32
  147.9 4.2 %all-to-all-start.7 = ((bf16[4,2,9216]{2,1,0:T(2,128)(2,1)}), bf16[4,2,9216]{2,1,0:T(2,128)(2,1)S(1)}, u32[]{:S(2)}, u32[]{:S(2)}) async-start(bf16[4,2,9216]{2,1,0:T(2,128)(2,1)} %reshape.278), calls=%async_computation.7 | async-start | bytes 294912 | tf_op jit(solution)/shard_map/all_to_all | solution.py:33
  152.2 4.9 %all-to-all-done.7 = bf16[4,2,9216]{2,1,0:T(2,128)(2,1)S(1)} async-done(((bf16[4,2,9216]{2,1,0:T(2,128)(2,1)}), bf16[4,2,9216]{2,1,0:T(2,128)(2,1)S(1)}, u32[]{:S(2)}, u32[]{:S(2)}) %all-to-all-start.7) | async-done | bytes 147488 | tf_op jit(solution)/shard_map/all_to_all | solution.py:33
  158.7 3.3 all-to-all-start.8
  163.6 4.4 %all-to-all-done.8 = bf16[4,2,9216]{2,1,0:T(2,128)(2,1)S(1)} async-done(((bf16[4,2,9216]{2,1,0:T(2,128)(2,1)}), bf16[4,2,9216]{2,1,0:T(2,128)(2,1)S(1)}, u32[]{:S(2)}, u32[]{:S(2)}) %all-to-all-start.8) | async-done | bytes 147488 | tf_op jit(solution)/shard_map/all_to_all | solution.py:34
  170.8 39.1 %psum.22 = f32[2,64]{1,0:T(2,128)S(1)} all-reduce(f32[2,64]{1,0:T(2,128)S(1)} %pad_maximum_fusion.26), channel_id=1, replica_groups=mesh['segment'=2,'row'=4,'col'=4] {'segment','row','col'}, use_global_device_ids=true, to_apply=%region_3.4 | all-reduce | flops 128 | bytes 1024 | tf_op jit(solution)/shard_map/psum | solution.py:153
  210.0 1.3 collective-permute-start.13
  211.3 4.8 %collective-permute-start.12 = (bf16[2,24,64]{2,1,0:T(8,128)(2,1)S(1)}, bf16[2,24,64]{2,1,0:T(8,128)(2,1)S(1)}, u32[]{:S(2)}, u32[]{:S(2)}) collective-permute-start(bf16[2,24,64]{2,1,0:T(8,128)(2,1)S(1)} %bitcast.442), channel_id=1, source_target_pairs={{0,4},{4,8},{8,12},{1,5},{5,9},{9,13},{2,6},{6,10},{10,14},{3,7},{... | collective-permute-start | bytes 18440 | tf_op jit(solution)/shard_map/ppermute | solution.py:17
  219.7 1.3 collective-permute-start.14
  221.0 4.5 %collective-permute-start.15 = (bf16[28,2,64]{2,1,0:T(2,128)(2,1)S(1)}, bf16[28,2,64]{2,1,0:T(2,128)(2,1)S(1)}, u32[]{:S(2)}, u32[]{:S(2)}) collective-permute-start(bf16[28,2,64]{2,1,0:T(2,128)(2,1)S(1)} %get-tuple-element.43), channel_id=1, source_target_pairs={{0,1},{1,2},{2,3},{4,5},{5,6},{6,7},{8,9},{9,10},{10,11},{12,13},{... | collective-permute-start | bytes 21512 | tf_op jit(solution)/shard_map/ppermute | solution.py:17
  229.5 118.9 %all-reduce.3.cloned.1.call-done = (f32[2,9,128,64]{2,3,1,0:T(8,128)}, f32[2,64,128]{2,1,0:T(8,128)}) async-done(((f32[2,9,128,64]{2,3,1,0:T(8,128)}, f32[2,64,128]{2,1,0:T(8,128)}), (f32[2,9,128,64]{2,3,1,0:T(8,128)}, f32[2,64,128]{2,1,0:T(8,128)})) %all-reduce.3.cloned.1.call-update) | async-done | bytes 655376 | tf_op jit(solution)/shard_map/psum | solution.py:153
  348.4 1.7 dynamic-slice_multiply_fusion
  350.1 1.4 dynamic-slice_multiply_fusion.1
  (192 shorter events, 43.7 us)
Async XLA Ops:
  8.1 20.3 %collective-permute-start = (bf16[2,24,128]{2,1,0:T(8,128)(2,1)S(1)}, bf16[2,24,128]{2,1,0:T(8,128)(2,1)S(1)}, u32[]{:S(2)}, u32[]{:S(2)}) collective-permute-start(bf16[2,24,128]{2,1,0:T(8,128)(2,1)S(1)} %get-tuple-element.58), channel_id=1, source_target_pairs={{0,4},{4,8},{8,12},{1,5},{5,9},{9,13},{2,6},{6,10},{10,14},{3,7},{... | collective-permute-start | bytes 36872 | tf_op jit(solution)/shard_map/ppermute | solution.py:17
  13.0 15.5 %collective-permute-start.1 = (bf16[2,24,128]{2,1,0:T(8,128)(2,1)S(1)}, bf16[2,24,128]{2,1,0:T(8,128)(2,1)S(1)}, u32[]{:S(2)}, u32[]{:S(2)}) collective-permute-start(bf16[2,24,128]{2,1,0:T(8,128)(2,1)S(1)} %get-tuple-element.59), channel_id=1, source_target_pairs={{4,0},{8,4},{12,8},{5,1},{9,5},{13,9},{6,2},{10,6},{14,10},{7,3},{... | collective-permute-start | bytes 36872 | tf_op jit(solution)/shard_map/ppermute | solution.py:18
  15.4 6.2 %copy-start = (bf16[1,24,24,128]{3,2,1,0:T(8,128)(2,1)S(1)}, bf16[1,24,24,128]{3,2,1,0:T(8,128)(2,1)}, u32[]{:S(2)}) copy-start(bf16[1,24,24,128]{3,2,1,0:T(8,128)(2,1)} %param.5) | copy-start | bytes 442372
  15.5 6.9 %copy-start.15 = (bf16[1,64]{1,0:T(2,128)(2,1)S(1)}, bf16[1,64]{1,0:T(2,128)(2,1)}, u32[]{:S(2)}) copy-start(bf16[1,64]{1,0:T(2,128)(2,1)} %param.8) | copy-start | bytes 388
  15.5 9.2 %copy-start.12 = (bf16[1,9,128,64]{2,3,1,0:T(8,128)(2,1)S(1)}, bf16[1,9,128,64]{2,3,1,0:T(8,128)(2,1)}, u32[]{:S(2)}) copy-start(bf16[1,9,128,64]{2,3,1,0:T(8,128)(2,1)} %param.7) | copy-start | bytes 442372
  15.5 11.1 %copy-start.13 = (bf16[1,64,128]{2,1,0:T(8,128)(2,1)S(1)}, bf16[1,64,128]{2,1,0:T(8,128)(2,1)}, u32[]{:S(2)}) copy-start(bf16[1,64,128]{2,1,0:T(8,128)(2,1)} %param.9) | copy-start | bytes 49156
  16.8 25.5 %all-to-all-start = ((bf16[4,2,9216]{2,1,0:T(2,128)(2,1)}), bf16[4,2,9216]{2,1,0:T(2,128)(2,1)S(1)}, u32[]{:S(2)}, u32[]{:S(2)}) async-start(bf16[4,2,9216]{2,1,0:T(2,128)(2,1)} %reshape.270), calls=%async_computation | async-start | bytes 294912 | tf_op jit(solution)/shard_map/all_to_all | solution.py:32
  28.4 11.3 %copy-start.9 = (bf16[2,64,128]{2,1,0:T(8,128)(2,1)}, bf16[2,64,128]{2,1,0:T(8,128)(2,1)S(1)}, u32[]{:S(2)}) copy-start(bf16[2,64,128]{2,1,0:T(8,128)(2,1)S(1)} %all_gather.11) | copy-start | bytes 98308
  28.5 5.5 %collective-permute-start.2 = (bf16[28,2,128]{2,1,0:T(2,128)(2,1)S(1)}, bf16[28,2,128]{2,1,0:T(2,128)(2,1)S(1)}, u32[]{:S(2)}, u32[]{:S(2)}) collective-permute-start(bf16[28,2,128]{2,1,0:T(2,128)(2,1)S(1)} %get-tuple-element.46), channel_id=1, source_target_pairs={{0,1},{1,2},{2,3},{4,5},{5,6},{6,7},{8,9},{9,10},{10,11},{12,13},{... | collective-permute-start | bytes 43016 | tf_op jit(solution)/shard_map/ppermute | solution.py:17
  32.4 5.6 %collective-permute-start.3 = (bf16[28,2,128]{2,1,0:T(2,128)(2,1)S(1)}, bf16[28,2,128]{2,1,0:T(2,128)(2,1)S(1)}, u32[]{:S(2)}, u32[]{:S(2)}) collective-permute-start(bf16[28,2,128]{2,1,0:T(2,128)(2,1)S(1)} %get-tuple-element.47), channel_id=1, source_target_pairs={{1,0},{2,1},{3,2},{5,4},{6,5},{7,6},{9,8},{10,9},{11,10},{13,12},{... | collective-permute-start | bytes 43016 | tf_op jit(solution)/shard_map/ppermute | solution.py:18
  33.8 5.8 %copy-start.1 = (bf16[24,24,128]{2,1,0:T(8,128)(2,1)}, bf16[24,24,128]{2,1,0:T(8,128)(2,1)S(1)}, u32[]{:S(2)}) copy-start(bf16[24,24,128]{2,1,0:T(8,128)(2,1)S(1)} %get-tuple-element.56) | copy-start | bytes 442372
  42.3 9.6 %all-to-all-start.3 = ((bf16[4,2,9216]{2,1,0:T(2,128)(2,1)}), bf16[4,2,9216]{2,1,0:T(2,128)(2,1)S(1)}, u32[]{:S(2)}, u32[]{:S(2)}) async-start(bf16[4,2,9216]{2,1,0:T(2,128)(2,1)} %reshape.264), calls=%async_computation.3 | async-start | bytes 294912 | tf_op jit(solution)/shard_map/all_to_all | solution.py:32
  51.9 9.9 %all-to-all-start.1 = ((bf16[4,2,9216]{2,1,0:T(2,128)(2,1)}), bf16[4,2,9216]{2,1,0:T(2,128)(2,1)S(1)}, u32[]{:S(2)}, u32[]{:S(2)}) async-start(bf16[4,2,9216]{2,1,0:T(2,128)(2,1)} %reshape.272), calls=%async_computation.1 | async-start | bytes 294912 | tf_op jit(solution)/shard_map/all_to_all | solution.py:33
  61.8 8.4 %all-to-all-start.4 = ((bf16[4,2,9216]{2,1,0:T(2,128)(2,1)}), bf16[4,2,9216]{2,1,0:T(2,128)(2,1)S(1)}, u32[]{:S(2)}, u32[]{:S(2)}) async-start(bf16[4,2,9216]{2,1,0:T(2,128)(2,1)} %reshape.266), calls=%async_computation.4 | async-start | bytes 294912 | tf_op jit(solution)/shard_map/all_to_all | solution.py:33
  70.2 9.3 %all-to-all-start.2 = ((bf16[4,2,9216]{2,1,0:T(2,128)(2,1)}), bf16[4,2,9216]{2,1,0:T(2,128)(2,1)S(1)}, u32[]{:S(2)}, u32[]{:S(2)}) async-start(bf16[4,2,9216]{2,1,0:T(2,128)(2,1)} %reshape.274), calls=%async_computation.2 | async-start | bytes 294912 | tf_op jit(solution)/shard_map/all_to_all | solution.py:34
  79.5 9.3 %all-to-all-start.5 = ((bf16[4,2,9216]{2,1,0:T(2,128)(2,1)}), bf16[4,2,9216]{2,1,0:T(2,128)(2,1)S(1)}, u32[]{:S(2)}, u32[]{:S(2)}) async-start(bf16[4,2,9216]{2,1,0:T(2,128)(2,1)} %reshape.268), calls=%async_computation.5 | async-start | bytes 294912 | tf_op jit(solution)/shard_map/all_to_all | solution.py:34
  83.6 0.9 copy-start.6
  89.5 1.0 copy-start.4
  90.6 4.6 %collective-permute-start.4 = (bf16[8,24,128]{2,0,1:T(8,128)(2,1)S(1)}, bf16[8,24,128]{2,0,1:T(8,128)(2,1)S(1)}, u32[]{:S(2)}, u32[]{:S(2)}) collective-permute-start(bf16[8,24,128]{2,0,1:T(8,128)(2,1)S(1)} %get-tuple-element.54), channel_id=1, source_target_pairs={{0,4},{4,8},{8,12},{1,5},{5,9},{9,13},{2,6},{6,10},{10,14},{3,7},{... | collective-permute-start | bytes 147464 | tf_op jit(solution)/shard_map/ppermute | solution.py:17
  93.5 6.0 %collective-permute-start.5 = (bf16[8,24,128]{2,0,1:T(8,128)(2,1)S(1)}, bf16[8,24,128]{2,0,1:T(8,128)(2,1)S(1)}, u32[]{:S(2)}, u32[]{:S(2)}) collective-permute-start(bf16[8,24,128]{2,0,1:T(8,128)(2,1)S(1)} %get-tuple-element.55), channel_id=1, source_target_pairs={{4,0},{8,4},{12,8},{5,1},{9,5},{13,9},{6,2},{10,6},{14,10},{7,3},{... | collective-permute-start | bytes 147464 | tf_op jit(solution)/shard_map/ppermute | solution.py:18
  99.5 6.3 %collective-permute-start.7 = (bf16[40,8,128]{2,0,1:T(8,128)(2,1)S(1)}, bf16[40,8,128]{2,0,1:T(8,128)(2,1)S(1)}, u32[]{:S(2)}, u32[]{:S(2)}) collective-permute-start(bf16[40,8,128]{2,0,1:T(8,128)(2,1)S(1)} %get-tuple-element.26), channel_id=1, source_target_pairs={{1,0},{2,1},{3,2},{5,4},{6,5},{7,6},{9,8},{10,9},{11,10},{13,12},{... | collective-permute-start | bytes 245768 | tf_op jit(solution)/shard_map/ppermute | solution.py:18
  100.8 6.6 %collective-permute-start.6 = (bf16[40,8,128]{2,0,1:T(8,128)(2,1)S(1)}, bf16[40,8,128]{2,0,1:T(8,128)(2,1)S(1)}, u32[]{:S(2)}, u32[]{:S(2)}) collective-permute-start(bf16[40,8,128]{2,0,1:T(8,128)(2,1)S(1)} %get-tuple-element.27), channel_id=1, source_target_pairs={{0,1},{1,2},{2,3},{4,5},{5,6},{6,7},{8,9},{9,10},{10,11},{12,13},{... | collective-permute-start | bytes 245768 | tf_op jit(solution)/shard_map/ppermute | solution.py:17
  105.6 3.4 copy-start.3
  108.3 0.9 copy-start.14
  108.5 0.9 copy-start.10
  112.2 10.9 %collective-permute-start.9 = (bf16[8,24,64]{2,1,0:T(8,128)(2,1)}, bf16[8,24,64]{2,1,0:T(8,128)(2,1)S(1)}, u32[]{:S(2)}, u32[]{:S(2)}) collective-permute-start(bf16[8,24,64]{2,1,0:T(8,128)(2,1)} %bitcast.53), channel_id=1, source_target_pairs={{4,0},{8,4},{12,8},{5,1},{9,5},{13,9},{6,2},{10,6},{14,10},{7,3},{... | collective-permute-start | bytes 73736 | tf_op jit(solution)/shard_map/ppermute | solution.py:18
  113.4 9.7 %collective-permute-start.8 = (bf16[8,24,64]{2,1,0:T(8,128)(2,1)}, bf16[8,24,64]{2,1,0:T(8,128)(2,1)S(1)}, u32[]{:S(2)}, u32[]{:S(2)}) collective-permute-start(bf16[8,24,64]{2,1,0:T(8,128)(2,1)} %bitcast.441), channel_id=1, source_target_pairs={{0,4},{4,8},{8,12},{1,5},{5,9},{9,13},{2,6},{6,10},{10,14},{3,7},{... | collective-permute-start | bytes 73736 | tf_op jit(solution)/shard_map/ppermute | solution.py:17
  123.2 6.7 %collective-permute-start.10 = (bf16[40,8,64]{2,1,0:T(8,128)(2,1)S(1)}, bf16[40,8,64]{2,1,0:T(8,128)(2,1)S(1)}, u32[]{:S(2)}, u32[]{:S(2)}) collective-permute-start(bf16[40,8,64]{2,1,0:T(8,128)(2,1)S(1)} %get-tuple-element.22), channel_id=1, source_target_pairs={{1,0},{2,1},{3,2},{5,4},{6,5},{7,6},{9,8},{10,9},{11,10},{13,12},{... | collective-permute-start | bytes 122888 | tf_op jit(solution)/shard_map/ppermute | solution.py:18
  124.5 7.0 %collective-permute-start.11 = (bf16[40,8,64]{2,1,0:T(8,128)(2,1)S(1)}, bf16[40,8,64]{2,1,0:T(8,128)(2,1)S(1)}, u32[]{:S(2)}, u32[]{:S(2)}) collective-permute-start(bf16[40,8,64]{2,1,0:T(8,128)(2,1)S(1)} %get-tuple-element.23), channel_id=1, source_target_pairs={{0,1},{1,2},{2,3},{4,5},{5,6},{6,7},{8,9},{9,10},{10,11},{12,13},{... | collective-permute-start | bytes 122888 | tf_op jit(solution)/shard_map/ppermute | solution.py:17
  134.5 11.9 %all-to-all-start.6 = ((bf16[4,2,9216]{2,1,0:T(2,128)(2,1)}), bf16[4,2,9216]{2,1,0:T(2,128)(2,1)S(1)}, u32[]{:S(2)}, u32[]{:S(2)}) async-start(bf16[4,2,9216]{2,1,0:T(2,128)(2,1)} %reshape.276), calls=%async_computation.6 | async-start | bytes 294912 | tf_op jit(solution)/shard_map/all_to_all | solution.py:32
  147.9 9.2 %all-to-all-start.7 = ((bf16[4,2,9216]{2,1,0:T(2,128)(2,1)}), bf16[4,2,9216]{2,1,0:T(2,128)(2,1)S(1)}, u32[]{:S(2)}, u32[]{:S(2)}) async-start(bf16[4,2,9216]{2,1,0:T(2,128)(2,1)} %reshape.278), calls=%async_computation.7 | async-start | bytes 294912 | tf_op jit(solution)/shard_map/all_to_all | solution.py:33
  158.7 9.3 %all-to-all-start.8 = ((bf16[4,2,9216]{2,1,0:T(2,128)(2,1)}), bf16[4,2,9216]{2,1,0:T(2,128)(2,1)S(1)}, u32[]{:S(2)}, u32[]{:S(2)}) async-start(bf16[4,2,9216]{2,1,0:T(2,128)(2,1)} %reshape.280), calls=%async_computation.8 | async-start | bytes 294912 | tf_op jit(solution)/shard_map/all_to_all | solution.py:34
  162.1 186.3 %all-reduce.3.cloned.1.call-start = ((), (), s32[]{:S(2)}) async-start(), calls=%async_computation.9 | async-start | bytes 1310720 | tf_op jit(solution)/shard_map/psum | solution.py:153
  168.7 1.0 copy-start.5
  168.8 1.2 copy-start.11
  170.3 46.9 %copy-start.2 = (bf16[24,24,128]{2,1,0:T(8,128)(2,1)S(1)}, bf16[24,24,128]{2,1,0:T(8,128)(2,1)}, u32[]{:S(2)}) copy-start(bf16[24,24,128]{2,1,0:T(8,128)(2,1)} %copy-done.1) | copy-start | bytes 442372
  170.7 47.4 %copy-start.7 = (f32[9,128,64]{1,2,0:T(8,128)S(1)}, f32[9,128,64]{1,2,0:T(8,128)}, u32[]{:S(2)}) copy-start(f32[9,128,64]{1,2,0:T(8,128)} %fusion.16) | copy-start | bytes 884740
  210.0 9.7 %collective-permute-start.13 = (bf16[2,24,64]{2,1,0:T(8,128)(2,1)S(1)}, bf16[2,24,64]{2,1,0:T(8,128)(2,1)S(1)}, u32[]{:S(2)}, u32[]{:S(2)}) collective-permute-start(bf16[2,24,64]{2,1,0:T(8,128)(2,1)S(1)} %bitcast.443), channel_id=1, source_target_pairs={{4,0},{8,4},{12,8},{5,1},{9,5},{13,9},{6,2},{10,6},{14,10},{7,3},{... | collective-permute-start | bytes 18440 | tf_op jit(solution)/shard_map/ppermute | solution.py:18
  211.3 8.3 %collective-permute-start.12 = (bf16[2,24,64]{2,1,0:T(8,128)(2,1)S(1)}, bf16[2,24,64]{2,1,0:T(8,128)(2,1)S(1)}, u32[]{:S(2)}, u32[]{:S(2)}) collective-permute-start(bf16[2,24,64]{2,1,0:T(8,128)(2,1)S(1)} %bitcast.442), channel_id=1, source_target_pairs={{0,4},{4,8},{8,12},{1,5},{5,9},{9,13},{2,6},{6,10},{10,14},{3,7},{... | collective-permute-start | bytes 18440 | tf_op jit(solution)/shard_map/ppermute | solution.py:17
  219.7 6.1 %collective-permute-start.14 = (bf16[28,2,64]{2,1,0:T(2,128)(2,1)S(1)}, bf16[28,2,64]{2,1,0:T(2,128)(2,1)S(1)}, u32[]{:S(2)}, u32[]{:S(2)}) collective-permute-start(bf16[28,2,64]{2,1,0:T(2,128)(2,1)S(1)} %get-tuple-element.42), channel_id=1, source_target_pairs={{1,0},{2,1},{3,2},{5,4},{6,5},{7,6},{9,8},{10,9},{11,10},{13,12},{... | collective-permute-start | bytes 21512 | tf_op jit(solution)/shard_map/ppermute | solution.py:18
  221.0 6.0 %collective-permute-start.15 = (bf16[28,2,64]{2,1,0:T(2,128)(2,1)S(1)}, bf16[28,2,64]{2,1,0:T(2,128)(2,1)S(1)}, u32[]{:S(2)}, u32[]{:S(2)}) collective-permute-start(bf16[28,2,64]{2,1,0:T(2,128)(2,1)S(1)} %get-tuple-element.43), channel_id=1, source_target_pairs={{0,1},{1,2},{2,3},{4,5},{5,6},{6,7},{8,9},{9,10},{10,11},{12,13},{... | collective-permute-start | bytes 21512 | tf_op jit(solution)/shard_map/ppermute | solution.py:17
  227.8 0.9 copy-start.8
Sparse Core Ops, SparseCore 0:
  219.8 128.5 all-reduce.2
where the time goes:
time: 360 us; the launch traced here: 358 us
  waiting for transfers between devices  166 us (46%)
  starting transfers between devices  82.7 us (23%)
  blocking collectives  44.7 us (12%)
  local copies, waits for them, and re-layouts  23.1 us (6%)
  matrix products  17.4 us (5%)
  between operations  15.1 us (4%)
  other arithmetic  9.61 us (3%)
    psum x1, waiting for transfers between devices, local(): lax.psum((conv_both, bias_both, proj_both), ('segment', 'row', 'col'))  119 us
    psum x1, blocking collectives, local(): lax.psum((conv_both, bias_both, proj_both), ('segment', 'row', 'col'))  39.1 us
    ppermute x8, starting transfers between devices, extended(): before = lax.ppermute(last, axis, up)  35.5 us
    all_to_all x6, starting transfers between devices, mirror(): lax.all_to_all(groups, 'col', split_axis=2, concat_axis=2, tiled=True)  24.4 us
    all_to_all x6, waiting for transfers between devices, mirror(): lax.all_to_all(groups, 'col', split_axis=2, concat_axis=2, tiled=True)  21.6 us
    unnamed x56, local copies, waits for them, and re-layouts  15.5 us
    all_to_all x3, starting transfers between devices, mirror(): lax.all_to_all(groups, 'row', split_axis=2, concat_axis=2, tiled=True)  12.4 us
    all_to_all x3, waiting for transfers between devices, mirror(): lax.all_to_all(groups, 'row', split_axis=2, concat_axis=2, tiled=True)  11.9 us
  transfers between devices with their start and end apart: 26, of which 17 were waited for; matrix products, arithmetic and copies ran while one was open for 8% of the time, Pallas kernels for 0%

commit v1 on v0

v1 whole, which is shorter than its diff:
```python
import jax
import jax.numpy as jnp
from jax import lax
from jax.sharding import PartitionSpec as P

FIRST_DILATION = 2
SECOND_DILATION = 8
HALO = FIRST_DILATION + SECOND_DILATION
GATHER_LIMIT = 16
GRID = ("row", "col")


def mirror_pairs():
    number = lax.axis_size("row")
    return [(r * number + c, c * number + r) for r in range(number) for c in range(number)]


def extended(x, width):
    for axis, dim in (("row", 0), ("col", 1)):
        count, length = (lax.axis_size(axis), x.shape[dim])
        up = [(i, i + 1) for i in range(count - 1)]
        down = [(j, i) for i, j in up]
        last = lax.slice_in_dim(x, length - width, length, axis=dim)
        first = lax.slice_in_dim(x, 0, width, axis=dim)
        before = lax.ppermute(last, axis, up)
        after = lax.ppermute(first, axis, down)
        x = jnp.concatenate([before, x, after], axis=dim)
    return x


def both_regions(tile, width):
    number, side, channels = lax.axis_size("row"), tile.shape[0], tile.shape[2]
    if number * number > GATHER_LIMIT:
        mirrored = jnp.swapaxes(lax.ppermute(tile, GRID, mirror_pairs()), 0, 1)
        return extended(jnp.concatenate([tile, mirrored], axis=2), width)
    tiles = lax.all_gather(tile, GRID)
    whole = tiles.reshape(number, number, side, side, channels).transpose(0, 2, 1, 3, 4)
    whole = whole.reshape(number * side, number * side, channels)
    whole = jnp.pad(whole, ((width, width), (width, width), (0, 0)))
    at_row, at_col = lax.axis_index("row") * side, lax.axis_index("col") * side
    size = (side + 2 * width, side + 2 * width, channels)
    own = lax.dynamic_slice(whole, (at_row, at_col, 0), size)
    other = lax.dynamic_slice(whole, (at_col, at_row, 0), size)
    return jnp.concatenate([own, jnp.swapaxes(other, 0, 1)], axis=2)


def inside(side, width):
    number = lax.axis_size("row") * side
    index = jnp.arange(side + 2 * width) - width
    rows = index + lax.axis_index("row") * side
    cols = index + lax.axis_index("col") * side
    rows = (rows >= 0) & (rows < number)
    cols = (cols >= 0) & (cols < number)
    return (rows[:, None] & cols[None, :])[:, :, None]


def middle(x, width):
    return x[width : x.shape[0] - width, width : x.shape[1] - width]


def window(x, dilation, a, b):
    rows, cols = x.shape[0] - 2 * dilation, x.shape[1] - 2 * dilation
    top, left = dilation * (1 + a), dilation * (1 + b)
    return x[top : top + rows, left : left + cols].reshape(rows * cols, x.shape[2])


TAPS = [(a, b) for a in (-1, 0, 1) for b in (-1, 0, 1)]


def tap(a, b):
    return 3 * (a + 1) + (b + 1)


def dot(x, y, dims=((1,), (0,))):
    return lax.dot_general(x, y, (dims, ((), ())), preferred_element_type=jnp.float32)


def diagonal(x, y):
    return jnp.block([[x, jnp.zeros((x.shape[0], y.shape[1]), x.dtype)], [jnp.zeros((y.shape[0], x.shape[1]), x.dtype), y]])


def half_sum(x, y):
    return ((x.astype(jnp.float32) + y.astype(jnp.float32)) * 0.5).astype(jnp.bfloat16)


def weight_grads(hidden, dilation, grad_pre, bottle, grad_branch):
    rows = [dot(grad_pre, window(hidden, dilation, a, b), ((0,), (0,))) for a, b in TAPS]
    rows.append(dot(bottle, grad_branch, ((0,), (0,))))
    return jnp.concatenate(rows), jnp.sum(grad_pre.astype(jnp.float32), axis=0)


def local(activations, cotangent, conv_weight, conv_bias, out_weight):
    side, channels, inner = activations.shape[1], activations.shape[3], conv_weight.shape[3]
    number = lax.axis_size("row")
    first, second = FIRST_DILATION, SECOND_DILATION

    bias_rows = jnp.pad(conv_bias, ((0, 7), (0, channels - inner)))
    packed = jnp.concatenate(
        [jnp.swapaxes(conv_weight[0], 1, 2).reshape(9 * inner, channels), out_weight[0], bias_rows]
    )
    packed = lax.all_gather(packed, "segment")
    conv = packed[:, : 9 * inner].reshape(2, 9, inner, channels)
    proj = packed[:, 9 * inner : 10 * inner]
    bias = packed[:, 10 * inner, :inner].astype(jnp.float32)

    tile = jnp.concatenate([activations[0], cotangent[0]], axis=2)
    mirrored = jnp.swapaxes(lax.ppermute(tile, GRID, mirror_pairs()), 0, 1)
    grad_branch = half_sum(tile[..., channels:], mirrored[..., channels:])
    stacked = extended(jnp.concatenate([tile[..., :channels], mirrored[..., :channels], grad_branch], axis=2), HALO)
    grad_branch = middle(stacked[..., 2 * channels :], second)
    both = stacked[..., : 2 * channels]

    hidden = jnp.maximum(both, 0)
    span = side + 2 * second
    pre_first = jnp.tile(bias[0], 2)
    for a, b in TAPS:
        weight = diagonal(conv[0, tap(a, b)].T, conv[0, tap(b, a)].T)
        pre_first = pre_first + dot(window(hidden, first, a, b), weight)
    bottle_first = jnp.maximum(pre_first, 0).astype(jnp.bfloat16)
    branch = dot(bottle_first, diagonal(proj[0], proj[0])).reshape(span, span, 2 * channels)
    branch = (middle(both, first).astype(jnp.float32) + branch).astype(jnp.bfloat16)
    current = jnp.where(inside(side, second), half_sum(branch[..., :channels], branch[..., channels:]), 0)
    pre_first = pre_first[:, :inner].reshape(span, span, inner)
    bottle_first = bottle_first[:, :inner].reshape(span, span, inner)

    hidden_second = jnp.maximum(current, 0)
    pre_second = bias[1]
    for a, b in TAPS:
        pre_second = pre_second + dot(window(hidden_second, second, a, b), conv[1, tap(a, b)], ((1,), (1,)))
    bottle_second = jnp.maximum(pre_second, 0).astype(jnp.bfloat16)
    grad_tile = middle(grad_branch, first).reshape(side * side, channels)
    grad_pre = jnp.where(pre_second > 0, dot(grad_tile, proj[1], ((1,), (1,))), 0).astype(jnp.bfloat16)
    around = both_regions(grad_pre.reshape(side, side, inner), HALO)
    second_sums = weight_grads(hidden_second, second, grad_pre, bottle_second, grad_tile)

    near = side + 2 * first
    summed = 0
    for a, b in TAPS:
        weight = diagonal(conv[1, tap(a, b)], conv[1, tap(b, a)])
        summed = summed + dot(window(around, second, -a, -b), weight)
    summed = summed.reshape(near, near, 2 * channels)
    positive = middle(current, second - first) > 0
    up_own, up_other = (
        (grad_branch.astype(jnp.float32) + jnp.where(positive, part, 0)).astype(jnp.bfloat16)
        for part in (summed[..., :channels], summed[..., channels:])
    )
    grad_branch = half_sum(up_own, up_other)

    alive = (middle(pre_first, second - first) > 0) & inside(side, first)
    grad_pre = dot(grad_branch.reshape(near * near, channels), proj[0], ((1,), (1,))).reshape(near, near, inner)
    grad_pre = jnp.where(alive, grad_pre, 0).astype(jnp.bfloat16)
    grad_tile = middle(grad_branch, first).reshape(side * side, channels)
    first_sums = weight_grads(
        middle(hidden[..., :channels], second),
        first,
        middle(grad_pre, first).reshape(side * side, inner),
        middle(bottle_first, second).reshape(side * side, inner),
        grad_tile,
    )

    devices = number * number
    share = -(-10 * inner // (8 * devices)) * 8
    parts = []
    for rows, ends in (first_sums, second_sums):
        rows = jnp.pad(rows, ((0, share * devices - 10 * inner), (0, 0))).reshape(devices, share, channels)
        ends = jnp.pad(ends[None], ((0, 7), (0, channels - inner)))
        parts.append(jnp.concatenate([rows, jnp.broadcast_to(ends, (devices, 8, channels))], axis=1))
    parts = jnp.concatenate(parts).astype(jnp.bfloat16)
    parts = lax.all_to_all(parts, ("segment",) + GRID, 0, 0, tiled=True)

    summed = 0
    for a, b in TAPS:
        summed = summed + dot(window(grad_pre, first, -a, -b), conv[0, tap(a, b)])
    masked = jnp.where(activations[0].reshape(side * side, channels) > 0, summed, 0)
    input_gradient = (grad_tile.astype(jnp.float32) + masked).astype(jnp.bfloat16).reshape(1, side, side, channels)

    cells = lax.axis_size("segment") * (side * number) * (side * number)
    total = jnp.sum(parts.astype(jnp.float32), axis=0) * (1.0 / jnp.sqrt(jnp.float32(cells)))
    rows = lax.all_gather(total[:share], GRID, tiled=True)
    conv_gradient = jnp.swapaxes(rows[: 9 * inner].reshape(1, 9, inner, channels), 2, 3)
    return (input_gradient, conv_gradient, total[share : share + 1, :inner], rows[None, 9 * inner : 10 * inner])


def solution(mesh):
    in_specs = (
        P("segment", "row", "col", None),
        P("segment", "row", "col", None),
        P("segment", None, None, None),
        P("segment", None),
        P("segment", None, None),
    )
    out_specs = (
        P("segment", "row", "col", None),
        P("segment", None, None, None),
        P("segment", None),
        P("segment", None, None),
    )
    return jax.shard_map(local, mesh=mesh, in_specs=in_specs, out_specs=out_specs, check_vma=False)
```

time: 360 us -> 245 us (0.68)
  waiting for transfers between devices: 166 us -> 76.6 us
  starting transfers between devices: 82.7 us -> 32.5 us
  matrix products: 17.4 us -> 30.8 us
  local copies, waits for them, and re-layouts: 23.1 us -> 33.4 us
  other arithmetic: 9.61 us -> 13.7 us
    psum x1 -> x0, waiting for transfers between devices: 119 us -> none  [local(): lax.psum((conv_both, bias_both, proj_both), ('segment', 'row', 'col'))]
    all_gather x0 -> x1, waiting for transfers between devices: none -> 51 us  [both_regions(): tiles = lax.all_gather(tile, GRID)]
    psum x1 -> x0, blocking collectives: 39.1 us -> none  [local(): lax.psum((conv_both, bias_both, proj_both), ('segment', 'row', 'col'))]
    all_gather x3 -> x2, blocking collectives: 5.58 us -> 41.7 us  [the longest x1 39.5 us: local(): rows = lax.all_gather(total[:share], GRID, tiled=True)]
    all_to_all x9 -> x1, starting transfers between devices: 36.8 us -> 3.41 us  [local(): parts = lax.all_to_all(parts, ('segment',) + GRID, 0, 0, tiled=True)]
    all_to_all x9 -> x1, waiting for transfers between devices: 33.5 us -> 11.1 us  [local(): parts = lax.all_to_all(parts, ('segment',) + GRID, 0, 0, tiled=True)]
    reshape x0 -> x11, local copies, waits for them, and re-layouts: none -> 14 us  [the longest x9 10.7 us: window(): return x[top:top + rows, left:left + cols].reshape(rows * cols, x.shape[2])]
    unnamed x56 -> x63, local copies, waits for them, and re-layouts: 15.5 us -> 1.89 us
  transfers between devices with their start and end apart: 26 -> 7, of which waited for: 17 -> 6; matrix products, arithmetic and copies ran while one was open for 8% -> 8% of each run, Pallas kernels for 0% -> 0%
where the time goes in v1:
time: 245 us; the launch traced here: 244 us
  waiting for transfers between devices  76.6 us (31%)
  blocking collectives  41.7 us (17%)
  local copies, waits for them, and re-layouts  33.4 us (14%)
  starting transfers between devices  32.5 us (13%)
  matrix products  30.8 us (13%)
  between operations  14.9 us (6%)
  other arithmetic  13.7 us (6%)
    all_gather x1, waiting for transfers between devices, both_regions(): tiles = lax.all_gather(tile, GRID)  51 us
    all_gather x1, blocking collectives, local(): rows = lax.all_gather(total[:share], GRID, tiled=True)  39.5 us
    dot_general x59, matrix products, dot(): lax.dot_general(x, y, (dims, ((), ())), preferred_element_type=jnp.float32)  30.8 us
    ppermute x2, starting transfers between devices, extended(): before = lax.ppermute(last, axis, up)  25.8 us
    all_to_all x1, waiting for transfers between devices, local(): parts = lax.all_to_all(parts, ('segment',) + GRID, 0, 0, tiled=True)  11.1 us
    slice x12, local copies, waits for them, and re-layouts, window(): return x[top:top + rows, left:left + cols].reshape(rows * cols, x.shape[2])  10.8 us
    reshape x9, local copies, waits for them, and re-layouts, window(): return x[top:top + rows, left:left + cols].reshape(rows * cols, x.shape[2])  10.7 us
    ppermute x2, waiting for transfers between devices, extended(): after = lax.ppermute(first, axis, down)  8.92 us
  transfers between devices with their start and end apart: 7, of which 6 were waited for; matrix products, arithmetic and copies ran while one was open for 8% of the time, Pallas kernels for 0%

profile of v1, /device:TPU:0, one launch (start us, length us, event | category | flops | bytes accessed | tf_op | source)
XLA Modules:
  0.0 243.6 jit_solution(878970508558027118)
XLA Ops:
  7.2 1.1 copy_bitcast_fusion
  9.0 1.0 fusion.43
  10.0 2.1 all-gather
  13.1 24.5 %collective-permute-start.1 = (bf16[10,24,384]{2,1,0:T(8,128)(2,1)S(1)}, bf16[10,24,384]{2,1,0:T(8,128)(2,1)S(1)}, u32[]{:S(2)}, u32[]{:S(2)}) collective-permute-start(bf16[10,24,384]{2,1,0:T(8,128)(2,1)S(1)} %get-tuple-element.28), channel_id=1, source_target_pairs={{0,4},{4,8},{8,12},{1,5},{5,9},{9,13},{2,6},{6,10},{10,14},{3,7},{... | collective-permute-start | bytes 552968 | tf_op jit(solution)/shard_map/ppermute | solution.py:25
  37.6 1.3 collective-permute-start.2
  39.5 1.1 collective-permute-done.1
  40.7 4.7 %collective-permute-done.2 = bf16[10,24,384]{2,1,0:T(8,128)(2,1)S(1)} collective-permute-done((bf16[10,24,384]{2,1,0:T(8,128)(2,1)S(1)}, bf16[10,24,384]{2,1,0:T(8,128)(2,1)S(1)}, u32[]{:S(2)}, u32[]{:S(2)}) %collective-permute-start.2) | collective-permute-done | bytes 184352 | tf_op jit(solution)/shard_map/ppermute | solution.py:26
  45.7 1.3 collective-permute-start.3
  47.1 1.3 collective-permute-start.4
  49.3 4.5 %collective-permute-done.3 = bf16[44,10,384]{2,0,1:T(8,128)(2,1)S(1)} collective-permute-done((bf16[44,10,384]{2,0,1:T(8,128)(2,1)S(1)}, bf16[44,10,384]{2,0,1:T(8,128)(2,1)S(1)}, u32[]{:S(2)}, u32[]{:S(2)}) %collective-permute-start.3) | collective-permute-done | bytes 337952 | tf_op jit(solution)/shard_map/ppermute | solution.py:25
  53.8 4.2 %collective-permute-done.4 = bf16[44,10,384]{2,0,1:T(8,128)(2,1)} collective-permute-done((bf16[44,10,384]{2,0,1:T(8,128)(2,1)S(1)}, bf16[44,10,384]{2,0,1:T(8,128)(2,1)}, u32[]{:S(2)}, u32[]{:S(2)}) %collective-permute-start.4) | collective-permute-done | bytes 337952 | tf_op jit(solution)/shard_map/ppermute | solution.py:26
  58.1 1.1 copy.37
  59.2 3.2 %pad_maximum_fusion = bf16[44,44,384]{2,1,0:T(8,128)(2,1)S(1)} fusion(bf16[44,10,384]{2,1,0:T(8,128)(2,1)S(1)} %copy.37, bf16[10,24,384]{2,1,0:T(8,128)(2,1)S(1)} %collective-permute-done.2, bf16[24,24,128]{2,1,0:T(8,128)(2,1)S(1)} %fusion.42, bf16[24,24,128]{2,1,0:T(8,128)(2,1)S(1)} %slice.440, bf16[24,24,128]{2,1,0:T(8,128)(2,1)S(1)} %bitcast.288, ...), kind=kLoop, calls=%fused_computation.12 | loop fusion | flops 10407936 | bytes 2973696 | tf_op jit(solution)/shard_map/concatenate | solution.py:27
  62.5 1.8 fusion.319
  67.3 1.3 maximum_convert_fusion
  69.7 1.1 broadcast_maximum_fusion
  72.8 1.0 convert_reduce_fusion.2
  76.0 1.7 fusion.33
  77.7 1.7 fusion.32
  79.4 1.7 fusion.31
  81.0 1.7 fusion.30
  83.5 1.7 fusion.28
  87.4 51.0 %all-gather.3.cloned.1.call-done = bf16[16,24,24,64]{3,2,1,0:T(8,128)(2,1)} async-done(((bf16[1,24,24,64]{3,2,1,0:T(8,128)(2,1)}), bf16[16,24,24,64]{3,2,1,0:T(8,128)(2,1)}) %all-gather.3.cloned.1.call-update) | async-done | bytes 1179664 | tf_op jit(solution)/shard_map/all_gather | solution.py:36
  138.4 2.1 copy.39
  140.5 1.1 pad_dynamic-slice_fusion.1
  141.7 2.0 pad_maximum_fusion.3
  144.5 1.6 reshape.302
  146.2 1.7 copy.42
  147.9 1.7 reshape.303
  149.5 1.7 copy.43
  151.2 1.7 reshape.304
  152.9 1.7 copy.44
  154.6 1.6 reshape.305
  156.3 1.7 copy.45
  158.0 1.6 reshape.306
  160.4 1.7 reshape.307
  163.2 1.2 fusion.124
  164.4 1.2 convolution_add_fusion.16
  168.3 1.2 convolution_add_fusion.9
  169.4 1.2 reshape.311
  170.7 1.3 multiply_convert_fusion.1
  172.0 1.0 fusion
  175.4 1.1 fusion.24
  176.6 1.7 maximum_maximum_fusion
  178.3 3.4 %all-to-all-start = ((bf16[32,48,128]{2,1,0:T(8,128)(2,1)}), bf16[32,48,128]{2,1,0:T(8,128)(2,1)S(1)}, u32[]{:S(2)}, u32[]{:S(2)}) async-start(bf16[32,48,128]{2,1,0:T(8,128)(2,1)} %maximum_maximum_fusion), calls=%async_computation | async-start | bytes 786432 | tf_op jit(solution)/shard_map/all_to_all | solution.py:169
  183.4 0.9 fusion.3
  184.2 11.1 %all-to-all-done = bf16[32,48,128]{2,1,0:T(8,128)(2,1)S(1)} async-done(((bf16[32,48,128]{2,1,0:T(8,128)(2,1)}), bf16[32,48,128]{2,1,0:T(8,128)(2,1)S(1)}, u32[]{:S(2)}, u32[]{:S(2)}) %all-to-all-start) | async-done | bytes 393248 | tf_op jit(solution)/shard_map/all_to_all | solution.py:169
  195.4 39.5 %all_gather.15 = f32[640,128]{1,0:T(8,128)S(1)} all-gather(f32[40,128]{1,0:T(8,128)S(1)} %slice.532), channel_id=1, replica_groups=mesh['segment'=2,'row'=4,'col'=4] {'row','col'}, dimensions={0}, use_global_device_ids=true | all-gather | bytes 348160 | tf_op jit(solution)/shard_map/all_gather | solution.py:179
  (159 shorter events, 26.1 us)
Async XLA Ops:
  7.2 5.1 %copy-start = (bf16[1,24,24,128]{3,2,1,0:T(8,128)(2,1)S(1)}, bf16[1,24,24,128]{3,2,1,0:T(8,128)(2,1)}, u32[]{:S(2)}) copy-start(bf16[1,24,24,128]{3,2,1,0:T(8,128)(2,1)} %param.5) | copy-start | bytes 442372
  7.2 131.2 %all-gather.3.cloned.1.call-start = ((), (), s32[]{:S(2)}) async-start(), calls=%async_computation.1 | async-start | bytes 2506752 | tf_op jit(solution)/shard_map/all_gather | solution.py:36
  8.3 4.6 %collective-permute-start = (bf16[24,24,256]{2,0,1:T(8,128)(2,1)S(1)}, bf16[24,24,256]{2,0,1:T(8,128)(2,1)S(1)}, u32[]{:S(2)}, u32[]{:S(2)}) collective-permute-start(bf16[24,24,256]{2,0,1:T(8,128)(2,1)S(1)} %pad_maximum_fusion.2), channel_id=1, source_target_pairs={{0,0},{1,4},{2,8},{3,12},{4,1},{5,5},{6,9},{7,13},{8,2},{9,6},{10,... | collective-permute-start | bytes 884744 | tf_op jit(solution)/shard_map/ppermute | solution.py:107
  12.1 36.3 %copy-start.13 = (bf16[1296,128]{1,0:T(8,128)(2,1)}, bf16[1296,128]{1,0:T(8,128)(2,1)S(1)}, u32[]{:S(2)}) copy-start(bf16[1296,128]{1,0:T(8,128)(2,1)S(1)} %all-gather) | copy-start | bytes 995332
  13.1 27.6 %collective-permute-start.1 = (bf16[10,24,384]{2,1,0:T(8,128)(2,1)S(1)}, bf16[10,24,384]{2,1,0:T(8,128)(2,1)S(1)}, u32[]{:S(2)}, u32[]{:S(2)}) collective-permute-start(bf16[10,24,384]{2,1,0:T(8,128)(2,1)S(1)} %get-tuple-element.28), channel_id=1, source_target_pairs={{0,4},{4,8},{8,12},{1,5},{5,9},{9,13},{2,6},{6,10},{10,14},{3,7},{... | collective-permute-start | bytes 552968 | tf_op jit(solution)/shard_map/ppermute | solution.py:25
  37.6 7.8 %collective-permute-start.2 = (bf16[10,24,384]{2,1,0:T(8,128)(2,1)S(1)}, bf16[10,24,384]{2,1,0:T(8,128)(2,1)S(1)}, u32[]{:S(2)}, u32[]{:S(2)}) collective-permute-start(bf16[10,24,384]{2,1,0:T(8,128)(2,1)S(1)} %get-tuple-element.29), channel_id=1, source_target_pairs={{4,0},{8,4},{12,8},{5,1},{9,5},{13,9},{6,2},{10,6},{14,10},{7,3},{... | collective-permute-start | bytes 552968 | tf_op jit(solution)/shard_map/ppermute | solution.py:26
  40.7 18.5 %copy-start.3 = (bf16[10,24,384]{2,1,0:T(8,128)(2,1)}, bf16[10,24,384]{2,1,0:T(8,128)(2,1)S(1)}, u32[]{:S(2)}) copy-start(bf16[10,24,384]{2,1,0:T(8,128)(2,1)S(1)} %collective-permute-done.1) | copy-start | bytes 552964
  45.4 13.8 %copy-start.4 = (bf16[10,24,384]{2,1,0:T(8,128)(2,1)}, bf16[10,24,384]{2,1,0:T(8,128)(2,1)S(1)}, u32[]{:S(2)}) copy-start(bf16[10,24,384]{2,1,0:T(8,128)(2,1)S(1)} %collective-permute-done.2) | copy-start | bytes 552964
  45.7 8.0 %collective-permute-start.3 = (bf16[44,10,384]{2,0,1:T(8,128)(2,1)S(1)}, bf16[44,10,384]{2,0,1:T(8,128)(2,1)S(1)}, u32[]{:S(2)}, u32[]{:S(2)}) collective-permute-start(bf16[44,10,384]{2,0,1:T(8,128)(2,1)S(1)} %copy.34), channel_id=1, source_target_pairs={{0,1},{1,2},{2,3},{4,5},{5,6},{6,7},{8,9},{9,10},{10,11},{12,13},{... | collective-permute-start | bytes 1013768 | tf_op jit(solution)/shard_map/ppermute | solution.py:25
  47.1 10.9 %collective-permute-start.4 = (bf16[44,10,384]{2,0,1:T(8,128)(2,1)S(1)}, bf16[44,10,384]{2,0,1:T(8,128)(2,1)}, u32[]{:S(2)}, u32[]{:S(2)}) collective-permute-start(bf16[44,10,384]{2,0,1:T(8,128)(2,1)S(1)} %copy.35), channel_id=1, source_target_pairs={{1,0},{2,1},{3,2},{5,4},{6,5},{7,6},{9,8},{10,9},{11,10},{13,12},{... | collective-permute-start | bytes 1013768 | tf_op jit(solution)/shard_map/ppermute | solution.py:26
  48.5 24.1 %copy-start.1 = (bf16[2,576,128]{2,1,0:T(8,128)(2,1)}, bf16[2,576,128]{2,1,0:T(8,128)(2,1)S(1)}, u32[]{:S(2)}) copy-start(bf16[2,576,128]{2,1,0:T(8,128)(2,1)S(1)} %slice.449) | copy-start | bytes 884740
  68.6 0.7 copy-start.5
  71.0 1.3 copy-start.6
  71.0 1.3 copy-start.7
  71.0 1.3 copy-start.9
  71.1 1.3 copy-start.10
  71.1 1.3 copy-start.11
  71.1 1.3 copy-start.12
  72.8 9.9 %copy-start.8 = (bf16[24,24,128]{2,1,0:T(8,128)(2,1)S(1)}, bf16[24,24,128]{2,1,0:T(8,128)(2,1)}, u32[]{:S(2)}) copy-start(bf16[24,24,128]{2,1,0:T(8,128)(2,1)} %copy-done.7) | copy-start | bytes 442372
  163.1 2.6 %copy-start.23 = (bf16[64,128]{1,0:T(8,128)(2,1)S(1)}, bf16[64,128]{1,0:T(8,128)(2,1)}, u32[]{:S(2)}) copy-start(bf16[64,128]{1,0:T(8,128)(2,1)} %get-tuple-element.50) | copy-start | bytes 49156
  163.1 2.6 %copy-start.24 = (bf16[64,128]{1,0:T(8,128)(2,1)S(1)}, bf16[64,128]{1,0:T(8,128)(2,1)}, u32[]{:S(2)}) copy-start(bf16[64,128]{1,0:T(8,128)(2,1)} %get-tuple-element.54) | copy-start | bytes 49156
  163.1 2.5 %copy-start.18 = (bf16[784,128]{1,0:T(8,128)(2,1)S(1)}, bf16[784,128]{1,0:T(8,128)(2,1)}, u32[]{:S(2)}) copy-start(bf16[784,128]{1,0:T(8,128)(2,1)} %reshape.304) | copy-start | bytes 602116
  164.4 1.6 copy-start.15
  164.4 1.6 copy-start.25
  164.4 1.6 copy-start.26
  165.7 0.9 copy-start.16
  165.7 0.9 copy-start.28
  166.0 1.0 copy-start.19
  166.6 1.0 copy-start.17
  167.5 0.7 copy-start.27
  170.6 1.3 copy-start.14
  170.6 1.3 copy-start.30
  172.0 3.4 %copy-start.20 = (bf16[28,28,128]{2,1,0:T(8,128)(2,1)}, bf16[28,28,128]{2,1,0:T(8,128)(2,1)S(1)}, u32[]{:S(2)}) copy-start(bf16[28,28,128]{2,1,0:T(8,128)(2,1)S(1)} %multiply_convert_fusion.1) | copy-start | bytes 602116
  174.6 1.9 copy-start.29
  175.1 6.6 %copy-start.2 = (bf16[2,576,128]{2,1,0:T(8,128)(2,1)S(1)}, bf16[2,576,128]{2,1,0:T(8,128)(2,1)}, u32[]{:S(2)}) copy-start(bf16[2,576,128]{2,1,0:T(8,128)(2,1)} %copy-done.1) | copy-start | bytes 884740
  178.3 17.0 %all-to-all-start = ((bf16[32,48,128]{2,1,0:T(8,128)(2,1)}), bf16[32,48,128]{2,1,0:T(8,128)(2,1)S(1)}, u32[]{:S(2)}, u32[]{:S(2)}) async-start(bf16[32,48,128]{2,1,0:T(8,128)(2,1)} %maximum_maximum_fusion), calls=%async_computation | async-start | bytes 786432 | tf_op jit(solution)/shard_map/all_to_all | solution.py:169
  182.0 0.9 copy-start.21
  182.4 1.0 copy-start.22
Sparse Core Ops, SparseCore 0:
  74.8 63.5 all-gather.2

commit v2 on v1

--- a/solution.py
+++ b/solution.py
@@ -6,7 +6,6 @@
 FIRST_DILATION = 2
 SECOND_DILATION = 8
 HALO = FIRST_DILATION + SECOND_DILATION
-GATHER_LIMIT = 16
 GRID = ("row", "col")
 
 
@@ -15,33 +14,42 @@
     return [(r * number + c, c * number + r) for r in range(number) for c in range(number)]
 
 
+def neighbours(strip_first, strip_last, axis):
+    count = lax.axis_size(axis)
+    up = [(i, i + 1) for i in range(count - 1)]
+    down = [(j, i) for i, j in up]
+    return lax.ppermute(strip_last, axis, up), lax.ppermute(strip_first, axis, down)
+
+
 def extended(x, width):
-    for axis, dim in (("row", 0), ("col", 1)):
-        count, length = (lax.axis_size(axis), x.shape[dim])
-        up = [(i, i + 1) for i in range(count - 1)]
-        down = [(j, i) for i, j in up]
-        last = lax.slice_in_dim(x, length - width, length, axis=dim)
-        first = lax.slice_in_dim(x, 0, width, axis=dim)
-        before = lax.ppermute(last, axis, up)
-        after = lax.ppermute(first, axis, down)
-        x = jnp.concatenate([before, x, after], axis=dim)
-    return x
-
-
-def both_regions(tile, width):
-    number, side, channels = lax.axis_size("row"), tile.shape[0], tile.shape[2]
-    if number * number > GATHER_LIMIT:
-        mirrored = jnp.swapaxes(lax.ppermute(tile, GRID, mirror_pairs()), 0, 1)
-        return extended(jnp.concatenate([tile, mirrored], axis=2), width)
-    tiles = lax.all_gather(tile, GRID)
-    whole = tiles.reshape(number, number, side, side, channels).transpose(0, 2, 1, 3, 4)
-    whole = whole.reshape(number * side, number * side, channels)
-    whole = jnp.pad(whole, ((width, width), (width, width), (0, 0)))
-    at_row, at_col = lax.axis_index("row") * side, lax.axis_index("col") * side
-    size = (side + 2 * width, side + 2 * width, channels)
-    own = lax.dynamic_slice(whole, (at_row, at_col, 0), size)
-    other = lax.dynamic_slice(whole, (at_col, at_row, 0), size)
-    return jnp.concatenate([own, jnp.swapaxes(other, 0, 1)], axis=2)
+    length = x.shape[0]
+    before, after = neighbours(x[:width], x[length - width :], "row")
+    x = jnp.concatenate([before, x, after])
+    length = x.shape[1]
+    before, after = neighbours(jnp.swapaxes(x[:, :width], 0, 1), jnp.swapaxes(x[:, length - width :], 0, 1), "col")
+    return jnp.concatenate([jnp.swapaxes(before, 0, 1), x, jnp.swapaxes(after, 0, 1)], axis=1)
+
+
+def extended_pair(x, y, width, narrow):
+    side, channels = x.shape[0], x.shape[2]
+    strips = neighbours(
+        jnp.concatenate([x[:width], y[:narrow]]), jnp.concatenate([x[side - width :], y[side - narrow :]]), "row"
+    )
+    x = jnp.concatenate([strips[0][:width], x, strips[1][:width]])
+    y = jnp.concatenate([strips[0][width:], y, strips[1][width:]])
+    gap = ((0, 0), (width - narrow, width - narrow), (0, 0))
+
+    def strip(at, to, low, high):
+        first = jnp.swapaxes(x[:, at:to], 0, 1)
+        second = jnp.swapaxes(y[:, low:high], 0, 1)
+        return jnp.concatenate([first, jnp.pad(second, gap)])
+
+    strips = neighbours(strip(0, width, 0, narrow), strip(side - width, side, side - narrow, side), "col")
+    before, after = (jnp.swapaxes(part, 0, 1) for part in strips)
+    inner = slice(width - narrow, before.shape[0] - width + narrow)
+    x = jnp.concatenate([before[:, :width], x, after[:, :width]], axis=1)
+    y = jnp.concatenate([before[inner, width:], y, after[inner, width:]], axis=1)
+    return x, y
 
 
 def inside(side, width):
@@ -103,12 +111,18 @@
     proj = packed[:, 9 * inner : 10 * inner]
     bias = packed[:, 10 * inner, :inner].astype(jnp.float32)
 
-    tile = jnp.concatenate([activations[0], cotangent[0]], axis=2)
+    tile = activations[0]
     mirrored = jnp.swapaxes(lax.ppermute(tile, GRID, mirror_pairs()), 0, 1)
-    grad_branch = half_sum(tile[..., channels:], mirrored[..., channels:])
-    stacked = extended(jnp.concatenate([tile[..., :channels], mirrored[..., :channels], grad_branch], axis=2), HALO)
-    grad_branch = middle(stacked[..., 2 * channels :], second)
-    both = stacked[..., : 2 * channels]
+    stacked = jnp.concatenate([tile, mirrored], axis=2)
+    before, after = neighbours(stacked[:HALO], stacked[side - HALO :], "row")
+    before, after, late = lax.optimization_barrier((before, after, cotangent[0]))
+    stacked = jnp.concatenate([before, stacked, after])
+    left, right = neighbours(
+        jnp.swapaxes(stacked[:, :HALO], 0, 1), jnp.swapaxes(stacked[:, side - HALO :], 0, 1), "col"
+    )
+    mirrored = jnp.swapaxes(lax.ppermute(late, GRID, mirror_pairs()), 0, 1)
+    grad_branch = half_sum(late, mirrored)
+    both = jnp.concatenate([jnp.swapaxes(left, 0, 1), stacked, jnp.swapaxes(right, 0, 1)], axis=1)
 
     hidden = jnp.maximum(both, 0)
     span = side + 2 * second
@@ -128,9 +142,15 @@
     for a, b in TAPS:
         pre_second = pre_second + dot(window(hidden_second, second, a, b), conv[1, tap(a, b)], ((1,), (1,)))
     bottle_second = jnp.maximum(pre_second, 0).astype(jnp.bfloat16)
-    grad_tile = middle(grad_branch, first).reshape(side * side, channels)
+    grad_tile = grad_branch.reshape(side * side, channels)
     grad_pre = jnp.where(pre_second > 0, dot(grad_tile, proj[1], ((1,), (1,))), 0).astype(jnp.bfloat16)
-    around = both_regions(grad_pre.reshape(side, side, inner), HALO)
+    square = grad_pre.reshape(side, side, inner)
+    half = side // 2
+    sent = jnp.concatenate([square[:half], square[half:]], axis=2)
+    sent = lax.ppermute(sent, GRID, mirror_pairs())
+    mirrored = jnp.concatenate([sent[..., :inner], sent[..., inner:]])
+    around = jnp.concatenate([square, jnp.swapaxes(mirrored, 0, 1)], axis=2)
+    around, grad_branch = extended_pair(around, grad_branch, HALO, first)
     second_sums = weight_grads(hidden_second, second, grad_pre, bottle_second, grad_tile)
 
     near = side + 2 * first
@@ -176,7 +196,8 @@
 
     cells = lax.axis_size("segment") * (side * number) * (side * number)
     total = jnp.sum(parts.astype(jnp.float32), axis=0) * (1.0 / jnp.sqrt(jnp.float32(cells)))
-    rows = lax.all_gather(total[:share], GRID, tiled=True)
+    rows = jnp.broadcast_to(total[None, :share], (devices, share, channels))
+    rows = lax.all_to_all(rows, GRID, 0, 0, tiled=True).reshape(devices * share, channels)
     conv_gradient = jnp.swapaxes(rows[: 9 * inner].reshape(1, 9, inner, channels), 2, 3)
     return (input_gradient, conv_gradient, total[share : share + 1, :inner], rows[None, 9 * inner : 10 * inner])
 

time: 245 us -> 145 us (0.59)
  blocking collectives: 41.7 us -> 2.13 us
  waiting for transfers between devices: 76.6 us -> 45.9 us
  starting transfers between devices: 32.5 us -> 49.1 us
  local copies, waits for them, and re-layouts: 33.4 us -> 18.7 us
  between operations: 14.9 us -> 1.63 us
  matrix products: 30.8 us -> 18.3 us
  other arithmetic: 13.7 us -> 8.09 us
    all_gather x1 -> x0, waiting for transfers between devices: 51 us -> none  [both_regions(): tiles = lax.all_gather(tile, GRID)]
    all_gather x1 -> x0, blocking collectives: 39.5 us -> none  [local(): rows = lax.all_gather(total[:share], GRID, tiled=True)]
    dot_general x59, matrix products: 30.8 us -> 18.3 us  [dot(): lax.dot_general(x, y, (dims, ((), ())), preferred_element_type=jnp.float32)]
    all_to_all x0 -> x1, waiting for transfers between devices: none -> 9.77 us  [local(): lax.all_to_all(rows, GRID, 0, 0, tiled=True)]
    ppermute x4 -> x10, starting transfers between devices: 28.4 us -> 37.5 us  [the longest x4 31 us: neighbours(): lax.ppermute(strip_last, axis, up)]
    ppermute x4 -> x10, waiting for transfers between devices: 14.5 us -> 23.5 us  [the longest x4 17 us: neighbours(): lax.ppermute(strip_first, axis, down)]
    slice x12 -> x6, local copies, waits for them, and re-layouts: 10.8 us -> 3.78 us  [window(): return x[top:top + rows, left:left + cols].reshape(rows * cols, x.shape[2])]
    reshape x9, local copies, waits for them, and re-layouts: 10.7 us -> 4.35 us  [window(): return x[top:top + rows, left:left + cols].reshape(rows * cols, x.shape[2])]
  transfers between devices with their start and end apart: 7 -> 13, of which waited for: 6 -> 10; matrix products, arithmetic and copies ran while one was open for 8% -> 6% of each run, Pallas kernels for 0% -> 0%
where the time goes in v2:
time: 145 us; the launch traced here: 144 us
  starting transfers between devices  49.1 us (34%)
  waiting for transfers between devices  45.9 us (32%)
  local copies, waits for them, and re-layouts  18.7 us (13%)
  matrix products  18.3 us (13%)
  other arithmetic  8.09 us (6%)
  blocking collectives  2.13 us (1%)
  between operations  1.63 us (1%)
    ppermute x4, starting transfers between devices, neighbours(): lax.ppermute(strip_last, axis, up)  31 us
    dot_general x59, matrix products, dot(): lax.dot_general(x, y, (dims, ((), ())), preferred_element_type=jnp.float32)  18.3 us
    ppermute x4, waiting for transfers between devices, neighbours(): lax.ppermute(strip_first, axis, down)  17 us
    all_to_all x1, waiting for transfers between devices, local(): parts = lax.all_to_all(parts, ('segment',) + GRID, 0, 0, tiled=True)  12.5 us
    all_to_all x1, waiting for transfers between devices, local(): lax.all_to_all(rows, GRID, 0, 0, tiled=True)  9.77 us
    all_to_all x1, starting transfers between devices, local(): parts = lax.all_to_all(parts, ('segment',) + GRID, 0, 0, tiled=True)  7.23 us
    ppermute x4, waiting for transfers between devices, neighbours(): lax.ppermute(strip_last, axis, up)  6.5 us
    ppermute x4, starting transfers between devices, neighbours(): lax.ppermute(strip_first, axis, down)  5.17 us
  transfers between devices with their start and end apart: 13, of which 10 were waited for; matrix products, arithmetic and copies ran while one was open for 6% of the time, Pallas kernels for 0%

profile of v2, /device:TPU:0, one launch (start us, length us, event | category | flops | bytes accessed | tf_op | source)
XLA Modules:
  0.0 143.8 jit_solution(11706044050195148659)
XLA Ops:
  0.6 1.0 copy.30
  1.6 0.7 collective-permute-start
  2.3 1.0 fusion.46
  3.3 2.1 %all-gather = bf16[1296,128]{1,0:T(8,128)(2,1)S(1)} all-gather(bf16[648,128]{1,0:T(8,128)(2,1)S(1)} %fusion.46), channel_id=2, replica_groups=mesh['segment'=2,'row'=4,'col'=4] {'segment'}, dimensions={0}, use_global_device_ids=true | all-gather | bytes 497664 | tf_op jit(solution)/shard_map/all_gather | solution.py:109
  5.5 0.7 broadcast_compare_fusion
  6.2 0.7 slice_bitcast_fusion.7
  7.1 14.1 %collective-permute-start.1 = (bf16[10,24,256]{2,1,0:T(8,128)(2,1)S(1)}, bf16[10,24,256]{2,1,0:T(8,128)(2,1)S(1)}, u32[]{:S(2)}, u32[]{:S(2)}) collective-permute-start(bf16[10,24,256]{2,1,0:T(8,128)(2,1)S(1)} %get-tuple-element.66), channel_id=1, source_target_pairs={{0,4},{4,8},{8,12},{1,5},{5,9},{9,13},{2,6},{6,10},{10,14},{3,7},{... | collective-permute-start | bytes 368648 | tf_op jit(solution)/shard_map/ppermute | solution.py:21
  21.2 1.3 collective-permute-start.2
  22.5 0.7 broadcast_and_fusion.1
  23.7 4.4 %collective-permute-done.2 = bf16[10,24,256]{2,1,0:T(8,128)(2,1)S(1)} collective-permute-done((bf16[10,24,256]{2,1,0:T(8,128)(2,1)S(1)}, bf16[10,24,256]{2,1,0:T(8,128)(2,1)S(1)}, u32[]{:S(2)}, u32[]{:S(2)}) %collective-permute-start.2) | collective-permute-done | bytes 122912 | tf_op jit(solution)/shard_map/ppermute | solution.py:21
  28.0 0.7 collective-permute-start.5
  28.9 5.5 %collective-permute-start.3 = (bf16[10,44,256]{2,0,1:T(8,128)(2,1)S(1)}, bf16[10,44,256]{2,0,1:T(8,128)(2,1)S(1)}, u32[]{:S(2)}, u32[]{:S(2)}) collective-permute-start(bf16[10,44,256]{2,0,1:T(8,128)(2,1)S(1)} %get-tuple-element.26), channel_id=1, source_target_pairs={{0,1},{1,2},{2,3},{4,5},{5,6},{6,7},{8,9},{9,10},{10,11},{12,13},{... | collective-permute-start | bytes 675848 | tf_op jit(solution)/shard_map/ppermute | solution.py:21
  34.5 1.3 collective-permute-start.4
  35.9 4.0 %collective-permute-done.3 = bf16[10,44,256]{2,0,1:T(8,128)(2,1)S(1)} collective-permute-done((bf16[10,44,256]{2,0,1:T(8,128)(2,1)S(1)}, bf16[10,44,256]{2,0,1:T(8,128)(2,1)S(1)}, u32[]{:S(2)}, u32[]{:S(2)}) %collective-permute-start.3) | collective-permute-done | bytes 225312 | tf_op jit(solution)/shard_map/ppermute | solution.py:21
  39.9 7.4 %collective-permute-done.4 = bf16[10,44,256]{2,0,1:T(8,128)(2,1)S(1)} collective-permute-done((bf16[10,44,256]{2,0,1:T(8,128)(2,1)S(1)}, bf16[10,44,256]{2,0,1:T(8,128)(2,1)S(1)}, u32[]{:S(2)}, u32[]{:S(2)}) %collective-permute-start.4) | collective-permute-done | bytes 225312 | tf_op jit(solution)/shard_map/ppermute | solution.py:21
  47.3 0.6 broadcast_maximum_fusion
  48.0 1.6 %fusion.327 = (bf16[40,40,256]{2,1,0:T(8,128)(2,1)S(1)}, bf16[40,40,256]{2,1,0:T(8,128)(2,1)S(1)}, bf16[40,40,256]{2,1,0:T(8,128)(2,1)S(1)}, bf16[40,40,256]{2,1...) fusion(bf16[44,44,256]{2,1,0:T(8,128)(2,1)S(1)} %get-tuple-elem, ...), kind=kLoop, calls=%fused_computation.424 | loop fusion | bytes 14745600 | tf_op jit(solution)/shard_map/slice | solution.py:72
  52.6 1.3 maximum_convert_fusion
  54.7 1.1 broadcast_maximum_fusion.1
  57.6 1.0 convert_reduce_fusion.2
  59.3 0.7 collective-permute-start.6
  61.6 6.6 %collective-permute-start.7 = (bf16[12,24,128]{2,1,0:T(8,128)(2,1)S(1)}, bf16[12,24,128]{2,1,0:T(8,128)(2,1)S(1)}, u32[]{:S(2)}, u32[]{:S(2)}) collective-permute-start(bf16[12,24,128]{2,1,0:T(8,128)(2,1)S(1)} %get-tuple-element.63), channel_id=1, source_target_pairs={{0,4},{4,8},{8,12},{1,5},{5,9},{9,13},{2,6},{6,10},{10,14},{3,7},{... | collective-permute-start | bytes 221192 | tf_op jit(solution)/shard_map/ppermute | solution.py:21
  68.3 1.3 collective-permute-start.8
  70.2 4.8 %collective-permute-done.8 = bf16[12,24,128]{2,1,0:T(8,128)(2,1)S(1)} collective-permute-done((bf16[12,24,128]{2,1,0:T(8,128)(2,1)S(1)}, bf16[12,24,128]{2,1,0:T(8,128)(2,1)S(1)}, u32[]{:S(2)}, u32[]{:S(2)}) %collective-permute-start.8) | collective-permute-done | bytes 73760 | tf_op jit(solution)/shard_map/ppermute | solution.py:21
  75.9 1.3 collective-permute-start.10
  77.3 4.7 %collective-permute-start.9 = (bf16[12,44,128]{2,0,1:T(8,128)(2,1)S(1)}, bf16[12,44,128]{2,0,1:T(8,128)(2,1)S(1)}, u32[]{:S(2)}, u32[]{:S(2)}) collective-permute-start(bf16[12,44,128]{2,0,1:T(8,128)(2,1)S(1)} %fusion.44), channel_id=1, source_target_pairs={{0,1},{1,2},{2,3},{4,5},{5,6},{6,7},{8,9},{9,10},{10,11},{12,13},{... | collective-permute-start | bytes 405512 | tf_op jit(solution)/shard_map/ppermute | solution.py:21
  82.2 0.7 pad_convert_fusion
  83.3 1.5 %collective-permute-done.9 = bf16[12,44,128]{2,0,1:T(8,128)(2,1)S(1)} collective-permute-done((bf16[12,44,128]{2,0,1:T(8,128)(2,1)S(1)}, bf16[12,44,128]{2,0,1:T(8,128)(2,1)S(1)}, u32[]{:S(2)}, u32[]{:S(2)}) %collective-permute-start.9) | collective-permute-done | bytes 135200 | tf_op jit(solution)/shard_map/ppermute | solution.py:21
  86.1 0.6 slice.569
  86.8 0.8 fusion.330
  87.7 1.7 %reshape.304 = bf16[784,128]{1,0:T(8,128)(2,1)} reshape(bf16[28,28,128]{2,1,0:T(8,128)(2,1)} %get-tuple-element.33) | data formatting | bytes 401408 | tf_op jit(solution)/shard_map/reshape | solution.py:72
  89.3 0.9 fusion.329
  90.2 1.7 %reshape.306 = bf16[784,128]{1,0:T(8,128)(2,1)} reshape(bf16[28,28,128]{2,1,0:T(8,128)(2,1)} %get-tuple-element.30) | data formatting | bytes 401408 | tf_op jit(solution)/shard_map/reshape | solution.py:72
  91.9 0.7 reshape.307
  93.3 1.2 fusion.132
  94.8 0.6 copy-done.6
  99.0 1.2 multiply_convert_fusion.1
  100.2 0.9 fusion
  103.6 1.1 fusion.24
  104.8 0.8 maximum_maximum_fusion.1
  105.6 7.2 %all-to-all-start = ((bf16[32,48,128]{2,1,0:T(8,128)(2,1)}), bf16[32,48,128]{2,1,0:T(8,128)(2,1)S(1)}, u32[]{:S(2)}, u32[]{:S(2)}) async-start(bf16[32,48,128]{2,1,0:T(8,128)(2,1)} %maximum_maximum_fusion.1), calls=%async_computation | async-start | bytes 786432 | tf_op jit(solution)/shard_map/all_to_all | solution.py:189
  113.9 12.5 %all-to-all-done = bf16[32,48,128]{2,1,0:T(8,128)(2,1)S(1)} async-done(((bf16[32,48,128]{2,1,0:T(8,128)(2,1)}), bf16[32,48,128]{2,1,0:T(8,128)(2,1)S(1)}, u32[]{:S(2)}, u32[]{:S(2)}) %all-to-all-start) | async-done | bytes 393248 | tf_op jit(solution)/shard_map/all_to_all | solution.py:189
  126.5 0.7 broadcast_in_dim.60
  127.3 3.7 %all-to-all-start.1 = ((f32[16,40,128]{2,1,0:T(8,128)}), f32[16,40,128]{2,1,0:T(8,128)S(1)}, u32[]{:S(2)}, u32[]{:S(2)}) async-start(f32[16,40,128]{2,1,0:T(8,128)} %broadcast_in_dim.60), calls=%async_computation.1 | async-start | bytes 655360 | tf_op jit(solution)/shard_map/all_to_all | solution.py:200
  131.3 0.9 fusion.3
  132.7 9.8 %all-to-all-done.1 = f32[16,40,128]{2,1,0:T(8,128)S(1)} async-done(((f32[16,40,128]{2,1,0:T(8,128)}), f32[16,40,128]{2,1,0:T(8,128)S(1)}, u32[]{:S(2)}, u32[]{:S(2)}) %all-to-all-start.1) | async-done | bytes 327712 | tf_op jit(solution)/shard_map/all_to_all | solution.py:200
  142.5 0.7 slice.610
  143.2 0.6 slice_bitcast_fusion.4
  (168 shorter events, 21.0 us)
Async XLA Ops:
  0.6 4.9 %copy-start = (bf16[1,24,24,128]{3,2,1,0:T(8,128)(2,1)S(1)}, bf16[1,24,24,128]{3,2,1,0:T(8,128)(2,1)}, u32[]{:S(2)}) copy-start(bf16[1,24,24,128]{3,2,1,0:T(8,128)(2,1)} %param.5) | copy-start | bytes 442372
  1.6 5.4 %collective-permute-start = (bf16[24,24,128]{2,0,1:T(8,128)(2,1)S(1)}, bf16[24,24,128]{2,0,1:T(8,128)(2,1)S(1)}, u32[]{:S(2)}, u32[]{:S(2)}) collective-permute-start(bf16[24,24,128]{2,0,1:T(8,128)(2,1)S(1)} %bitcast.401), channel_id=1, source_target_pairs={{0,0},{1,4},{2,8},{3,12},{4,1},{5,5},{6,9},{7,13},{8,2},{9,6},{10,... | collective-permute-start | bytes 442376 | tf_op jit(solution)/shard_map/ppermute | solution.py:115
  2.3 4.6 %copy-start.16 = (bf16[1,24,24,128]{3,2,1,0:T(8,128)(2,1)S(1)}, bf16[1,24,24,128]{3,2,1,0:T(8,128)(2,1)}, u32[]{:S(2)}) copy-start(bf16[1,24,24,128]{3,2,1,0:T(8,128)(2,1)} %param.6) | copy-start | bytes 442372
  5.5 1.7 %copy-start.2 = (bf16[1296,128]{1,0:T(8,128)(2,1)}, bf16[1296,128]{1,0:T(8,128)(2,1)S(1)}, u32[]{:S(2)}) copy-start(bf16[1296,128]{1,0:T(8,128)(2,1)S(1)} %all-gather) | copy-start | bytes 995332
  7.1 16.5 %collective-permute-start.1 = (bf16[10,24,256]{2,1,0:T(8,128)(2,1)S(1)}, bf16[10,24,256]{2,1,0:T(8,128)(2,1)S(1)}, u32[]{:S(2)}, u32[]{:S(2)}) collective-permute-start(bf16[10,24,256]{2,1,0:T(8,128)(2,1)S(1)} %get-tuple-element.66), channel_id=1, source_target_pairs={{0,4},{4,8},{8,12},{1,5},{5,9},{9,13},{2,6},{6,10},{10,14},{3,7},{... | collective-permute-start | bytes 368648 | tf_op jit(solution)/shard_map/ppermute | solution.py:21
  21.2 6.8 %collective-permute-start.2 = (bf16[10,24,256]{2,1,0:T(8,128)(2,1)S(1)}, bf16[10,24,256]{2,1,0:T(8,128)(2,1)S(1)}, u32[]{:S(2)}, u32[]{:S(2)}) collective-permute-start(bf16[10,24,256]{2,1,0:T(8,128)(2,1)S(1)} %get-tuple-element.65), channel_id=1, source_target_pairs={{4,0},{8,4},{12,8},{5,1},{9,5},{13,9},{6,2},{10,6},{14,10},{7,3},{... | collective-permute-start | bytes 368648 | tf_op jit(solution)/shard_map/ppermute | solution.py:21
  28.0 7.7 %collective-permute-start.5 = (bf16[24,24,128]{2,0,1:T(8,128)(2,1)S(1)}, bf16[24,24,128]{2,0,1:T(8,128)(2,1)S(1)}, u32[]{:S(2)}, u32[]{:S(2)}) collective-permute-start(bf16[24,24,128]{2,0,1:T(8,128)(2,1)S(1)} %bitcast.380), channel_id=1, source_target_pairs={{0,0},{1,4},{2,8},{3,12},{4,1},{5,5},{6,9},{7,13},{8,2},{9,6},{10,... | collective-permute-start | bytes 442376 | tf_op jit(solution)/shard_map/ppermute | solution.py:123
  28.9 11.0 %collective-permute-start.3 = (bf16[10,44,256]{2,0,1:T(8,128)(2,1)S(1)}, bf16[10,44,256]{2,0,1:T(8,128)(2,1)S(1)}, u32[]{:S(2)}, u32[]{:S(2)}) collective-permute-start(bf16[10,44,256]{2,0,1:T(8,128)(2,1)S(1)} %get-tuple-element.26), channel_id=1, source_target_pairs={{0,1},{1,2},{2,3},{4,5},{5,6},{6,7},{8,9},{9,10},{10,11},{12,13},{... | collective-permute-start | bytes 675848 | tf_op jit(solution)/shard_map/ppermute | solution.py:21
  34.5 12.9 %collective-permute-start.4 = (bf16[10,44,256]{2,0,1:T(8,128)(2,1)S(1)}, bf16[10,44,256]{2,0,1:T(8,128)(2,1)S(1)}, u32[]{:S(2)}, u32[]{:S(2)}) collective-permute-start(bf16[10,44,256]{2,0,1:T(8,128)(2,1)S(1)} %get-tuple-element.27), channel_id=1, source_target_pairs={{1,0},{2,1},{3,2},{5,4},{6,5},{7,6},{9,8},{10,9},{11,10},{13,12},{... | collective-permute-start | bytes 675848 | tf_op jit(solution)/shard_map/ppermute | solution.py:21
  53.9 0.8 copy-start.1
  59.3 2.0 %collective-permute-start.6 = (bf16[12,24,128]{2,0,1:T(8,128)(2,1)S(1)}, bf16[12,24,128]{2,0,1:T(8,128)(2,1)S(1)}, u32[]{:S(2)}, u32[]{:S(2)}) collective-permute-start(bf16[12,24,128]{2,0,1:T(8,128)(2,1)S(1)} %pad_maximum_fusion.7), channel_id=1, source_target_pairs={{0,0},{1,4},{2,8},{3,12},{4,1},{5,5},{6,9},{7,13},{8,2},{9,6},{10,... | collective-permute-start | bytes 221192 | tf_op jit(solution)/shard_map/ppermute | solution.py:150
  61.6 8.6 %collective-permute-start.7 = (bf16[12,24,128]{2,1,0:T(8,128)(2,1)S(1)}, bf16[12,24,128]{2,1,0:T(8,128)(2,1)S(1)}, u32[]{:S(2)}, u32[]{:S(2)}) collective-permute-start(bf16[12,24,128]{2,1,0:T(8,128)(2,1)S(1)} %get-tuple-element.63), channel_id=1, source_target_pairs={{0,4},{4,8},{8,12},{1,5},{5,9},{9,13},{2,6},{6,10},{10,14},{3,7},{... | collective-permute-start | bytes 221192 | tf_op jit(solution)/shard_map/ppermute | solution.py:21
  68.3 6.8 %collective-permute-start.8 = (bf16[12,24,128]{2,1,0:T(8,128)(2,1)S(1)}, bf16[12,24,128]{2,1,0:T(8,128)(2,1)S(1)}, u32[]{:S(2)}, u32[]{:S(2)}) collective-permute-start(bf16[12,24,128]{2,1,0:T(8,128)(2,1)S(1)} %get-tuple-element.64), channel_id=1, source_target_pairs={{4,0},{8,4},{12,8},{5,1},{9,5},{13,9},{6,2},{10,6},{14,10},{7,3},{... | collective-permute-start | bytes 221192 | tf_op jit(solution)/shard_map/ppermute | solution.py:21
  75.3 0.6 copy-start.17
  75.9 7.4 %collective-permute-start.10 = (bf16[12,44,128]{2,0,1:T(8,128)(2,1)S(1)}, bf16[12,44,128]{2,0,1:T(8,128)(2,1)S(1)}, u32[]{:S(2)}, u32[]{:S(2)}) collective-permute-start(bf16[12,44,128]{2,0,1:T(8,128)(2,1)S(1)} %fusion.45), channel_id=1, source_target_pairs={{1,0},{2,1},{3,2},{5,4},{6,5},{7,6},{9,8},{10,9},{11,10},{13,12},{... | collective-permute-start | bytes 405512 | tf_op jit(solution)/shard_map/ppermute | solution.py:21
  77.3 7.5 %collective-permute-start.9 = (bf16[12,44,128]{2,0,1:T(8,128)(2,1)S(1)}, bf16[12,44,128]{2,0,1:T(8,128)(2,1)S(1)}, u32[]{:S(2)}, u32[]{:S(2)}) collective-permute-start(bf16[12,44,128]{2,0,1:T(8,128)(2,1)S(1)} %fusion.44), channel_id=1, source_target_pairs={{0,1},{1,2},{2,3},{4,5},{5,6},{6,7},{8,9},{9,10},{10,11},{12,13},{... | collective-permute-start | bytes 405512 | tf_op jit(solution)/shard_map/ppermute | solution.py:21
  82.2 3.2 %copy-start.8 = (bf16[640,128]{1,0:T(8,128)(2,1)}, bf16[640,128]{1,0:T(8,128)(2,1)S(1)}, u32[]{:S(2)}) copy-start(bf16[640,128]{1,0:T(8,128)(2,1)S(1)} %fusion.25) | copy-start | bytes 491524
  90.2 2.5 %copy-start.3 = (bf16[28,28,128]{2,1,0:T(8,128)(2,1)S(1)}, bf16[28,28,128]{2,1,0:T(8,128)(2,1)}, u32[]{:S(2)}) copy-start(bf16[28,28,128]{2,1,0:T(8,128)(2,1)} %get-tuple-element.29) | copy-start | bytes 602116
  92.6 0.7 copy-start.21
  92.7 1.8 %copy-start.14 = (bf16[64,128]{1,0:T(8,128)(2,1)S(1)}, bf16[64,128]{1,0:T(8,128)(2,1)}, u32[]{:S(2)}) copy-start(bf16[64,128]{1,0:T(8,128)(2,1)} %get-tuple-element.59) | copy-start | bytes 49156
  92.7 1.8 %copy-start.15 = (bf16[64,128]{1,0:T(8,128)(2,1)S(1)}, bf16[64,128]{1,0:T(8,128)(2,1)}, u32[]{:S(2)}) copy-start(bf16[64,128]{1,0:T(8,128)(2,1)} %get-tuple-element.61) | copy-start | bytes 49156
  94.5 0.9 copy-start.6
  94.5 0.9 copy-start.12
  94.5 0.9 copy-start.13
  94.8 1.0 copy-start.5
  95.8 0.7 copy-start.20
  96.0 0.7 copy-start.10
  96.0 0.7 copy-start.11
  97.3 0.7 copy-start.19
  98.2 0.7 copy-start.18
  98.2 0.7 copy-start.22
  98.3 0.7 copy-start.23
  98.4 1.9 %copy-start.4 = (f32[1600,128]{1,0:T(8,128)S(1)}, f32[1600,128]{1,0:T(8,128)}, u32[]{:S(2)}) copy-start(f32[1600,128]{1,0:T(8,128)} %get-tuple-element.89) | copy-start | bytes 2457604
  98.4 1.9 %copy-start.25 = (pred[28,28]{1,0:T(8,128)(4,1)S(1)}, pred[28,28]{1,0:T(8,128)(4,1)}, u32[]{:S(2)}) copy-start(pred[28,28]{1,0:T(8,128)(4,1)} %broadcast_and_fusion.1) | copy-start | bytes 2356
  103.1 1.7 %copy-start.24 = (bf16[8,128]{1,0:T(8,128)(2,1)S(1)}, bf16[8,128]{1,0:T(8,128)(2,1)}, u32[]{:S(2)}) copy-start(bf16[8,128]{1,0:T(8,128)(2,1)} %pad_convert_fusion) | copy-start | bytes 6148
  103.1 1.7 %copy-start.9 = (bf16[640,128]{1,0:T(8,128)(2,1)S(1)}, bf16[640,128]{1,0:T(8,128)(2,1)}, u32[]{:S(2)}) copy-start(bf16[640,128]{1,0:T(8,128)(2,1)} %copy-done.8) | copy-start | bytes 491524
  105.6 20.9 %all-to-all-start = ((bf16[32,48,128]{2,1,0:T(8,128)(2,1)}), bf16[32,48,128]{2,1,0:T(8,128)(2,1)S(1)}, u32[]{:S(2)}, u32[]{:S(2)}) async-start(bf16[32,48,128]{2,1,0:T(8,128)(2,1)} %maximum_maximum_fusion.1), calls=%async_computation | async-start | bytes 786432 | tf_op jit(solution)/shard_map/all_to_all | solution.py:189
  127.3 4.0 %copy-start.7 = (pred[1,24,24,128]{3,2,1,0:T(8,128)(4,1)S(1)}, pred[1,24,24,128]{3,2,1,0:T(8,128)(4,1)}, u32[]{:S(2)}) copy-start(pred[1,24,24,128]{3,2,1,0:T(8,128)(4,1)} %broadcast_compare_fusion) | copy-start | bytes 221188
  127.3 15.2 %all-to-all-start.1 = ((f32[16,40,128]{2,1,0:T(8,128)}), f32[16,40,128]{2,1,0:T(8,128)S(1)}, u32[]{:S(2)}, u32[]{:S(2)}) async-start(f32[16,40,128]{2,1,0:T(8,128)} %broadcast_in_dim.60), calls=%async_computation.1 | async-start | bytes 655360 | tf_op jit(solution)/shard_map/all_to_all | solution.py:200

commit v3 on v1

v3 whole, which is shorter than its diff:
```python
import functools

import jax
import jax.numpy as jnp
from jax import lax
from jax.experimental import pallas as pl
from jax.experimental.pallas import tpu as pltpu
from jax.sharding import PartitionSpec as P

FIRST_DILATION = 2
SECOND_DILATION = 8
HALO = FIRST_DILATION + SECOND_DILATION
GRID = ("row", "col")
TAPS = [(a, b) for a in (-1, 0, 1) for b in (-1, 0, 1)]
LEAD = 16
F32, BF16 = jnp.float32, jnp.bfloat16


def tap(a, b):
    return 3 * (a + 1) + (b + 1)


def dot(x, y):
    return jnp.dot(x, y, preferred_element_type=F32)


def rounded(x):
    return x.astype(BF16).astype(F32)


def up16(n):
    return -(-n // 16) * 16


def send(x, to):
    number = lax.axis_size("row")
    pairs = []
    for r in range(number):
        for c in range(number):
            row, col = to(r, c)
            if 0 <= row < number and 0 <= col < number:
                pairs.append((r * number + c, row * number + col))
    return lax.ppermute(x, GRID, pairs)


def inside(shape, side, width, top):
    number = lax.axis_size("row") * side
    rows = lax.broadcasted_iota(jnp.int32, shape, 0) + top - width
    cols = lax.broadcasted_iota(jnp.int32, shape, 1) - width
    at_row = lax.axis_index("row") * side + rows
    at_col = lax.axis_index("col") * side + cols
    return (at_row >= 0) & (at_row < number) & (at_col >= 0) & (at_col < number) & (cols < side + width)


def forward_kernel(
    tile, mirrored, above, below, above_other, below_other, left, right, w_first, p_first, b_first, w_second, b_second,
    gate_first, bottle_first, near_hidden, gate_second, hidden_second, pre_second,
    area, shifted, pre, current,
):
    side, channels = tile.shape[0], tile.shape[2]
    first, second, inner = FIRST_DILATION, SECOND_DILATION, p_first.shape[0] // 2
    full, span, near = side + 2 * HALO, side + 2 * second, side + 2 * first
    wide, small = pre.shape[1], pre_second.shape[1]
    own, other = slice(0, channels), slice(channels, 2 * channels)
    middle = slice(LEAD, LEAD + side)

    area[:, :LEAD] = jnp.zeros((full, LEAD, 2 * channels), F32)
    area[:, LEAD + side :] = jnp.zeros((full, area.shape[1] - LEAD - side, 2 * channels), F32)
    area[HALO : HALO + side, middle, own] = tile[...].astype(F32)
    area[HALO : HALO + side, middle, other] = jnp.swapaxes(mirrored[...].astype(F32), 0, 1)
    area[:HALO, middle, own] = above[...].astype(F32)
    area[:HALO, middle, other] = above_other[...].astype(F32)
    area[HALO + side :, middle, own] = below[...].astype(F32)
    area[HALO + side :, middle, other] = below_other[...].astype(F32)
    area[:, LEAD - HALO : LEAD] = left[...].astype(F32)
    area[:, LEAD + side : LEAD + side + HALO] = right[...].astype(F32)

    start = LEAD - second

    def shift(step, _):
        rows = pl.ds(step * 4, 4)
        for b in (-1, 0, 1):
            at = start + first * b
            shifted[b + 1, rows] = jnp.maximum(area[rows, at : at + wide], 0).astype(BF16)
        return 0

    lax.fori_loop(0, full // 4, shift, 0)
    for b in (-1, 0, 1):
        at = LEAD + first * b
        part = area[HALO - first : HALO + side + first, at : at + small, own]
        near_hidden[b + 1] = jnp.maximum(part, 0).astype(BF16)

    def first_section(step, _):
        top = step * 8
        size = 8 * wide
        total = jnp.broadcast_to(b_first[...], (size, 2 * inner))
        for a, b in TAPS:
            window = shifted[b + 1, pl.ds(top + first * (1 + a), 8)].reshape(size, 2 * channels)
            total = total + dot(window, w_first[tap(a, b)])
        pre[pl.ds(top, 8)] = total.reshape(8, wide, 2 * inner)
        branch = dot(jnp.maximum(total, 0).astype(BF16), p_first[...])
        middle_part = area[pl.ds(top + first, 8), start : start + wide].reshape(size, 2 * channels)
        branch = rounded(middle_part + branch)
        sym = rounded((branch[:, own] + branch[:, other]) * 0.5).reshape(8, wide, channels)
        current[pl.ds(top, 8)] = jnp.where(inside(sym.shape, side, second, top), sym, 0)
        return 0

    lax.fori_loop(0, span // 8, first_section, 0)

    edge = second - first
    part = pre[edge : edge + near, edge : edge + small]
    alive = (part > 0) & inside(part.shape, side, first, 0)
    gate_first[...] = jnp.where(alive, 1.0, 0.0).astype(BF16)
    part = current[edge : edge + near, edge : edge + small]
    gate_second[...] = jnp.where(part > 0, 1.0, 0.0).astype(BF16)
    bottle_first[...] = jnp.maximum(pre[second : second + side, second : second + small], 0).astype(BF16)
    for b in (-1, 0, 1):
        at = second * (1 + b)
        hidden_second[b + 1] = jnp.maximum(current[:, at : at + small], 0).astype(BF16)

    def second_section(step, _):
        top = step * 8
        total = jnp.broadcast_to(b_second[...], (8 * small, 2 * inner))
        for a, b in TAPS:
            window = hidden_second[b + 1, pl.ds(top + second * (1 + a), 8)].reshape(8 * small, channels)
            total = total + dot(window, w_second[tap(a, b)])
        pre_second[pl.ds(top, 8)] = total.reshape(8, small, 2 * inner)
        return 0

    lax.fori_loop(0, side // 8, second_section, 0)


def turn_kernel(cotangent, mirrored, pre_second, p_second, grad_tile, grad_pre, above, below, padded):
    side, channels = cotangent.shape[0], cotangent.shape[2]
    small, first = pre_second.shape[1], FIRST_DILATION
    branch = (cotangent[...].astype(F32) + jnp.swapaxes(mirrored[...].astype(F32), 0, 1)) * 0.5
    padded[:, side:] = jnp.zeros((side, small - side, channels), F32)
    padded[:, :side] = rounded(branch)
    branch = padded[...].astype(BF16)
    grad_tile[...] = branch
    grad = dot(branch.reshape(side * small, channels), p_second[...]).reshape(side, small, channels)
    grad = jnp.where(pre_second[...] > 0, grad, 0)
    grad_pre[...] = grad.astype(BF16)
    grad, branch = grad[:, :side].astype(BF16), padded[:, :side].astype(BF16)
    above[:HALO], above[HALO:] = grad[:HALO], branch[:first]
    below[:HALO], below[HALO:] = grad[side - HALO :], branch[side - first :]


def weight_sums(rows, ends, grad_pre, hidden, dilation, bottle, grad_tile):
    side, small, lanes = grad_pre.shape
    inner = lanes // 2
    size = side * small
    flat = grad_pre.reshape(size, lanes)
    turned = flat.T[:inner].astype(BF16)
    for a, b in TAPS:
        top = dilation * (1 + a)
        window = hidden[b + 1, top : top + side].reshape(size, lanes)
        at = tap(a, b) * inner
        rows[at : at + inner] = dot(turned, window)
    turned = bottle[...].reshape(size, lanes).astype(F32).T[:inner].astype(BF16)
    rows[9 * inner : 10 * inner] = dot(turned, grad_tile.reshape(size, lanes))
    ends[...] = jnp.broadcast_to(jnp.sum(flat, axis=0, keepdims=True), ends.shape)


def second_sums_kernel(grad_pre, hidden, pre_second, grad_tile, rows, ends):
    bottle = jnp.maximum(pre_second[...], 0).astype(BF16)
    weight_sums(rows, ends, grad_pre[...].astype(F32), hidden, SECOND_DILATION, bottle, grad_tile[...])


def backward_kernel(
    grad_pre, grad_tile, above, below, left, right, left_branch, right_branch, gate_second, gate_first, near_hidden,
    bottle_first, v_second, p_first, rows_second, ends_second,
    parts, windows, grad_first,
    area, shifted, branch, grads, rows, ends,
):
    side, channels = grad_first.shape[0], grad_first.shape[2]
    first, second = FIRST_DILATION, SECOND_DILATION
    full, near = side + 2 * HALO, side + 2 * first
    small = grad_pre.shape[1]
    middle = slice(LEAD, LEAD + side)

    area[:, :LEAD] = jnp.zeros((full, LEAD, channels), F32)
    area[:, LEAD + side :] = jnp.zeros((full, area.shape[1] - LEAD - side, channels), F32)
    area[HALO : HALO + side, LEAD : LEAD + small] = grad_pre[...].astype(F32)
    area[:HALO, middle] = above[:HALO].astype(F32)
    area[HALO + side :, middle] = below[:HALO].astype(F32)
    area[:, LEAD - HALO : LEAD] = left[...].astype(F32)
    area[:, LEAD + side : LEAD + side + HALO] = right[...].astype(F32)
    branch[...] = jnp.zeros(branch.shape, F32)
    branch[first : first + side, first : first + side] = grad_tile[:, :side].astype(F32)
    branch[:first, first : first + side] = above[HALO:].astype(F32)
    branch[first + side :, first : first + side] = below[HALO:].astype(F32)
    branch[:, :first] = left_branch[...].astype(F32)
    branch[:, first + side : near] = right_branch[...].astype(F32)
    for b in (-1, 0, 1):
        at = LEAD - HALO + second * (1 - b)
        shifted[b + 1] = area[:, at : at + small].astype(BF16)
    grads[:, small:] = jnp.zeros((near, grads.shape[1] - small, channels), F32)

    def sections(step, _):
        top = step * 7
        size = 7 * small
        total = jnp.zeros((size, 2 * channels), F32)
        for a, b in TAPS:
            window = shifted[b + 1, pl.ds(top + second * (1 - a), 7)].reshape(size, channels)
            total = total + dot(window, v_second[tap(a, b)])
        here = pl.ds(top, 7)
        grad = branch[here, :small].reshape(size, channels)
        gate = gate_second[here].astype(F32).reshape(size, channels) > 0
        own = rounded(grad + jnp.where(gate, total[:, :channels], 0))
        other = rounded(grad + jnp.where(gate, total[:, channels:], 0))
        grad = ((own + other) * 0.5).astype(BF16)
        branch[here, :small] = grad.astype(F32).reshape(7, small, channels)
        gate = gate_first[here].astype(F32).reshape(size, channels) > 0
        grad = rounded(jnp.where(gate, dot(grad, p_first[...]), 0))
        grads[here, :small] = grad.reshape(7, small, channels)
        return 0

    lax.fori_loop(0, near // 7, sections, 0)
    for b in (-1, 0, 1):
        at = first * (1 - b)
        windows[b + 1] = grads[:, at : at + small].astype(BF16)
    part = branch[first : first + side, first : first + small]
    grad_first[...] = part[:, :side].astype(BF16)
    keep = lax.broadcasted_iota(jnp.int32, part.shape, 1) < side
    part = jnp.where(keep, part, 0).astype(BF16)
    grad = jnp.where(keep, grads[first : first + side, first : first + small], 0)
    weight_sums(rows, ends, grad, near_hidden, first, bottle_first, part)

    devices, share = parts.shape[0] // 2, parts.shape[1] - 8
    count = rows.shape[0]
    for section, (table, end) in enumerate(((rows, ends), (rows_second, ends_second))):
        for j in range(devices):
            at = section * devices + j
            low, high = min(j * share, count), min((j + 1) * share, count)
            pieces = [table[low:high]] if low < high else []
            if high - low < share:
                pieces.append(jnp.zeros((share - (high - low), channels), F32))
            parts[at] = jnp.concatenate(pieces + [end[...]]).astype(BF16)


def input_kernel(windows, grad_first, tile, v_first, out):
    side, channels = tile.shape[0], tile.shape[2]
    small = windows.shape[2]
    first = FIRST_DILATION

    def rows(step, _):
        top = step * 8
        total = jnp.zeros((8 * small, channels), F32)
        for a, b in TAPS:
            window = windows[b + 1, pl.ds(top + first * (1 - a), 8)].reshape(8 * small, channels)
            total = total + dot(window, v_first[tap(a, b)])
        here = pl.ds(top, 8)
        total = total.reshape(8, small, channels)[:, :side]
        total = jnp.where(tile[here].astype(F32) > 0, total, 0)
        out[here] = (grad_first[here].astype(F32) + total).astype(BF16)
        return 0

    lax.fori_loop(0, side // 8, rows, 0)


def total_kernel(scale, parts, rows, ends):
    share = rows.shape[1]
    total = jnp.sum(parts[...].astype(F32), axis=0) * scale
    rows[...] = jnp.broadcast_to(total[:share].astype(BF16)[None], rows.shape)
    ends[...] = total[share:]


def call(kernel, name, outs, scratch, flops, *operands):
    outs = [jax.ShapeDtypeStruct(shape, dtype) for shape, dtype in outs]
    moved = sum(x.size * x.dtype.itemsize for x in list(operands) + outs)
    return pl.pallas_call(
        kernel,
        name=name,
        out_shape=outs,
        scratch_shapes=[pltpu.VMEM(shape, dtype) for shape, dtype in scratch],
        cost_estimate=pl.CostEstimate(flops=flops, bytes_accessed=moved, transcendentals=0),
        compiler_params=pltpu.CompilerParams(vmem_limit_bytes=40 * 1024 * 1024),
    )(*operands)


def beside(x, y, axis):
    if axis is not None:
        return jnp.concatenate([x, y], axis=axis)
    zero = jnp.zeros_like(x)
    return jnp.concatenate([jnp.concatenate([x, zero], axis=-1), jnp.concatenate([zero, y], axis=-1)], axis=-2)


def local(activations, cotangent, conv_weight, conv_bias, out_weight):
    side, channels, inner = activations.shape[1], activations.shape[3], conv_weight.shape[3]
    number = lax.axis_size("row")
    first, second = FIRST_DILATION, SECOND_DILATION
    full, span, near = side + 2 * HALO, side + 2 * second, side + 2 * first
    wide, small = up16(span), up16(near)
    tile = activations[0]

    mirrored = send(tile, lambda r, c: (c, r))
    above = send(tile[side - HALO :], lambda r, c: (r + 1, c))
    below = send(tile[:HALO], lambda r, c: (r - 1, c))
    above_other = send(jnp.swapaxes(tile[:, side - HALO :], 0, 1), lambda r, c: (c + 1, r))
    below_other = send(jnp.swapaxes(tile[:, :HALO], 0, 1), lambda r, c: (c - 1, r))

    bias_rows = jnp.pad(conv_bias, ((0, 7), (0, channels - inner)))
    packed = jnp.concatenate(
        [jnp.swapaxes(conv_weight[0], 1, 2).reshape(9 * inner, channels), out_weight[0], bias_rows]
    )
    packed = lax.all_gather(packed, "segment")
    conv = packed[:, : 9 * inner].reshape(2, 9, inner, channels)
    swapped = jnp.stack([conv[:, tap(b, a)] for a, b in TAPS], axis=1)
    proj = packed[:, 9 * inner : 10 * inner]
    bias = jnp.tile(packed[:, 10 * inner, :inner].astype(F32), (1, 2))[:, None]
    w_first = beside(jnp.swapaxes(conv[0], 1, 2), jnp.swapaxes(swapped[0], 1, 2), None)
    w_second = beside(jnp.swapaxes(conv[1], 1, 2), jnp.swapaxes(swapped[1], 1, 2), 2)
    v_second = beside(conv[1], swapped[1], None)
    v_first = jnp.pad(conv[0], ((0, 0), (0, inner), (0, 0)))
    p_first = beside(proj[0], proj[0], None)
    p_second = beside(proj[1].T, proj[1].T, 1)
    p_back = jnp.pad(proj[0].T, ((0, 0), (0, inner)))

    other = jnp.swapaxes(mirrored, 0, 1)

    def columns(low, high):
        own = jnp.concatenate([above[:, low:high], tile[:, low:high], below[:, low:high]])
        turned = jnp.concatenate([above_other[:, low:high], other[:, low:high], below_other[:, low:high]])
        return jnp.swapaxes(jnp.concatenate([own, turned], axis=2), 0, 1)

    left = send(columns(side - HALO, side), lambda r, c: (r, c + 1))
    right = send(columns(0, HALO), lambda r, c: (r, c - 1))
    left, right, late = lax.optimization_barrier((left, right, cotangent[0]))
    late_mirrored = send(late, lambda r, c: (c, r))

    gate_first, bottle_first, near_hidden, gate_second, hidden_second, pre_second = call(
        forward_kernel,
        "forward",
        [
            ((near, small, channels), BF16),
            ((side, small, channels), BF16),
            ((3, near, small, channels), BF16),
            ((near, small, channels), BF16),
            ((3, span, small, channels), BF16),
            ((side, small, 2 * inner), F32),
        ],
        [
            ((full, LEAD + up16(side + LEAD + second + first), 2 * channels), F32),
            ((3, full, wide, 2 * channels), BF16),
            ((span, wide, 2 * inner), F32),
            ((span, wide, channels), F32),
        ],
        span * wide * 2 * channels * 2 * inner * 20,
        *(tile, mirrored, above, below, above_other, below_other),
        *(jnp.swapaxes(left, 0, 1), jnp.swapaxes(right, 0, 1)),
        *(w_first, p_first, bias[0], w_second, bias[1]),
    )

    grad_tile, grad_pre, strip_above, strip_below = call(
        turn_kernel,
        "turn",
        [
            ((side, small, channels), BF16),
            ((side, small, 2 * inner), BF16),
            ((HALO + first, side, channels), BF16),
            ((HALO + first, side, channels), BF16),
        ],
        [((side, small, channels), F32)],
        2 * side * small * channels * 2 * inner,
        *(late, late_mirrored, pre_second, p_second),
    )

    above = send(strip_below, lambda r, c: (r + 1, c))
    below = send(strip_above, lambda r, c: (r - 1, c))
    rows_second, ends_second = call(
        second_sums_kernel,
        "second_sums",
        [((10 * inner, channels), F32), ((8, channels), F32)],
        [],
        20 * side * small * channels * inner,
        *(grad_pre, hidden_second, pre_second, grad_tile),
    )

    def columns(low, high, low_branch, high_branch):
        grads = jnp.concatenate([above[:HALO, low:high], grad_pre[:, low:high], below[:HALO, low:high]])
        here = slice(low_branch, high_branch)
        branches = jnp.concatenate([above[HALO:, here], grad_tile[:, here], below[HALO:, here]])
        branches = jnp.pad(branches, ((second, second), (0, 0), (0, 0)))
        return jnp.swapaxes(jnp.concatenate([grads, branches], axis=1), 0, 1)

    left = send(columns(side - HALO, side, side - first, side), lambda r, c: (r, c + 1))
    right = send(columns(0, HALO, 0, first), lambda r, c: (r, c - 1))
    left, right = jnp.swapaxes(left, 0, 1), jnp.swapaxes(right, 0, 1)

    devices = number * number
    share = -(-10 * inner // (8 * devices)) * 8
    parts, windows, grad_first = call(
        backward_kernel,
        "backward",
        [
            ((2 * devices, share + 8, channels), BF16),
            ((3, near, small, channels), BF16),
            ((side, side, channels), BF16),
        ],
        [
            ((full, LEAD + up16(side + HALO + first), channels), F32),
            ((3, full, small, channels), BF16),
            ((near, small + 16, channels), F32),
            ((near, small + 16, channels), F32),
            ((10 * inner, channels), F32),
            ((8, channels), F32),
        ],
        36 * near * small * channels * channels,
        *(grad_pre, grad_tile, above, below, left[:, :HALO], right[:, :HALO]),
        *(left[second : second + near, HALO:], right[second : second + near, HALO:]),
        *(gate_second, gate_first, near_hidden, bottle_first, v_second, p_back, rows_second, ends_second),
    )

    parts = lax.all_to_all(parts, ("segment",) + GRID, 0, 0, tiled=True)
    (input_gradient,) = call(
        input_kernel,
        "input",
        [((side, side, channels), BF16)],
        [],
        18 * side * small * channels * channels,
        *(windows, grad_first, tile, v_first),
    )
    cells = lax.axis_size("segment") * (side * number) * (side * number)
    rows, ends = call(
        functools.partial(total_kernel, float(cells) ** -0.5),
        "total",
        [((devices, share, channels), BF16), ((8, channels), F32)],
        [],
        parts.size,
        parts,
    )
    rows = lax.all_to_all(rows, GRID, 0, 0, tiled=True).reshape(devices * share, channels).astype(F32)
    conv_gradient = jnp.swapaxes(rows[: 9 * inner].reshape(1, 9, inner, channels), 2, 3)
    return (input_gradient[None], conv_gradient, ends[:1, :inner], rows[None, 9 * inner : 10 * inner])


def solution(mesh):
    in_specs = (
        P("segment", "row", "col", None),
        P("segment", "row", "col", None),
        P("segment", None, None, None),
        P("segment", None),
        P("segment", None, None),
    )
    out_specs = (
        P("segment", "row", "col", None),
        P("segment", None, None, None),
        P("segment", None),
        P("segment", None, None),
    )
    return jax.shard_map(local, mesh=mesh, in_specs=in_specs, out_specs=out_specs, check_vma=False)
```

time: 245 us -> 110 us (0.45)
  waiting for transfers between devices: 76.6 us -> 23 us
  matrix products: 30.8 us -> 0 us
  local copies, waits for them, and re-layouts: 33.4 us -> 6.51 us
  blocking collectives: 41.7 us -> 21.4 us
  between operations: 14.9 us -> 1.24 us
  Pallas kernels: 0 us -> 12.5 us
  other arithmetic: 13.7 us -> 1.39 us
  starting transfers between devices: 32.5 us -> 43.4 us
    all_gather x1 -> x0, waiting for transfers between devices: 51 us -> none  [both_regions(): tiles = lax.all_gather(tile, GRID)]
    all_gather x1 -> x0, blocking collectives: 39.5 us -> none  [local(): rows = lax.all_gather(total[:share], GRID, tiled=True)]
    dot_general x59 -> x0, matrix products: 30.8 us -> none  [dot(): lax.dot_general(x, y, (dims, ((), ())), preferred_element_type=jnp.float32)]
    all_to_all x0 -> x1, blocking collectives: none -> 19.3 us  [local(): parts = lax.all_to_all(parts, ('segment',) + GRID, 0, 0, tiled=True)]
    reshape x11 -> x0, local copies, waits for them, and re-layouts: 14 us -> none  [the longest x9 10.7 us: window(): return x[top:top + rows, left:left + cols].reshape(rows * cols, x.shape[2])]
    pallas_call x0 -> x6, Pallas kernels: none -> 12.5 us  [call(): pl.pallas_call(kernel, name=name, out_shape=outs, scratch_shapes=[pltpu.V...]
    ppermute x5 -> x12, starting transfers between devices: 29 us -> 39.9 us  [send(): return lax.ppermute(x, GRID, pairs)]
    slice x19 -> x22, local copies, waits for them, and re-layouts: 11.7 us -> 1.87 us  [the longest x1 1.04 us: columns(): tile[:, low:high]]
  transfers between devices with their start and end apart: 7 -> 13, of which waited for: 6 -> 8; matrix products, arithmetic and copies ran while one was open for 8% -> 4% of each run, Pallas kernels for 0% -> 8%
where the time goes in v3:
time: 110 us; the launch traced here: 109 us
  starting transfers between devices  43.4 us (39%)
  waiting for transfers between devices  23 us (21%)
  blocking collectives  21.4 us (19%)
  Pallas kernels  12.5 us (11%)
  local copies, waits for them, and re-layouts  6.51 us (6%)
  other arithmetic  1.39 us (1%)
  between operations  1.24 us (1%)
    ppermute x12, starting transfers between devices, send(): return lax.ppermute(x, GRID, pairs)  39.9 us
    all_to_all x1, blocking collectives, local(): parts = lax.all_to_all(parts, ('segment',) + GRID, 0, 0, tiled=True)  19.3 us
    ppermute x12, waiting for transfers between devices, send(): return lax.ppermute(x, GRID, pairs)  17.2 us
    pallas_call x6, Pallas kernels, call(): pl.pallas_call(kernel, name=name, out_shape=outs, scratch_shapes=[pltpu.V...  12.5 us
    all_to_all x1, waiting for transfers between devices, local(): lax.all_to_all(rows, GRID, 0, 0, tiled=True)  5.83 us
    all_to_all x1, starting transfers between devices, local(): lax.all_to_all(rows, GRID, 0, 0, tiled=True)  3.52 us
  transfers between devices with their start and end apart: 13, of which 8 were waited for; matrix products, arithmetic and copies ran while one was open for 4% of the time, Pallas kernels for 8%

profile of v3, /device:TPU:0, one launch (start us, length us, event | category | flops | bytes accessed | tf_op | source)
XLA Modules:
  0.0 109.4 jit_solution(7524025665986034595)
XLA Ops:
  0.7 1.0 fusion.16
  1.7 1.3 %collective-permute-start.4 = (bf16[10,24,128]{2,1,0:T(8,128)(2,1)S(1)}, bf16[10,24,128]{2,1,0:T(8,128)(2,1)S(1)}, u32[]{:S(2)}, u32[]{:S(2)}) collective-permute-start(bf16[10,24,128]{2,1,0:T(8,128)(2,1)S(1)} %bitcast.105), channel_id=1, source_target_pairs={{1,0},{2,4},{3,8},{5,1},{6,5},{7,9},{9,2},{10,6},{11,10},{13,3},{1... | collective-permute-start | bytes 184328 | tf_op jit(solution)/shard_map/ppermute | solution.py:43
  3.0 4.8 %collective-permute-start.2 = (bf16[10,24,128]{2,0,1:T(8,128)(2,1)S(1)}, bf16[10,24,128]{2,0,1:T(8,128)(2,1)S(1)}, u32[]{:S(2)}, u32[]{:S(2)}) collective-permute-start(bf16[10,24,128]{2,0,1:T(8,128)(2,1)S(1)} %get-tuple-element.60), channel_id=1, source_target_pairs={{0,4},{1,8},{2,12},{4,5},{5,9},{6,13},{8,6},{9,10},{10,14},{12,7},... | collective-permute-start | bytes 184328 | tf_op jit(solution)/shard_map/ppermute | solution.py:43
  7.9 0.9 copy.21
  8.8 0.7 collective-permute-start.3
  9.5 6.1 %collective-permute-start = (bf16[10,24,128]{2,1,0:T(8,128)(2,1)S(1)}, bf16[10,24,128]{2,1,0:T(8,128)(2,1)S(1)}, u32[]{:S(2)}, u32[]{:S(2)}) collective-permute-start(bf16[10,24,128]{2,1,0:T(8,128)(2,1)S(1)} %get-tuple-element.57), channel_id=1, source_target_pairs={{0,4},{1,5},{2,6},{3,7},{4,8},{5,9},{6,10},{7,11},{8,12},{9,13},{1... | collective-permute-start | bytes 184328 | tf_op jit(solution)/shard_map/ppermute | solution.py:43
  15.7 1.3 %collective-permute-start.1 = (bf16[10,24,128]{2,1,0:T(8,128)(2,1)S(1)}, bf16[10,24,128]{2,1,0:T(8,128)(2,1)S(1)}, u32[]{:S(2)}, u32[]{:S(2)}) collective-permute-start(bf16[10,24,128]{2,1,0:T(8,128)(2,1)S(1)} %get-tuple-element.58), channel_id=1, source_target_pairs={{4,0},{5,1},{6,2},{7,3},{8,4},{9,5},{10,6},{11,7},{12,8},{13,9},{1... | collective-permute-start | bytes 184328 | tf_op jit(solution)/shard_map/ppermute | solution.py:43
  17.0 2.0 %all-gather = bf16[1296,128]{1,0:T(8,128)(2,1)S(1)} all-gather(bf16[648,128]{1,0:T(8,128)(2,1)S(1)} %fusion.7), channel_id=2, replica_groups=mesh['segment'=2,'row'=4,'col'=4] {'segment'}, dimensions={0}, use_global_device_ids=true | all-gather | bytes 497664 | tf_op jit(solution)/shard_map/all_gather | solution.py:307
  19.3 0.7 slice_bitcast_fusion.2
  20.0 0.1 copy.32
  20.3 2.5 %collective-permute-done.1.below = bf16[10,24,128]{2,1,0:T(8,128)(2,1)S(1)} collective-permute-done((bf16[10,24,128]{2,1,0:T(8,128)(2,1)S(1)}, bf16[10,24,128]{2,1,0:T(8,128)(2,1)S(1)}, u32[]{:S(2)}, u32[]{:S(2)}) %collective-permute-start.1) | collective-permute-done | bytes 61472 | tf_op jit(solution)/shard_map/ppermute | solution.py:43
  23.0 1.3 %collective-permute-start.6 = (bf16[10,44,256]{2,0,1:T(8,128)(2,1)S(1)}, bf16[10,44,256]{2,0,1:T(8,128)(2,1)S(1)}, u32[]{:S(2)}, u32[]{:S(2)}) collective-permute-start(bf16[10,44,256]{2,0,1:T(8,128)(2,1)S(1)} %maximum_bitcast_fusion.1), channel_id=1, source_target_pairs={{1,0},{2,1},{3,2},{5,4},{6,5},{7,6},{9,8},{10,9},{11,10},{13,12},{... | collective-permute-start | bytes 675848 | tf_op jit(solution)/shard_map/ppermute | solution.py:43
  24.3 0.8 maximum_bitcast_fusion
  25.1 6.7 %collective-permute-start.5 = (bf16[10,44,256]{2,0,1:T(8,128)(2,1)}, bf16[10,44,256]{2,0,1:T(8,128)(2,1)S(1)}, u32[]{:S(2)}, u32[]{:S(2)}) collective-permute-start(bf16[10,44,256]{2,0,1:T(8,128)(2,1)} %maximum_bitcast_fusion), channel_id=1, source_target_pairs={{0,1},{1,2},{2,3},{4,5},{5,6},{6,7},{8,9},{9,10},{10,11},{12,13},{... | collective-permute-start | bytes 675848 | tf_op jit(solution)/shard_map/ppermute | solution.py:43
  31.8 0.1 fusion.10
  31.9 0.1 copy.33
  32.1 5.2 %collective-permute-done.6 = bf16[10,44,256]{2,0,1:T(8,128)(2,1)S(1)} collective-permute-done((bf16[10,44,256]{2,0,1:T(8,128)(2,1)S(1)}, bf16[10,44,256]{2,0,1:T(8,128)(2,1)S(1)}, u32[]{:S(2)}, u32[]{:S(2)}) %collective-permute-start.6) | collective-permute-done | bytes 225312 | tf_op jit(solution)/shard_map/ppermute | solution.py:43
  37.2 2.3 %collective-permute-done.5 = bf16[10,44,256]{2,0,1:T(8,128)(2,1)S(1)} collective-permute-done((bf16[10,44,256]{2,0,1:T(8,128)(2,1)}, bf16[10,44,256]{2,0,1:T(8,128)(2,1)S(1)}, u32[]{:S(2)}, u32[]{:S(2)}) %collective-permute-start.5) | collective-permute-done | bytes 225312 | tf_op jit(solution)/shard_map/ppermute | solution.py:43
  39.5 0.7 collective-permute-start.7
  40.2 0.1 pad_maximum_fusion.1.p_second
  40.3 0.3 copy.28.w_first
  40.6 0.2 copy.30.w_second
  40.8 0.1 copy.29.p_first
  40.9 0.1 tile.13.b_first
  41.0 0.1 tile.15.b_second
  41.2 0.3 copy-done.3
  41.5 6.4 %forward.1 = (bf16[28,32,128]{2,1,0:T(8,128)(2,1)S(1)}, bf16[24,32,128]{2,1,0:T(8,128)(2,1)S(1)}, bf16[3,28,32,128]{3,2,1,0:T(8,128)(2,1)S(1)}, bf16[28,32,128]{...) custom-call(bf16[24,24,128]{2,1,0:T(8,128)(2,1)S(1)} %bitcast.71, ...), custom_call_target="tpu_custom_call" | custom-call | flops 1258291200 | bytes 4662272 | tf_op jit(solution)/shard_map/forward/pallas_call | solution.py:272
  47.9 0.3 turn.1
  48.2 9.8 %collective-permute-start.8 = (bf16[12,24,128]{2,1,0:T(8,128)(2,1)S(1)}, bf16[12,24,128]{2,1,0:T(8,128)(2,1)S(1)}, u32[]{:S(2)}, u32[]{:S(2)}) collective-permute-start(bf16[12,24,128]{2,1,0:T(8,128)(2,1)S(1)} %get-tuple-element.30), channel_id=1, source_target_pairs={{0,4},{1,5},{2,6},{3,7},{4,8},{5,9},{6,10},{7,11},{8,12},{9,13},{1... | collective-permute-start | bytes 221192 | tf_op jit(solution)/shard_map/ppermute | solution.py:43
  58.0 1.3 %collective-permute-start.9 = (bf16[12,24,128]{2,1,0:T(8,128)(2,1)S(1)}, bf16[12,24,128]{2,1,0:T(8,128)(2,1)S(1)}, u32[]{:S(2)}, u32[]{:S(2)}) collective-permute-start(bf16[12,24,128]{2,1,0:T(8,128)(2,1)S(1)} %get-tuple-element.31), channel_id=1, source_target_pairs={{4,0},{5,1},{6,2},{7,3},{8,4},{9,5},{10,6},{11,7},{12,8},{13,9},{1... | collective-permute-start | bytes 221192 | tf_op jit(solution)/shard_map/ppermute | solution.py:43
  59.4 0.6 collective-permute-done.8.above
  60.0 4.3 %collective-permute-done.9.below = bf16[12,24,128]{2,1,0:T(8,128)(2,1)S(1)} collective-permute-done((bf16[12,24,128]{2,1,0:T(8,128)(2,1)S(1)}, bf16[12,24,128]{2,1,0:T(8,128)(2,1)S(1)}, u32[]{:S(2)}, u32[]{:S(2)}) %collective-permute-start.9) | collective-permute-done | bytes 73760 | tf_op jit(solution)/shard_map/ppermute | solution.py:43
  64.3 0.1 maximum_bitcast_fusion.3
  64.4 1.3 %collective-permute-start.11 = (bf16[12,44,128]{2,0,1:T(8,128)(2,1)S(1)}, bf16[12,44,128]{2,0,1:T(8,128)(2,1)S(1)}, u32[]{:S(2)}, u32[]{:S(2)}) collective-permute-start(bf16[12,44,128]{2,0,1:T(8,128)(2,1)S(1)} %maximum_bitcast_fusion.3), channel_id=1, source_target_pairs={{1,0},{2,1},{3,2},{5,4},{6,5},{7,6},{9,8},{10,9},{11,10},{13,12},{... | collective-permute-start | bytes 405512 | tf_op jit(solution)/shard_map/ppermute | solution.py:43
  65.7 0.1 maximum_bitcast_fusion.2
  65.8 4.6 %collective-permute-start.10 = (bf16[12,44,128]{2,0,1:T(8,128)(2,1)S(1)}, bf16[12,44,128]{2,0,1:T(8,128)(2,1)S(1)}, u32[]{:S(2)}, u32[]{:S(2)}) collective-permute-start(bf16[12,44,128]{2,0,1:T(8,128)(2,1)S(1)} %maximum_bitcast_fusion.2), channel_id=1, source_target_pairs={{0,1},{1,2},{2,3},{4,5},{5,6},{6,7},{8,9},{9,10},{10,11},{12,13},{... | collective-permute-start | bytes 405512 | tf_op jit(solution)/shard_map/ppermute | solution.py:43
  70.5 0.5 second_sums.1
  71.0 0.9 collective-permute-done.11
  71.8 1.5 %collective-permute-done.10 = bf16[12,44,128]{2,0,1:T(8,128)(2,1)S(1)} collective-permute-done((bf16[12,44,128]{2,0,1:T(8,128)(2,1)S(1)}, bf16[12,44,128]{2,0,1:T(8,128)(2,1)S(1)}, u32[]{:S(2)}, u32[]{:S(2)}) %collective-permute-start.10) | collective-permute-done | bytes 135200 | tf_op jit(solution)/shard_map/ppermute | solution.py:43
  73.4 3.1 %backward.1 = (bf16[32,48,128]{2,1,0:T(8,128)(2,1)S(1)}, bf16[3,28,32,128]{3,2,1,0:T(8,128)(2,1)S(1)}, bf16[24,24,128]{2,1,0:T(8,128)(2,1)S(1)}) custom-call(bf16[24,32,128]{2,1,0:T(8,128)(2,1)S(1)} %get-tuple-element.28.grad_pre, bf16[24,32,128]{2,1,0:T(8,128)(2,1)S(1)} %get-tuple-element.29.grad_tile, ...), custom_call_target="tpu_custom_call" | custom-call | flops 528482304 | bytes 4321280 | tf_op jit(solution)/shard_map/backward/pallas_call | solution.py:272
  76.5 19.3 %all_to_all.10.parts = bf16[32,48,128]{2,1,0:T(8,128)(2,1)S(1)} all-to-all(bf16[32,48,128]{2,1,0:T(8,128)(2,1)S(1)} %get-tuple-element.41), channel_id=1, replica_groups=mesh['segment'=2,'row'=4,'col'=4] {'segment','row','col'}, dimensions={0} | all-to-all | bytes 786432 | tf_op jit(solution)/shard_map/all_to_all | solution.py:415
  95.8 0.7 total.1
  96.5 3.5 %all-to-all-start.1 = ((bf16[16,40,128]{2,1,0:T(8,128)(2,1)}), bf16[16,40,128]{2,1,0:T(8,128)(2,1)S(1)}, u32[]{:S(2)}, u32[]{:S(2)}) async-start(bf16[16,40,128]{2,1,0:T(8,128)(2,1)} %get-tuple-element.42), calls=%async_computation.1 | async-start | bytes 327680 | tf_op jit(solution)/shard_map/all_to_all | solution.py:433
  100.1 1.6 %input.1 = bf16[24,24,128]{2,1,0:T(8,128)(2,1)} custom-call(bf16[3,28,32,128]{3,2,1,0:T(8,128)(2,1)S(1)} %get-tuple-element.39.windows, bf16[24,24,128]{2,1,0:T(8,128)(2,1)S(1)} %get-tuple-element.40.grad_first, bf16[24,24,128]{2,1,0:T(8,128)(2,1)S(1)} %bitcast.72, bf16[9,128,128]{2,1,0:T(8,128)(2,1)S(1)} %pad.29.v_first), custom_call_target="tpu_custom_call" | custom-call | flops 226492416 | bytes 1425408 | tf_op jit(solution)/shard_map/input/pallas_call | solution.py:272
  101.7 0.5 slice.241
  102.2 5.8 %all-to-all-done.1 = bf16[16,40,128]{2,1,0:T(8,128)(2,1)S(1)} async-done(((bf16[16,40,128]{2,1,0:T(8,128)(2,1)}), bf16[16,40,128]{2,1,0:T(8,128)(2,1)S(1)}, u32[]{:S(2)}, u32[]{:S(2)}) %all-to-all-start.1) | async-done | bytes 163872 | tf_op jit(solution)/shard_map/all_to_all | solution.py:433
  108.1 0.7 slice.284
  108.8 0.6 slice_bitcast_fusion.5
  (69 shorter events, 0.9 us)
Async XLA Ops:
  0.6 8.9 %copy-start = (bf16[1,24,24,128]{3,2,1,0:T(8,128)(2,1)S(1)}, bf16[1,24,24,128]{3,2,1,0:T(8,128)(2,1)}, u32[]{:S(2)}) copy-start(bf16[1,24,24,128]{3,2,1,0:T(8,128)(2,1)} %param.5) | copy-start | bytes 442372
  0.6 16.3 %copy-start.7 = (bf16[1,9,128,64]{2,3,1,0:T(8,128)(2,1)S(1)}, bf16[1,9,128,64]{2,3,1,0:T(8,128)(2,1)}, u32[]{:S(2)}) copy-start(bf16[1,9,128,64]{2,3,1,0:T(8,128)(2,1)} %param.7) | copy-start | bytes 442372
  0.7 16.3 %copy-start.8 = (bf16[1,64,128]{2,1,0:T(8,128)(2,1)S(1)}, bf16[1,64,128]{2,1,0:T(8,128)(2,1)}, u32[]{:S(2)}) copy-start(bf16[1,64,128]{2,1,0:T(8,128)(2,1)} %param.9) | copy-start | bytes 49156
  0.7 16.3 %copy-start.9 = (bf16[1,64]{1,0:T(2,128)(2,1)S(1)}, bf16[1,64]{1,0:T(2,128)(2,1)}, u32[]{:S(2)}) copy-start(bf16[1,64]{1,0:T(2,128)(2,1)} %param.8) | copy-start | bytes 388
  1.7 18.5 %collective-permute-start.4 = (bf16[10,24,128]{2,1,0:T(8,128)(2,1)S(1)}, bf16[10,24,128]{2,1,0:T(8,128)(2,1)S(1)}, u32[]{:S(2)}, u32[]{:S(2)}) collective-permute-start(bf16[10,24,128]{2,1,0:T(8,128)(2,1)S(1)} %bitcast.105), channel_id=1, source_target_pairs={{1,0},{2,4},{3,8},{5,1},{6,5},{7,9},{9,2},{10,6},{11,10},{13,3},{1... | collective-permute-start | bytes 184328 | tf_op jit(solution)/shard_map/ppermute | solution.py:43
  3.0 17.2 %collective-permute-start.2 = (bf16[10,24,128]{2,0,1:T(8,128)(2,1)S(1)}, bf16[10,24,128]{2,0,1:T(8,128)(2,1)S(1)}, u32[]{:S(2)}, u32[]{:S(2)}) collective-permute-start(bf16[10,24,128]{2,0,1:T(8,128)(2,1)S(1)} %get-tuple-element.60), channel_id=1, source_target_pairs={{0,4},{1,8},{2,12},{4,5},{5,9},{6,13},{8,6},{9,10},{10,14},{12,7},... | collective-permute-start | bytes 184328 | tf_op jit(solution)/shard_map/ppermute | solution.py:43
  8.8 14.0 %collective-permute-start.3 = (bf16[24,24,128]{2,0,1:T(8,128)(2,1)S(1)}, bf16[24,24,128]{2,0,1:T(8,128)(2,1)S(1)}, u32[]{:S(2)}, u32[]{:S(2)}) collective-permute-start(bf16[24,24,128]{2,0,1:T(8,128)(2,1)S(1)} %copy.21), channel_id=1, source_target_pairs={{0,0},{1,4},{2,8},{3,12},{4,1},{5,5},{6,9},{7,13},{8,2},{9,6},{10,... | collective-permute-start | bytes 442376 | tf_op jit(solution)/shard_map/ppermute | solution.py:43
  9.5 10.7 %collective-permute-start = (bf16[10,24,128]{2,1,0:T(8,128)(2,1)S(1)}, bf16[10,24,128]{2,1,0:T(8,128)(2,1)S(1)}, u32[]{:S(2)}, u32[]{:S(2)}) collective-permute-start(bf16[10,24,128]{2,1,0:T(8,128)(2,1)S(1)} %get-tuple-element.57), channel_id=1, source_target_pairs={{0,4},{1,5},{2,6},{3,7},{4,8},{5,9},{6,10},{7,11},{8,12},{9,13},{1... | collective-permute-start | bytes 184328 | tf_op jit(solution)/shard_map/ppermute | solution.py:43
  15.7 7.2 %collective-permute-start.1 = (bf16[10,24,128]{2,1,0:T(8,128)(2,1)S(1)}, bf16[10,24,128]{2,1,0:T(8,128)(2,1)S(1)}, u32[]{:S(2)}, u32[]{:S(2)}) collective-permute-start(bf16[10,24,128]{2,1,0:T(8,128)(2,1)S(1)} %get-tuple-element.58), channel_id=1, source_target_pairs={{4,0},{5,1},{6,2},{7,3},{8,4},{9,5},{10,6},{11,7},{12,8},{13,9},{1... | collective-permute-start | bytes 184328 | tf_op jit(solution)/shard_map/ppermute | solution.py:43
  20.2 2.7 %copy-start.5 = (bf16[10,24,128]{2,0,1:T(8,128)(2,1)}, bf16[10,24,128]{2,0,1:T(8,128)(2,1)S(1)}, u32[]{:S(2)}) copy-start(bf16[10,24,128]{2,0,1:T(8,128)(2,1)S(1)} %collective-permute-done.2) | copy-start | bytes 184324
  22.9 9.2 %copy-start.2 = (bf16[24,24,128]{2,0,1:T(8,128)(2,1)}, bf16[24,24,128]{2,0,1:T(8,128)(2,1)S(1)}, u32[]{:S(2)}) copy-start(bf16[24,24,128]{2,0,1:T(8,128)(2,1)S(1)} %collective-permute-done.3) | copy-start | bytes 442372
  22.9 16.6 %copy-start.1 = (bf16[1,24,24,128]{3,2,1,0:T(8,128)(2,1)S(1)}, bf16[1,24,24,128]{3,2,1,0:T(8,128)(2,1)}, u32[]{:S(2)}) copy-start(bf16[1,24,24,128]{3,2,1,0:T(8,128)(2,1)} %param.6) | copy-start | bytes 442372
  23.0 14.2 %collective-permute-start.6 = (bf16[10,44,256]{2,0,1:T(8,128)(2,1)S(1)}, bf16[10,44,256]{2,0,1:T(8,128)(2,1)S(1)}, u32[]{:S(2)}, u32[]{:S(2)}) collective-permute-start(bf16[10,44,256]{2,0,1:T(8,128)(2,1)S(1)} %maximum_bitcast_fusion.1), channel_id=1, source_target_pairs={{1,0},{2,1},{3,2},{5,4},{6,5},{7,6},{9,8},{10,9},{11,10},{13,12},{... | collective-permute-start | bytes 675848 | tf_op jit(solution)/shard_map/ppermute | solution.py:43
  25.1 14.4 %collective-permute-start.5 = (bf16[10,44,256]{2,0,1:T(8,128)(2,1)}, bf16[10,44,256]{2,0,1:T(8,128)(2,1)S(1)}, u32[]{:S(2)}, u32[]{:S(2)}) collective-permute-start(bf16[10,44,256]{2,0,1:T(8,128)(2,1)} %maximum_bitcast_fusion), channel_id=1, source_target_pairs={{0,1},{1,2},{2,3},{4,5},{5,6},{6,7},{8,9},{9,10},{10,11},{12,13},{... | collective-permute-start | bytes 675848 | tf_op jit(solution)/shard_map/ppermute | solution.py:43
  39.5 8.4 %collective-permute-start.7 = (bf16[24,24,128]{2,1,0:T(8,128)(2,1)S(1)}, bf16[24,24,128]{2,1,0:T(8,128)(2,1)S(1)}, u32[]{:S(2)}, u32[]{:S(2)}) collective-permute-start(bf16[24,24,128]{2,1,0:T(8,128)(2,1)S(1)} %bitcast.77), channel_id=1, source_target_pairs={{0,0},{1,4},{2,8},{3,12},{4,1},{5,5},{6,9},{7,13},{8,2},{9,6},{10,... | collective-permute-start | bytes 442376 | tf_op jit(solution)/shard_map/ppermute | solution.py:43
  40.3 0.9 copy-start.6
  40.6 0.9 copy-start.3
  48.2 22.2 %copy-start.4 = (bf16[9,64,128]{2,1,0:T(8,128)(2,1)S(1)}, bf16[9,64,128]{2,1,0:T(8,128)(2,1)}, u32[]{:S(2)}) copy-start(bf16[9,64,128]{2,1,0:T(8,128)(2,1)} %get-tuple-element.48) | copy-start | bytes 442372
  48.2 11.8 %collective-permute-start.8 = (bf16[12,24,128]{2,1,0:T(8,128)(2,1)S(1)}, bf16[12,24,128]{2,1,0:T(8,128)(2,1)S(1)}, u32[]{:S(2)}, u32[]{:S(2)}) collective-permute-start(bf16[12,24,128]{2,1,0:T(8,128)(2,1)S(1)} %get-tuple-element.30), channel_id=1, source_target_pairs={{0,4},{1,5},{2,6},{3,7},{4,8},{5,9},{6,10},{7,11},{8,12},{9,13},{1... | collective-permute-start | bytes 221192 | tf_op jit(solution)/shard_map/ppermute | solution.py:43
  58.0 6.2 %collective-permute-start.9 = (bf16[12,24,128]{2,1,0:T(8,128)(2,1)S(1)}, bf16[12,24,128]{2,1,0:T(8,128)(2,1)S(1)}, u32[]{:S(2)}, u32[]{:S(2)}) collective-permute-start(bf16[12,24,128]{2,1,0:T(8,128)(2,1)S(1)} %get-tuple-element.31), channel_id=1, source_target_pairs={{4,0},{5,1},{6,2},{7,3},{8,4},{9,5},{10,6},{11,7},{12,8},{13,9},{1... | collective-permute-start | bytes 221192 | tf_op jit(solution)/shard_map/ppermute | solution.py:43
  64.4 7.4 %collective-permute-start.11 = (bf16[12,44,128]{2,0,1:T(8,128)(2,1)S(1)}, bf16[12,44,128]{2,0,1:T(8,128)(2,1)S(1)}, u32[]{:S(2)}, u32[]{:S(2)}) collective-permute-start(bf16[12,44,128]{2,0,1:T(8,128)(2,1)S(1)} %maximum_bitcast_fusion.3), channel_id=1, source_target_pairs={{1,0},{2,1},{3,2},{5,4},{6,5},{7,6},{9,8},{10,9},{11,10},{13,12},{... | collective-permute-start | bytes 405512 | tf_op jit(solution)/shard_map/ppermute | solution.py:43
  65.8 7.5 %collective-permute-start.10 = (bf16[12,44,128]{2,0,1:T(8,128)(2,1)S(1)}, bf16[12,44,128]{2,0,1:T(8,128)(2,1)S(1)}, u32[]{:S(2)}, u32[]{:S(2)}) collective-permute-start(bf16[12,44,128]{2,0,1:T(8,128)(2,1)S(1)} %maximum_bitcast_fusion.2), channel_id=1, source_target_pairs={{0,1},{1,2},{2,3},{4,5},{5,6},{6,7},{8,9},{9,10},{10,11},{12,13},{... | collective-permute-start | bytes 405512 | tf_op jit(solution)/shard_map/ppermute | solution.py:43
  96.5 11.5 %all-to-all-start.1 = ((bf16[16,40,128]{2,1,0:T(8,128)(2,1)}), bf16[16,40,128]{2,1,0:T(8,128)(2,1)S(1)}, u32[]{:S(2)}, u32[]{:S(2)}) async-start(bf16[16,40,128]{2,1,0:T(8,128)(2,1)} %get-tuple-element.42), calls=%async_computation.1 | async-start | bytes 327680 | tf_op jit(solution)/shard_map/all_to_all | solution.py:433

commit v4 on v3

v4 whole, which is shorter than its diff:
```python
import functools

import jax
import jax.numpy as jnp
from jax import lax
from jax.experimental import pallas as pl
from jax.experimental.pallas import tpu as pltpu
from jax.sharding import PartitionSpec as P

FIRST_DILATION = 2
SECOND_DILATION = 8
HALO = FIRST_DILATION + SECOND_DILATION
GRID = ("row", "col")
TAPS = [(a, b) for a in (-1, 0, 1) for b in (-1, 0, 1)]
LEAD = 16
F32, BF16 = jnp.float32, jnp.bfloat16


ORDER = [0, 1, 3, 4, 6, 7, 2, 5, 8]


def dot(x, y):
    return jnp.dot(x, y, preferred_element_type=F32)


def rounded(x):
    return x.astype(BF16).astype(F32)


def up16(n):
    return -(-n // 16) * 16


def send(x, to):
    number = lax.axis_size("row")
    pairs = []
    for r in range(number):
        for c in range(number):
            row, col = to(r, c)
            if 0 <= row < number and 0 <= col < number:
                pairs.append((r * number + c, row * number + col))
    return lax.ppermute(x, GRID, pairs)


def inside(shape, side, width, top):
    number = lax.axis_size("row") * side
    rows = lax.broadcasted_iota(jnp.int32, shape, 0) + top - width
    cols = lax.broadcasted_iota(jnp.int32, shape, 1) - width
    at_row = lax.axis_index("row") * side + rows
    at_col = lax.axis_index("col") * side + cols
    return (at_row >= 0) & (at_row < number) & (at_col >= 0) & (at_col < number) & (cols < side + width)


def paired(source, starts, width, dilation, pairs, last, change):
    lanes = source.shape[2]
    low, high = slice(0, lanes), slice(lanes, 2 * lanes)

    def step(k, _):
        rows, lower = pl.ds(4 * k, 4), pl.ds(4 * k + dilation, 4)
        window = [change(source[rows, at : at + width]).astype(BF16) for at in starts]
        pairs[rows, :, low] = window[0]
        pairs[rows, :, high] = window[1]
        last[lower, :, low] = window[2]
        last[rows, :, high] = window[2]
        return 0

    lax.fori_loop(0, source.shape[0] // 4, step, 0)


def taps_sum(pairs, last, top, rows, dilation, weights):
    width, lanes = pairs.shape[1], pairs.shape[2] // 2
    size = rows * width
    total = None
    for k in range(5):
        if k < 3:
            window = pairs[pl.ds(top + dilation * k, rows)]
        elif k == 3:
            window = last[pl.ds(top + dilation, rows)]
        else:
            window = last[pl.ds(top + 3 * dilation, rows), :, :lanes]
        weight = weights[2 * lanes * k : min(2 * lanes * (k + 1), 9 * lanes)]
        term = dot(window.reshape(size, window.shape[2]), weight)
        total = term if total is None else total + term
    return total


def positive(x):
    return jnp.maximum(x, 0)


def assemble(area, tile, above, below, left, right):
    side = tile.shape[0]
    full, wide, channels = area.shape
    middle = slice(LEAD, LEAD + side)
    area[:, :LEAD] = jnp.zeros((full, LEAD, channels), F32)
    area[:, LEAD + side :] = jnp.zeros((full, wide - LEAD - side, channels), F32)
    area[HALO : HALO + side, middle] = tile
    area[:HALO, middle] = above[:HALO].astype(F32)
    area[HALO + side :, middle] = below[:HALO].astype(F32)
    area[:, LEAD - HALO : LEAD] = left[...].astype(F32)
    area[:, LEAD + side : LEAD + side + HALO] = right[...].astype(F32)


def first_branch(area, pairs, last, weights, bias, proj, store):
    full, wide = pairs.shape[:2]
    start = LEAD - SECOND_DILATION
    starts = [start + FIRST_DILATION * b for b in (-1, 0, 1)]
    paired(area, starts, wide, FIRST_DILATION, pairs, last, positive)

    def rows(step, _):
        top = step * 8
        pre = taps_sum(pairs, last, top, 8, FIRST_DILATION, weights) + bias[...]
        branch = dot(positive(pre).astype(BF16), proj[...])
        inputs = area[pl.ds(top + FIRST_DILATION, 8), start : start + wide]
        branch = rounded(inputs + branch.reshape(inputs.shape))
        store(top, pre.reshape(8, wide, pre.shape[1]), branch)
        return 0

    lax.fori_loop(0, (full - 2 * FIRST_DILATION) // 8, rows, 0)


def own_kernel(
    tile, above, below, left, right, weights, bias, proj,
    branch_own, gate_first, bottle_first, near_hidden,
    area, pairs, last, pre,
):
    side, first, second = tile.shape[0], FIRST_DILATION, SECOND_DILATION
    near, small = gate_first.shape[:2]
    assemble(area, tile[...].astype(F32), above, below, left, right)

    def store(top, pre_act, branch):
        pre[pl.ds(top, 8)] = pre_act
        branch_own[pl.ds(top, 8)] = branch

    first_branch(area, pairs, last, weights, bias, proj, store)
    for b in (-1, 0, 1):
        at = LEAD + first * b
        near_hidden[b + 1] = positive(area[HALO - first : HALO + side + first, at : at + small]).astype(BF16)
    edge = second - first
    part = pre[edge : edge + near, edge : edge + small]
    alive = (part > 0) & inside(part.shape, side, first, 0)
    gate_first[...] = jnp.where(alive, 1.0, 0.0).astype(BF16)
    bottle_first[...] = positive(pre[second : second + side, second : second + small]).astype(BF16)


def other_kernel(
    tile, above, below, left, right, weights, bias, proj, branch_own, w_second, b_second,
    gate_second, hidden_pairs, hidden_last, pre_second,
    area, pairs, last, current,
):
    side, first, second = tile.shape[0], FIRST_DILATION, SECOND_DILATION
    near, small = gate_second.shape[:2]
    assemble(area, tile[...].astype(F32), above, below, left, right)

    def store(top, pre_act, branch):
        here = pl.ds(top, 8)
        sym = rounded((branch_own[here] + branch) * 0.5)
        current[here] = jnp.where(inside(sym.shape, side, second, top), sym, 0)

    first_branch(area, pairs, last, weights, bias, proj, store)
    edge = second - first
    part = current[edge : edge + near, edge : edge + small]
    gate_second[...] = jnp.where(part > 0, 1.0, 0.0).astype(BF16)
    paired(current, [0, second, 2 * second], small, second, hidden_pairs, hidden_last, positive)

    def rows(step, _):
        top = step * 8
        total = taps_sum(hidden_pairs, hidden_last, top, 8, second, w_second) + b_second[...]
        pre_second[pl.ds(top, 8)] = total.reshape(8, small, total.shape[1])
        return 0

    lax.fori_loop(0, side // 8, rows, 0)


def turn_kernel(cotangent, mirrored, pre_second, p_second, grad_tile, grad_pre, above, below, padded):
    side, channels = cotangent.shape[0], cotangent.shape[2]
    small, first = pre_second.shape[1], FIRST_DILATION
    branch = (cotangent[...].astype(F32) + jnp.swapaxes(mirrored[...].astype(F32), 0, 1)) * 0.5
    padded[:, side:] = jnp.zeros((side, small - side, channels), F32)
    padded[:, :side] = rounded(branch)
    branch = padded[...].astype(BF16)
    grad_tile[...] = branch
    grad = dot(branch.reshape(side * small, channels), p_second[...]).reshape(side, small, channels)
    grad = jnp.where(pre_second[...] > 0, grad, 0)
    grad_pre[...] = grad.astype(BF16)
    grad, branch = grad[:, :side].astype(BF16), padded[:, :side].astype(BF16)
    above[:HALO], above[HALO:] = grad[:HALO], branch[:first]
    below[:HALO], below[HALO:] = grad[side - HALO :], branch[side - first :]


def weight_sums(rows, ends, grad_pre, hidden, bottle, grad_tile):
    side, small, lanes = grad_pre.shape
    inner = bottle.shape[2]
    size = side * small
    flat = grad_pre.reshape(size, lanes)
    turned = flat.T[:inner].astype(BF16)
    for a in range(3):
        b = 0
        while b < 3:
            window = hidden(a, b)
            grads = dot(turned, window.reshape(size, window.shape[2]))
            for at in range(0, window.shape[2], grad_tile.shape[2]):
                rows[(3 * a + b) * inner : (3 * a + b + 1) * inner] = grads[:, at : at + grad_tile.shape[2]]
                b += 1
    turned = bottle[...].reshape(size, inner).astype(F32).T.astype(BF16)
    rows[9 * inner : 10 * inner] = dot(turned, grad_tile.reshape(size, grad_tile.shape[2]))
    ends[...] = jnp.zeros(ends.shape, F32)
    ends[:, :lanes] = jnp.broadcast_to(jnp.sum(flat, axis=0, keepdims=True), (ends.shape[0], lanes))


def second_sums_kernel(grad_pre, pairs, last, pre_second, grad_tile, rows, ends):
    side, inner = grad_pre.shape[0], grad_pre.shape[2] // 2
    channels = grad_tile.shape[2]

    def hidden(a, b):
        top = SECOND_DILATION * a
        if b == 0:
            return pairs[top : top + side]
        return last[top + SECOND_DILATION : top + SECOND_DILATION + side, :, :channels]

    bottle = positive(pre_second[:, :, :inner]).astype(BF16)
    weight_sums(rows, ends, grad_pre[...].astype(F32), hidden, bottle, grad_tile[...])


def backward_kernel(
    grad_pre, grad_tile, above, below, left, right, left_branch, right_branch, gate_second, gate_first, near_hidden,
    bottle_first, v_second, p_first, rows_second, ends_second,
    parts, windows, windows_last, grad_first,
    area, pairs, last, branch, grads, rows, ends,
):
    side, channels, inner = grad_first.shape[0], grad_first.shape[2], bottle_first.shape[2]
    first, second = FIRST_DILATION, SECOND_DILATION
    near, small = gate_first.shape[:2]
    assemble(area, grad_pre[:, :side].astype(F32), above, below, left, right)
    branch[...] = jnp.zeros(branch.shape, F32)
    branch[first : first + side, first : first + side] = grad_tile[:, :side].astype(F32)
    branch[:first, first : first + side] = above[HALO:].astype(F32)
    branch[first + side :, first : first + side] = below[HALO:].astype(F32)
    branch[:, :first] = left_branch[...].astype(F32)
    branch[:, first + side : near] = right_branch[...].astype(F32)
    starts = [LEAD - HALO + second * (1 + b) for b in (-1, 0, 1)]
    paired(area, starts, small, second, pairs, last, lambda x: x)
    grads[:, small:] = jnp.zeros((near, grads.shape[1] - small, inner), F32)

    def sections(step, _):
        top = step * 7
        size = 7 * small
        total = taps_sum(pairs, last, top, 7, second, v_second)
        here = pl.ds(top, 7)
        grad = branch[here, :small].reshape(size, channels)
        gate = gate_second[here].astype(F32).reshape(size, channels) > 0
        own = rounded(grad + jnp.where(gate, total[:, :channels], 0))
        other = rounded(grad + jnp.where(gate, total[:, channels:], 0))
        grad = ((own + other) * 0.5).astype(BF16)
        branch[here, :small] = grad.astype(F32).reshape(7, small, channels)
        gate = gate_first[here].astype(F32).reshape(size, inner) > 0
        grad = rounded(jnp.where(gate, dot(grad, p_first[...]), 0))
        grads[here, :small] = grad.reshape(7, small, inner)
        return 0

    lax.fori_loop(0, near // 7, sections, 0)
    paired(grads, [0, first, 2 * first], small, first, windows, windows_last, lambda x: x)
    part = branch[first : first + side, first : first + small]
    grad_first[...] = part[:, :side].astype(BF16)
    def kept(x):
        return jnp.where(lax.broadcasted_iota(jnp.int32, x.shape, 1) < side, x, 0)

    part = kept(part).astype(BF16)
    grad = kept(grads[first : first + side, first : first + small])

    def hidden(a, b):
        return near_hidden[b, first * a : first * a + side]

    weight_sums(rows, ends, grad, hidden, bottle_first, part)

    devices, share = parts.shape[0] // 2, parts.shape[1] - 8
    count = rows.shape[0]
    for section, (table, end) in enumerate(((rows, ends), (rows_second, ends_second))):
        for j in range(devices):
            at = section * devices + j
            low, high = min(j * share, count), min((j + 1) * share, count)
            pieces = [table[low:high]] if low < high else []
            if high - low < share:
                pieces.append(jnp.zeros((share - (high - low), channels), F32))
            parts[at] = jnp.concatenate(pieces + [end[...]]).astype(BF16)


def input_kernel(windows, windows_last, grad_first, tile, v_first, out):
    side, channels = tile.shape[0], tile.shape[2]
    small = windows.shape[1]

    def rows(step, _):
        top = step * 8
        total = taps_sum(windows, windows_last, top, 8, FIRST_DILATION, v_first)
        here = pl.ds(top, 8)
        total = total.reshape(8, small, channels)[:, :side]
        total = jnp.where(tile[here].astype(F32) > 0, total, 0)
        out[here] = (grad_first[here].astype(F32) + total).astype(BF16)
        return 0

    lax.fori_loop(0, side // 8, rows, 0)


def total_kernel(scale, parts, rows, ends):
    share = rows.shape[1]
    total = jnp.sum(parts[...].astype(F32), axis=0) * scale
    rows[...] = jnp.broadcast_to(total[:share].astype(BF16)[None], rows.shape)
    ends[...] = total[share:]


def call(kernel, name, outs, scratch, flops, *operands):
    outs = [jax.ShapeDtypeStruct(shape, dtype) for shape, dtype in outs]
    moved = sum(x.size * x.dtype.itemsize for x in list(operands) + outs)
    return pl.pallas_call(
        kernel,
        name=name,
        out_shape=outs,
        scratch_shapes=[pltpu.VMEM(shape, dtype) for shape, dtype in scratch],
        cost_estimate=pl.CostEstimate(flops=flops, bytes_accessed=moved, transcendentals=0),
        compiler_params=pltpu.CompilerParams(vmem_limit_bytes=40 * 1024 * 1024),
    )(*operands)


def diagonal(x, y):
    zero = jnp.zeros_like(x)
    return jnp.concatenate([jnp.concatenate([x, zero], axis=-1), jnp.concatenate([zero, y], axis=-1)], axis=-2)


def local(activations, cotangent, conv_weight, conv_bias, out_weight):
    side, channels, inner = activations.shape[1], activations.shape[3], conv_weight.shape[3]
    number = lax.axis_size("row")
    first, second = FIRST_DILATION, SECOND_DILATION
    full, span, near = side + 2 * HALO, side + 2 * second, side + 2 * first
    wide, small = up16(span), up16(near)
    tile = activations[0]

    def row_strips(x):
        return send(x[side - HALO :], lambda r, c: (r + 1, c)), send(x[:HALO], lambda r, c: (r - 1, c))

    def column_strips(x, above, below):
        whole = jnp.concatenate([above, x, below])
        left = send(jnp.swapaxes(whole[:, side - HALO :], 0, 1), lambda r, c: (r, c + 1))
        right = send(jnp.swapaxes(whole[:, :HALO], 0, 1), lambda r, c: (r, c - 1))
        return jnp.swapaxes(left, 0, 1), jnp.swapaxes(right, 0, 1)

    mirrored = send(tile, lambda r, c: (c, r))
    above, below = row_strips(tile)
    left, right = column_strips(tile, above, below)
    own = (tile, above, below, left, right)
    other = jnp.swapaxes(mirrored, 0, 1)
    above, below = row_strips(other)
    left, right = column_strips(other, above, below)
    other = (other, above, below, left, right)

    bias_rows = jnp.pad(conv_bias, ((0, 7), (0, channels - inner)))
    packed = jnp.concatenate(
        [jnp.swapaxes(conv_weight[0], 1, 2).reshape(9 * inner, channels), out_weight[0], bias_rows]
    )
    packed = lax.all_gather(packed, "segment")
    conv = packed[:, : 9 * inner].reshape(2, 9, inner, channels)
    swapped = conv.reshape(2, 3, 3, inner, channels).swapaxes(1, 2).reshape(conv.shape)
    proj = packed[:, 9 * inner : 10 * inner]
    bias = packed[:, 10 * inner, :inner].astype(F32)[:, None]

    def ordered(x):
        return jnp.concatenate([x[k] for k in ORDER])

    w_own = ordered(jnp.swapaxes(conv[0], 1, 2))
    w_other = ordered(jnp.swapaxes(swapped[0], 1, 2))
    w_second = ordered(jnp.swapaxes(jnp.concatenate([conv[1], swapped[1]], axis=1), 1, 2))
    v_second = ordered(diagonal(conv[1, ::-1], swapped[1, ::-1]))
    v_first = ordered(conv[0, ::-1])
    p_second = jnp.concatenate([proj[1].T, proj[1].T], axis=1)
    p_back = proj[0].T

    late, _ = lax.optimization_barrier((cotangent[0], own[3]))
    late_mirrored = send(late, lambda r, c: (c, r))

    area = ((full, LEAD + up16(side + LEAD), channels), F32)
    pairs = ((full, wide, 2 * channels), BF16)
    last = ((full + first, wide, 2 * channels), BF16)
    branch_own, gate_first, bottle_first, near_hidden = call(
        own_kernel,
        "own_branch",
        [
            ((span, wide, channels), F32),
            ((near, small, inner), BF16),
            ((side, small, inner), BF16),
            ((3, near, small, channels), BF16),
        ],
        [area, pairs, last, ((span, wide, inner), F32)],
        span * wide * channels * inner * 20,
        *own,
        *(w_own, bias[0], proj[0]),
    )
    gate_second, hidden_pairs, hidden_last, pre_second = call(
        other_kernel,
        "other_branch",
        [
            ((near, small, channels), BF16),
            ((span, small, 2 * channels), BF16),
            ((span + second, small, 2 * channels), BF16),
            ((side, small, 2 * inner), F32),
        ],
        [area, pairs, last, ((span, wide, channels), F32)],
        span * wide * channels * inner * 30,
        *other,
        *(w_other, bias[0], proj[0], branch_own, w_second, jnp.tile(bias[1], (1, 2))),
    )

    grad_tile, grad_pre, strip_above, strip_below = call(
        turn_kernel,
        "turn",
        [
            ((side, small, channels), BF16),
            ((side, small, 2 * inner), BF16),
            ((HALO + first, side, channels), BF16),
            ((HALO + first, side, channels), BF16),
        ],
        [((side, small, channels), F32)],
        2 * side * small * channels * 2 * inner,
        *(late, late_mirrored, pre_second, p_second),
    )

    above = send(strip_below, lambda r, c: (r + 1, c))
    below = send(strip_above, lambda r, c: (r - 1, c))
    rows_second, ends_second = call(
        second_sums_kernel,
        "second_sums",
        [((10 * inner, channels), F32), ((8, channels), F32)],
        [],
        20 * side * small * channels * inner,
        *(grad_pre, hidden_pairs, hidden_last, pre_second, grad_tile),
    )

    def columns(low, high, low_branch, high_branch):
        grads = jnp.concatenate([above[:HALO, low:high], grad_pre[:, low:high], below[:HALO, low:high]])
        here = slice(low_branch, high_branch)
        branches = jnp.concatenate([above[HALO:, here], grad_tile[:, here], below[HALO:, here]])
        branches = jnp.pad(branches, ((second, second), (0, 0), (0, 0)))
        return jnp.swapaxes(jnp.concatenate([grads, branches], axis=1), 0, 1)

    left = send(columns(side - HALO, side, side - first, side), lambda r, c: (r, c + 1))
    right = send(columns(0, HALO, 0, first), lambda r, c: (r, c - 1))
    left, right = jnp.swapaxes(left, 0, 1), jnp.swapaxes(right, 0, 1)

    devices = number * number
    share = -(-10 * inner // (8 * devices)) * 8
    parts, windows, windows_last, grad_first = call(
        backward_kernel,
        "backward",
        [
            ((2 * devices, share + 8, channels), BF16),
            ((near, small, 2 * inner), BF16),
            ((near + first, small, 2 * inner), BF16),
            ((side, side, channels), BF16),
        ],
        [
            area,
            ((full, small, 2 * channels), BF16),
            ((full + second, small, 2 * channels), BF16),
            ((near, small + 16, channels), F32),
            ((near, small + 16, inner), F32),
            ((10 * inner, channels), F32),
            ((8, channels), F32),
        ],
        36 * near * small * channels * channels,
        *(grad_pre, grad_tile, above, below, left[:, :HALO], right[:, :HALO]),
        *(left[second : second + near, HALO:], right[second : second + near, HALO:]),
        *(gate_second, gate_first, near_hidden, bottle_first, v_second, p_back, rows_second, ends_second),
    )

    parts = lax.all_to_all(parts, ("segment",) + GRID, 0, 0, tiled=True)
    (input_gradient,) = call(
        input_kernel,
        "input",
        [((side, side, channels), BF16)],
        [],
        18 * side * small * channels * channels,
        *(windows, windows_last, grad_first, tile, v_first),
    )
    cells = lax.axis_size("segment") * (side * number) * (side * number)
    rows, ends = call(
        functools.partial(total_kernel, float(cells) ** -0.5),
        "total",
        [((devices, share, channels), BF16), ((8, channels), F32)],
        [],
        parts.size,
        parts,
    )
    rows = lax.all_to_all(rows, GRID, 0, 0, tiled=True).reshape(devices * share, channels).astype(F32)
    conv_gradient = jnp.swapaxes(rows[: 9 * inner].reshape(1, 9, inner, channels), 2, 3)
    return (input_gradient[None], conv_gradient, ends[:1, :inner], rows[None, 9 * inner : 10 * inner])


def solution(mesh):
    in_specs = (
        P("segment", "row", "col", None),
        P("segment", "row", "col", None),
        P("segment", None, None, None),
        P("segment", None),
        P("segment", None, None),
    )
    out_specs = (
        P("segment", "row", "col", None),
        P("segment", None, None, None),
        P("segment", None),
        P("segment", None, None),
    )
    return jax.shard_map(local, mesh=mesh, in_specs=in_specs, out_specs=out_specs, check_vma=False)
```

time: 110 us -> 107 us (0.973)
  blocking collectives: 21.4 us -> 2.04 us
  waiting for transfers between devices: 23 us -> 38.7 us
  Pallas kernels: 12.5 us -> 15 us
  starting transfers between devices: 43.4 us -> 42 us
    all_to_all x1 -> x0, blocking collectives: 19.3 us -> none  [local(): parts = lax.all_to_all(parts, ('segment',) + GRID, 0, 0, tiled=True)]
    all_to_all x0 -> x1, waiting for transfers between devices: none -> 13.6 us  [local(): parts = lax.all_to_all(parts, ('segment',) + GRID, 0, 0, tiled=True)]
    ppermute x12 -> x14, starting transfers between devices: 39.9 us -> 35.8 us  [send(): return lax.ppermute(x, GRID, pairs)]
    all_to_all x0 -> x1, starting transfers between devices: none -> 2.68 us  [local(): parts = lax.all_to_all(parts, ('segment',) + GRID, 0, 0, tiled=True)]
    pallas_call x6 -> x7, Pallas kernels: 12.5 us -> 15 us  [call(): pl.pallas_call(kernel, name=name, out_shape=outs, scratch_shapes=[pltpu.V...]
    ppermute x12 -> x14, waiting for transfers between devices: 17.2 us -> 19.1 us  [send(): return lax.ppermute(x, GRID, pairs)]
    squeeze x2 -> x3, local copies, waits for them, and re-layouts: 1.65 us -> 0.48 us  [the longest x1 0.23 us: local(): w_own = ordered(jnp.swapaxes(conv[0], 1, 2))]
  transfers between devices with their start and end apart: 13 -> 16, of which waited for: 8 -> 8; matrix products, arithmetic and copies ran while one was open for 4% -> 4% of each run, Pallas kernels for 8% -> 9%
where the time goes in v4:
time: 107 us; the launch traced here: 106 us
  starting transfers between devices  42 us (39%)
  waiting for transfers between devices  38.7 us (36%)
  Pallas kernels  15 us (14%)
  local copies, waits for them, and re-layouts  5.52 us (5%)
  blocking collectives  2.04 us (2%)
  other arithmetic  1.6 us (1%)
  between operations  1.34 us (1%)
    ppermute x14, starting transfers between devices, send(): return lax.ppermute(x, GRID, pairs)  35.8 us
    ppermute x14, waiting for transfers between devices, send(): return lax.ppermute(x, GRID, pairs)  19.1 us
    pallas_call x7, Pallas kernels, call(): pl.pallas_call(kernel, name=name, out_shape=outs, scratch_shapes=[pltpu.V...  15 us
    all_to_all x1, waiting for transfers between devices, local(): parts = lax.all_to_all(parts, ('segment',) + GRID, 0, 0, tiled=True)  13.6 us
    all_to_all x1, waiting for transfers between devices, local(): lax.all_to_all(rows, GRID, 0, 0, tiled=True)  6.06 us
    all_to_all x1, starting transfers between devices, local(): lax.all_to_all(rows, GRID, 0, 0, tiled=True)  3.52 us
    all_to_all x1, starting transfers between devices, local(): parts = lax.all_to_all(parts, ('segment',) + GRID, 0, 0, tiled=True)  2.68 us
  transfers between devices with their start and end apart: 16, of which 8 were waited for; matrix products, arithmetic and copies ran while one was open for 4% of the time, Pallas kernels for 9%

profile of v4, /device:TPU:0, one launch (start us, length us, event | category | flops | bytes accessed | tf_op | source)
XLA Modules:
  0.0 106.2 jit_solution(1963557280630266994)
XLA Ops:
  0.6 0.9 slice_bitcast_fusion.12
  1.5 1.3 %collective-permute-start.1 = (bf16[10,24,128]{2,1,0:T(8,128)(2,1)S(1)}, bf16[10,24,128]{2,1,0:T(8,128)(2,1)S(1)}, u32[]{:S(2)}, u32[]{:S(2)}) collective-permute-start(bf16[10,24,128]{2,1,0:T(8,128)(2,1)S(1)} %get-tuple-element.64), channel_id=1, source_target_pairs={{4,0},{5,1},{6,2},{7,3},{8,4},{9,5},{10,6},{11,7},{12,8},{13,9},{1... | collective-permute-start | bytes 184328 | tf_op jit(solution)/shard_map/ppermute | solution.py:42
  2.8 5.5 %collective-permute-start = (bf16[10,24,128]{2,1,0:T(8,128)(2,1)S(1)}, bf16[10,24,128]{2,1,0:T(8,128)(2,1)S(1)}, u32[]{:S(2)}, u32[]{:S(2)}) collective-permute-start(bf16[10,24,128]{2,1,0:T(8,128)(2,1)S(1)} %get-tuple-element.63), channel_id=1, source_target_pairs={{0,4},{1,5},{2,6},{3,7},{4,8},{5,9},{6,10},{7,11},{8,12},{9,13},{1... | collective-permute-start | bytes 184328 | tf_op jit(solution)/shard_map/ppermute | solution.py:42
  8.3 1.6 %collective-permute-start.4 = (bf16[24,24,128]{2,1,0:T(8,128)(2,1)}, bf16[24,24,128]{2,1,0:T(8,128)(2,1)S(1)}, u32[]{:S(2)}, u32[]{:S(2)}) collective-permute-start(bf16[24,24,128]{2,1,0:T(8,128)(2,1)} %bitcast.254), channel_id=1, source_target_pairs={{0,0},{1,4},{2,8},{3,12},{4,1},{5,5},{6,9},{7,13},{8,2},{9,6},{10,... | collective-permute-start | bytes 442376 | tf_op jit(solution)/shard_map/ppermute | solution.py:42
  9.9 1.0 fusion.4
  10.8 2.0 %all-gather = bf16[1296,128]{1,0:T(8,128)(2,1)S(1)} all-gather(bf16[648,128]{1,0:T(8,128)(2,1)S(1)} %fusion.4), channel_id=2, replica_groups=mesh['segment'=2,'row'=4,'col'=4] {'segment'}, dimensions={0}, use_global_device_ids=true | all-gather | bytes 497664 | tf_op jit(solution)/shard_map/all_gather | solution.py:359
  13.0 0.2 copy.27
  13.2 0.2 copy.23
  13.6 0.2 copy.25
  13.9 0.2 copy.28
  14.2 0.2 maximum_bitcast_fusion
  14.8 0.6 copy-done
  15.5 6.6 %collective-permute-start.2 = (bf16[10,44,128]{2,0,1:T(8,128)(2,1)S(1)}, bf16[10,44,128]{2,0,1:T(8,128)(2,1)S(1)}, u32[]{:S(2)}, u32[]{:S(2)}) collective-permute-start(bf16[10,44,128]{2,0,1:T(8,128)(2,1)S(1)} %get-tuple-element.56), channel_id=1, source_target_pairs={{0,1},{1,2},{2,3},{4,5},{5,6},{6,7},{8,9},{9,10},{10,11},{12,13},{... | collective-permute-start | bytes 337928 | tf_op jit(solution)/shard_map/ppermute | solution.py:42
  22.2 5.3 %collective-permute-start.5 = (bf16[10,24,128]{2,0,1:T(8,128)(2,1)S(1)}, bf16[10,24,128]{2,0,1:T(8,128)(2,1)S(1)}, u32[]{:S(2)}, u32[]{:S(2)}) collective-permute-start(bf16[10,24,128]{2,0,1:T(8,128)(2,1)S(1)} %get-tuple-element.62), channel_id=1, source_target_pairs={{0,4},{1,5},{2,6},{3,7},{4,8},{5,9},{6,10},{7,11},{8,12},{9,13},{1... | collective-permute-start | bytes 184328 | tf_op jit(solution)/shard_map/ppermute | solution.py:42
  27.5 1.3 %collective-permute-start.6 = (bf16[10,24,128]{2,0,1:T(8,128)(2,1)S(1)}, bf16[10,24,128]{2,0,1:T(8,128)(2,1)S(1)}, u32[]{:S(2)}, u32[]{:S(2)}) collective-permute-start(bf16[10,24,128]{2,0,1:T(8,128)(2,1)S(1)} %get-tuple-element.61), channel_id=1, source_target_pairs={{4,0},{5,1},{6,2},{7,3},{8,4},{9,5},{10,6},{11,7},{12,8},{13,9},{1... | collective-permute-start | bytes 184328 | tf_op jit(solution)/shard_map/ppermute | solution.py:42
  28.8 0.1 tile.12.b_second
  28.9 0.1 copy.38
  29.0 0.1 copy.37
  29.2 1.3 %collective-permute-start.9 = (bf16[10,44,128]{2,0,1:T(8,128)(2,1)S(1)}, bf16[10,44,128]{2,0,1:T(8,128)(2,1)S(1)}, u32[]{:S(2)}, u32[]{:S(2)}) collective-permute-start(bf16[10,44,128]{2,0,1:T(8,128)(2,1)S(1)} %get-tuple-element.55), channel_id=1, source_target_pairs={{1,0},{2,1},{3,2},{5,4},{6,5},{7,6},{9,8},{10,9},{11,10},{13,12},{... | collective-permute-start | bytes 337928 | tf_op jit(solution)/shard_map/ppermute | solution.py:42
  30.5 0.7 collective-permute-start.3
  31.2 2.9 %collective-permute-done.6 = bf16[10,24,128]{2,0,1:T(8,128)(2,1)S(1)} collective-permute-done((bf16[10,24,128]{2,0,1:T(8,128)(2,1)S(1)}, bf16[10,24,128]{2,0,1:T(8,128)(2,1)S(1)}, u32[]{:S(2)}, u32[]{:S(2)}) %collective-permute-start.6) | collective-permute-done | bytes 61472 | tf_op jit(solution)/shard_map/ppermute | solution.py:42
  34.0 0.1 fusion.5
  34.1 4.4 %collective-permute-start.7 = (bf16[10,44,128]{2,1,0:T(8,128)(2,1)S(1)}, bf16[10,44,128]{2,1,0:T(8,128)(2,1)S(1)}, u32[]{:S(2)}, u32[]{:S(2)}) collective-permute-start(bf16[10,44,128]{2,1,0:T(8,128)(2,1)S(1)} %get-tuple-element.47), channel_id=1, source_target_pairs={{0,1},{1,2},{2,3},{4,5},{5,6},{6,7},{8,9},{9,10},{10,11},{12,13},{... | collective-permute-start | bytes 337928 | tf_op jit(solution)/shard_map/ppermute | solution.py:42
  38.5 1.3 %collective-permute-start.8 = (bf16[10,44,128]{2,1,0:T(8,128)(2,1)S(1)}, bf16[10,44,128]{2,1,0:T(8,128)(2,1)S(1)}, u32[]{:S(2)}, u32[]{:S(2)}) collective-permute-start(bf16[10,44,128]{2,1,0:T(8,128)(2,1)S(1)} %get-tuple-element.46), channel_id=1, source_target_pairs={{1,0},{2,1},{3,2},{5,4},{6,5},{7,6},{9,8},{10,9},{11,10},{13,12},{... | collective-permute-start | bytes 337928 | tf_op jit(solution)/shard_map/ppermute | solution.py:42
  39.8 0.1 pad_maximum_fusion.3.p_second
  39.9 3.8 %collective-permute-done.9 = bf16[10,44,128]{2,0,1:T(8,128)(2,1)S(1)} collective-permute-done((bf16[10,44,128]{2,0,1:T(8,128)(2,1)S(1)}, bf16[10,44,128]{2,0,1:T(8,128)(2,1)S(1)}, u32[]{:S(2)}, u32[]{:S(2)}) %collective-permute-start.9) | collective-permute-done | bytes 112672 | tf_op jit(solution)/shard_map/ppermute | solution.py:42
  43.8 3.5 %own_branch.1 = (f32[40,48,128]{2,1,0:T(8,128)S(1)}, bf16[28,32,64]{2,1,0:T(8,128)(2,1)S(1)}, bf16[24,32,64]{2,1,0:T(8,128)(2,1)S(1)}, bf16[3,28,32,128]{3,2,1,0:T(8,128)(2,1)S(1)}) custom-call(bf16[24,24,128]{2,1,0:T(8,128)(2,1)S(1)} %bitcast.256, bf16[10,24,128]{2,1,0:T(8,128)(2,1)S(1)} %collective-permute-done.above, ...), custom_call_target="tpu_custom_call" | custom-call | flops 314572800 | bytes 2543872 | tf_op jit(solution)/shard_map/own_branch/pallas_call | solution.py:314
  47.4 2.0 %collective-permute-done.8 = bf16[10,44,128]{2,1,0:T(8,128)(2,1)S(1)} collective-permute-done((bf16[10,44,128]{2,1,0:T(8,128)(2,1)S(1)}, bf16[10,44,128]{2,1,0:T(8,128)(2,1)S(1)}, u32[]{:S(2)}, u32[]{:S(2)}) %collective-permute-start.8) | collective-permute-done | bytes 112672 | tf_op jit(solution)/shard_map/ppermute | solution.py:42
  49.4 4.5 %other_branch.1 = (bf16[28,32,128]{2,1,0:T(8,128)(2,1)S(1)}, bf16[40,32,256]{2,1,0:T(8,128)(2,1)S(1)}, bf16[48,32,256]{2,1,0:T(8,128)(2,1)S(1)}, f32[24,32,128]{2,1,0:T(8,128)S(1)}) custom-call(bf16[24,24,128]{2,1,0:T(8,128)(2,1)S(1)} %copy.29.tile, bf16[10,24,128]{2,1,0:T(8,128)(2,1)S(1)} %copy.30.above, bf16[10,24,128]{2,1,0:T(8,128)(2,1)S(1)} %copy.31.below, ...), custom_call_target="tpu_custom_call" | custom-call | flops 471859200 | bytes 4002560 | tf_op jit(solution)/shard_map/other_branch/pallas_call | solution.py:314
  53.9 0.3 turn.1
  54.1 1.3 %collective-permute-start.10 = (bf16[12,24,128]{2,1,0:T(8,128)(2,1)S(1)}, bf16[12,24,128]{2,1,0:T(8,128)(2,1)S(1)}, u32[]{:S(2)}, u32[]{:S(2)}) collective-permute-start(bf16[12,24,128]{2,1,0:T(8,128)(2,1)S(1)} %get-tuple-element.30), channel_id=1, source_target_pairs={{0,4},{1,5},{2,6},{3,7},{4,8},{5,9},{6,10},{7,11},{8,12},{9,13},{1... | collective-permute-start | bytes 221192 | tf_op jit(solution)/shard_map/ppermute | solution.py:42
  55.4 1.3 %collective-permute-start.11 = (bf16[12,24,128]{2,1,0:T(8,128)(2,1)S(1)}, bf16[12,24,128]{2,1,0:T(8,128)(2,1)S(1)}, u32[]{:S(2)}, u32[]{:S(2)}) collective-permute-start(bf16[12,24,128]{2,1,0:T(8,128)(2,1)S(1)} %get-tuple-element.31), channel_id=1, source_target_pairs={{4,0},{5,1},{6,2},{7,3},{8,4},{9,5},{10,6},{11,7},{12,8},{13,9},{1... | collective-permute-start | bytes 221192 | tf_op jit(solution)/shard_map/ppermute | solution.py:42
  56.8 4.9 %collective-permute-done.11.below = bf16[12,24,128]{2,1,0:T(8,128)(2,1)S(1)} collective-permute-done((bf16[12,24,128]{2,1,0:T(8,128)(2,1)S(1)}, bf16[12,24,128]{2,1,0:T(8,128)(2,1)S(1)}, u32[]{:S(2)}, u32[]{:S(2)}) %collective-permute-start.11) | collective-permute-done | bytes 73760 | tf_op jit(solution)/shard_map/ppermute | solution.py:42
  61.9 2.7 %collective-permute-start.12 = (bf16[12,44,128]{2,0,1:T(8,128)(2,1)S(1)}, bf16[12,44,128]{2,0,1:T(8,128)(2,1)S(1)}, u32[]{:S(2)}, u32[]{:S(2)}) collective-permute-start(bf16[12,44,128]{2,0,1:T(8,128)(2,1)S(1)} %maximum_bitcast_fusion.1), channel_id=1, source_target_pairs={{0,1},{1,2},{2,3},{4,5},{5,6},{6,7},{8,9},{9,10},{10,11},{12,13},{... | collective-permute-start | bytes 405512 | tf_op jit(solution)/shard_map/ppermute | solution.py:42
  64.7 1.3 %collective-permute-start.13 = (bf16[12,44,128]{2,0,1:T(8,128)(2,1)S(1)}, bf16[12,44,128]{2,0,1:T(8,128)(2,1)S(1)}, u32[]{:S(2)}, u32[]{:S(2)}) collective-permute-start(bf16[12,44,128]{2,0,1:T(8,128)(2,1)S(1)} %maximum_bitcast_fusion.2), channel_id=1, source_target_pairs={{1,0},{2,1},{3,2},{5,4},{6,5},{7,6},{9,8},{10,9},{11,10},{13,12},{... | collective-permute-start | bytes 405512 | tf_op jit(solution)/shard_map/ppermute | solution.py:42
  66.0 0.5 second_sums.1
  66.5 1.1 collective-permute-done.12
  67.6 4.5 %collective-permute-done.13 = bf16[12,44,128]{2,0,1:T(8,128)(2,1)S(1)} collective-permute-done((bf16[12,44,128]{2,0,1:T(8,128)(2,1)S(1)}, bf16[12,44,128]{2,0,1:T(8,128)(2,1)S(1)}, u32[]{:S(2)}, u32[]{:S(2)}) %collective-permute-start.13) | collective-permute-done | bytes 135200 | tf_op jit(solution)/shard_map/ppermute | solution.py:42
  72.1 4.2 %backward.1 = (bf16[32,48,128]{2,1,0:T(8,128)(2,1)}, bf16[28,32,128]{2,1,0:T(8,128)(2,1)S(1)}, bf16[30,32,128]{2,1,0:T(8,128)(2,1)S(1)}, bf16[24,24,128]{2,1,0:T(8,128)(2,1)S(1)}) custom-call(bf16[24,32,128]{2,1,0:T(8,128)(2,1)S(1)} %get-tuple-element.28.grad_pre, bf16[24,32,128]{2,1,0:T(8,128)(2,1)S(1)} %get-tuple-element.29.grad_tile, ...), custom_call_target="tpu_custom_call" | custom-call | flops 528482304 | bytes 3878912 | tf_op jit(solution)/shard_map/backward/pallas_call | solution.py:314
  76.3 2.7 %all-to-all-start = ((bf16[32,48,128]{2,1,0:T(8,128)(2,1)}), bf16[32,48,128]{2,1,0:T(8,128)(2,1)S(1)}, u32[]{:S(2)}, u32[]{:S(2)}) async-start(bf16[32,48,128]{2,1,0:T(8,128)(2,1)} %get-tuple-element.43), calls=%async_computation | async-start | bytes 786432 | tf_op jit(solution)/shard_map/all_to_all | solution.py:473
  79.0 13.6 %all-to-all-done.parts = bf16[32,48,128]{2,1,0:T(8,128)(2,1)S(1)} async-done(((bf16[32,48,128]{2,1,0:T(8,128)(2,1)}), bf16[32,48,128]{2,1,0:T(8,128)(2,1)S(1)}, u32[]{:S(2)}, u32[]{:S(2)}) %all-to-all-start) | async-done | bytes 393248 | tf_op jit(solution)/shard_map/all_to_all | solution.py:473
  92.6 0.7 total.1
  93.3 3.5 %all-to-all-start.1 = ((bf16[16,40,128]{2,1,0:T(8,128)(2,1)}), bf16[16,40,128]{2,1,0:T(8,128)(2,1)S(1)}, u32[]{:S(2)}, u32[]{:S(2)}) async-start(bf16[16,40,128]{2,1,0:T(8,128)(2,1)} %get-tuple-element.44), calls=%async_computation.1 | async-start | bytes 327680 | tf_op jit(solution)/shard_map/all_to_all | solution.py:491
  96.9 1.4 %input.1 = bf16[24,24,128]{2,1,0:T(8,128)(2,1)} custom-call(bf16[28,32,128]{2,1,0:T(8,128)(2,1)S(1)} %get-tuple-element.40.windows, bf16[30,32,128]{2,1,0:T(8,128)(2,1)S(1)} %get-tuple-element.41.windows_last, bf16[24,24,128]{2,1,0:T(8,128)(2,1)S(1)} %get-tuple-element.42.grad_first, bf16[24,24,128]{2,1,0:T(8,128)(2,1)S(1)} %bitcast.257, ...), custom_call_target="tpu_custom_call" | custom-call | flops 226492416 | bytes 1064960 | tf_op jit(solution)/shard_map/input/pallas_call | solution.py:314
  98.3 0.5 slice.384
  98.8 6.1 %all-to-all-done.1 = bf16[16,40,128]{2,1,0:T(8,128)(2,1)S(1)} async-done(((bf16[16,40,128]{2,1,0:T(8,128)(2,1)}), bf16[16,40,128]{2,1,0:T(8,128)(2,1)S(1)}, u32[]{:S(2)}, u32[]{:S(2)}) %all-to-all-start.1) | async-done | bytes 163872 | tf_op jit(solution)/shard_map/all_to_all | solution.py:491
  104.9 0.7 slice.457
  105.6 0.6 slice_bitcast_fusion.13
  (87 shorter events, 1.3 us)
Async XLA Ops:
  1.5 13.3 %collective-permute-start.1 = (bf16[10,24,128]{2,1,0:T(8,128)(2,1)S(1)}, bf16[10,24,128]{2,1,0:T(8,128)(2,1)S(1)}, u32[]{:S(2)}, u32[]{:S(2)}) collective-permute-start(bf16[10,24,128]{2,1,0:T(8,128)(2,1)S(1)} %get-tuple-element.64), channel_id=1, source_target_pairs={{4,0},{5,1},{6,2},{7,3},{8,4},{9,5},{10,6},{11,7},{12,8},{13,9},{1... | collective-permute-start | bytes 184328 | tf_op jit(solution)/shard_map/ppermute | solution.py:42
  2.8 12.0 %collective-permute-start = (bf16[10,24,128]{2,1,0:T(8,128)(2,1)S(1)}, bf16[10,24,128]{2,1,0:T(8,128)(2,1)S(1)}, u32[]{:S(2)}, u32[]{:S(2)}) collective-permute-start(bf16[10,24,128]{2,1,0:T(8,128)(2,1)S(1)} %get-tuple-element.63), channel_id=1, source_target_pairs={{0,4},{1,5},{2,6},{3,7},{4,8},{5,9},{6,10},{7,11},{8,12},{9,13},{1... | collective-permute-start | bytes 184328 | tf_op jit(solution)/shard_map/ppermute | solution.py:42
  8.3 13.9 %collective-permute-start.4 = (bf16[24,24,128]{2,1,0:T(8,128)(2,1)}, bf16[24,24,128]{2,1,0:T(8,128)(2,1)S(1)}, u32[]{:S(2)}, u32[]{:S(2)}) collective-permute-start(bf16[24,24,128]{2,1,0:T(8,128)(2,1)} %bitcast.254), channel_id=1, source_target_pairs={{0,0},{1,4},{2,8},{3,12},{4,1},{5,5},{6,9},{7,13},{8,2},{9,6},{10,... | collective-permute-start | bytes 442376 | tf_op jit(solution)/shard_map/ppermute | solution.py:42
  14.5 0.9 copy-start
  14.7 15.8 %copy-start.1 = (bf16[1,24,24,128]{3,2,1,0:T(8,128)(2,1)S(1)}, bf16[1,24,24,128]{3,2,1,0:T(8,128)(2,1)}, u32[]{:S(2)}) copy-start(bf16[1,24,24,128]{3,2,1,0:T(8,128)(2,1)} %param.6) | copy-start | bytes 442372
  15.5 14.9 %collective-permute-start.2 = (bf16[10,44,128]{2,0,1:T(8,128)(2,1)S(1)}, bf16[10,44,128]{2,0,1:T(8,128)(2,1)S(1)}, u32[]{:S(2)}, u32[]{:S(2)}) collective-permute-start(bf16[10,44,128]{2,0,1:T(8,128)(2,1)S(1)} %get-tuple-element.56), channel_id=1, source_target_pairs={{0,1},{1,2},{2,3},{4,5},{5,6},{6,7},{8,9},{9,10},{10,11},{12,13},{... | collective-permute-start | bytes 337928 | tf_op jit(solution)/shard_map/ppermute | solution.py:42
  22.2 8.9 %collective-permute-start.5 = (bf16[10,24,128]{2,0,1:T(8,128)(2,1)S(1)}, bf16[10,24,128]{2,0,1:T(8,128)(2,1)S(1)}, u32[]{:S(2)}, u32[]{:S(2)}) collective-permute-start(bf16[10,24,128]{2,0,1:T(8,128)(2,1)S(1)} %get-tuple-element.62), channel_id=1, source_target_pairs={{0,4},{1,5},{2,6},{3,7},{4,8},{5,9},{6,10},{7,11},{8,12},{9,13},{1... | collective-permute-start | bytes 184328 | tf_op jit(solution)/shard_map/ppermute | solution.py:42
  27.5 6.5 %collective-permute-start.6 = (bf16[10,24,128]{2,0,1:T(8,128)(2,1)S(1)}, bf16[10,24,128]{2,0,1:T(8,128)(2,1)S(1)}, u32[]{:S(2)}, u32[]{:S(2)}) collective-permute-start(bf16[10,24,128]{2,0,1:T(8,128)(2,1)S(1)} %get-tuple-element.61), channel_id=1, source_target_pairs={{4,0},{5,1},{6,2},{7,3},{8,4},{9,5},{10,6},{11,7},{12,8},{13,9},{1... | collective-permute-start | bytes 184328 | tf_op jit(solution)/shard_map/ppermute | solution.py:42
  29.2 14.6 %collective-permute-start.9 = (bf16[10,44,128]{2,0,1:T(8,128)(2,1)S(1)}, bf16[10,44,128]{2,0,1:T(8,128)(2,1)S(1)}, u32[]{:S(2)}, u32[]{:S(2)}) collective-permute-start(bf16[10,44,128]{2,0,1:T(8,128)(2,1)S(1)} %get-tuple-element.55), channel_id=1, source_target_pairs={{1,0},{2,1},{3,2},{5,4},{6,5},{7,6},{9,8},{10,9},{11,10},{13,12},{... | collective-permute-start | bytes 337928 | tf_op jit(solution)/shard_map/ppermute | solution.py:42
  30.5 23.4 %collective-permute-start.3 = (bf16[24,24,128]{2,1,0:T(8,128)(2,1)S(1)}, bf16[24,24,128]{2,1,0:T(8,128)(2,1)S(1)}, u32[]{:S(2)}, u32[]{:S(2)}) collective-permute-start(bf16[24,24,128]{2,1,0:T(8,128)(2,1)S(1)} %bitcast.262), channel_id=1, source_target_pairs={{0,0},{1,4},{2,8},{3,12},{4,1},{5,5},{6,9},{7,13},{8,2},{9,6},{10,... | collective-permute-start | bytes 442376 | tf_op jit(solution)/shard_map/ppermute | solution.py:42
  34.1 13.2 %collective-permute-start.7 = (bf16[10,44,128]{2,1,0:T(8,128)(2,1)S(1)}, bf16[10,44,128]{2,1,0:T(8,128)(2,1)S(1)}, u32[]{:S(2)}, u32[]{:S(2)}) collective-permute-start(bf16[10,44,128]{2,1,0:T(8,128)(2,1)S(1)} %get-tuple-element.47), channel_id=1, source_target_pairs={{0,1},{1,2},{2,3},{4,5},{5,6},{6,7},{8,9},{9,10},{10,11},{12,13},{... | collective-permute-start | bytes 337928 | tf_op jit(solution)/shard_map/ppermute | solution.py:42
  38.5 10.8 %collective-permute-start.8 = (bf16[10,44,128]{2,1,0:T(8,128)(2,1)S(1)}, bf16[10,44,128]{2,1,0:T(8,128)(2,1)S(1)}, u32[]{:S(2)}, u32[]{:S(2)}) collective-permute-start(bf16[10,44,128]{2,1,0:T(8,128)(2,1)S(1)} %get-tuple-element.46), channel_id=1, source_target_pairs={{1,0},{2,1},{3,2},{5,4},{6,5},{7,6},{9,8},{10,9},{11,10},{13,12},{... | collective-permute-start | bytes 337928 | tf_op jit(solution)/shard_map/ppermute | solution.py:42
  54.1 7.6 %collective-permute-start.10 = (bf16[12,24,128]{2,1,0:T(8,128)(2,1)S(1)}, bf16[12,24,128]{2,1,0:T(8,128)(2,1)S(1)}, u32[]{:S(2)}, u32[]{:S(2)}) collective-permute-start(bf16[12,24,128]{2,1,0:T(8,128)(2,1)S(1)} %get-tuple-element.30), channel_id=1, source_target_pairs={{0,4},{1,5},{2,6},{3,7},{4,8},{5,9},{6,10},{7,11},{8,12},{9,13},{1... | collective-permute-start | bytes 221192 | tf_op jit(solution)/shard_map/ppermute | solution.py:42
  55.4 6.2 %collective-permute-start.11 = (bf16[12,24,128]{2,1,0:T(8,128)(2,1)S(1)}, bf16[12,24,128]{2,1,0:T(8,128)(2,1)S(1)}, u32[]{:S(2)}, u32[]{:S(2)}) collective-permute-start(bf16[12,24,128]{2,1,0:T(8,128)(2,1)S(1)} %get-tuple-element.31), channel_id=1, source_target_pairs={{4,0},{5,1},{6,2},{7,3},{8,4},{9,5},{10,6},{11,7},{12,8},{13,9},{1... | collective-permute-start | bytes 221192 | tf_op jit(solution)/shard_map/ppermute | solution.py:42
  61.9 5.7 %collective-permute-start.12 = (bf16[12,44,128]{2,0,1:T(8,128)(2,1)S(1)}, bf16[12,44,128]{2,0,1:T(8,128)(2,1)S(1)}, u32[]{:S(2)}, u32[]{:S(2)}) collective-permute-start(bf16[12,44,128]{2,0,1:T(8,128)(2,1)S(1)} %maximum_bitcast_fusion.1), channel_id=1, source_target_pairs={{0,1},{1,2},{2,3},{4,5},{5,6},{6,7},{8,9},{9,10},{10,11},{12,13},{... | collective-permute-start | bytes 405512 | tf_op jit(solution)/shard_map/ppermute | solution.py:42
  64.7 7.4 %collective-permute-start.13 = (bf16[12,44,128]{2,0,1:T(8,128)(2,1)S(1)}, bf16[12,44,128]{2,0,1:T(8,128)(2,1)S(1)}, u32[]{:S(2)}, u32[]{:S(2)}) collective-permute-start(bf16[12,44,128]{2,0,1:T(8,128)(2,1)S(1)} %maximum_bitcast_fusion.2), channel_id=1, source_target_pairs={{1,0},{2,1},{3,2},{5,4},{6,5},{7,6},{9,8},{10,9},{11,10},{13,12},{... | collective-permute-start | bytes 405512 | tf_op jit(solution)/shard_map/ppermute | solution.py:42
  76.3 16.3 %all-to-all-start = ((bf16[32,48,128]{2,1,0:T(8,128)(2,1)}), bf16[32,48,128]{2,1,0:T(8,128)(2,1)S(1)}, u32[]{:S(2)}, u32[]{:S(2)}) async-start(bf16[32,48,128]{2,1,0:T(8,128)(2,1)} %get-tuple-element.43), calls=%async_computation | async-start | bytes 786432 | tf_op jit(solution)/shard_map/all_to_all | solution.py:473
  93.3 11.5 %all-to-all-start.1 = ((bf16[16,40,128]{2,1,0:T(8,128)(2,1)}), bf16[16,40,128]{2,1,0:T(8,128)(2,1)S(1)}, u32[]{:S(2)}, u32[]{:S(2)}) async-start(bf16[16,40,128]{2,1,0:T(8,128)(2,1)} %get-tuple-element.44), calls=%async_computation.1 | async-start | bytes 327680 | tf_op jit(solution)/shard_map/all_to_all | solution.py:491

commit v5 on v3

--- a/solution.py
+++ b/solution.py
@@ -53,11 +53,11 @@
 
 
 def forward_kernel(
-    tile, mirrored, above, below, above_other, below_other, left, right, w_first, p_first, b_first, w_second, b_second,
+    stacked, above, below, left, right, w_first, p_first, b_first, w_second, b_second,
     gate_first, bottle_first, near_hidden, gate_second, hidden_second, pre_second,
     area, shifted, pre, current,
 ):
-    side, channels = tile.shape[0], tile.shape[2]
+    side, channels = stacked.shape[0], stacked.shape[2] // 2
     first, second, inner = FIRST_DILATION, SECOND_DILATION, p_first.shape[0] // 2
     full, span, near = side + 2 * HALO, side + 2 * second, side + 2 * first
     wide, small = pre.shape[1], pre_second.shape[1]
@@ -66,12 +66,9 @@
 
     area[:, :LEAD] = jnp.zeros((full, LEAD, 2 * channels), F32)
     area[:, LEAD + side :] = jnp.zeros((full, area.shape[1] - LEAD - side, 2 * channels), F32)
-    area[HALO : HALO + side, middle, own] = tile[...].astype(F32)
-    area[HALO : HALO + side, middle, other] = jnp.swapaxes(mirrored[...].astype(F32), 0, 1)
-    area[:HALO, middle, own] = above[...].astype(F32)
-    area[:HALO, middle, other] = above_other[...].astype(F32)
-    area[HALO + side :, middle, own] = below[...].astype(F32)
-    area[HALO + side :, middle, other] = below_other[...].astype(F32)
+    area[HALO : HALO + side, middle] = stacked[...].astype(F32)
+    area[:HALO, middle] = above[...].astype(F32)
+    area[HALO + side :, middle] = below[...].astype(F32)
     area[:, LEAD - HALO : LEAD] = left[...].astype(F32)
     area[:, LEAD + side : LEAD + side + HALO] = right[...].astype(F32)
 
@@ -266,6 +263,13 @@
     ends[...] = total[share:]
 
 
+def outputs_kernel(rows, ends, conv_gradient, bias_gradient, out_gradient):
+    count, inner = conv_gradient.shape[0], out_gradient.shape[0]
+    conv_gradient[...] = rows[:count].astype(F32)
+    out_gradient[...] = rows[count : count + inner].astype(F32)
+    bias_gradient[...] = ends[:1, :inner]
+
+
 def call(kernel, name, outs, scratch, flops, *operands):
     outs = [jax.ShapeDtypeStruct(shape, dtype) for shape, dtype in outs]
     moved = sum(x.size * x.dtype.itemsize for x in list(operands) + outs)
@@ -295,10 +299,18 @@
     tile = activations[0]
 
     mirrored = send(tile, lambda r, c: (c, r))
-    above = send(tile[side - HALO :], lambda r, c: (r + 1, c))
-    below = send(tile[:HALO], lambda r, c: (r - 1, c))
-    above_other = send(jnp.swapaxes(tile[:, side - HALO :], 0, 1), lambda r, c: (c + 1, r))
-    below_other = send(jnp.swapaxes(tile[:, :HALO], 0, 1), lambda r, c: (c - 1, r))
+    stacked = jnp.concatenate([tile, jnp.swapaxes(mirrored, 0, 1)], axis=2)
+    above = send(stacked[side - HALO :], lambda r, c: (r + 1, c))
+    below = send(stacked[:HALO], lambda r, c: (r - 1, c))
+
+    def columns(low, high):
+        strip = jnp.concatenate([above[:, low:high], stacked[:, low:high], below[:, low:high]])
+        return jnp.swapaxes(strip, 0, 1)
+
+    left = send(columns(side - HALO, side), lambda r, c: (r, c + 1))
+    right = send(columns(0, HALO), lambda r, c: (r, c - 1))
+    left, late = lax.optimization_barrier((left, cotangent[0]))
+    late_mirrored = send(late, lambda r, c: (c, r))
 
     bias_rows = jnp.pad(conv_bias, ((0, 7), (0, channels - inner)))
     packed = jnp.concatenate(
@@ -317,18 +329,6 @@
     p_second = beside(proj[1].T, proj[1].T, 1)
     p_back = jnp.pad(proj[0].T, ((0, 0), (0, inner)))
 
-    other = jnp.swapaxes(mirrored, 0, 1)
-
-    def columns(low, high):
-        own = jnp.concatenate([above[:, low:high], tile[:, low:high], below[:, low:high]])
-        turned = jnp.concatenate([above_other[:, low:high], other[:, low:high], below_other[:, low:high]])
-        return jnp.swapaxes(jnp.concatenate([own, turned], axis=2), 0, 1)
-
-    left = send(columns(side - HALO, side), lambda r, c: (r, c + 1))
-    right = send(columns(0, HALO), lambda r, c: (r, c - 1))
-    left, right, late = lax.optimization_barrier((left, right, cotangent[0]))
-    late_mirrored = send(late, lambda r, c: (c, r))
-
     gate_first, bottle_first, near_hidden, gate_second, hidden_second, pre_second = call(
         forward_kernel,
         "forward",
@@ -341,13 +341,13 @@
             ((side, small, 2 * inner), F32),
         ],
         [
-            ((full, LEAD + up16(side + LEAD + second + first), 2 * channels), F32),
+            ((full, LEAD + up16(side + LEAD), 2 * channels), F32),
             ((3, full, wide, 2 * channels), BF16),
             ((span, wide, 2 * inner), F32),
             ((span, wide, channels), F32),
         ],
         span * wide * 2 * channels * 2 * inner * 20,
-        *(tile, mirrored, above, below, above_other, below_other),
+        *(stacked, above, below),
         *(jnp.swapaxes(left, 0, 1), jnp.swapaxes(right, 0, 1)),
         *(w_first, p_first, bias[0], w_second, bias[1]),
     )
@@ -430,9 +430,17 @@
         parts.size,
         parts,
     )
-    rows = lax.all_to_all(rows, GRID, 0, 0, tiled=True).reshape(devices * share, channels).astype(F32)
-    conv_gradient = jnp.swapaxes(rows[: 9 * inner].reshape(1, 9, inner, channels), 2, 3)
-    return (input_gradient[None], conv_gradient, ends[:1, :inner], rows[None, 9 * inner : 10 * inner])
+    rows = lax.all_to_all(rows, GRID, 0, 0, tiled=True).reshape(devices * share, channels)
+    conv_gradient, bias_gradient, out_gradient = call(
+        outputs_kernel,
+        "outputs",
+        [((9 * inner, channels), F32), ((1, inner), F32), ((inner, channels), F32)],
+        [],
+        rows.size,
+        *(rows, ends),
+    )
+    conv_gradient = jnp.swapaxes(conv_gradient.reshape(1, 9, inner, channels), 2, 3)
+    return (input_gradient[None], conv_gradient, bias_gradient, out_gradient[None])
 
 
 def solution(mesh):

time: 110 us -> 107 us (0.973)
  waiting for transfers between devices: 23 us -> 31.6 us
  starting transfers between devices: 43.4 us -> 36 us
  local copies, waits for them, and re-layouts: 6.51 us -> 3.01 us
  blocking collectives: 21.4 us -> 20.2 us
    ppermute x12 -> x10, waiting for transfers between devices: 17.2 us -> 25.3 us  [send(): return lax.ppermute(x, GRID, pairs)]
    ppermute x12 -> x10, starting transfers between devices: 39.9 us -> 32.5 us  [send(): return lax.ppermute(x, GRID, pairs)]
    slice x10 -> x0, local copies, waits for them, and re-layouts: 2.4 us -> none  [the longest x1 1.04 us: columns(): tile[:, low:high]]
    all_to_all x1, blocking collectives: 19.3 us -> 18.1 us  [local(): parts = lax.all_to_all(parts, ('segment',) + GRID, 0, 0, tiled=True)]
    pallas_call x6 -> x7, Pallas kernels: 12.5 us -> 13.1 us  [call(): pl.pallas_call(kernel, name=name, out_shape=outs, scratch_shapes=[pltpu.V...]
  transfers between devices with their start and end apart: 13 -> 11, of which waited for: 8 -> 8; matrix products, arithmetic and copies ran while one was open for 4% -> 3% of each run, Pallas kernels for 8% -> 8%
where the time goes in v5:
time: 107 us
  starting transfers between devices  36 us (34%)
  waiting for transfers between devices  31.6 us (30%)
  blocking collectives  20.2 us (19%)
  Pallas kernels  13.1 us (12%)
  local copies, waits for them, and re-layouts  3.01 us (3%)
  other arithmetic  1.71 us (2%)
    ppermute x10, starting transfers between devices, send(): return lax.ppermute(x, GRID, pairs)  32.5 us
    ppermute x10, waiting for transfers between devices, send(): return lax.ppermute(x, GRID, pairs)  25.3 us
    all_to_all x1, blocking collectives, local(): parts = lax.all_to_all(parts, ('segment',) + GRID, 0, 0, tiled=True)  18.1 us
    pallas_call x7, Pallas kernels, call(): pl.pallas_call(kernel, name=name, out_shape=outs, scratch_shapes=[pltpu.V...  13.1 us
    all_to_all x1, waiting for transfers between devices, local(): lax.all_to_all(rows, GRID, 0, 0, tiled=True)  6.34 us
    all_to_all x1, starting transfers between devices, local(): lax.all_to_all(rows, GRID, 0, 0, tiled=True)  3.52 us
  transfers between devices with their start and end apart: 11, of which 8 were waited for; matrix products, arithmetic and copies ran while one was open for 3% of the time, Pallas kernels for 8%

profile of v5, /device:TPU:0, one launch (start us, length us, event | category | flops | bytes accessed | tf_op | source)
XLA Modules:
  0.0 106.7 jit_solution(1133631430422439427)
XLA Ops:
  0.6 0.9 copy.16
  1.6 0.7 collective-permute-start
  2.2 1.0 fusion.9
  3.2 2.1 %all-gather = bf16[1296,128]{1,0:T(8,128)(2,1)S(1)} all-gather(bf16[648,128]{1,0:T(8,128)(2,1)S(1)} %fusion.9), channel_id=2, replica_groups=mesh['segment'=2,'row'=4,'col'=4] {'segment'}, dimensions={0}, use_global_device_ids=true | all-gather | bytes 497664 | tf_op jit(solution)/shard_map/all_gather | solution.py:319
  5.6 0.1 slice_bitcast_fusion.2
  5.7 0.1 copy.22
  5.8 0.1 fusion.5
  5.9 0.6 copy-done
  6.5 14.7 %collective-permute-start.1 = (bf16[10,24,256]{2,1,0:T(8,128)(2,1)S(1)}, bf16[10,24,256]{2,1,0:T(8,128)(2,1)S(1)}, u32[]{:S(2)}, u32[]{:S(2)}) collective-permute-start(bf16[10,24,256]{2,1,0:T(8,128)(2,1)S(1)} %get-tuple-element.57), channel_id=1, source_target_pairs={{0,4},{1,5},{2,6},{3,7},{4,8},{5,9},{6,10},{7,11},{8,12},{9,13},{1... | collective-permute-start | bytes 368648 | tf_op jit(solution)/shard_map/ppermute | solution.py:43
  21.2 0.1 fusion.14
  21.2 0.3 copy.18.w_first
  21.6 0.2 copy.20.w_second
  21.8 0.1 copy.19.p_first
  21.9 0.1 tile.13.b_first
  22.0 0.1 tile.15.b_second
  22.1 0.1 copy.23
  22.2 1.3 %collective-permute-start.2 = (bf16[10,24,256]{2,1,0:T(8,128)(2,1)S(1)}, bf16[10,24,256]{2,1,0:T(8,128)(2,1)S(1)}, u32[]{:S(2)}, u32[]{:S(2)}) collective-permute-start(bf16[10,24,256]{2,1,0:T(8,128)(2,1)S(1)} %get-tuple-element.58), channel_id=1, source_target_pairs={{4,0},{5,1},{6,2},{7,3},{8,4},{9,5},{10,6},{11,7},{12,8},{13,9},{1... | collective-permute-start | bytes 368648 | tf_op jit(solution)/shard_map/ppermute | solution.py:43
  23.5 0.1 fusion.8
  23.6 5.3 %collective-permute-done.2.below = bf16[10,24,256]{2,1,0:T(8,128)(2,1)S(1)} collective-permute-done((bf16[10,24,256]{2,1,0:T(8,128)(2,1)S(1)}, bf16[10,24,256]{2,1,0:T(8,128)(2,1)S(1)}, u32[]{:S(2)}, u32[]{:S(2)}) %collective-permute-start.2) | collective-permute-done | bytes 122912 | tf_op jit(solution)/shard_map/ppermute | solution.py:43
  29.0 0.1 maximum_bitcast_fusion
  29.1 1.3 %collective-permute-start.3 = (bf16[10,44,256]{2,0,1:T(8,128)(2,1)S(1)}, bf16[10,44,256]{2,0,1:T(8,128)(2,1)S(1)}, u32[]{:S(2)}, u32[]{:S(2)}) collective-permute-start(bf16[10,44,256]{2,0,1:T(8,128)(2,1)S(1)} %maximum_bitcast_fusion), channel_id=1, source_target_pairs={{0,1},{1,2},{2,3},{4,5},{5,6},{6,7},{8,9},{9,10},{10,11},{12,13},{... | collective-permute-start | bytes 675848 | tf_op jit(solution)/shard_map/ppermute | solution.py:43
  30.4 0.1 maximum_bitcast_fusion.1
  30.5 1.3 %collective-permute-start.5 = (bf16[10,44,256]{2,0,1:T(8,128)(2,1)S(1)}, bf16[10,44,256]{2,0,1:T(8,128)(2,1)S(1)}, u32[]{:S(2)}, u32[]{:S(2)}) collective-permute-start(bf16[10,44,256]{2,0,1:T(8,128)(2,1)S(1)} %maximum_bitcast_fusion.1), channel_id=1, source_target_pairs={{1,0},{2,1},{3,2},{5,4},{6,5},{7,6},{9,8},{10,9},{11,10},{13,12},{... | collective-permute-start | bytes 675848 | tf_op jit(solution)/shard_map/ppermute | solution.py:43
  31.8 0.1 pad_maximum_fusion.2.p_second
  31.9 4.3 %collective-permute-done.3 = bf16[10,44,256]{2,0,1:T(8,128)(2,1)S(1)} collective-permute-done((bf16[10,44,256]{2,0,1:T(8,128)(2,1)S(1)}, bf16[10,44,256]{2,0,1:T(8,128)(2,1)S(1)}, u32[]{:S(2)}, u32[]{:S(2)}) %collective-permute-start.3) | collective-permute-done | bytes 225312 | tf_op jit(solution)/shard_map/ppermute | solution.py:43
  36.1 0.7 collective-permute-start.4
  36.8 8.4 %collective-permute-done.5 = bf16[10,44,256]{2,0,1:T(8,128)(2,1)S(1)} collective-permute-done((bf16[10,44,256]{2,0,1:T(8,128)(2,1)S(1)}, bf16[10,44,256]{2,0,1:T(8,128)(2,1)S(1)}, u32[]{:S(2)}, u32[]{:S(2)}) %collective-permute-start.5) | collective-permute-done | bytes 225312 | tf_op jit(solution)/shard_map/ppermute | solution.py:43
  45.2 6.2 %forward.1 = (bf16[28,32,128]{2,1,0:T(8,128)(2,1)S(1)}, bf16[24,32,128]{2,1,0:T(8,128)(2,1)S(1)}, bf16[3,28,32,128]{3,2,1,0:T(8,128)(2,1)S(1)}, bf16[28,32,128]{...) custom-call(bf16[24,24,256]{2,1,0:T(8,128)(2,1)S(1)} %pad_maximum_fusion.stacked, ...), custom_call_target="tpu_custom_call" | custom-call | flops 1258291200 | bytes 4662272 | tf_op jit(solution)/shard_map/forward/pallas_call | solution.py:276
  51.5 0.2 turn.1
  51.7 2.2 %collective-permute-start.6 = (bf16[12,24,128]{2,1,0:T(8,128)(2,1)S(1)}, bf16[12,24,128]{2,1,0:T(8,128)(2,1)S(1)}, u32[]{:S(2)}, u32[]{:S(2)}) collective-permute-start(bf16[12,24,128]{2,1,0:T(8,128)(2,1)S(1)} %get-tuple-element.31), channel_id=1, source_target_pairs={{0,4},{1,5},{2,6},{3,7},{4,8},{5,9},{6,10},{7,11},{8,12},{9,13},{1... | collective-permute-start | bytes 221192 | tf_op jit(solution)/shard_map/ppermute | solution.py:43
  54.0 1.3 %collective-permute-start.7 = (bf16[12,24,128]{2,1,0:T(8,128)(2,1)S(1)}, bf16[12,24,128]{2,1,0:T(8,128)(2,1)S(1)}, u32[]{:S(2)}, u32[]{:S(2)}) collective-permute-start(bf16[12,24,128]{2,1,0:T(8,128)(2,1)S(1)} %get-tuple-element.32), channel_id=1, source_target_pairs={{4,0},{5,1},{6,2},{7,3},{8,4},{9,5},{10,6},{11,7},{12,8},{13,9},{1... | collective-permute-start | bytes 221192 | tf_op jit(solution)/shard_map/ppermute | solution.py:43
  55.3 0.6 collective-permute-done.6.above
  55.9 4.3 %collective-permute-done.7.below = bf16[12,24,128]{2,1,0:T(8,128)(2,1)S(1)} collective-permute-done((bf16[12,24,128]{2,1,0:T(8,128)(2,1)S(1)}, bf16[12,24,128]{2,1,0:T(8,128)(2,1)S(1)}, u32[]{:S(2)}, u32[]{:S(2)}) %collective-permute-start.7) | collective-permute-done | bytes 73760 | tf_op jit(solution)/shard_map/ppermute | solution.py:43
  60.3 0.1 maximum_bitcast_fusion.3
  60.4 1.3 %collective-permute-start.9 = (bf16[12,44,128]{2,0,1:T(8,128)(2,1)S(1)}, bf16[12,44,128]{2,0,1:T(8,128)(2,1)S(1)}, u32[]{:S(2)}, u32[]{:S(2)}) collective-permute-start(bf16[12,44,128]{2,0,1:T(8,128)(2,1)S(1)} %maximum_bitcast_fusion.3), channel_id=1, source_target_pairs={{1,0},{2,1},{3,2},{5,4},{6,5},{7,6},{9,8},{10,9},{11,10},{13,12},{... | collective-permute-start | bytes 405512 | tf_op jit(solution)/shard_map/ppermute | solution.py:43
  61.7 0.1 maximum_bitcast_fusion.2
  61.8 7.8 %collective-permute-start.8 = (bf16[12,44,128]{2,0,1:T(8,128)(2,1)S(1)}, bf16[12,44,128]{2,0,1:T(8,128)(2,1)S(1)}, u32[]{:S(2)}, u32[]{:S(2)}) collective-permute-start(bf16[12,44,128]{2,0,1:T(8,128)(2,1)S(1)} %maximum_bitcast_fusion.2), channel_id=1, source_target_pairs={{0,1},{1,2},{2,3},{4,5},{5,6},{6,7},{8,9},{9,10},{10,11},{12,13},{... | collective-permute-start | bytes 405512 | tf_op jit(solution)/shard_map/ppermute | solution.py:43
  69.6 0.1 fusion.4.v_second
  69.6 0.5 second_sums.1
  70.1 0.9 collective-permute-done.9
  71.0 1.5 %collective-permute-done.8 = bf16[12,44,128]{2,0,1:T(8,128)(2,1)S(1)} collective-permute-done((bf16[12,44,128]{2,0,1:T(8,128)(2,1)S(1)}, bf16[12,44,128]{2,0,1:T(8,128)(2,1)S(1)}, u32[]{:S(2)}, u32[]{:S(2)}) %collective-permute-start.8) | collective-permute-done | bytes 135200 | tf_op jit(solution)/shard_map/ppermute | solution.py:43
  72.6 3.1 %backward.1 = (bf16[32,48,128]{2,1,0:T(8,128)(2,1)S(1)}, bf16[3,28,32,128]{3,2,1,0:T(8,128)(2,1)S(1)}, bf16[24,24,128]{2,1,0:T(8,128)(2,1)S(1)}) custom-call(bf16[24,32,128]{2,1,0:T(8,128)(2,1)S(1)} %get-tuple-element.29.grad_pre, bf16[24,32,128]{2,1,0:T(8,128)(2,1)S(1)} %get-tuple-element.30.grad_tile, ...), custom_call_target="tpu_custom_call" | custom-call | flops 528482304 | bytes 4321280 | tf_op jit(solution)/shard_map/backward/pallas_call | solution.py:276
  75.7 18.1 %all_to_all.10.parts = bf16[32,48,128]{2,1,0:T(8,128)(2,1)S(1)} all-to-all(bf16[32,48,128]{2,1,0:T(8,128)(2,1)S(1)} %get-tuple-element.42), channel_id=1, replica_groups=mesh['segment'=2,'row'=4,'col'=4] {'segment','row','col'}, dimensions={0} | all-to-all | bytes 786432 | tf_op jit(solution)/shard_map/all_to_all | solution.py:415
  93.7 0.7 total.1
  94.5 3.5 %all-to-all-start.1 = ((bf16[16,40,128]{2,1,0:T(8,128)(2,1)}), bf16[16,40,128]{2,1,0:T(8,128)(2,1)S(1)}, u32[]{:S(2)}, u32[]{:S(2)}) async-start(bf16[16,40,128]{2,1,0:T(8,128)(2,1)} %get-tuple-element.43), calls=%async_computation.1 | async-start | bytes 327680 | tf_op jit(solution)/shard_map/all_to_all | solution.py:433
  98.0 1.6 %input.1 = bf16[24,24,128]{2,1,0:T(8,128)(2,1)} custom-call(bf16[3,28,32,128]{3,2,1,0:T(8,128)(2,1)S(1)} %get-tuple-element.40.windows, bf16[24,24,128]{2,1,0:T(8,128)(2,1)S(1)} %get-tuple-element.41.grad_first, bf16[24,24,128]{2,1,0:T(8,128)(2,1)S(1)} %bitcast.61, bf16[9,128,128]{2,1,0:T(8,128)(2,1)S(1)} %pad.29.v_first), custom_call_target="tpu_custom_call" | custom-call | flops 226492416 | bytes 1425408 | tf_op jit(solution)/shard_map/input/pallas_call | solution.py:276
  99.6 6.3 %all-to-all-done.1 = bf16[16,40,128]{2,1,0:T(8,128)(2,1)S(1)} async-done(((bf16[16,40,128]{2,1,0:T(8,128)(2,1)}), bf16[16,40,128]{2,1,0:T(8,128)(2,1)S(1)}, u32[]{:S(2)}, u32[]{:S(2)}) %all-to-all-start.1) | async-done | bytes 163872 | tf_op jit(solution)/shard_map/all_to_all | solution.py:433
  106.0 0.7 outputs.1
  (39 shorter events, 0.5 us)
Async XLA Ops:
  1.6 4.3 %collective-permute-start = (bf16[24,24,128]{2,0,1:T(8,128)(2,1)S(1)}, bf16[24,24,128]{2,0,1:T(8,128)(2,1)S(1)}, u32[]{:S(2)}, u32[]{:S(2)}) collective-permute-start(bf16[24,24,128]{2,0,1:T(8,128)(2,1)S(1)} %copy.16), channel_id=1, source_target_pairs={{0,0},{1,4},{2,8},{3,12},{4,1},{5,5},{6,9},{7,13},{8,2},{9,6},{10,... | collective-permute-start | bytes 442376 | tf_op jit(solution)/shard_map/ppermute | solution.py:43
  5.6 0.9 copy-start
  6.5 17.1 %collective-permute-start.1 = (bf16[10,24,256]{2,1,0:T(8,128)(2,1)S(1)}, bf16[10,24,256]{2,1,0:T(8,128)(2,1)S(1)}, u32[]{:S(2)}, u32[]{:S(2)}) collective-permute-start(bf16[10,24,256]{2,1,0:T(8,128)(2,1)S(1)} %get-tuple-element.57), channel_id=1, source_target_pairs={{0,4},{1,5},{2,6},{3,7},{4,8},{5,9},{6,10},{7,11},{8,12},{9,13},{1... | collective-permute-start | bytes 368648 | tf_op jit(solution)/shard_map/ppermute | solution.py:43
  22.2 6.8 %collective-permute-start.2 = (bf16[10,24,256]{2,1,0:T(8,128)(2,1)S(1)}, bf16[10,24,256]{2,1,0:T(8,128)(2,1)S(1)}, u32[]{:S(2)}, u32[]{:S(2)}) collective-permute-start(bf16[10,24,256]{2,1,0:T(8,128)(2,1)S(1)} %get-tuple-element.58), channel_id=1, source_target_pairs={{4,0},{5,1},{6,2},{7,3},{8,4},{9,5},{10,6},{11,7},{12,8},{13,9},{1... | collective-permute-start | bytes 368648 | tf_op jit(solution)/shard_map/ppermute | solution.py:43
  23.6 12.5 %copy-start.1 = (bf16[1,24,24,128]{3,2,1,0:T(8,128)(2,1)S(1)}, bf16[1,24,24,128]{3,2,1,0:T(8,128)(2,1)}, u32[]{:S(2)}) copy-start(bf16[1,24,24,128]{3,2,1,0:T(8,128)(2,1)} %param.6) | copy-start | bytes 442372
  29.1 7.0 %collective-permute-start.3 = (bf16[10,44,256]{2,0,1:T(8,128)(2,1)S(1)}, bf16[10,44,256]{2,0,1:T(8,128)(2,1)S(1)}, u32[]{:S(2)}, u32[]{:S(2)}) collective-permute-start(bf16[10,44,256]{2,0,1:T(8,128)(2,1)S(1)} %maximum_bitcast_fusion), channel_id=1, source_target_pairs={{0,1},{1,2},{2,3},{4,5},{5,6},{6,7},{8,9},{9,10},{10,11},{12,13},{... | collective-permute-start | bytes 675848 | tf_op jit(solution)/shard_map/ppermute | solution.py:43
  30.5 14.8 %collective-permute-start.5 = (bf16[10,44,256]{2,0,1:T(8,128)(2,1)S(1)}, bf16[10,44,256]{2,0,1:T(8,128)(2,1)S(1)}, u32[]{:S(2)}, u32[]{:S(2)}) collective-permute-start(bf16[10,44,256]{2,0,1:T(8,128)(2,1)S(1)} %maximum_bitcast_fusion.1), channel_id=1, source_target_pairs={{1,0},{2,1},{3,2},{5,4},{6,5},{7,6},{9,8},{10,9},{11,10},{13,12},{... | collective-permute-start | bytes 675848 | tf_op jit(solution)/shard_map/ppermute | solution.py:43
  36.1 15.3 %collective-permute-start.4 = (bf16[24,24,128]{2,1,0:T(8,128)(2,1)S(1)}, bf16[24,24,128]{2,1,0:T(8,128)(2,1)S(1)}, u32[]{:S(2)}, u32[]{:S(2)}) collective-permute-start(bf16[24,24,128]{2,1,0:T(8,128)(2,1)S(1)} %bitcast.67), channel_id=1, source_target_pairs={{0,0},{1,4},{2,8},{3,12},{4,1},{5,5},{6,9},{7,13},{8,2},{9,6},{10,... | collective-permute-start | bytes 442376 | tf_op jit(solution)/shard_map/ppermute | solution.py:43
  51.7 4.2 %collective-permute-start.6 = (bf16[12,24,128]{2,1,0:T(8,128)(2,1)S(1)}, bf16[12,24,128]{2,1,0:T(8,128)(2,1)S(1)}, u32[]{:S(2)}, u32[]{:S(2)}) collective-permute-start(bf16[12,24,128]{2,1,0:T(8,128)(2,1)S(1)} %get-tuple-element.31), channel_id=1, source_target_pairs={{0,4},{1,5},{2,6},{3,7},{4,8},{5,9},{6,10},{7,11},{8,12},{9,13},{1... | collective-permute-start | bytes 221192 | tf_op jit(solution)/shard_map/ppermute | solution.py:43
  54.0 6.2 %collective-permute-start.7 = (bf16[12,24,128]{2,1,0:T(8,128)(2,1)S(1)}, bf16[12,24,128]{2,1,0:T(8,128)(2,1)S(1)}, u32[]{:S(2)}, u32[]{:S(2)}) collective-permute-start(bf16[12,24,128]{2,1,0:T(8,128)(2,1)S(1)} %get-tuple-element.32), channel_id=1, source_target_pairs={{4,0},{5,1},{6,2},{7,3},{8,4},{9,5},{10,6},{11,7},{12,8},{13,9},{1... | collective-permute-start | bytes 221192 | tf_op jit(solution)/shard_map/ppermute | solution.py:43
  60.4 10.6 %collective-permute-start.9 = (bf16[12,44,128]{2,0,1:T(8,128)(2,1)S(1)}, bf16[12,44,128]{2,0,1:T(8,128)(2,1)S(1)}, u32[]{:S(2)}, u32[]{:S(2)}) collective-permute-start(bf16[12,44,128]{2,0,1:T(8,128)(2,1)S(1)} %maximum_bitcast_fusion.3), channel_id=1, source_target_pairs={{1,0},{2,1},{3,2},{5,4},{6,5},{7,6},{9,8},{10,9},{11,10},{13,12},{... | collective-permute-start | bytes 405512 | tf_op jit(solution)/shard_map/ppermute | solution.py:43
  61.8 10.8 %collective-permute-start.8 = (bf16[12,44,128]{2,0,1:T(8,128)(2,1)S(1)}, bf16[12,44,128]{2,0,1:T(8,128)(2,1)S(1)}, u32[]{:S(2)}, u32[]{:S(2)}) collective-permute-start(bf16[12,44,128]{2,0,1:T(8,128)(2,1)S(1)} %maximum_bitcast_fusion.2), channel_id=1, source_target_pairs={{0,1},{1,2},{2,3},{4,5},{5,6},{6,7},{8,9},{9,10},{10,11},{12,13},{... | collective-permute-start | bytes 405512 | tf_op jit(solution)/shard_map/ppermute | solution.py:43
  94.5 11.5 %all-to-all-start.1 = ((bf16[16,40,128]{2,1,0:T(8,128)(2,1)}), bf16[16,40,128]{2,1,0:T(8,128)(2,1)S(1)}, u32[]{:S(2)}, u32[]{:S(2)}) async-start(bf16[16,40,128]{2,1,0:T(8,128)(2,1)} %get-tuple-element.43), calls=%async_computation.1 | async-start | bytes 327680 | tf_op jit(solution)/shard_map/all_to_all | solution.py:433

commit v6 on v5

--- a/solution.py
+++ b/solution.py
@@ -298,10 +298,18 @@
     wide, small = up16(span), up16(near)
     tile = activations[0]
 
+    def row_strips(x):
+        return send(x[side - HALO :], lambda r, c: (r + 1, c)), send(x[:HALO], lambda r, c: (r - 1, c))
+
     mirrored = send(tile, lambda r, c: (c, r))
-    stacked = jnp.concatenate([tile, jnp.swapaxes(mirrored, 0, 1)], axis=2)
-    above = send(stacked[side - HALO :], lambda r, c: (r + 1, c))
-    below = send(stacked[:HALO], lambda r, c: (r - 1, c))
+    above, below = row_strips(tile)
+    other = jnp.swapaxes(mirrored, 0, 1)
+    above_other, below_other = row_strips(other)
+    above_other, late = lax.optimization_barrier((above_other, cotangent[0]))
+    late_mirrored = send(late, lambda r, c: (c, r))
+    stacked = jnp.concatenate([tile, other], axis=2)
+    above = jnp.concatenate([above, above_other], axis=2)
+    below = jnp.concatenate([below, below_other], axis=2)
 
     def columns(low, high):
         strip = jnp.concatenate([above[:, low:high], stacked[:, low:high], below[:, low:high]])
@@ -309,8 +317,6 @@
 
     left = send(columns(side - HALO, side), lambda r, c: (r, c + 1))
     right = send(columns(0, HALO), lambda r, c: (r, c - 1))
-    left, late = lax.optimization_barrier((left, cotangent[0]))
-    late_mirrored = send(late, lambda r, c: (c, r))
 
     bias_rows = jnp.pad(conv_bias, ((0, 7), (0, channels - inner)))
     packed = jnp.concatenate(

time: 107 us -> 109 us (1.019)
  waiting for transfers between devices: 31.6 us -> 25.1 us
  starting transfers between devices: 36 us -> 40.4 us
  blocking collectives: 20.2 us -> 23.2 us
    ppermute x10 -> x12, waiting for transfers between devices: 25.3 us -> 18.7 us  [send(): return lax.ppermute(x, GRID, pairs)]
    ppermute x10 -> x12, starting transfers between devices: 32.5 us -> 36.9 us  [send(): return lax.ppermute(x, GRID, pairs)]
    all_to_all x1, blocking collectives: 18.1 us -> 21.2 us  [local(): parts = lax.all_to_all(parts, ('segment',) + GRID, 0, 0, tiled=True)]
  transfers between devices with their start and end apart: 11 -> 13, of which waited for: 8 -> 10; matrix products, arithmetic and copies ran while one was open for 3% -> 4% of each run, Pallas kernels for 8% -> 8%
where the time goes in v6:
time: 109 us; the launch traced here: 108 us
  starting transfers between devices  40.4 us (37%)
  waiting for transfers between devices  25.1 us (23%)
  blocking collectives  23.2 us (21%)
  Pallas kernels  13.1 us (12%)
  local copies, waits for them, and re-layouts  3.38 us (3%)
  other arithmetic  1.66 us (2%)
  between operations  1.13 us (1%)
    ppermute x12, starting transfers between devices, send(): return lax.ppermute(x, GRID, pairs)  36.9 us
    all_to_all x1, blocking collectives, local(): parts = lax.all_to_all(parts, ('segment',) + GRID, 0, 0, tiled=True)  21.2 us
    ppermute x12, waiting for transfers between devices, send(): return lax.ppermute(x, GRID, pairs)  18.7 us
    pallas_call x7, Pallas kernels, call(): pl.pallas_call(kernel, name=name, out_shape=outs, scratch_shapes=[pltpu.V...  13.1 us
    all_to_all x1, waiting for transfers between devices, local(): lax.all_to_all(rows, GRID, 0, 0, tiled=True)  6.34 us
    all_to_all x1, starting transfers between devices, local(): lax.all_to_all(rows, GRID, 0, 0, tiled=True)  3.52 us
  transfers between devices with their start and end apart: 13, of which 10 were waited for; matrix products, arithmetic and copies ran while one was open for 4% of the time, Pallas kernels for 8%

profile of v6, /device:TPU:0, one launch (start us, length us, event | category | flops | bytes accessed | tf_op | source)
XLA Modules:
  0.0 108.0 jit_solution(5025654219871341482)
XLA Ops:
  0.6 0.9 copy.16
  1.6 0.7 collective-permute-start
  2.2 0.9 slice_bitcast_fusion.3
  3.1 7.6 %collective-permute-start.3 = (bf16[10,24,128]{2,1,0:T(8,128)(2,1)S(1)}, bf16[10,24,128]{2,1,0:T(8,128)(2,1)S(1)}, u32[]{:S(2)}, u32[]{:S(2)}) collective-permute-start(bf16[10,24,128]{2,1,0:T(8,128)(2,1)S(1)} %get-tuple-element.64), channel_id=1, source_target_pairs={{0,4},{1,5},{2,6},{3,7},{4,8},{5,9},{6,10},{7,11},{8,12},{9,13},{1... | collective-permute-start | bytes 184328 | tf_op jit(solution)/shard_map/ppermute | solution.py:43
  10.8 1.3 %collective-permute-start.4 = (bf16[10,24,128]{2,1,0:T(8,128)(2,1)S(1)}, bf16[10,24,128]{2,1,0:T(8,128)(2,1)S(1)}, u32[]{:S(2)}, u32[]{:S(2)}) collective-permute-start(bf16[10,24,128]{2,1,0:T(8,128)(2,1)S(1)} %get-tuple-element.63), channel_id=1, source_target_pairs={{4,0},{5,1},{6,2},{7,3},{8,4},{9,5},{10,6},{11,7},{12,8},{13,9},{1... | collective-permute-start | bytes 184328 | tf_op jit(solution)/shard_map/ppermute | solution.py:43
  12.1 1.0 fusion.9
  13.0 2.0 %all-gather = bf16[1296,128]{1,0:T(8,128)(2,1)S(1)} all-gather(bf16[648,128]{1,0:T(8,128)(2,1)S(1)} %fusion.9), channel_id=2, replica_groups=mesh['segment'=2,'row'=4,'col'=4] {'segment'}, dimensions={0}, use_global_device_ids=true | all-gather | bytes 497664 | tf_op jit(solution)/shard_map/all_gather | solution.py:325
  15.3 0.1 slice_bitcast_fusion.2
  15.4 0.3 copy.18.w_first
  15.8 0.2 copy.20.w_second
  16.0 0.1 copy.22
  16.1 0.1 fusion.12
  16.2 0.1 copy.19.p_first
  16.3 0.1 tile.13.b_first
  16.4 0.1 tile.15.b_second
  16.5 0.1 copy.23
  16.7 0.7 collective-permute-done.4
  17.4 4.8 %collective-permute-start.1 = (bf16[10,24,128]{2,1,0:T(8,128)(2,1)S(1)}, bf16[10,24,128]{2,1,0:T(8,128)(2,1)S(1)}, u32[]{:S(2)}, u32[]{:S(2)}) collective-permute-start(bf16[10,24,128]{2,1,0:T(8,128)(2,1)S(1)} %get-tuple-element.62), channel_id=1, source_target_pairs={{0,4},{1,5},{2,6},{3,7},{4,8},{5,9},{6,10},{7,11},{8,12},{9,13},{1... | collective-permute-start | bytes 184328 | tf_op jit(solution)/shard_map/ppermute | solution.py:43
  22.2 1.3 %collective-permute-start.5 = (bf16[10,24,128]{2,1,0:T(8,128)(2,1)S(1)}, bf16[10,24,128]{2,1,0:T(8,128)(2,1)S(1)}, u32[]{:S(2)}, u32[]{:S(2)}) collective-permute-start(bf16[10,24,128]{2,1,0:T(8,128)(2,1)S(1)} %get-tuple-element.61), channel_id=1, source_target_pairs={{4,0},{5,1},{6,2},{7,3},{8,4},{9,5},{10,6},{11,7},{12,8},{13,9},{1... | collective-permute-start | bytes 184328 | tf_op jit(solution)/shard_map/ppermute | solution.py:43
  23.5 0.1 fusion.8
  23.6 0.5 collective-permute-done.1
  24.1 4.7 %collective-permute-done.5 = bf16[10,24,128]{2,1,0:T(8,128)(2,1)S(1)} collective-permute-done((bf16[10,24,128]{2,1,0:T(8,128)(2,1)S(1)}, bf16[10,24,128]{2,1,0:T(8,128)(2,1)S(1)}, u32[]{:S(2)}, u32[]{:S(2)}) %collective-permute-start.5) | collective-permute-done | bytes 61472 | tf_op jit(solution)/shard_map/ppermute | solution.py:43
  28.9 1.3 %collective-permute-start.7 = (bf16[10,44,256]{2,0,1:T(8,128)(2,1)S(1)}, bf16[10,44,256]{2,0,1:T(8,128)(2,1)S(1)}, u32[]{:S(2)}, u32[]{:S(2)}) collective-permute-start(bf16[10,44,256]{2,0,1:T(8,128)(2,1)S(1)} %maximum_bitcast_fusion.1), channel_id=1, source_target_pairs={{1,0},{2,1},{3,2},{5,4},{6,5},{7,6},{9,8},{10,9},{11,10},{13,12},{... | collective-permute-start | bytes 675848 | tf_op jit(solution)/shard_map/ppermute | solution.py:43
  30.3 4.6 %collective-permute-start.6 = (bf16[10,44,256]{2,0,1:T(8,128)(2,1)S(1)}, bf16[10,44,256]{2,0,1:T(8,128)(2,1)S(1)}, u32[]{:S(2)}, u32[]{:S(2)}) collective-permute-start(bf16[10,44,256]{2,0,1:T(8,128)(2,1)S(1)} %maximum_bitcast_fusion), channel_id=1, source_target_pairs={{0,1},{1,2},{2,3},{4,5},{5,6},{6,7},{8,9},{9,10},{10,11},{12,13},{... | collective-permute-start | bytes 675848 | tf_op jit(solution)/shard_map/ppermute | solution.py:43
  34.8 0.1 pad_maximum_fusion.2.p_second
  34.9 0.7 collective-permute-start.2
  35.7 4.7 %collective-permute-done.7 = bf16[10,44,256]{2,0,1:T(8,128)(2,1)S(1)} collective-permute-done((bf16[10,44,256]{2,0,1:T(8,128)(2,1)S(1)}, bf16[10,44,256]{2,0,1:T(8,128)(2,1)S(1)}, u32[]{:S(2)}, u32[]{:S(2)}) %collective-permute-start.7) | collective-permute-done | bytes 225312 | tf_op jit(solution)/shard_map/ppermute | solution.py:43
  40.3 1.0 collective-permute-done.6
  41.3 6.2 %forward.1 = (bf16[28,32,128]{2,1,0:T(8,128)(2,1)S(1)}, bf16[24,32,128]{2,1,0:T(8,128)(2,1)S(1)}, bf16[3,28,32,128]{3,2,1,0:T(8,128)(2,1)S(1)}, bf16[28,32,128]{...) custom-call(bf16[24,24,256]{2,1,0:T(8,128)(2,1)S(1)} %pad_maximum_fusion.stacked, ...), custom_call_target="tpu_custom_call" | custom-call | flops 1258291200 | bytes 4662272 | tf_op jit(solution)/shard_map/forward/pallas_call | solution.py:276
  47.6 0.2 turn.1
  47.8 6.1 %collective-permute-start.8 = (bf16[12,24,128]{2,1,0:T(8,128)(2,1)S(1)}, bf16[12,24,128]{2,1,0:T(8,128)(2,1)S(1)}, u32[]{:S(2)}, u32[]{:S(2)}) collective-permute-start(bf16[12,24,128]{2,1,0:T(8,128)(2,1)S(1)} %get-tuple-element.31), channel_id=1, source_target_pairs={{0,4},{1,5},{2,6},{3,7},{4,8},{5,9},{6,10},{7,11},{8,12},{9,13},{1... | collective-permute-start | bytes 221192 | tf_op jit(solution)/shard_map/ppermute | solution.py:43
  54.0 1.3 %collective-permute-start.9 = (bf16[12,24,128]{2,1,0:T(8,128)(2,1)S(1)}, bf16[12,24,128]{2,1,0:T(8,128)(2,1)S(1)}, u32[]{:S(2)}, u32[]{:S(2)}) collective-permute-start(bf16[12,24,128]{2,1,0:T(8,128)(2,1)S(1)} %get-tuple-element.32), channel_id=1, source_target_pairs={{4,0},{5,1},{6,2},{7,3},{8,4},{9,5},{10,6},{11,7},{12,8},{13,9},{1... | collective-permute-start | bytes 221192 | tf_op jit(solution)/shard_map/ppermute | solution.py:43
  55.3 0.6 collective-permute-done.8.above
  55.9 4.3 %collective-permute-done.9.below = bf16[12,24,128]{2,1,0:T(8,128)(2,1)S(1)} collective-permute-done((bf16[12,24,128]{2,1,0:T(8,128)(2,1)S(1)}, bf16[12,24,128]{2,1,0:T(8,128)(2,1)S(1)}, u32[]{:S(2)}, u32[]{:S(2)}) %collective-permute-start.9) | collective-permute-done | bytes 73760 | tf_op jit(solution)/shard_map/ppermute | solution.py:43
  60.3 0.1 maximum_bitcast_fusion.3
  60.4 1.3 %collective-permute-start.11 = (bf16[12,44,128]{2,0,1:T(8,128)(2,1)S(1)}, bf16[12,44,128]{2,0,1:T(8,128)(2,1)S(1)}, u32[]{:S(2)}, u32[]{:S(2)}) collective-permute-start(bf16[12,44,128]{2,0,1:T(8,128)(2,1)S(1)} %maximum_bitcast_fusion.3), channel_id=1, source_target_pairs={{1,0},{2,1},{3,2},{5,4},{6,5},{7,6},{9,8},{10,9},{11,10},{13,12},{... | collective-permute-start | bytes 405512 | tf_op jit(solution)/shard_map/ppermute | solution.py:43
  61.7 0.1 maximum_bitcast_fusion.2
  61.8 5.9 %collective-permute-start.10 = (bf16[12,44,128]{2,0,1:T(8,128)(2,1)S(1)}, bf16[12,44,128]{2,0,1:T(8,128)(2,1)S(1)}, u32[]{:S(2)}, u32[]{:S(2)}) collective-permute-start(bf16[12,44,128]{2,0,1:T(8,128)(2,1)S(1)} %maximum_bitcast_fusion.2), channel_id=1, source_target_pairs={{0,1},{1,2},{2,3},{4,5},{5,6},{6,7},{8,9},{9,10},{10,11},{12,13},{... | collective-permute-start | bytes 405512 | tf_op jit(solution)/shard_map/ppermute | solution.py:43
  67.8 0.5 second_sums.1
  68.3 0.9 collective-permute-done.11
  69.2 1.5 %collective-permute-done.10 = bf16[12,44,128]{2,0,1:T(8,128)(2,1)S(1)} collective-permute-done((bf16[12,44,128]{2,0,1:T(8,128)(2,1)S(1)}, bf16[12,44,128]{2,0,1:T(8,128)(2,1)S(1)}, u32[]{:S(2)}, u32[]{:S(2)}) %collective-permute-start.10) | collective-permute-done | bytes 135200 | tf_op jit(solution)/shard_map/ppermute | solution.py:43
  70.7 3.1 %backward.1 = (bf16[32,48,128]{2,1,0:T(8,128)(2,1)S(1)}, bf16[3,28,32,128]{3,2,1,0:T(8,128)(2,1)S(1)}, bf16[24,24,128]{2,1,0:T(8,128)(2,1)S(1)}) custom-call(bf16[24,32,128]{2,1,0:T(8,128)(2,1)S(1)} %get-tuple-element.29.grad_pre, bf16[24,32,128]{2,1,0:T(8,128)(2,1)S(1)} %get-tuple-element.30.grad_tile, ...), custom_call_target="tpu_custom_call" | custom-call | flops 528482304 | bytes 4321280 | tf_op jit(solution)/shard_map/backward/pallas_call | solution.py:276
  73.8 21.2 %all_to_all.10.parts = bf16[32,48,128]{2,1,0:T(8,128)(2,1)S(1)} all-to-all(bf16[32,48,128]{2,1,0:T(8,128)(2,1)S(1)} %get-tuple-element.42), channel_id=1, replica_groups=mesh['segment'=2,'row'=4,'col'=4] {'segment','row','col'}, dimensions={0} | all-to-all | bytes 786432 | tf_op jit(solution)/shard_map/all_to_all | solution.py:421
  95.0 0.7 total.1
  95.7 3.5 %all-to-all-start.1 = ((bf16[16,40,128]{2,1,0:T(8,128)(2,1)}), bf16[16,40,128]{2,1,0:T(8,128)(2,1)S(1)}, u32[]{:S(2)}, u32[]{:S(2)}) async-start(bf16[16,40,128]{2,1,0:T(8,128)(2,1)} %get-tuple-element.43), calls=%async_computation.1 | async-start | bytes 327680 | tf_op jit(solution)/shard_map/all_to_all | solution.py:439
  99.3 1.6 %input.1 = bf16[24,24,128]{2,1,0:T(8,128)(2,1)} custom-call(bf16[3,28,32,128]{3,2,1,0:T(8,128)(2,1)S(1)} %get-tuple-element.40.windows, bf16[24,24,128]{2,1,0:T(8,128)(2,1)S(1)} %get-tuple-element.41.grad_first, bf16[24,24,128]{2,1,0:T(8,128)(2,1)S(1)} %bitcast.64, bf16[9,128,128]{2,1,0:T(8,128)(2,1)S(1)} %pad.29.v_first), custom_call_target="tpu_custom_call" | custom-call | flops 226492416 | bytes 1425408 | tf_op jit(solution)/shard_map/input/pallas_call | solution.py:276
  100.9 6.3 %all-to-all-done.1 = bf16[16,40,128]{2,1,0:T(8,128)(2,1)S(1)} async-done(((bf16[16,40,128]{2,1,0:T(8,128)(2,1)}), bf16[16,40,128]{2,1,0:T(8,128)(2,1)S(1)}, u32[]{:S(2)}, u32[]{:S(2)}) %all-to-all-start.1) | async-done | bytes 163872 | tf_op jit(solution)/shard_map/all_to_all | solution.py:439
  107.2 0.7 outputs.1
  (48 shorter events, 0.8 us)
Async XLA Ops:
  1.6 15.8 %collective-permute-start = (bf16[24,24,128]{2,0,1:T(8,128)(2,1)S(1)}, bf16[24,24,128]{2,0,1:T(8,128)(2,1)S(1)}, u32[]{:S(2)}, u32[]{:S(2)}) collective-permute-start(bf16[24,24,128]{2,0,1:T(8,128)(2,1)S(1)} %copy.16), channel_id=1, source_target_pairs={{0,0},{1,4},{2,8},{3,12},{4,1},{5,5},{6,9},{7,13},{8,2},{9,6},{10,... | collective-permute-start | bytes 442376 | tf_op jit(solution)/shard_map/ppermute | solution.py:43
  3.1 13.5 %collective-permute-start.3 = (bf16[10,24,128]{2,1,0:T(8,128)(2,1)S(1)}, bf16[10,24,128]{2,1,0:T(8,128)(2,1)S(1)}, u32[]{:S(2)}, u32[]{:S(2)}) collective-permute-start(bf16[10,24,128]{2,1,0:T(8,128)(2,1)S(1)} %get-tuple-element.64), channel_id=1, source_target_pairs={{0,4},{1,5},{2,6},{3,7},{4,8},{5,9},{6,10},{7,11},{8,12},{9,13},{1... | collective-permute-start | bytes 184328 | tf_op jit(solution)/shard_map/ppermute | solution.py:43
  10.8 6.6 %collective-permute-start.4 = (bf16[10,24,128]{2,1,0:T(8,128)(2,1)S(1)}, bf16[10,24,128]{2,1,0:T(8,128)(2,1)S(1)}, u32[]{:S(2)}, u32[]{:S(2)}) collective-permute-start(bf16[10,24,128]{2,1,0:T(8,128)(2,1)S(1)} %get-tuple-element.63), channel_id=1, source_target_pairs={{4,0},{5,1},{6,2},{7,3},{8,4},{9,5},{10,6},{11,7},{12,8},{13,9},{1... | collective-permute-start | bytes 184328 | tf_op jit(solution)/shard_map/ppermute | solution.py:43
  15.7 7.8 %copy-start = (bf16[1,24,24,128]{3,2,1,0:T(8,128)(2,1)S(1)}, bf16[1,24,24,128]{3,2,1,0:T(8,128)(2,1)}, u32[]{:S(2)}) copy-start(bf16[1,24,24,128]{3,2,1,0:T(8,128)(2,1)} %param.5) | copy-start | bytes 442372
  17.4 6.7 %collective-permute-start.1 = (bf16[10,24,128]{2,1,0:T(8,128)(2,1)S(1)}, bf16[10,24,128]{2,1,0:T(8,128)(2,1)S(1)}, u32[]{:S(2)}, u32[]{:S(2)}) collective-permute-start(bf16[10,24,128]{2,1,0:T(8,128)(2,1)S(1)} %get-tuple-element.62), channel_id=1, source_target_pairs={{0,4},{1,5},{2,6},{3,7},{4,8},{5,9},{6,10},{7,11},{8,12},{9,13},{1... | collective-permute-start | bytes 184328 | tf_op jit(solution)/shard_map/ppermute | solution.py:43
  22.2 6.6 %collective-permute-start.5 = (bf16[10,24,128]{2,1,0:T(8,128)(2,1)S(1)}, bf16[10,24,128]{2,1,0:T(8,128)(2,1)S(1)}, u32[]{:S(2)}, u32[]{:S(2)}) collective-permute-start(bf16[10,24,128]{2,1,0:T(8,128)(2,1)S(1)} %get-tuple-element.61), channel_id=1, source_target_pairs={{4,0},{5,1},{6,2},{7,3},{8,4},{9,5},{10,6},{11,7},{12,8},{13,9},{1... | collective-permute-start | bytes 184328 | tf_op jit(solution)/shard_map/ppermute | solution.py:43
  24.1 10.8 %copy-start.1 = (bf16[1,24,24,128]{3,2,1,0:T(8,128)(2,1)S(1)}, bf16[1,24,24,128]{3,2,1,0:T(8,128)(2,1)}, u32[]{:S(2)}) copy-start(bf16[1,24,24,128]{3,2,1,0:T(8,128)(2,1)} %param.6) | copy-start | bytes 442372
  28.9 11.4 %collective-permute-start.7 = (bf16[10,44,256]{2,0,1:T(8,128)(2,1)S(1)}, bf16[10,44,256]{2,0,1:T(8,128)(2,1)S(1)}, u32[]{:S(2)}, u32[]{:S(2)}) collective-permute-start(bf16[10,44,256]{2,0,1:T(8,128)(2,1)S(1)} %maximum_bitcast_fusion.1), channel_id=1, source_target_pairs={{1,0},{2,1},{3,2},{5,4},{6,5},{7,6},{9,8},{10,9},{11,10},{13,12},{... | collective-permute-start | bytes 675848 | tf_op jit(solution)/shard_map/ppermute | solution.py:43
  30.3 11.1 %collective-permute-start.6 = (bf16[10,44,256]{2,0,1:T(8,128)(2,1)S(1)}, bf16[10,44,256]{2,0,1:T(8,128)(2,1)S(1)}, u32[]{:S(2)}, u32[]{:S(2)}) collective-permute-start(bf16[10,44,256]{2,0,1:T(8,128)(2,1)S(1)} %maximum_bitcast_fusion), channel_id=1, source_target_pairs={{0,1},{1,2},{2,3},{4,5},{5,6},{6,7},{8,9},{9,10},{10,11},{12,13},{... | collective-permute-start | bytes 675848 | tf_op jit(solution)/shard_map/ppermute | solution.py:43
  34.9 12.6 %collective-permute-start.2 = (bf16[24,24,128]{2,1,0:T(8,128)(2,1)S(1)}, bf16[24,24,128]{2,1,0:T(8,128)(2,1)S(1)}, u32[]{:S(2)}, u32[]{:S(2)}) collective-permute-start(bf16[24,24,128]{2,1,0:T(8,128)(2,1)S(1)} %bitcast.70), channel_id=1, source_target_pairs={{0,0},{1,4},{2,8},{3,12},{4,1},{5,5},{6,9},{7,13},{8,2},{9,6},{10,... | collective-permute-start | bytes 442376 | tf_op jit(solution)/shard_map/ppermute | solution.py:43
  47.8 8.1 %collective-permute-start.8 = (bf16[12,24,128]{2,1,0:T(8,128)(2,1)S(1)}, bf16[12,24,128]{2,1,0:T(8,128)(2,1)S(1)}, u32[]{:S(2)}, u32[]{:S(2)}) collective-permute-start(bf16[12,24,128]{2,1,0:T(8,128)(2,1)S(1)} %get-tuple-element.31), channel_id=1, source_target_pairs={{0,4},{1,5},{2,6},{3,7},{4,8},{5,9},{6,10},{7,11},{8,12},{9,13},{1... | collective-permute-start | bytes 221192 | tf_op jit(solution)/shard_map/ppermute | solution.py:43
  54.0 6.2 %collective-permute-start.9 = (bf16[12,24,128]{2,1,0:T(8,128)(2,1)S(1)}, bf16[12,24,128]{2,1,0:T(8,128)(2,1)S(1)}, u32[]{:S(2)}, u32[]{:S(2)}) collective-permute-start(bf16[12,24,128]{2,1,0:T(8,128)(2,1)S(1)} %get-tuple-element.32), channel_id=1, source_target_pairs={{4,0},{5,1},{6,2},{7,3},{8,4},{9,5},{10,6},{11,7},{12,8},{13,9},{1... | collective-permute-start | bytes 221192 | tf_op jit(solution)/shard_map/ppermute | solution.py:43
  60.4 8.8 %collective-permute-start.11 = (bf16[12,44,128]{2,0,1:T(8,128)(2,1)S(1)}, bf16[12,44,128]{2,0,1:T(8,128)(2,1)S(1)}, u32[]{:S(2)}, u32[]{:S(2)}) collective-permute-start(bf16[12,44,128]{2,0,1:T(8,128)(2,1)S(1)} %maximum_bitcast_fusion.3), channel_id=1, source_target_pairs={{1,0},{2,1},{3,2},{5,4},{6,5},{7,6},{9,8},{10,9},{11,10},{13,12},{... | collective-permute-start | bytes 405512 | tf_op jit(solution)/shard_map/ppermute | solution.py:43
  61.8 8.9 %collective-permute-start.10 = (bf16[12,44,128]{2,0,1:T(8,128)(2,1)S(1)}, bf16[12,44,128]{2,0,1:T(8,128)(2,1)S(1)}, u32[]{:S(2)}, u32[]{:S(2)}) collective-permute-start(bf16[12,44,128]{2,0,1:T(8,128)(2,1)S(1)} %maximum_bitcast_fusion.2), channel_id=1, source_target_pairs={{0,1},{1,2},{2,3},{4,5},{5,6},{6,7},{8,9},{9,10},{10,11},{12,13},{... | collective-permute-start | bytes 405512 | tf_op jit(solution)/shard_map/ppermute | solution.py:43
  95.7 11.5 %all-to-all-start.1 = ((bf16[16,40,128]{2,1,0:T(8,128)(2,1)}), bf16[16,40,128]{2,1,0:T(8,128)(2,1)S(1)}, u32[]{:S(2)}, u32[]{:S(2)}) async-start(bf16[16,40,128]{2,1,0:T(8,128)(2,1)} %get-tuple-element.43), calls=%async_computation.1 | async-start | bytes 327680 | tf_op jit(solution)/shard_map/all_to_all | solution.py:439

commit v7 on v5

--- a/solution.py
+++ b/solution.py
@@ -11,6 +11,7 @@
 SECOND_DILATION = 8
 HALO = FIRST_DILATION + SECOND_DILATION
 GRID = ("row", "col")
+ALL = ("segment",) + GRID
 TAPS = [(a, b) for a in (-1, 0, 1) for b in (-1, 0, 1)]
 LEAD = 16
 F32, BF16 = jnp.float32, jnp.bfloat16
@@ -32,23 +33,59 @@
     return -(-n // 16) * 16
 
 
+def home(batch, r, c):
+    number = lax.axis_size("row")
+    core, row, col = (batch, r, c) if r == c else (int(r > c), r, c)
+    if r != c and (r < c) == (batch == 1):
+        row, col = c, r
+    return (core * number + row) * number + col
+
+
+def place():
+    row, col = lax.axis_index("row"), lax.axis_index("col")
+    low, high = jnp.minimum(row, col), jnp.maximum(row, col)
+    upper = lax.axis_index("segment") == 0
+    return jnp.where(upper, low, high), jnp.where(upper, high, low)
+
+
+def permute(x, pair):
+    number = lax.axis_size("row")
+    tiles = [(m, r, c) for m in range(lax.axis_size("segment")) for r in range(number) for c in range(number)]
+    pairs = [pair(*tile) for tile in tiles]
+    return lax.ppermute(x, ALL, [found for found in pairs if found is not None])
+
+
+def stored(batch, r, c):
+    number = lax.axis_size("row")
+    return (batch * number + r) * number + c
+
+
+def bring(x):
+    return permute(x, lambda m, r, c: (stored(m, r, c), home(m, r, c)))
+
+
+def take_back(x):
+    return permute(x, lambda m, r, c: (home(m, r, c), stored(m, r, c)))
+
+
 def send(x, to):
     number = lax.axis_size("row")
-    pairs = []
-    for r in range(number):
-        for c in range(number):
-            row, col = to(r, c)
-            if 0 <= row < number and 0 <= col < number:
-                pairs.append((r * number + c, row * number + col))
-    return lax.ppermute(x, GRID, pairs)
+
+    def pair(batch, r, c):
+        row, col = to(r, c)
+        if 0 <= row < number and 0 <= col < number:
+            return home(batch, r, c), home(batch, row, col)
+
+    return permute(x, pair)
 
 
 def inside(shape, side, width, top):
     number = lax.axis_size("row") * side
     rows = lax.broadcasted_iota(jnp.int32, shape, 0) + top - width
     cols = lax.broadcasted_iota(jnp.int32, shape, 1) - width
-    at_row = lax.axis_index("row") * side + rows
-    at_col = lax.axis_index("col") * side + cols
+    row, col = place()
+    at_row = row * side + rows
+    at_col = col * side + cols
     return (at_row >= 0) & (at_row < number) & (at_col >= 0) & (at_col < number) & (cols < side + width)
 
 
@@ -296,7 +333,7 @@
     first, second = FIRST_DILATION, SECOND_DILATION
     full, span, near = side + 2 * HALO, side + 2 * second, side + 2 * first
     wide, small = up16(span), up16(near)
-    tile = activations[0]
+    tile = bring(activations[0])
 
     mirrored = send(tile, lambda r, c: (c, r))
     stacked = jnp.concatenate([tile, jnp.swapaxes(mirrored, 0, 1)], axis=2)
@@ -309,7 +346,8 @@
 
     left = send(columns(side - HALO, side), lambda r, c: (r, c + 1))
     right = send(columns(0, HALO), lambda r, c: (r, c - 1))
-    left, late = lax.optimization_barrier((left, cotangent[0]))
+    _, late = lax.optimization_barrier((tile, cotangent[0]))
+    _, late = lax.optimization_barrier((above, bring(late)))
     late_mirrored = send(late, lambda r, c: (c, r))
 
     bias_rows = jnp.pad(conv_bias, ((0, 7), (0, channels - inner)))
@@ -412,7 +450,7 @@
         *(gate_second, gate_first, near_hidden, bottle_first, v_second, p_back, rows_second, ends_second),
     )
 
-    parts = lax.all_to_all(parts, ("segment",) + GRID, 0, 0, tiled=True)
+    parts = lax.all_to_all(parts, ALL, 0, 0, tiled=True)
     (input_gradient,) = call(
         input_kernel,
         "input",
@@ -440,7 +478,7 @@
         *(rows, ends),
     )
     conv_gradient = jnp.swapaxes(conv_gradient.reshape(1, 9, inner, channels), 2, 3)
-    return (input_gradient[None], conv_gradient, bias_gradient, out_gradient[None])
+    return (take_back(input_gradient)[None], conv_gradient, bias_gradient, out_gradient[None])
 
 
 def solution(mesh):

time: 107 us -> 106 us (level)
  the two profiles are of different devices: /device:TPU:0 before, /device:TPU:2 now
where the time goes in v7:
time: 106 us; the launch traced here: 105 us
  starting transfers between devices  40.2 us (38%)
  waiting for transfers between devices  27.8 us (26%)
  blocking collectives  19.6 us (18%)
  Pallas kernels  12.4 us (12%)
  local copies, waits for them, and re-layouts  2.16 us (2%)
  other arithmetic  1.7 us (2%)
  between operations  1.09 us (1%)
    ppermute x13, starting transfers between devices, permute(): return lax.ppermute(x, ALL, [found for found in pairs if found is not None])  35.7 us
    ppermute x13, waiting for transfers between devices, permute(): return lax.ppermute(x, ALL, [found for found in pairs if found is not None])  27.8 us
    all_to_all x1, blocking collectives, local(): parts = lax.all_to_all(parts, ALL, 0, 0, tiled=True)  17.6 us
    pallas_call x7, Pallas kernels, call(): pl.pallas_call(kernel, name=name, out_shape=outs, scratch_shapes=[pltpu.V...  12.4 us
    all_to_all x1, starting transfers between devices, local(): lax.all_to_all(rows, GRID, 0, 0, tiled=True)  4.54 us
  transfers between devices with their start and end apart: 14, of which 10 were waited for; matrix products, arithmetic and copies ran while one was open for 3% of the time, Pallas kernels for 7%

profile of v7, /device:TPU:2, one launch (start us, length us, event | category | flops | bytes accessed | tf_op | source)
XLA Modules:
  0.0 105.0 jit_solution(7978510569295455248)
XLA Ops:
  0.6 2.9 %collective-permute-start = (bf16[24,24,128]{2,1,0:T(8,128)(2,1)}, bf16[24,24,128]{2,1,0:T(8,128)(2,1)S(1)}, u32[]{:S(2)}, u32[]{:S(2)}) collective-permute-start(bf16[24,24,128]{2,1,0:T(8,128)(2,1)} %bitcast.92), channel_id=1, source_target_pairs={{0,0},{1,1},{2,2},{3,3},{4,17},{5,5},{6,6},{7,7},{8,18},{9,22},{10... | collective-permute-start | bytes 442376 | tf_op jit(solution)/shard_map/ppermute | solution.py:55
  3.5 1.0 fusion.9
  4.5 2.0 %all-gather = bf16[1296,128]{1,0:T(8,128)(2,1)S(1)} all-gather(bf16[648,128]{1,0:T(8,128)(2,1)S(1)} %fusion.9), channel_id=2, replica_groups=mesh['segment'=2,'row'=4,'col'=4] {'segment'}, dimensions={0}, use_global_device_ids=true | all-gather | bytes 497664 | tf_op jit(solution)/shard_map/all_gather | solution.py:357
  6.9 0.3 copy.18.w_first
  7.2 0.2 copy.20.w_second
  7.4 0.1 copy.22
  7.6 0.1 fusion.14
  7.7 0.1 copy.19.p_first
  7.8 3.6 %collective-permute-done.tile = bf16[24,24,128]{2,1,0:T(8,128)(2,1)S(1)} collective-permute-done((bf16[24,24,128]{2,1,0:T(8,128)(2,1)}, bf16[24,24,128]{2,1,0:T(8,128)(2,1)S(1)}, u32[]{:S(2)}, u32[]{:S(2)}) %collective-permute-start) | collective-permute-done | bytes 147488 | tf_op jit(solution)/shard_map/ppermute | solution.py:55
  11.4 1.9 %collective-permute-start.1 = (bf16[24,24,128]{2,0,1:T(8,128)(2,1)S(1)}, bf16[24,24,128]{2,0,1:T(8,128)(2,1)S(1)}, u32[]{:S(2)}, u32[]{:S(2)}) collective-permute-start(bf16[24,24,128]{2,0,1:T(8,128)(2,1)S(1)} %copy.16), channel_id=1, source_target_pairs={{0,0},{1,17},{2,18},{3,19},{17,1},{5,5},{6,22},{7,23},{18,2},{22,6... | collective-permute-start | bytes 442376 | tf_op jit(solution)/shard_map/ppermute | solution.py:55
  13.3 1.3 %collective-permute-done.1 = bf16[24,24,128]{2,0,1:T(8,128)(2,1)S(1)} collective-permute-done((bf16[24,24,128]{2,0,1:T(8,128)(2,1)S(1)}, bf16[24,24,128]{2,0,1:T(8,128)(2,1)S(1)}, u32[]{:S(2)}, u32[]{:S(2)}) %collective-permute-start.1) | collective-permute-done | bytes 147488 | tf_op jit(solution)/shard_map/ppermute | solution.py:55
  14.7 1.3 %collective-permute-start.2 = (bf16[10,24,256]{2,1,0:T(8,128)(2,1)S(1)}, bf16[10,24,256]{2,1,0:T(8,128)(2,1)S(1)}, u32[]{:S(2)}, u32[]{:S(2)}) collective-permute-start(bf16[10,24,256]{2,1,0:T(8,128)(2,1)S(1)} %get-tuple-element.58), channel_id=1, source_target_pairs={{0,17},{1,5},{2,6},{3,7},{17,18},{5,22},{6,10},{7,11},{18,19},{22,... | collective-permute-start | bytes 368648 | tf_op jit(solution)/shard_map/ppermute | solution.py:55
  16.0 0.1 tile.13.b_first
  16.1 0.1 tile.15.b_second
  16.2 0.1 copy.23
  16.3 2.6 %collective-permute-start.3 = (bf16[24,24,128]{2,1,0:T(8,128)(2,1)S(1)}, bf16[24,24,128]{2,1,0:T(8,128)(2,1)S(1)}, u32[]{:S(2)}, u32[]{:S(2)}) collective-permute-start(bf16[24,24,128]{2,1,0:T(8,128)(2,1)S(1)} %bitcast.93), channel_id=1, source_target_pairs={{0,0},{1,1},{2,2},{3,3},{4,17},{5,5},{6,6},{7,7},{8,18},{9,22},{10... | collective-permute-start | bytes 442376 | tf_op jit(solution)/shard_map/ppermute | solution.py:55
  19.0 1.3 %collective-permute-start.5 = (bf16[10,24,256]{2,1,0:T(8,128)(2,1)S(1)}, bf16[10,24,256]{2,1,0:T(8,128)(2,1)S(1)}, u32[]{:S(2)}, u32[]{:S(2)}) collective-permute-start(bf16[10,24,256]{2,1,0:T(8,128)(2,1)S(1)} %get-tuple-element.57), channel_id=1, source_target_pairs={{17,0},{5,1},{6,2},{7,3},{18,17},{22,5},{10,6},{11,7},{19,18},{23,... | collective-permute-start | bytes 368648 | tf_op jit(solution)/shard_map/ppermute | solution.py:55
  20.3 0.1 fusion.8
  20.4 4.8 %collective-permute-done.5.below = bf16[10,24,256]{2,1,0:T(8,128)(2,1)S(1)} collective-permute-done((bf16[10,24,256]{2,1,0:T(8,128)(2,1)S(1)}, bf16[10,24,256]{2,1,0:T(8,128)(2,1)S(1)}, u32[]{:S(2)}, u32[]{:S(2)}) %collective-permute-start.5) | collective-permute-done | bytes 122912 | tf_op jit(solution)/shard_map/ppermute | solution.py:55
  25.3 1.9 %collective-permute-start.7 = (bf16[10,44,256]{2,0,1:T(8,128)(2,1)S(1)}, bf16[10,44,256]{2,0,1:T(8,128)(2,1)S(1)}, u32[]{:S(2)}, u32[]{:S(2)}) collective-permute-start(bf16[10,44,256]{2,0,1:T(8,128)(2,1)S(1)} %maximum_bitcast_fusion.1), channel_id=1, source_target_pairs={{1,0},{2,1},{3,2},{5,17},{6,5},{7,6},{22,18},{10,22},{11,10},{23,1... | collective-permute-start | bytes 675848 | tf_op jit(solution)/shard_map/ppermute | solution.py:55
  27.2 0.1 maximum_bitcast_fusion
  27.2 6.9 %collective-permute-start.6 = (bf16[10,44,256]{2,0,1:T(8,128)(2,1)S(1)}, bf16[10,44,256]{2,0,1:T(8,128)(2,1)S(1)}, u32[]{:S(2)}, u32[]{:S(2)}) collective-permute-start(bf16[10,44,256]{2,0,1:T(8,128)(2,1)S(1)} %maximum_bitcast_fusion), channel_id=1, source_target_pairs={{0,1},{1,2},{2,3},{17,5},{5,6},{6,7},{18,22},{22,10},{10,11},{19,2... | collective-permute-start | bytes 675848 | tf_op jit(solution)/shard_map/ppermute | solution.py:55
  34.1 0.1 pad_maximum_fusion.2.p_second
  34.2 1.9 %collective-permute-start.4 = (bf16[24,24,128]{2,1,0:T(8,128)(2,1)S(1)}, bf16[24,24,128]{2,1,0:T(8,128)(2,1)S(1)}, u32[]{:S(2)}, u32[]{:S(2)}) collective-permute-start(bf16[24,24,128]{2,1,0:T(8,128)(2,1)S(1)} %collective-permute-done.3.cotangent), channel_id=1, source_target_pairs={{0,0},{1,17},{2,18},{3,19},{17,1},{5,5},{6,22},{7,23},{18,2},{22,6... | collective-permute-start | bytes 442376 | tf_op jit(solution)/shard_map/ppermute | solution.py:55
  36.2 1.3 %collective-permute-done.7 = bf16[10,44,256]{2,0,1:T(8,128)(2,1)S(1)} collective-permute-done((bf16[10,44,256]{2,0,1:T(8,128)(2,1)S(1)}, bf16[10,44,256]{2,0,1:T(8,128)(2,1)S(1)}, u32[]{:S(2)}, u32[]{:S(2)}) %collective-permute-start.7) | collective-permute-done | bytes 225312 | tf_op jit(solution)/shard_map/ppermute | solution.py:55
  37.5 1.5 %collective-permute-done.6 = bf16[10,44,256]{2,0,1:T(8,128)(2,1)S(1)} collective-permute-done((bf16[10,44,256]{2,0,1:T(8,128)(2,1)S(1)}, bf16[10,44,256]{2,0,1:T(8,128)(2,1)S(1)}, u32[]{:S(2)}, u32[]{:S(2)}) %collective-permute-start.6) | collective-permute-done | bytes 225312 | tf_op jit(solution)/shard_map/ppermute | solution.py:55
  39.0 6.2 %forward.1 = (bf16[28,32,128]{2,1,0:T(8,128)(2,1)S(1)}, bf16[24,32,128]{2,1,0:T(8,128)(2,1)S(1)}, bf16[3,28,32,128]{3,2,1,0:T(8,128)(2,1)S(1)}, bf16[28,32,128]{...) custom-call(bf16[24,24,256]{2,1,0:T(8,128)(2,1)S(1)} %pad_maximum_fusion.stacked, ...), custom_call_target="tpu_custom_call" | custom-call | flops 1258291200 | bytes 4662272 | tf_op jit(solution)/shard_map/forward/pallas_call | solution.py:313
  45.3 0.2 turn.1
  45.5 3.0 %collective-permute-start.8 = (bf16[12,24,128]{2,1,0:T(8,128)(2,1)S(1)}, bf16[12,24,128]{2,1,0:T(8,128)(2,1)S(1)}, u32[]{:S(2)}, u32[]{:S(2)}) collective-permute-start(bf16[12,24,128]{2,1,0:T(8,128)(2,1)S(1)} %get-tuple-element.31), channel_id=1, source_target_pairs={{0,17},{1,5},{2,6},{3,7},{17,18},{5,22},{6,10},{7,11},{18,19},{22,... | collective-permute-start | bytes 221192 | tf_op jit(solution)/shard_map/ppermute | solution.py:55
  48.5 1.3 %collective-permute-start.9 = (bf16[12,24,128]{2,1,0:T(8,128)(2,1)S(1)}, bf16[12,24,128]{2,1,0:T(8,128)(2,1)S(1)}, u32[]{:S(2)}, u32[]{:S(2)}) collective-permute-start(bf16[12,24,128]{2,1,0:T(8,128)(2,1)S(1)} %get-tuple-element.32), channel_id=1, source_target_pairs={{17,0},{5,1},{6,2},{7,3},{18,17},{22,5},{10,6},{11,7},{19,18},{23,... | collective-permute-start | bytes 221192 | tf_op jit(solution)/shard_map/ppermute | solution.py:55
  49.9 0.6 collective-permute-done.8.above
  50.5 3.7 %collective-permute-done.9.below = bf16[12,24,128]{2,1,0:T(8,128)(2,1)S(1)} collective-permute-done((bf16[12,24,128]{2,1,0:T(8,128)(2,1)S(1)}, bf16[12,24,128]{2,1,0:T(8,128)(2,1)S(1)}, u32[]{:S(2)}, u32[]{:S(2)}) %collective-permute-start.9) | collective-permute-done | bytes 73760 | tf_op jit(solution)/shard_map/ppermute | solution.py:55
  54.3 0.1 maximum_bitcast_fusion.3
  54.3 1.9 %collective-permute-start.11 = (bf16[12,44,128]{2,0,1:T(8,128)(2,1)S(1)}, bf16[12,44,128]{2,0,1:T(8,128)(2,1)S(1)}, u32[]{:S(2)}, u32[]{:S(2)}) collective-permute-start(bf16[12,44,128]{2,0,1:T(8,128)(2,1)S(1)} %maximum_bitcast_fusion.3), channel_id=1, source_target_pairs={{1,0},{2,1},{3,2},{5,17},{6,5},{7,6},{22,18},{10,22},{11,10},{23,1... | collective-permute-start | bytes 405512 | tf_op jit(solution)/shard_map/ppermute | solution.py:55
  56.3 0.1 maximum_bitcast_fusion.2
  56.4 6.8 %collective-permute-start.10 = (bf16[12,44,128]{2,0,1:T(8,128)(2,1)S(1)}, bf16[12,44,128]{2,0,1:T(8,128)(2,1)S(1)}, u32[]{:S(2)}, u32[]{:S(2)}) collective-permute-start(bf16[12,44,128]{2,0,1:T(8,128)(2,1)S(1)} %maximum_bitcast_fusion.2), channel_id=1, source_target_pairs={{0,1},{1,2},{2,3},{17,5},{5,6},{6,7},{18,22},{22,10},{10,11},{19,2... | collective-permute-start | bytes 405512 | tf_op jit(solution)/shard_map/ppermute | solution.py:55
  63.2 0.5 second_sums.1
  63.7 0.9 collective-permute-done.11
  64.6 1.5 %collective-permute-done.10 = bf16[12,44,128]{2,0,1:T(8,128)(2,1)S(1)} collective-permute-done((bf16[12,44,128]{2,0,1:T(8,128)(2,1)S(1)}, bf16[12,44,128]{2,0,1:T(8,128)(2,1)S(1)}, u32[]{:S(2)}, u32[]{:S(2)}) %collective-permute-start.10) | collective-permute-done | bytes 135200 | tf_op jit(solution)/shard_map/ppermute | solution.py:55
  66.2 3.1 %backward.1 = (bf16[32,48,128]{2,1,0:T(8,128)(2,1)S(1)}, bf16[3,28,32,128]{3,2,1,0:T(8,128)(2,1)S(1)}, bf16[24,24,128]{2,1,0:T(8,128)(2,1)S(1)}) custom-call(bf16[24,32,128]{2,1,0:T(8,128)(2,1)S(1)} %get-tuple-element.29.grad_pre, bf16[24,32,128]{2,1,0:T(8,128)(2,1)S(1)} %get-tuple-element.30.grad_tile, ...), custom_call_target="tpu_custom_call" | custom-call | flops 528482304 | bytes 4321280 | tf_op jit(solution)/shard_map/backward/pallas_call | solution.py:313
  69.3 17.6 %all_to_all.10.parts = bf16[32,48,128]{2,1,0:T(8,128)(2,1)S(1)} all-to-all(bf16[32,48,128]{2,1,0:T(8,128)(2,1)S(1)} %get-tuple-element.42), channel_id=1, replica_groups=mesh['segment'=2,'row'=4,'col'=4] {'segment','row','col'}, dimensions={0} | all-to-all | bytes 786432 | tf_op jit(solution)/shard_map/all_to_all | solution.py:453
  86.8 0.7 total.1
  87.6 4.5 %all-to-all-start.1 = ((bf16[16,40,128]{2,1,0:T(8,128)(2,1)}), bf16[16,40,128]{2,1,0:T(8,128)(2,1)S(1)}, u32[]{:S(2)}, u32[]{:S(2)}) async-start(bf16[16,40,128]{2,1,0:T(8,128)(2,1)} %get-tuple-element.43), calls=%async_computation.1 | async-start | bytes 327680 | tf_op jit(solution)/shard_map/all_to_all | solution.py:471
  92.1 0.9 input.1
  93.1 1.9 %collective-permute-start.12 = (bf16[24,24,128]{2,1,0:T(8,128)(2,1)S(1)}, bf16[24,24,128]{2,1,0:T(8,128)(2,1)S(1)}, u32[]{:S(2)}, u32[]{:S(2)}) collective-permute-start(bf16[24,24,128]{2,1,0:T(8,128)(2,1)S(1)} %input.1), channel_id=1, source_target_pairs={{0,0},{1,1},{2,2},{3,3},{17,4},{5,5},{6,6},{7,7},{18,8},{22,9},{10... | collective-permute-start | bytes 442376 | tf_op jit(solution)/shard_map/ppermute | solution.py:55
  95.0 8.6 %collective-permute-done.12 = bf16[24,24,128]{2,1,0:T(8,128)(2,1)S(1)} collective-permute-done((bf16[24,24,128]{2,1,0:T(8,128)(2,1)S(1)}, bf16[24,24,128]{2,1,0:T(8,128)(2,1)S(1)}, u32[]{:S(2)}, u32[]{:S(2)}) %collective-permute-start.12) | collective-permute-done | bytes 147488 | tf_op jit(solution)/shard_map/ppermute | solution.py:55
  103.6 0.7 outputs.1
  104.3 0.7 copy.33
  (44 shorter events, 0.8 us)
Async XLA Ops:
  0.6 10.7 %collective-permute-start = (bf16[24,24,128]{2,1,0:T(8,128)(2,1)}, bf16[24,24,128]{2,1,0:T(8,128)(2,1)S(1)}, u32[]{:S(2)}, u32[]{:S(2)}) collective-permute-start(bf16[24,24,128]{2,1,0:T(8,128)(2,1)} %bitcast.92), channel_id=1, source_target_pairs={{0,0},{1,1},{2,2},{3,3},{4,17},{5,5},{6,6},{7,7},{8,18},{9,22},{10... | collective-permute-start | bytes 442376 | tf_op jit(solution)/shard_map/ppermute | solution.py:55
  7.2 9.1 %copy-start = (bf16[1,24,24,128]{3,2,1,0:T(8,128)(2,1)S(1)}, bf16[1,24,24,128]{3,2,1,0:T(8,128)(2,1)}, u32[]{:S(2)}) copy-start(bf16[1,24,24,128]{3,2,1,0:T(8,128)(2,1)} %param.6) | copy-start | bytes 442372
  11.4 3.3 %collective-permute-start.1 = (bf16[24,24,128]{2,0,1:T(8,128)(2,1)S(1)}, bf16[24,24,128]{2,0,1:T(8,128)(2,1)S(1)}, u32[]{:S(2)}, u32[]{:S(2)}) collective-permute-start(bf16[24,24,128]{2,0,1:T(8,128)(2,1)S(1)} %copy.16), channel_id=1, source_target_pairs={{0,0},{1,17},{2,18},{3,19},{17,1},{5,5},{6,22},{7,23},{18,2},{22,6... | collective-permute-start | bytes 442376 | tf_op jit(solution)/shard_map/ppermute | solution.py:55
  14.7 5.7 %collective-permute-start.2 = (bf16[10,24,256]{2,1,0:T(8,128)(2,1)S(1)}, bf16[10,24,256]{2,1,0:T(8,128)(2,1)S(1)}, u32[]{:S(2)}, u32[]{:S(2)}) collective-permute-start(bf16[10,24,256]{2,1,0:T(8,128)(2,1)S(1)} %get-tuple-element.58), channel_id=1, source_target_pairs={{0,17},{1,5},{2,6},{3,7},{17,18},{5,22},{6,10},{7,11},{18,19},{22,... | collective-permute-start | bytes 368648 | tf_op jit(solution)/shard_map/ppermute | solution.py:55
  16.3 17.9 %collective-permute-start.3 = (bf16[24,24,128]{2,1,0:T(8,128)(2,1)S(1)}, bf16[24,24,128]{2,1,0:T(8,128)(2,1)S(1)}, u32[]{:S(2)}, u32[]{:S(2)}) collective-permute-start(bf16[24,24,128]{2,1,0:T(8,128)(2,1)S(1)} %bitcast.93), channel_id=1, source_target_pairs={{0,0},{1,1},{2,2},{3,3},{4,17},{5,5},{6,6},{7,7},{8,18},{9,22},{10... | collective-permute-start | bytes 442376 | tf_op jit(solution)/shard_map/ppermute | solution.py:55
  19.0 6.2 %collective-permute-start.5 = (bf16[10,24,256]{2,1,0:T(8,128)(2,1)S(1)}, bf16[10,24,256]{2,1,0:T(8,128)(2,1)S(1)}, u32[]{:S(2)}, u32[]{:S(2)}) collective-permute-start(bf16[10,24,256]{2,1,0:T(8,128)(2,1)S(1)} %get-tuple-element.57), channel_id=1, source_target_pairs={{17,0},{5,1},{6,2},{7,3},{18,17},{22,5},{10,6},{11,7},{19,18},{23,... | collective-permute-start | bytes 368648 | tf_op jit(solution)/shard_map/ppermute | solution.py:55
  25.3 12.3 %collective-permute-start.7 = (bf16[10,44,256]{2,0,1:T(8,128)(2,1)S(1)}, bf16[10,44,256]{2,0,1:T(8,128)(2,1)S(1)}, u32[]{:S(2)}, u32[]{:S(2)}) collective-permute-start(bf16[10,44,256]{2,0,1:T(8,128)(2,1)S(1)} %maximum_bitcast_fusion.1), channel_id=1, source_target_pairs={{1,0},{2,1},{3,2},{5,17},{6,5},{7,6},{22,18},{10,22},{11,10},{23,1... | collective-permute-start | bytes 675848 | tf_op jit(solution)/shard_map/ppermute | solution.py:55
  27.2 11.8 %collective-permute-start.6 = (bf16[10,44,256]{2,0,1:T(8,128)(2,1)S(1)}, bf16[10,44,256]{2,0,1:T(8,128)(2,1)S(1)}, u32[]{:S(2)}, u32[]{:S(2)}) collective-permute-start(bf16[10,44,256]{2,0,1:T(8,128)(2,1)S(1)} %maximum_bitcast_fusion), channel_id=1, source_target_pairs={{0,1},{1,2},{2,3},{17,5},{5,6},{6,7},{18,22},{22,10},{10,11},{19,2... | collective-permute-start | bytes 675848 | tf_op jit(solution)/shard_map/ppermute | solution.py:55
  34.2 11.0 %collective-permute-start.4 = (bf16[24,24,128]{2,1,0:T(8,128)(2,1)S(1)}, bf16[24,24,128]{2,1,0:T(8,128)(2,1)S(1)}, u32[]{:S(2)}, u32[]{:S(2)}) collective-permute-start(bf16[24,24,128]{2,1,0:T(8,128)(2,1)S(1)} %collective-permute-done.3.cotangent), channel_id=1, source_target_pairs={{0,0},{1,17},{2,18},{3,19},{17,1},{5,5},{6,22},{7,23},{18,2},{22,6... | collective-permute-start | bytes 442376 | tf_op jit(solution)/shard_map/ppermute | solution.py:55
  45.5 5.0 %collective-permute-start.8 = (bf16[12,24,128]{2,1,0:T(8,128)(2,1)S(1)}, bf16[12,24,128]{2,1,0:T(8,128)(2,1)S(1)}, u32[]{:S(2)}, u32[]{:S(2)}) collective-permute-start(bf16[12,24,128]{2,1,0:T(8,128)(2,1)S(1)} %get-tuple-element.31), channel_id=1, source_target_pairs={{0,17},{1,5},{2,6},{3,7},{17,18},{5,22},{6,10},{7,11},{18,19},{22,... | collective-permute-start | bytes 221192 | tf_op jit(solution)/shard_map/ppermute | solution.py:55
  48.5 5.7 %collective-permute-start.9 = (bf16[12,24,128]{2,1,0:T(8,128)(2,1)S(1)}, bf16[12,24,128]{2,1,0:T(8,128)(2,1)S(1)}, u32[]{:S(2)}, u32[]{:S(2)}) collective-permute-start(bf16[12,24,128]{2,1,0:T(8,128)(2,1)S(1)} %get-tuple-element.32), channel_id=1, source_target_pairs={{17,0},{5,1},{6,2},{7,3},{18,17},{22,5},{10,6},{11,7},{19,18},{23,... | collective-permute-start | bytes 221192 | tf_op jit(solution)/shard_map/ppermute | solution.py:55
  54.3 10.3 %collective-permute-start.11 = (bf16[12,44,128]{2,0,1:T(8,128)(2,1)S(1)}, bf16[12,44,128]{2,0,1:T(8,128)(2,1)S(1)}, u32[]{:S(2)}, u32[]{:S(2)}) collective-permute-start(bf16[12,44,128]{2,0,1:T(8,128)(2,1)S(1)} %maximum_bitcast_fusion.3), channel_id=1, source_target_pairs={{1,0},{2,1},{3,2},{5,17},{6,5},{7,6},{22,18},{10,22},{11,10},{23,1... | collective-permute-start | bytes 405512 | tf_op jit(solution)/shard_map/ppermute | solution.py:55
  56.4 9.8 %collective-permute-start.10 = (bf16[12,44,128]{2,0,1:T(8,128)(2,1)S(1)}, bf16[12,44,128]{2,0,1:T(8,128)(2,1)S(1)}, u32[]{:S(2)}, u32[]{:S(2)}) collective-permute-start(bf16[12,44,128]{2,0,1:T(8,128)(2,1)S(1)} %maximum_bitcast_fusion.2), channel_id=1, source_target_pairs={{0,1},{1,2},{2,3},{17,5},{5,6},{6,7},{18,22},{22,10},{10,11},{19,2... | collective-permute-start | bytes 405512 | tf_op jit(solution)/shard_map/ppermute | solution.py:55
  87.6 16.0 %all-to-all-start.1 = ((bf16[16,40,128]{2,1,0:T(8,128)(2,1)}), bf16[16,40,128]{2,1,0:T(8,128)(2,1)S(1)}, u32[]{:S(2)}, u32[]{:S(2)}) async-start(bf16[16,40,128]{2,1,0:T(8,128)(2,1)} %get-tuple-element.43), calls=%async_computation.1 | async-start | bytes 327680 | tf_op jit(solution)/shard_map/all_to_all | solution.py:471
  93.1 10.5 %collective-permute-start.12 = (bf16[24,24,128]{2,1,0:T(8,128)(2,1)S(1)}, bf16[24,24,128]{2,1,0:T(8,128)(2,1)S(1)}, u32[]{:S(2)}, u32[]{:S(2)}) collective-permute-start(bf16[24,24,128]{2,1,0:T(8,128)(2,1)S(1)} %input.1), channel_id=1, source_target_pairs={{0,0},{1,1},{2,2},{3,3},{17,4},{5,5},{6,6},{7,7},{18,8},{22,9},{10... | collective-permute-start | bytes 442376 | tf_op jit(solution)/shard_map/ppermute | solution.py:55

commit v8 on v4

--- a/solution.py
+++ b/solution.py
@@ -11,12 +11,15 @@
 SECOND_DILATION = 8
 HALO = FIRST_DILATION + SECOND_DILATION
 GRID = ("row", "col")
+ALL = ("segment",) + GRID
+ORDER = [0, 1, 3, 4, 6, 7, 2, 5, 8]
 TAPS = [(a, b) for a in (-1, 0, 1) for b in (-1, 0, 1)]
 LEAD = 16
 F32, BF16 = jnp.float32, jnp.bfloat16
 
 
-ORDER = [0, 1, 3, 4, 6, 7, 2, 5, 8]
+def tap(a, b):
+    return 3 * (a + 1) + (b + 1)
 
 
 def dot(x, y):
@@ -31,23 +34,59 @@
     return -(-n // 16) * 16
 
 
+def home(batch, r, c):
+    number = lax.axis_size("row")
+    core, row, col = (batch, r, c) if r == c else (int(r > c), r, c)
+    if r != c and (r < c) == (batch == 1):
+        row, col = c, r
+    return (core * number + row) * number + col
+
+
+def place():
+    row, col = lax.axis_index("row"), lax.axis_index("col")
+    low, high = jnp.minimum(row, col), jnp.maximum(row, col)
+    upper = lax.axis_index("segment") == 0
+    return jnp.where(upper, low, high), jnp.where(upper, high, low)
+
+
+def permute(x, pair):
+    number = lax.axis_size("row")
+    tiles = [(m, r, c) for m in range(lax.axis_size("segment")) for r in range(number) for c in range(number)]
+    pairs = [pair(*tile) for tile in tiles]
+    return lax.ppermute(x, ALL, [found for found in pairs if found is not None])
+
+
+def stored(batch, r, c):
+    number = lax.axis_size("row")
+    return (batch * number + r) * number + c
+
+
+def bring(x):
+    return permute(x, lambda m, r, c: (stored(m, r, c), home(m, r, c)))
+
+
+def take_back(x):
+    return permute(x, lambda m, r, c: (home(m, r, c), stored(m, r, c)))
+
+
 def send(x, to):
     number = lax.axis_size("row")
-    pairs = []
-    for r in range(number):
-        for c in range(number):
-            row, col = to(r, c)
-            if 0 <= row < number and 0 <= col < number:
-                pairs.append((r * number + c, row * number + col))
-    return lax.ppermute(x, GRID, pairs)
+
+    def pair(batch, r, c):
+        row, col = to(r, c)
+        if 0 <= row < number and 0 <= col < number:
+            return home(batch, r, c), home(batch, row, col)
+
+    return permute(x, pair)
 
 
 def inside(shape, side, width, top):
     number = lax.axis_size("row") * side
     rows = lax.broadcasted_iota(jnp.int32, shape, 0) + top - width
     cols = lax.broadcasted_iota(jnp.int32, shape, 1) - width
-    at_row = lax.axis_index("row") * side + rows
-    at_col = lax.axis_index("col") * side + cols
+    row, col = place()
+    at_row = row * side + rows
+    at_col = col * side + cols
     return (at_row >= 0) & (at_row < number) & (at_col >= 0) & (at_col < number) & (cols < side + width)
 
 
@@ -120,44 +159,44 @@
 
 
 def own_kernel(
-    tile, above, below, left, right, weights, bias, proj,
-    branch_own, gate_first, bottle_first, near_hidden,
+    tile, above, below, left, right, late, weights, bias, proj,
+    swapped, gate_first, bottle_first, near_hidden,
     area, pairs, last, pre,
 ):
-    side, first, second = tile.shape[0], FIRST_DILATION, SECOND_DILATION
+    side, first, second, inner = tile.shape[0], FIRST_DILATION, SECOND_DILATION, bias.shape[1]
     near, small = gate_first.shape[:2]
+    span = side + 2 * second
     assemble(area, tile[...].astype(F32), above, below, left, right)
 
     def store(top, pre_act, branch):
         pre[pl.ds(top, 8)] = pre_act
-        branch_own[pl.ds(top, 8)] = branch
+        swapped[pl.ds(top, 8)] = branch[:, :span].astype(BF16)
 
     first_branch(area, pairs, last, weights, bias, proj, store)
+    swapped[span:, :side] = late[...]
     for b in (-1, 0, 1):
         at = LEAD + first * b
         near_hidden[b + 1] = positive(area[HALO - first : HALO + side + first, at : at + small]).astype(BF16)
     edge = second - first
     part = pre[edge : edge + near, edge : edge + small]
     alive = (part > 0) & inside(part.shape, side, first, 0)
-    gate_first[...] = jnp.where(alive, 1.0, 0.0).astype(BF16)
+    gate_first[:, :, :inner] = jnp.where(alive, 1.0, 0.0).astype(BF16)
+    gate_first[:, :, inner:] = jnp.zeros((near, small, gate_first.shape[2] - inner), BF16)
     bottle_first[...] = positive(pre[second : second + side, second : second + small]).astype(BF16)
 
 
-def other_kernel(
-    tile, above, below, left, right, weights, bias, proj, branch_own, w_second, b_second,
-    gate_second, hidden_pairs, hidden_last, pre_second,
-    area, pairs, last, current,
+def middle_kernel(
+    kept, other, w_second, b_second, p_second,
+    gate_second, hidden_pairs, hidden_last, bottle_second, grad_tile, grad_pre, above, below,
+    current, padded, pre_second,
 ):
-    side, first, second = tile.shape[0], FIRST_DILATION, SECOND_DILATION
+    side, channels, span = above.shape[1], kept.shape[2], kept.shape[1]
+    first, second, inner = FIRST_DILATION, SECOND_DILATION, bottle_second.shape[2]
     near, small = gate_second.shape[:2]
-    assemble(area, tile[...].astype(F32), above, below, left, right)
-
-    def store(top, pre_act, branch):
-        here = pl.ds(top, 8)
-        sym = rounded((branch_own[here] + branch) * 0.5)
-        current[here] = jnp.where(inside(sym.shape, side, second, top), sym, 0)
-
-    first_branch(area, pairs, last, weights, bias, proj, store)
+    turned = jnp.swapaxes(other[:span].astype(F32), 0, 1)
+    sym = rounded((kept[:span].astype(F32) + turned) * 0.5)
+    current[:, :span] = jnp.where(inside(sym.shape, side, second, 0), sym, 0)
+    current[:, span:] = jnp.zeros((span, current.shape[1] - span, channels), F32)
     edge = second - first
     part = current[edge : edge + near, edge : edge + small]
     gate_second[...] = jnp.where(part > 0, 1.0, 0.0).astype(BF16)
@@ -170,17 +209,14 @@
         return 0
 
     lax.fori_loop(0, side // 8, rows, 0)
-
-
-def turn_kernel(cotangent, mirrored, pre_second, p_second, grad_tile, grad_pre, above, below, padded):
-    side, channels = cotangent.shape[0], cotangent.shape[2]
-    small, first = pre_second.shape[1], FIRST_DILATION
-    branch = (cotangent[...].astype(F32) + jnp.swapaxes(mirrored[...].astype(F32), 0, 1)) * 0.5
+    bottle_second[...] = positive(pre_second[:, :, :inner]).astype(BF16)
+
+    turned = jnp.swapaxes(other[span:, :side].astype(F32), 0, 1)
     padded[:, side:] = jnp.zeros((side, small - side, channels), F32)
-    padded[:, :side] = rounded(branch)
+    padded[:, :side] = rounded((kept[span:, :side].astype(F32) + turned) * 0.5)
     branch = padded[...].astype(BF16)
     grad_tile[...] = branch
-    grad = dot(branch.reshape(side * small, channels), p_second[...]).reshape(side, small, channels)
+    grad = dot(branch.reshape(side * small, channels), p_second[...]).reshape(side, small, 2 * inner)
     grad = jnp.where(pre_second[...] > 0, grad, 0)
     grad_pre[...] = grad.astype(BF16)
     grad, branch = grad[:, :side].astype(BF16), padded[:, :side].astype(BF16)
@@ -208,8 +244,8 @@
     ends[:, :lanes] = jnp.broadcast_to(jnp.sum(flat, axis=0, keepdims=True), (ends.shape[0], lanes))
 
 
-def second_sums_kernel(grad_pre, pairs, last, pre_second, grad_tile, rows, ends):
-    side, inner = grad_pre.shape[0], grad_pre.shape[2] // 2
+def second_sums_kernel(grad_pre, pairs, last, bottle, grad_tile, rows, ends):
+    side = grad_pre.shape[0]
     channels = grad_tile.shape[2]
 
     def hidden(a, b):
@@ -218,34 +254,46 @@
             return pairs[top : top + side]
         return last[top + SECOND_DILATION : top + SECOND_DILATION + side, :, :channels]
 
-    bottle = positive(pre_second[:, :, :inner]).astype(BF16)
     weight_sums(rows, ends, grad_pre[...].astype(F32), hidden, bottle, grad_tile[...])
 
 
 def backward_kernel(
     grad_pre, grad_tile, above, below, left, right, left_branch, right_branch, gate_second, gate_first, near_hidden,
     bottle_first, v_second, p_first, rows_second, ends_second,
-    parts, windows, windows_last, grad_first,
-    area, pairs, last, branch, grads, rows, ends,
+    parts, windows, grad_first,
+    area, shifted, branch, grads, rows, ends,
 ):
-    side, channels, inner = grad_first.shape[0], grad_first.shape[2], bottle_first.shape[2]
+    side, channels = grad_first.shape[0], grad_first.shape[2]
     first, second = FIRST_DILATION, SECOND_DILATION
-    near, small = gate_first.shape[:2]
-    assemble(area, grad_pre[:, :side].astype(F32), above, below, left, right)
+    full, near = side + 2 * HALO, side + 2 * first
+    small = grad_pre.shape[1]
+    middle = slice(LEAD, LEAD + side)
+
+    area[:, :LEAD] = jnp.zeros((full, LEAD, channels), F32)
+    area[:, LEAD + side :] = jnp.zeros((full, area.shape[1] - LEAD - side, channels), F32)
+    area[HALO : HALO + side, LEAD : LEAD + small] = grad_pre[...].astype(F32)
+    area[:HALO, middle] = above[:HALO].astype(F32)
+    area[HALO + side :, middle] = below[:HALO].astype(F32)
+    area[:, LEAD - HALO : LEAD] = left[...].astype(F32)
+    area[:, LEAD + side : LEAD + side + HALO] = right[...].astype(F32)
     branch[...] = jnp.zeros(branch.shape, F32)
     branch[first : first + side, first : first + side] = grad_tile[:, :side].astype(F32)
     branch[:first, first : first + side] = above[HALO:].astype(F32)
     branch[first + side :, first : first + side] = below[HALO:].astype(F32)
     branch[:, :first] = left_branch[...].astype(F32)
     branch[:, first + side : near] = right_branch[...].astype(F32)
-    starts = [LEAD - HALO + second * (1 + b) for b in (-1, 0, 1)]
-    paired(area, starts, small, second, pairs, last, lambda x: x)
-    grads[:, small:] = jnp.zeros((near, grads.shape[1] - small, inner), F32)
+    for b in (-1, 0, 1):
+        at = LEAD - HALO + second * (1 - b)
+        shifted[b + 1] = area[:, at : at + small].astype(BF16)
+    grads[:, small:] = jnp.zeros((near, grads.shape[1] - small, channels), F32)
 
     def sections(step, _):
         top = step * 7
         size = 7 * small
-        total = taps_sum(pairs, last, top, 7, second, v_second)
+        total = jnp.zeros((size, 2 * channels), F32)
+        for a, b in TAPS:
+            window = shifted[b + 1, pl.ds(top + second * (1 - a), 7)].reshape(size, channels)
+            total = total + dot(window, v_second[tap(a, b)])
         here = pl.ds(top, 7)
         grad = branch[here, :small].reshape(size, channels)
         gate = gate_second[here].astype(F32).reshape(size, channels) > 0
@@ -253,20 +301,20 @@
         other = rounded(grad + jnp.where(gate, total[:, channels:], 0))
         grad = ((own + other) * 0.5).astype(BF16)
         branch[here, :small] = grad.astype(F32).reshape(7, small, channels)
-        gate = gate_first[here].astype(F32).reshape(size, inner) > 0
+        gate = gate_first[here].astype(F32).reshape(size, channels) > 0
         grad = rounded(jnp.where(gate, dot(grad, p_first[...]), 0))
-        grads[here, :small] = grad.reshape(7, small, inner)
+        grads[here, :small] = grad.reshape(7, small, channels)
         return 0
 
     lax.fori_loop(0, near // 7, sections, 0)
-    paired(grads, [0, first, 2 * first], small, first, windows, windows_last, lambda x: x)
+    for b in (-1, 0, 1):
+        at = first * (1 - b)
+        windows[b + 1] = grads[:, at : at + small].astype(BF16)
     part = branch[first : first + side, first : first + small]
     grad_first[...] = part[:, :side].astype(BF16)
-    def kept(x):
-        return jnp.where(lax.broadcasted_iota(jnp.int32, x.shape, 1) < side, x, 0)
-
-    part = kept(part).astype(BF16)
-    grad = kept(grads[first : first + side, first : first + small])
+    keep = lax.broadcasted_iota(jnp.int32, part.shape, 1) < side
+    part = jnp.where(keep, part, 0).astype(BF16)
+    grad = jnp.where(keep, grads[first : first + side, first : first + small], 0)
 
     def hidden(a, b):
         return near_hidden[b, first * a : first * a + side]
@@ -285,13 +333,17 @@
             parts[at] = jnp.concatenate(pieces + [end[...]]).astype(BF16)
 
 
-def input_kernel(windows, windows_last, grad_first, tile, v_first, out):
+def input_kernel(windows, grad_first, tile, v_first, out):
     side, channels = tile.shape[0], tile.shape[2]
-    small = windows.shape[1]
+    small = windows.shape[2]
+    first = FIRST_DILATION
 
     def rows(step, _):
         top = step * 8
-        total = taps_sum(windows, windows_last, top, 8, FIRST_DILATION, v_first)
+        total = jnp.zeros((8 * small, channels), F32)
+        for a, b in TAPS:
+            window = windows[b + 1, pl.ds(top + first * (1 - a), 8)].reshape(8 * small, channels)
+            total = total + dot(window, v_first[tap(a, b)])
         here = pl.ds(top, 8)
         total = total.reshape(8, small, channels)[:, :side]
         total = jnp.where(tile[here].astype(F32) > 0, total, 0)
@@ -306,6 +358,13 @@
     total = jnp.sum(parts[...].astype(F32), axis=0) * scale
     rows[...] = jnp.broadcast_to(total[:share].astype(BF16)[None], rows.shape)
     ends[...] = total[share:]
+
+
+def outputs_kernel(rows, ends, conv_gradient, bias_gradient, out_gradient):
+    count, inner = conv_gradient.shape[0], out_gradient.shape[0]
+    conv_gradient[...] = rows[:count].astype(F32)
+    out_gradient[...] = rows[count : count + inner].astype(F32)
+    bias_gradient[...] = ends[:1, :inner]
 
 
 def call(kernel, name, outs, scratch, flops, *operands):
@@ -332,25 +391,19 @@
     first, second = FIRST_DILATION, SECOND_DILATION
     full, span, near = side + 2 * HALO, side + 2 * second, side + 2 * first
     wide, small = up16(span), up16(near)
-    tile = activations[0]
-
-    def row_strips(x):
-        return send(x[side - HALO :], lambda r, c: (r + 1, c)), send(x[:HALO], lambda r, c: (r - 1, c))
-
-    def column_strips(x, above, below):
-        whole = jnp.concatenate([above, x, below])
-        left = send(jnp.swapaxes(whole[:, side - HALO :], 0, 1), lambda r, c: (r, c + 1))
-        right = send(jnp.swapaxes(whole[:, :HALO], 0, 1), lambda r, c: (r, c - 1))
-        return jnp.swapaxes(left, 0, 1), jnp.swapaxes(right, 0, 1)
-
-    mirrored = send(tile, lambda r, c: (c, r))
-    above, below = row_strips(tile)
-    left, right = column_strips(tile, above, below)
-    own = (tile, above, below, left, right)
-    other = jnp.swapaxes(mirrored, 0, 1)
-    above, below = row_strips(other)
-    left, right = column_strips(other, above, below)
-    other = (other, above, below, left, right)
+    tile = bring(activations[0])
+
+    above = send(tile[side - HALO :], lambda r, c: (r + 1, c))
+    below = send(tile[:HALO], lambda r, c: (r - 1, c))
+
+    def columns(low, high):
+        strip = jnp.concatenate([above[:, low:high], tile[:, low:high], below[:, low:high]])
+        return jnp.swapaxes(strip, 0, 1)
+
+    left = send(columns(side - HALO, side), lambda r, c: (r, c + 1))
+    right = send(columns(0, HALO), lambda r, c: (r, c - 1))
+    _, late = lax.optimization_barrier((tile, cotangent[0]))
+    late = bring(late)
 
     bias_rows = jnp.pad(conv_bias, ((0, 7), (0, channels - inner)))
     packed = jnp.concatenate(
@@ -365,61 +418,53 @@
     def ordered(x):
         return jnp.concatenate([x[k] for k in ORDER])
 
-    w_own = ordered(jnp.swapaxes(conv[0], 1, 2))
-    w_other = ordered(jnp.swapaxes(swapped[0], 1, 2))
+    w_first = ordered(jnp.swapaxes(conv[0], 1, 2))
     w_second = ordered(jnp.swapaxes(jnp.concatenate([conv[1], swapped[1]], axis=1), 1, 2))
-    v_second = ordered(diagonal(conv[1, ::-1], swapped[1, ::-1]))
-    v_first = ordered(conv[0, ::-1])
+    v_second = diagonal(conv[1], swapped[1])
+    v_first = jnp.pad(conv[0], ((0, 0), (0, inner), (0, 0)))
     p_second = jnp.concatenate([proj[1].T, proj[1].T], axis=1)
-    p_back = proj[0].T
-
-    late, _ = lax.optimization_barrier((cotangent[0], own[3]))
-    late_mirrored = send(late, lambda r, c: (c, r))
-
-    area = ((full, LEAD + up16(side + LEAD), channels), F32)
-    pairs = ((full, wide, 2 * channels), BF16)
-    last = ((full + first, wide, 2 * channels), BF16)
-    branch_own, gate_first, bottle_first, near_hidden = call(
+    p_back = jnp.pad(proj[0].T, ((0, 0), (0, inner)))
+
+    kept, gate_first, bottle_first, near_hidden = call(
         own_kernel,
         "own_branch",
         [
-            ((span, wide, channels), F32),
-            ((near, small, inner), BF16),
+            ((span + side, span, channels), BF16),
+            ((near, small, channels), BF16),
             ((side, small, inner), BF16),
             ((3, near, small, channels), BF16),
         ],
-        [area, pairs, last, ((span, wide, inner), F32)],
+        [
+            ((full, LEAD + up16(side + LEAD), channels), F32),
+            ((full, wide, 2 * channels), BF16),
+            ((full + first, wide, 2 * channels), BF16),
+            ((span, wide, inner), F32),
+        ],
         span * wide * channels * inner * 20,
-        *own,
-        *(w_own, bias[0], proj[0]),
-    )
-    gate_second, hidden_pairs, hidden_last, pre_second = call(
-        other_kernel,
-        "other_branch",
+        *(tile, above, below, jnp.swapaxes(left, 0, 1), jnp.swapaxes(right, 0, 1), late),
+        *(w_first, bias[0], proj[0]),
+    )
+    other = send(kept, lambda r, c: (c, r))
+    gate_second, hidden_pairs, hidden_last, bottle_second, grad_tile, grad_pre, strip_above, strip_below = call(
+        middle_kernel,
+        "middle",
         [
             ((near, small, channels), BF16),
             ((span, small, 2 * channels), BF16),
             ((span + second, small, 2 * channels), BF16),
-            ((side, small, 2 * inner), F32),
-        ],
-        [area, pairs, last, ((span, wide, channels), F32)],
-        span * wide * channels * inner * 30,
-        *other,
-        *(w_other, bias[0], proj[0], branch_own, w_second, jnp.tile(bias[1], (1, 2))),
-    )
-
-    grad_tile, grad_pre, strip_above, strip_below = call(
-        turn_kernel,
-        "turn",
-        [
+            ((side, small, inner), BF16),
             ((side, small, channels), BF16),
             ((side, small, 2 * inner), BF16),
             ((HALO + first, side, channels), BF16),
             ((HALO + first, side, channels), BF16),
         ],
-        [((side, small, channels), F32)],
-        2 * side * small * channels * 2 * inner,
-        *(late, late_mirrored, pre_second, p_second),
+        [
+            ((span, wide, channels), F32),
+            ((side, small, channels), F32),
+            ((side, small, 2 * inner), F32),
+        ],
+        24 * side * small * channels * 2 * inner,
+        *(kept, other, w_second, jnp.tile(bias[1], (1, 2)), p_second),
     )
 
     above = send(strip_below, lambda r, c: (r + 1, c))
@@ -430,7 +475,7 @@
         [((10 * inner, channels), F32), ((8, channels), F32)],
         [],
         20 * side * small * channels * inner,
-        *(grad_pre, hidden_pairs, hidden_last, pre_second, grad_tile),
+        *(grad_pre, hidden_pairs, hidden_last, bottle_second, grad_tile),
     )
 
     def columns(low, high, low_branch, high_branch):
@@ -446,21 +491,19 @@
 
     devices = number * number
     share = -(-10 * inner // (8 * devices)) * 8
-    parts, windows, windows_last, grad_first = call(
+    parts, windows, grad_first = call(
         backward_kernel,
         "backward",
         [
             ((2 * devices, share + 8, channels), BF16),
-            ((near, small, 2 * inner), BF16),
-            ((near + first, small, 2 * inner), BF16),
+            ((3, near, small, channels), BF16),
             ((side, side, channels), BF16),
         ],
         [
-            area,
-            ((full, small, 2 * channels), BF16),
-            ((full + second, small, 2 * channels), BF16),
+            ((full, LEAD + up16(side + HALO + first), channels), F32),
+            ((3, full, small, channels), BF16),
             ((near, small + 16, channels), F32),
-            ((near, small + 16, inner), F32),
+            ((near, small + 16, channels), F32),
             ((10 * inner, channels), F32),
             ((8, channels), F32),
         ],
@@ -470,15 +513,17 @@
         *(gate_second, gate_first, near_hidden, bottle_first, v_second, p_back, rows_second, ends_second),
     )
 
-    parts = lax.all_to_all(parts, ("segment",) + GRID, 0, 0, tiled=True)
+    parts = lax.all_to_all(parts, ALL, 0, 0, tiled=True)
     (input_gradient,) = call(
         input_kernel,
         "input",
         [((side, side, channels), BF16)],
         [],
         18 * side * small * channels * channels,
-        *(windows, windows_last, grad_first, tile, v_first),
-    )
+        *(windows, grad_first, tile, v_first),
+    )
+    parts, input_gradient = lax.optimization_barrier((parts, input_gradient))
+    input_gradient = take_back(input_gradient)
     cells = lax.axis_size("segment") * (side * number) * (side * number)
     rows, ends = call(
         functools.partial(total_kernel, float(cells) ** -0.5),
@@ -488,9 +533,17 @@
         parts.size,
         parts,
     )
-    rows = lax.all_to_all(rows, GRID, 0, 0, tiled=True).reshape(devices * share, channels).astype(F32)
-    conv_gradient = jnp.swapaxes(rows[: 9 * inner].reshape(1, 9, inner, channels), 2, 3)
-    return (input_gradient[None], conv_gradient, ends[:1, :inner], rows[None, 9 * inner : 10 * inner])
+    rows = lax.all_to_all(rows, GRID, 0, 0, tiled=True).reshape(devices * share, channels)
+    conv_gradient, bias_gradient, out_gradient = call(
+        outputs_kernel,
+        "outputs",
+        [((9 * inner, channels), F32), ((1, inner), F32), ((inner, channels), F32)],
+        [],
+        rows.size,
+        *(rows, ends),
+    )
+    conv_gradient = jnp.swapaxes(conv_gradient.reshape(1, 9, inner, channels), 2, 3)
+    return (input_gradient[None], conv_gradient, bias_gradient, out_gradient[None])
 
 
 def solution(mesh):

time: 107 us -> 102 us (0.953)
  the two profiles are of different devices: /device:TPU:0 before, /device:TPU:2 now
where the time goes in v8:
time: 102 us; the launch traced here: 101 us
  starting transfers between devices  42.4 us (42%)
  waiting for transfers between devices  33.7 us (33%)
  Pallas kernels  12.3 us (12%)
  local copies, waits for them, and re-layouts  8.37 us (8%)
  blocking collectives  2.04 us (2%)
  other arithmetic  1.38 us (1%)
  between operations  1.06 us (1%)
    ppermute x12, starting transfers between devices, permute(): return lax.ppermute(x, ALL, [found for found in pairs if found is not None])  31.8 us
    ppermute x12, waiting for transfers between devices, permute(): return lax.ppermute(x, ALL, [found for found in pairs if found is not None])  22 us
    pallas_call x7, Pallas kernels, call(): pl.pallas_call(kernel, name=name, out_shape=outs, scratch_shapes=[pltpu.V...  12.3 us
    all_to_all x1, waiting for transfers between devices, local(): parts = lax.all_to_all(parts, ALL, 0, 0, tiled=True)  11.7 us
    all_to_all x1, starting transfers between devices, local(): parts = lax.all_to_all(parts, ALL, 0, 0, tiled=True)  6 us
    unnamed x21, local copies, waits for them, and re-layouts  5.92 us
    all_to_all x1, starting transfers between devices, local(): lax.all_to_all(rows, GRID, 0, 0, tiled=True)  4.54 us
    all_gather x1, blocking collectives, local(): packed = lax.all_gather(packed, 'segment')  2.04 us
  transfers between devices with their start and end apart: 14, of which 9 were waited for; matrix products, arithmetic and copies ran while one was open for 9% of the time, Pallas kernels for 1%

profile of v8, /device:TPU:2, one launch (start us, length us, event | category | flops | bytes accessed | tf_op | source)
XLA Modules:
  0.0 101.2 jit_solution(12894096130409876241)
XLA Ops:
  0.6 2.9 %collective-permute-start = (bf16[24,24,128]{2,1,0:T(8,128)(2,1)}, bf16[24,24,128]{2,1,0:T(8,128)(2,1)S(1)}, u32[]{:S(2)}, u32[]{:S(2)}) collective-permute-start(bf16[24,24,128]{2,1,0:T(8,128)(2,1)} %bitcast.155), channel_id=1, source_target_pairs={{0,0},{1,1},{2,2},{3,3},{4,17},{5,5},{6,6},{7,7},{8,18},{9,22},{10... | collective-permute-start | bytes 442376 | tf_op jit(solution)/shard_map/ppermute | solution.py:56
  3.5 1.0 fusion.4
  4.5 2.0 %all-gather = bf16[1296,128]{1,0:T(8,128)(2,1)S(1)} all-gather(bf16[648,128]{1,0:T(8,128)(2,1)S(1)} %fusion.4), channel_id=2, replica_groups=mesh['segment'=2,'row'=4,'col'=4] {'segment'}, dimensions={0}, use_global_device_ids=true | all-gather | bytes 497664 | tf_op jit(solution)/shard_map/all_gather | solution.py:412
  6.7 0.2 copy.17.weights
  7.0 0.6 constant_dynamic-update-slice_fusion.17
  7.7 0.6 constant_dynamic-update-slice_fusion.16
  8.3 0.6 constant_dynamic-update-slice_fusion.15
  8.9 0.6 constant_dynamic-update-slice_fusion.14
  9.5 0.6 constant_dynamic-update-slice_fusion.13
  10.1 0.6 constant_dynamic-update-slice_fusion.12
  10.7 0.6 collective-permute-done.tile
  11.4 1.3 %collective-permute-start.1 = (bf16[10,24,128]{2,1,0:T(8,128)(2,1)S(1)}, bf16[10,24,128]{2,1,0:T(8,128)(2,1)S(1)}, u32[]{:S(2)}, u32[]{:S(2)}) collective-permute-start(bf16[10,24,128]{2,1,0:T(8,128)(2,1)S(1)} %get-tuple-element.66), channel_id=1, source_target_pairs={{0,17},{1,5},{2,6},{3,7},{17,18},{5,22},{6,10},{7,11},{18,19},{22,... | collective-permute-start | bytes 184328 | tf_op jit(solution)/shard_map/ppermute | solution.py:56
  12.7 1.3 %collective-permute-start.2 = (bf16[10,24,128]{2,1,0:T(8,128)(2,1)S(1)}, bf16[10,24,128]{2,1,0:T(8,128)(2,1)S(1)}, u32[]{:S(2)}, u32[]{:S(2)}) collective-permute-start(bf16[10,24,128]{2,1,0:T(8,128)(2,1)S(1)} %get-tuple-element.65), channel_id=1, source_target_pairs={{17,0},{5,1},{6,2},{7,3},{18,17},{22,5},{10,6},{11,7},{19,18},{23,... | collective-permute-start | bytes 184328 | tf_op jit(solution)/shard_map/ppermute | solution.py:56
  14.0 5.9 %collective-permute-start.5 = (bf16[24,24,128]{2,1,0:T(8,128)(2,1)S(1)}, bf16[24,24,128]{2,1,0:T(8,128)(2,1)S(1)}, u32[]{:S(2)}, u32[]{:S(2)}) collective-permute-start(bf16[24,24,128]{2,1,0:T(8,128)(2,1)S(1)} %bitcast.156), channel_id=1, source_target_pairs={{0,0},{1,1},{2,2},{3,3},{4,17},{5,5},{6,6},{7,7},{8,18},{9,22},{10... | collective-permute-start | bytes 442376 | tf_op jit(solution)/shard_map/ppermute | solution.py:56
  20.1 2.1 %collective-permute-start.4 = (bf16[10,44,128]{2,0,1:T(8,128)(2,1)S(1)}, bf16[10,44,128]{2,0,1:T(8,128)(2,1)S(1)}, u32[]{:S(2)}, u32[]{:S(2)}) collective-permute-start(bf16[10,44,128]{2,0,1:T(8,128)(2,1)S(1)} %maximum_bitcast_fusion.2), channel_id=1, source_target_pairs={{1,0},{2,1},{3,2},{5,17},{6,5},{7,6},{22,18},{10,22},{11,10},{23,1... | collective-permute-start | bytes 337928 | tf_op jit(solution)/shard_map/ppermute | solution.py:56
  22.2 4.7 %collective-permute-start.3 = (bf16[10,44,128]{2,0,1:T(8,128)(2,1)S(1)}, bf16[10,44,128]{2,0,1:T(8,128)(2,1)S(1)}, u32[]{:S(2)}, u32[]{:S(2)}) collective-permute-start(bf16[10,44,128]{2,0,1:T(8,128)(2,1)S(1)} %maximum_bitcast_fusion.1), channel_id=1, source_target_pairs={{0,1},{1,2},{2,3},{17,5},{5,6},{6,7},{18,22},{22,10},{10,11},{19,2... | collective-permute-start | bytes 337928 | tf_op jit(solution)/shard_map/ppermute | solution.py:56
  26.9 1.5 %collective-permute-done.4 = bf16[10,44,128]{2,0,1:T(8,128)(2,1)S(1)} collective-permute-done((bf16[10,44,128]{2,0,1:T(8,128)(2,1)S(1)}, bf16[10,44,128]{2,0,1:T(8,128)(2,1)S(1)}, u32[]{:S(2)}, u32[]{:S(2)}) %collective-permute-start.4) | collective-permute-done | bytes 112672 | tf_op jit(solution)/shard_map/ppermute | solution.py:56
  28.4 1.5 %collective-permute-done.3 = bf16[10,44,128]{2,0,1:T(8,128)(2,1)S(1)} collective-permute-done((bf16[10,44,128]{2,0,1:T(8,128)(2,1)S(1)}, bf16[10,44,128]{2,0,1:T(8,128)(2,1)S(1)}, u32[]{:S(2)}, u32[]{:S(2)}) %collective-permute-start.3) | collective-permute-done | bytes 112672 | tf_op jit(solution)/shard_map/ppermute | solution.py:56
  29.9 3.5 %own_branch.1 = (bf16[64,40,128]{2,1,0:T(8,128)(2,1)S(1)}, bf16[28,32,128]{2,1,0:T(8,128)(2,1)S(1)}, bf16[24,32,64]{2,1,0:T(8,128)(2,1)S(1)}, bf16[3,28,32,128]{3,2,1,0:T(8,128)(2,1)S(1)}) custom-call(bf16[24,24,128]{2,1,0:T(8,128)(2,1)S(1)} %collective-permute-done.tile, bf16[10,24,128]{2,1,0:T(8,128)(2,1)S(1)} %collective-permute-done.1.above, ...), custom_call_target="tpu_custom_call" | custom-call | flops 314572800 | bytes 2478336 | tf_op jit(solution)/shard_map/own_branch/pallas_call | solution.py:373
  33.4 1.9 %collective-permute-start.6 = (bf16[64,40,128]{2,1,0:T(8,128)(2,1)S(1)}, bf16[64,40,128]{2,1,0:T(8,128)(2,1)S(1)}, u32[]{:S(2)}, u32[]{:S(2)}) collective-permute-start(bf16[64,40,128]{2,1,0:T(8,128)(2,1)S(1)} %get-tuple-element.30.kept), channel_id=1, source_target_pairs={{0,0},{1,17},{2,18},{3,19},{17,1},{5,5},{6,22},{7,23},{18,2},{22,6... | collective-permute-start | bytes 1966088 | tf_op jit(solution)/shard_map/ppermute | solution.py:56
  35.4 0.6 constant_dynamic-update-slice_fusion.11
  36.0 0.6 constant_dynamic-update-slice_fusion.10
  36.6 0.6 constant_dynamic-update-slice_fusion.9
  37.2 1.2 %copy.21.w_second = bf16[1152,128]{1,0:T(8,128)(2,1)S(1)} copy(bf16[1152,128]{0,1:T(8,128)(2,1)} %constant_dynamic-update-slice_fusion.9) | data formatting | bytes 589824 | tf_op jit(solution)/shard_map/concatenate | solution.py:419
  38.4 0.1 copy.23
  38.5 0.1 tile.12.b_second
  38.6 0.1 copy.22
  38.7 0.1 pad_maximum_fusion.p_second
  38.8 2.0 %middle.1 = (bf16[28,32,128]{2,1,0:T(8,128)(2,1)S(1)}, bf16[40,32,256]{2,1,0:T(8,128)(2,1)S(1)}, bf16[48,32,256]{2,1,0:T(8,128)(2,1)S(1)}, bf16[24,32,64]{2,1,0:...) custom-call(bf16[64,40,128]{2,1,0:T(8,128)(2,1)S(1)} %get-tuple-elem, ...), custom_call_target="tpu_custom_call" | custom-call | flops 301989888 | bytes 3949056 | tf_op jit(solution)/shard_map/middle/pallas_call | solution.py:373
  40.9 1.8 %collective-permute-start.7 = (bf16[12,24,128]{2,1,0:T(8,128)(2,1)S(1)}, bf16[12,24,128]{2,1,0:T(8,128)(2,1)S(1)}, u32[]{:S(2)}, u32[]{:S(2)}) collective-permute-start(bf16[12,24,128]{2,1,0:T(8,128)(2,1)S(1)} %get-tuple-element.33), channel_id=1, source_target_pairs={{0,17},{1,5},{2,6},{3,7},{17,18},{5,22},{6,10},{7,11},{18,19},{22,... | collective-permute-start | bytes 221192 | tf_op jit(solution)/shard_map/ppermute | solution.py:56
  42.7 1.3 %collective-permute-start.8 = (bf16[12,24,128]{2,1,0:T(8,128)(2,1)S(1)}, bf16[12,24,128]{2,1,0:T(8,128)(2,1)S(1)}, u32[]{:S(2)}, u32[]{:S(2)}) collective-permute-start(bf16[12,24,128]{2,1,0:T(8,128)(2,1)S(1)} %get-tuple-element.34), channel_id=1, source_target_pairs={{17,0},{5,1},{6,2},{7,3},{18,17},{22,5},{10,6},{11,7},{19,18},{23,... | collective-permute-start | bytes 221192 | tf_op jit(solution)/shard_map/ppermute | solution.py:56
  44.0 0.6 collective-permute-done.7.above
  44.6 6.7 %collective-permute-done.8.below = bf16[12,24,128]{2,1,0:T(8,128)(2,1)S(1)} collective-permute-done((bf16[12,24,128]{2,1,0:T(8,128)(2,1)S(1)}, bf16[12,24,128]{2,1,0:T(8,128)(2,1)S(1)}, u32[]{:S(2)}, u32[]{:S(2)}) %collective-permute-start.8) | collective-permute-done | bytes 73760 | tf_op jit(solution)/shard_map/ppermute | solution.py:56
  51.4 2.0 %collective-permute-start.10 = (bf16[12,44,128]{2,0,1:T(8,128)(2,1)S(1)}, bf16[12,44,128]{2,0,1:T(8,128)(2,1)S(1)}, u32[]{:S(2)}, u32[]{:S(2)}) collective-permute-start(bf16[12,44,128]{2,0,1:T(8,128)(2,1)S(1)} %maximum_bitcast_fusion.4), channel_id=1, source_target_pairs={{1,0},{2,1},{3,2},{5,17},{6,5},{7,6},{22,18},{10,22},{11,10},{23,1... | collective-permute-start | bytes 405512 | tf_op jit(solution)/shard_map/ppermute | solution.py:56
  53.5 4.8 %collective-permute-start.9 = (bf16[12,44,128]{2,0,1:T(8,128)(2,1)S(1)}, bf16[12,44,128]{2,0,1:T(8,128)(2,1)S(1)}, u32[]{:S(2)}, u32[]{:S(2)}) collective-permute-start(bf16[12,44,128]{2,0,1:T(8,128)(2,1)S(1)} %maximum_bitcast_fusion.3), channel_id=1, source_target_pairs={{0,1},{1,2},{2,3},{17,5},{5,6},{6,7},{18,22},{22,10},{10,11},{19,2... | collective-permute-start | bytes 405512 | tf_op jit(solution)/shard_map/ppermute | solution.py:56
  58.4 0.5 second_sums.1
  58.9 0.9 collective-permute-done.10
  59.8 1.5 %collective-permute-done.9 = bf16[12,44,128]{2,0,1:T(8,128)(2,1)S(1)} collective-permute-done((bf16[12,44,128]{2,0,1:T(8,128)(2,1)S(1)}, bf16[12,44,128]{2,0,1:T(8,128)(2,1)S(1)}, u32[]{:S(2)}, u32[]{:S(2)}) %collective-permute-start.9) | collective-permute-done | bytes 135200 | tf_op jit(solution)/shard_map/ppermute | solution.py:56
  61.3 3.8 %backward.1 = (bf16[32,48,128]{2,1,0:T(8,128)(2,1)}, bf16[3,28,32,128]{3,2,1,0:T(8,128)(2,1)S(1)}, bf16[24,24,128]{2,1,0:T(8,128)(2,1)S(1)}) custom-call(bf16[24,32,128]{2,1,0:T(8,128)(2,1)S(1)} %get-tuple-element.31.grad_pre, bf16[24,32,128]{2,1,0:T(8,128)(2,1)S(1)} %get-tuple-element.32.grad_tile, bf16[12,24,128]{2,1,0:T(8,128)(2,1)S(1)} %collective-permute-done.7.above, ...), custom_call_target="tpu_custom_call" | custom-call | flops 528482304 | bytes 4222976 | tf_op jit(solution)/shard_map/backward/pallas_call | solution.py:373
  65.2 6.0 %all-to-all-start = ((bf16[32,48,128]{2,1,0:T(8,128)(2,1)}), bf16[32,48,128]{2,1,0:T(8,128)(2,1)S(1)}, u32[]{:S(2)}, u32[]{:S(2)}) async-start(bf16[32,48,128]{2,1,0:T(8,128)(2,1)} %get-tuple-element.44), calls=%async_computation | async-start | bytes 786432 | tf_op jit(solution)/shard_map/all_to_all | solution.py:516
  71.2 0.9 input.1
  72.2 11.7 %all-to-all-done.parts = bf16[32,48,128]{2,1,0:T(8,128)(2,1)S(1)} async-done(((bf16[32,48,128]{2,1,0:T(8,128)(2,1)}), bf16[32,48,128]{2,1,0:T(8,128)(2,1)S(1)}, u32[]{:S(2)}, u32[]{:S(2)}) %all-to-all-start) | async-done | bytes 393248 | tf_op jit(solution)/shard_map/all_to_all | solution.py:516
  83.8 0.7 total.1
  84.6 4.5 %all-to-all-start.1 = ((bf16[16,40,128]{2,1,0:T(8,128)(2,1)}), bf16[16,40,128]{2,1,0:T(8,128)(2,1)S(1)}, u32[]{:S(2)}, u32[]{:S(2)}) async-start(bf16[16,40,128]{2,1,0:T(8,128)(2,1)} %get-tuple-element.49), calls=%async_computation.1 | async-start | bytes 327680 | tf_op jit(solution)/shard_map/all_to_all | solution.py:536
  89.1 1.9 %collective-permute-start.11 = (bf16[24,24,128]{2,1,0:T(8,128)(2,1)S(1)}, bf16[24,24,128]{2,1,0:T(8,128)(2,1)S(1)}, u32[]{:S(2)}, u32[]{:S(2)}) collective-permute-start(bf16[24,24,128]{2,1,0:T(8,128)(2,1)S(1)} %input.1), channel_id=1, source_target_pairs={{0,0},{1,1},{2,2},{3,3},{17,4},{5,5},{6,6},{7,7},{18,8},{22,9},{10... | collective-permute-start | bytes 442376 | tf_op jit(solution)/shard_map/ppermute | solution.py:56
  91.0 8.8 %collective-permute-done.11 = bf16[24,24,128]{2,1,0:T(8,128)(2,1)S(1)} collective-permute-done((bf16[24,24,128]{2,1,0:T(8,128)(2,1)S(1)}, bf16[24,24,128]{2,1,0:T(8,128)(2,1)S(1)}, u32[]{:S(2)}, u32[]{:S(2)}) %collective-permute-start.11) | collective-permute-done | bytes 147488 | tf_op jit(solution)/shard_map/ppermute | solution.py:56
  99.8 0.7 outputs.1
  100.6 0.7 copy.42
  (46 shorter events, 0.8 us)
Async XLA Ops:
  0.6 10.7 %collective-permute-start = (bf16[24,24,128]{2,1,0:T(8,128)(2,1)}, bf16[24,24,128]{2,1,0:T(8,128)(2,1)S(1)}, u32[]{:S(2)}, u32[]{:S(2)}) collective-permute-start(bf16[24,24,128]{2,1,0:T(8,128)(2,1)} %bitcast.155), channel_id=1, source_target_pairs={{0,0},{1,1},{2,2},{3,3},{4,17},{5,5},{6,6},{7,7},{8,18},{9,22},{10... | collective-permute-start | bytes 442376 | tf_op jit(solution)/shard_map/ppermute | solution.py:56
  7.0 7.0 %copy-start = (bf16[1,24,24,128]{3,2,1,0:T(8,128)(2,1)S(1)}, bf16[1,24,24,128]{3,2,1,0:T(8,128)(2,1)}, u32[]{:S(2)}) copy-start(bf16[1,24,24,128]{3,2,1,0:T(8,128)(2,1)} %param.6) | copy-start | bytes 442372
  11.4 8.6 %collective-permute-start.1 = (bf16[10,24,128]{2,1,0:T(8,128)(2,1)S(1)}, bf16[10,24,128]{2,1,0:T(8,128)(2,1)S(1)}, u32[]{:S(2)}, u32[]{:S(2)}) collective-permute-start(bf16[10,24,128]{2,1,0:T(8,128)(2,1)S(1)} %get-tuple-element.66), channel_id=1, source_target_pairs={{0,17},{1,5},{2,6},{3,7},{17,18},{5,22},{6,10},{7,11},{18,19},{22,... | collective-permute-start | bytes 184328 | tf_op jit(solution)/shard_map/ppermute | solution.py:56
  12.7 7.3 %collective-permute-start.2 = (bf16[10,24,128]{2,1,0:T(8,128)(2,1)S(1)}, bf16[10,24,128]{2,1,0:T(8,128)(2,1)S(1)}, u32[]{:S(2)}, u32[]{:S(2)}) collective-permute-start(bf16[10,24,128]{2,1,0:T(8,128)(2,1)S(1)} %get-tuple-element.65), channel_id=1, source_target_pairs={{17,0},{5,1},{6,2},{7,3},{18,17},{22,5},{10,6},{11,7},{19,18},{23,... | collective-permute-start | bytes 184328 | tf_op jit(solution)/shard_map/ppermute | solution.py:56
  14.0 12.9 %collective-permute-start.5 = (bf16[24,24,128]{2,1,0:T(8,128)(2,1)S(1)}, bf16[24,24,128]{2,1,0:T(8,128)(2,1)S(1)}, u32[]{:S(2)}, u32[]{:S(2)}) collective-permute-start(bf16[24,24,128]{2,1,0:T(8,128)(2,1)S(1)} %bitcast.156), channel_id=1, source_target_pairs={{0,0},{1,1},{2,2},{3,3},{4,17},{5,5},{6,6},{7,7},{8,18},{9,22},{10... | collective-permute-start | bytes 442376 | tf_op jit(solution)/shard_map/ppermute | solution.py:56
  20.1 8.3 %collective-permute-start.4 = (bf16[10,44,128]{2,0,1:T(8,128)(2,1)S(1)}, bf16[10,44,128]{2,0,1:T(8,128)(2,1)S(1)}, u32[]{:S(2)}, u32[]{:S(2)}) collective-permute-start(bf16[10,44,128]{2,0,1:T(8,128)(2,1)S(1)} %maximum_bitcast_fusion.2), channel_id=1, source_target_pairs={{1,0},{2,1},{3,2},{5,17},{6,5},{7,6},{22,18},{10,22},{11,10},{23,1... | collective-permute-start | bytes 337928 | tf_op jit(solution)/shard_map/ppermute | solution.py:56
  22.2 7.7 %collective-permute-start.3 = (bf16[10,44,128]{2,0,1:T(8,128)(2,1)S(1)}, bf16[10,44,128]{2,0,1:T(8,128)(2,1)S(1)}, u32[]{:S(2)}, u32[]{:S(2)}) collective-permute-start(bf16[10,44,128]{2,0,1:T(8,128)(2,1)S(1)} %maximum_bitcast_fusion.1), channel_id=1, source_target_pairs={{0,1},{1,2},{2,3},{17,5},{5,6},{6,7},{18,22},{22,10},{10,11},{19,2... | collective-permute-start | bytes 337928 | tf_op jit(solution)/shard_map/ppermute | solution.py:56
  33.4 5.4 %collective-permute-start.6 = (bf16[64,40,128]{2,1,0:T(8,128)(2,1)S(1)}, bf16[64,40,128]{2,1,0:T(8,128)(2,1)S(1)}, u32[]{:S(2)}, u32[]{:S(2)}) collective-permute-start(bf16[64,40,128]{2,1,0:T(8,128)(2,1)S(1)} %get-tuple-element.30.kept), channel_id=1, source_target_pairs={{0,0},{1,17},{2,18},{3,19},{17,1},{5,5},{6,22},{7,23},{18,2},{22,6... | collective-permute-start | bytes 1966088 | tf_op jit(solution)/shard_map/ppermute | solution.py:56
  40.9 3.8 %collective-permute-start.7 = (bf16[12,24,128]{2,1,0:T(8,128)(2,1)S(1)}, bf16[12,24,128]{2,1,0:T(8,128)(2,1)S(1)}, u32[]{:S(2)}, u32[]{:S(2)}) collective-permute-start(bf16[12,24,128]{2,1,0:T(8,128)(2,1)S(1)} %get-tuple-element.33), channel_id=1, source_target_pairs={{0,17},{1,5},{2,6},{3,7},{17,18},{5,22},{6,10},{7,11},{18,19},{22,... | collective-permute-start | bytes 221192 | tf_op jit(solution)/shard_map/ppermute | solution.py:56
  42.7 8.6 %collective-permute-start.8 = (bf16[12,24,128]{2,1,0:T(8,128)(2,1)S(1)}, bf16[12,24,128]{2,1,0:T(8,128)(2,1)S(1)}, u32[]{:S(2)}, u32[]{:S(2)}) collective-permute-start(bf16[12,24,128]{2,1,0:T(8,128)(2,1)S(1)} %get-tuple-element.34), channel_id=1, source_target_pairs={{17,0},{5,1},{6,2},{7,3},{18,17},{22,5},{10,6},{11,7},{19,18},{23,... | collective-permute-start | bytes 221192 | tf_op jit(solution)/shard_map/ppermute | solution.py:56
  51.4 8.3 %collective-permute-start.10 = (bf16[12,44,128]{2,0,1:T(8,128)(2,1)S(1)}, bf16[12,44,128]{2,0,1:T(8,128)(2,1)S(1)}, u32[]{:S(2)}, u32[]{:S(2)}) collective-permute-start(bf16[12,44,128]{2,0,1:T(8,128)(2,1)S(1)} %maximum_bitcast_fusion.4), channel_id=1, source_target_pairs={{1,0},{2,1},{3,2},{5,17},{6,5},{7,6},{22,18},{10,22},{11,10},{23,1... | collective-permute-start | bytes 405512 | tf_op jit(solution)/shard_map/ppermute | solution.py:56
  53.5 7.8 %collective-permute-start.9 = (bf16[12,44,128]{2,0,1:T(8,128)(2,1)S(1)}, bf16[12,44,128]{2,0,1:T(8,128)(2,1)S(1)}, u32[]{:S(2)}, u32[]{:S(2)}) collective-permute-start(bf16[12,44,128]{2,0,1:T(8,128)(2,1)S(1)} %maximum_bitcast_fusion.3), channel_id=1, source_target_pairs={{0,1},{1,2},{2,3},{17,5},{5,6},{6,7},{18,22},{22,10},{10,11},{19,2... | collective-permute-start | bytes 405512 | tf_op jit(solution)/shard_map/ppermute | solution.py:56
  65.2 18.7 %all-to-all-start = ((bf16[32,48,128]{2,1,0:T(8,128)(2,1)}), bf16[32,48,128]{2,1,0:T(8,128)(2,1)S(1)}, u32[]{:S(2)}, u32[]{:S(2)}) async-start(bf16[32,48,128]{2,1,0:T(8,128)(2,1)} %get-tuple-element.44), calls=%async_computation | async-start | bytes 786432 | tf_op jit(solution)/shard_map/all_to_all | solution.py:516
  84.6 15.3 %all-to-all-start.1 = ((bf16[16,40,128]{2,1,0:T(8,128)(2,1)}), bf16[16,40,128]{2,1,0:T(8,128)(2,1)S(1)}, u32[]{:S(2)}, u32[]{:S(2)}) async-start(bf16[16,40,128]{2,1,0:T(8,128)(2,1)} %get-tuple-element.49), calls=%async_computation.1 | async-start | bytes 327680 | tf_op jit(solution)/shard_map/all_to_all | solution.py:536
  89.1 10.7 %collective-permute-start.11 = (bf16[24,24,128]{2,1,0:T(8,128)(2,1)S(1)}, bf16[24,24,128]{2,1,0:T(8,128)(2,1)S(1)}, u32[]{:S(2)}, u32[]{:S(2)}) collective-permute-start(bf16[24,24,128]{2,1,0:T(8,128)(2,1)S(1)} %input.1), channel_id=1, source_target_pairs={{0,0},{1,1},{2,2},{3,3},{17,4},{5,5},{6,6},{7,7},{18,8},{22,9},{10... | collective-permute-start | bytes 442376 | tf_op jit(solution)/shard_map/ppermute | solution.py:56

commit v9 on v8

--- a/solution.py
+++ b/solution.py
@@ -244,6 +244,37 @@
     ends[:, :lanes] = jnp.broadcast_to(jnp.sum(flat, axis=0, keepdims=True), (ends.shape[0], lanes))
 
 
+def weights_kernel(
+    mine, theirs, w_first, w_second, v_second, v_first, p_first, p_second, p_back, b_first, b_second, packed
+):
+    inner, channels = p_first.shape
+    section = lax.axis_index("segment")
+    packed[section] = mine[...]
+    packed[1 - section] = theirs[...]
+
+    def conv(section, k):
+        return packed[section, k * inner : (k + 1) * inner]
+
+    def turned(x):
+        return x.astype(F32).T.astype(BF16)
+
+    zero = jnp.zeros((inner, channels), BF16)
+    for at, k in enumerate(ORDER):
+        here = slice(at * channels, (at + 1) * channels)
+        own, other = conv(1, k), conv(1, 3 * (k % 3) + k // 3)
+        w_first[here] = turned(conv(0, k))
+        w_second[here] = turned(jnp.concatenate([own, other], axis=0))
+        v_second[k, :inner, :channels], v_second[k, :inner, channels:] = own, zero
+        v_second[k, inner:, :channels], v_second[k, inner:, channels:] = zero, other
+        v_first[k, :inner], v_first[k, inner:] = conv(0, k), zero
+    p_first[...] = conv(0, 9)
+    p_second[...] = turned(jnp.concatenate([conv(1, 9), conv(1, 9)], axis=0))
+    p_back[...] = turned(jnp.concatenate([conv(0, 9), zero], axis=0))
+    b_first[...] = packed[0, 10 * inner :].astype(F32)[:1, :inner]
+    bias = packed[1, 10 * inner :].astype(F32)[:1, :inner]
+    b_second[...] = jnp.concatenate([bias, bias], axis=1)
+
+
 def second_sums_kernel(grad_pre, pairs, last, bottle, grad_tile, rows, ends):
     side = grad_pre.shape[0]
     channels = grad_tile.shape[2]
@@ -380,11 +411,6 @@
     )(*operands)
 
 
-def diagonal(x, y):
-    zero = jnp.zeros_like(x)
-    return jnp.concatenate([jnp.concatenate([x, zero], axis=-1), jnp.concatenate([zero, y], axis=-1)], axis=-2)
-
-
 def local(activations, cotangent, conv_weight, conv_bias, out_weight):
     side, channels, inner = activations.shape[1], activations.shape[3], conv_weight.shape[3]
     number = lax.axis_size("row")
@@ -402,28 +428,31 @@
 
     left = send(columns(side - HALO, side), lambda r, c: (r, c + 1))
     right = send(columns(0, HALO), lambda r, c: (r, c - 1))
-    _, late = lax.optimization_barrier((tile, cotangent[0]))
-    late = bring(late)
-
-    bias_rows = jnp.pad(conv_bias, ((0, 7), (0, channels - inner)))
+    late = bring(cotangent[0])
+
+    bias_rows = jnp.pad(conv_bias, ((0, 15), (0, channels - inner)))
     packed = jnp.concatenate(
         [jnp.swapaxes(conv_weight[0], 1, 2).reshape(9 * inner, channels), out_weight[0], bias_rows]
     )
-    packed = lax.all_gather(packed, "segment")
-    conv = packed[:, : 9 * inner].reshape(2, 9, inner, channels)
-    swapped = conv.reshape(2, 3, 3, inner, channels).swapaxes(1, 2).reshape(conv.shape)
-    proj = packed[:, 9 * inner : 10 * inner]
-    bias = packed[:, 10 * inner, :inner].astype(F32)[:, None]
-
-    def ordered(x):
-        return jnp.concatenate([x[k] for k in ORDER])
-
-    w_first = ordered(jnp.swapaxes(conv[0], 1, 2))
-    w_second = ordered(jnp.swapaxes(jnp.concatenate([conv[1], swapped[1]], axis=1), 1, 2))
-    v_second = diagonal(conv[1], swapped[1])
-    v_first = jnp.pad(conv[0], ((0, 0), (0, inner), (0, 0)))
-    p_second = jnp.concatenate([proj[1].T, proj[1].T], axis=1)
-    p_back = jnp.pad(proj[0].T, ((0, 0), (0, inner)))
+    others = lax.ppermute(packed, "segment", [(0, 1), (1, 0)])
+    w_first, w_second, v_second, v_first, p_first, p_second, p_back, b_first, b_second = call(
+        weights_kernel,
+        "weights",
+        [
+            ((9 * channels, inner), BF16),
+            ((9 * channels, 2 * inner), BF16),
+            ((9, 2 * inner, 2 * channels), BF16),
+            ((9, 2 * inner, channels), BF16),
+            ((inner, channels), BF16),
+            ((channels, 2 * inner), BF16),
+            ((channels, 2 * inner), BF16),
+            ((1, inner), F32),
+            ((1, 2 * inner), F32),
+        ],
+        [((2,) + packed.shape, BF16)],
+        packed.size,
+        *(packed, others),
+    )
 
     kept, gate_first, bottle_first, near_hidden = call(
         own_kernel,
@@ -442,7 +471,7 @@
         ],
         span * wide * channels * inner * 20,
         *(tile, above, below, jnp.swapaxes(left, 0, 1), jnp.swapaxes(right, 0, 1), late),
-        *(w_first, bias[0], proj[0]),
+        *(w_first, b_first, p_first),
     )
     other = send(kept, lambda r, c: (c, r))
     gate_second, hidden_pairs, hidden_last, bottle_second, grad_tile, grad_pre, strip_above, strip_below = call(
@@ -464,7 +493,7 @@
             ((side, small, 2 * inner), F32),
         ],
         24 * side * small * channels * 2 * inner,
-        *(kept, other, w_second, jnp.tile(bias[1], (1, 2)), p_second),
+        *(kept, other, w_second, b_second, p_second),
     )
 
     above = send(strip_below, lambda r, c: (r + 1, c))
@@ -522,8 +551,7 @@
         18 * side * small * channels * channels,
         *(windows, grad_first, tile, v_first),
     )
-    parts, input_gradient = lax.optimization_barrier((parts, input_gradient))
-    input_gradient = take_back(input_gradient)
+    parts, input_gradient = lax.optimization_barrier((parts, take_back(input_gradient)))
     cells = lax.axis_size("segment") * (side * number) * (side * number)
     rows, ends = call(
         functools.partial(total_kernel, float(cells) ** -0.5),

time: 102 us -> 101 us (level)
  the two profiles are of different devices: /device:TPU:2 before, /device:TPU:0 now
where the time goes in v9:
time: 101 us
  starting transfers between devices  43.7 us (43%)
  waiting for transfers between devices  40.8 us (40%)
  Pallas kernels  12.7 us (13%)
  local copies, waits for them, and re-layouts  1.54 us (2%)
  other arithmetic  1.2 us (1%)
    ppermute x12, starting transfers between devices, permute(): return lax.ppermute(x, ALL, [found for found in pairs if found is not None])  35.6 us
    ppermute x12, waiting for transfers between devices, permute(): return lax.ppermute(x, ALL, [found for found in pairs if found is not None])  18.3 us
    all_to_all x1, waiting for transfers between devices, local(): parts = lax.all_to_all(parts, ALL, 0, 0, tiled=True)  13.2 us
    pallas_call x8, Pallas kernels, call(): pl.pallas_call(kernel, name=name, out_shape=outs, scratch_shapes=[pltpu.V...  12.7 us
    all_to_all x1, waiting for transfers between devices, local(): lax.all_to_all(rows, GRID, 0, 0, tiled=True)  9.24 us
    all_to_all x1, starting transfers between devices, local(): lax.all_to_all(rows, GRID, 0, 0, tiled=True)  4.22 us
    all_to_all x1, starting transfers between devices, local(): parts = lax.all_to_all(parts, ALL, 0, 0, tiled=True)  3.37 us
  transfers between devices with their start and end apart: 15, of which 10 were waited for; matrix products, arithmetic and copies ran while one was open for 1% of the time, Pallas kernels for 2%

profile of v9, /device:TPU:0, one launch (start us, length us, event | category | flops | bytes accessed | tf_op | source)
XLA Modules:
  0.0 100.8 jit_solution(362917097158113502)
XLA Ops:
  0.6 1.6 %collective-permute-start = (bf16[24,24,128]{2,1,0:T(8,128)(2,1)}, bf16[24,24,128]{2,1,0:T(8,128)(2,1)S(1)}, u32[]{:S(2)}, u32[]{:S(2)}) collective-permute-start(bf16[24,24,128]{2,1,0:T(8,128)(2,1)} %bitcast.39), channel_id=1, source_target_pairs={{0,0},{1,1},{2,2},{3,3},{4,17},{5,5},{6,6},{7,7},{8,18},{9,22},{10... | collective-permute-start | bytes 442376 | tf_op jit(solution)/shard_map/ppermute | solution.py:56
  2.2 1.6 %collective-permute-start.5 = (bf16[24,24,128]{2,1,0:T(8,128)(2,1)}, bf16[24,24,128]{2,1,0:T(8,128)(2,1)S(1)}, u32[]{:S(2)}, u32[]{:S(2)}) collective-permute-start(bf16[24,24,128]{2,1,0:T(8,128)(2,1)} %bitcast.40), channel_id=1, source_target_pairs={{0,0},{1,1},{2,2},{3,3},{4,17},{5,5},{6,6},{7,7},{8,18},{9,22},{10... | collective-permute-start | bytes 442376 | tf_op jit(solution)/shard_map/ppermute | solution.py:56
  3.8 0.0 copy-start
  3.8 0.7 copy-done
  4.4 0.9 fusion.1.mine
  5.4 0.5 collective-permute-start.6
  5.9 0.0 collective-permute-done.tile
  5.9 1.3 %collective-permute-start.2 = (bf16[10,24,128]{2,1,0:T(8,128)(2,1)S(1)}, bf16[10,24,128]{2,1,0:T(8,128)(2,1)S(1)}, u32[]{:S(2)}, u32[]{:S(2)}) collective-permute-start(bf16[10,24,128]{2,1,0:T(8,128)(2,1)S(1)} %get-tuple-element.76), channel_id=1, source_target_pairs={{17,0},{5,1},{6,2},{7,3},{18,17},{22,5},{10,6},{11,7},{19,18},{23,... | collective-permute-start | bytes 184328 | tf_op jit(solution)/shard_map/ppermute | solution.py:56
  7.2 8.9 %collective-permute-start.1 = (bf16[10,24,128]{2,1,0:T(8,128)(2,1)S(1)}, bf16[10,24,128]{2,1,0:T(8,128)(2,1)S(1)}, u32[]{:S(2)}, u32[]{:S(2)}) collective-permute-start(bf16[10,24,128]{2,1,0:T(8,128)(2,1)S(1)} %get-tuple-element.77), channel_id=1, source_target_pairs={{0,17},{1,5},{2,6},{3,7},{17,18},{5,22},{6,10},{7,11},{18,19},{22,... | collective-permute-start | bytes 184328 | tf_op jit(solution)/shard_map/ppermute | solution.py:56
  16.1 1.8 %collective-permute-done.1.above = bf16[10,24,128]{2,1,0:T(8,128)(2,1)S(1)} collective-permute-done((bf16[10,24,128]{2,1,0:T(8,128)(2,1)S(1)}, bf16[10,24,128]{2,1,0:T(8,128)(2,1)S(1)}, u32[]{:S(2)}, u32[]{:S(2)}) %collective-permute-start.1) | collective-permute-done | bytes 61472 | tf_op jit(solution)/shard_map/ppermute | solution.py:56
  18.0 0.3 collective-permute-done.2.below
  18.3 3.1 %collective-permute-start.3 = (bf16[10,44,128]{2,0,1:T(8,128)(2,1)S(1)}, bf16[10,44,128]{2,0,1:T(8,128)(2,1)S(1)}, u32[]{:S(2)}, u32[]{:S(2)}) collective-permute-start(bf16[10,44,128]{2,0,1:T(8,128)(2,1)S(1)} %maximum_bitcast_fusion), channel_id=1, source_target_pairs={{0,1},{1,2},{2,3},{17,5},{5,6},{6,7},{18,22},{22,10},{10,11},{19,2... | collective-permute-start | bytes 337928 | tf_op jit(solution)/shard_map/ppermute | solution.py:56
  21.4 1.3 %collective-permute-start.4 = (bf16[10,44,128]{2,0,1:T(8,128)(2,1)S(1)}, bf16[10,44,128]{2,0,1:T(8,128)(2,1)S(1)}, u32[]{:S(2)}, u32[]{:S(2)}) collective-permute-start(bf16[10,44,128]{2,0,1:T(8,128)(2,1)S(1)} %maximum_bitcast_fusion.1), channel_id=1, source_target_pairs={{1,0},{2,1},{3,2},{5,17},{6,5},{7,6},{22,18},{10,22},{11,10},{23,1... | collective-permute-start | bytes 337928 | tf_op jit(solution)/shard_map/ppermute | solution.py:56
  22.7 0.0 collective-permute-done.6.theirs
  22.7 0.4 weights.1
  23.1 0.0 collective-permute-done.5.late
  23.1 1.2 %collective-permute-done.3 = bf16[10,44,128]{2,0,1:T(8,128)(2,1)S(1)} collective-permute-done((bf16[10,44,128]{2,0,1:T(8,128)(2,1)S(1)}, bf16[10,44,128]{2,0,1:T(8,128)(2,1)S(1)}, u32[]{:S(2)}, u32[]{:S(2)}) %collective-permute-start.3) | collective-permute-done | bytes 112672 | tf_op jit(solution)/shard_map/ppermute | solution.py:56
  24.4 4.9 %collective-permute-done.4 = bf16[10,44,128]{2,0,1:T(8,128)(2,1)S(1)} collective-permute-done((bf16[10,44,128]{2,0,1:T(8,128)(2,1)S(1)}, bf16[10,44,128]{2,0,1:T(8,128)(2,1)S(1)}, u32[]{:S(2)}, u32[]{:S(2)}) %collective-permute-start.4) | collective-permute-done | bytes 112672 | tf_op jit(solution)/shard_map/ppermute | solution.py:56
  29.3 3.5 %own_branch.1 = (bf16[64,40,128]{2,1,0:T(8,128)(2,1)S(1)}, bf16[28,32,128]{2,1,0:T(8,128)(2,1)S(1)}, bf16[24,32,64]{2,1,0:T(8,128)(2,1)S(1)}, bf16[3,28,32,128]{3,2,1,0:T(8,128)(2,1)S(1)}) custom-call(bf16[24,24,128]{2,1,0:T(8,128)(2,1)S(1)} %collective-permute-done.tile, bf16[10,24,128]{2,1,0:T(8,128)(2,1)S(1)} %collective-permute-done.1.above, ...), custom_call_target="tpu_custom_call" | custom-call | flops 314572800 | bytes 2478336 | tf_op jit(solution)/shard_map/own_branch/pallas_call | solution.py:404
  32.8 0.7 collective-permute-start.7
  33.5 0.0 collective-permute-done.7.other
  33.5 2.0 %middle.1 = (bf16[28,32,128]{2,1,0:T(8,128)(2,1)S(1)}, bf16[40,32,256]{2,1,0:T(8,128)(2,1)S(1)}, bf16[48,32,256]{2,1,0:T(8,128)(2,1)S(1)}, bf16[24,32,64]{2,1,0:...) custom-call(bf16[64,40,128]{2,1,0:T(8,128)(2,1)S(1)} %get-tuple-elem, ...), custom_call_target="tpu_custom_call" | custom-call | flops 301989888 | bytes 3949056 | tf_op jit(solution)/shard_map/middle/pallas_call | solution.py:404
  35.6 8.3 %collective-permute-start.8 = (bf16[12,24,128]{2,1,0:T(8,128)(2,1)S(1)}, bf16[12,24,128]{2,1,0:T(8,128)(2,1)S(1)}, u32[]{:S(2)}, u32[]{:S(2)}) collective-permute-start(bf16[12,24,128]{2,1,0:T(8,128)(2,1)S(1)} %get-tuple-element.46), channel_id=1, source_target_pairs={{0,17},{1,5},{2,6},{3,7},{17,18},{5,22},{6,10},{7,11},{18,19},{22,... | collective-permute-start | bytes 221192 | tf_op jit(solution)/shard_map/ppermute | solution.py:56
  44.0 1.3 %collective-permute-start.9 = (bf16[12,24,128]{2,1,0:T(8,128)(2,1)S(1)}, bf16[12,24,128]{2,1,0:T(8,128)(2,1)S(1)}, u32[]{:S(2)}, u32[]{:S(2)}) collective-permute-start(bf16[12,24,128]{2,1,0:T(8,128)(2,1)S(1)} %get-tuple-element.47), channel_id=1, source_target_pairs={{17,0},{5,1},{6,2},{7,3},{18,17},{22,5},{10,6},{11,7},{19,18},{23,... | collective-permute-start | bytes 221192 | tf_op jit(solution)/shard_map/ppermute | solution.py:56
  45.3 0.6 collective-permute-done.8.above
  45.8 3.9 %collective-permute-done.9.below = bf16[12,24,128]{2,1,0:T(8,128)(2,1)S(1)} collective-permute-done((bf16[12,24,128]{2,1,0:T(8,128)(2,1)S(1)}, bf16[12,24,128]{2,1,0:T(8,128)(2,1)S(1)}, u32[]{:S(2)}, u32[]{:S(2)}) %collective-permute-start.9) | collective-permute-done | bytes 73760 | tf_op jit(solution)/shard_map/ppermute | solution.py:56
  49.8 0.1 maximum_bitcast_fusion.2
  49.9 5.7 %collective-permute-start.10 = (bf16[12,44,128]{2,0,1:T(8,128)(2,1)S(1)}, bf16[12,44,128]{2,0,1:T(8,128)(2,1)S(1)}, u32[]{:S(2)}, u32[]{:S(2)}) collective-permute-start(bf16[12,44,128]{2,0,1:T(8,128)(2,1)S(1)} %maximum_bitcast_fusion.2), channel_id=1, source_target_pairs={{0,1},{1,2},{2,3},{17,5},{5,6},{6,7},{18,22},{22,10},{10,11},{19,2... | collective-permute-start | bytes 405512 | tf_op jit(solution)/shard_map/ppermute | solution.py:56
  55.6 0.1 maximum_bitcast_fusion.3
  55.7 1.3 %collective-permute-start.11 = (bf16[12,44,128]{2,0,1:T(8,128)(2,1)S(1)}, bf16[12,44,128]{2,0,1:T(8,128)(2,1)S(1)}, u32[]{:S(2)}, u32[]{:S(2)}) collective-permute-start(bf16[12,44,128]{2,0,1:T(8,128)(2,1)S(1)} %maximum_bitcast_fusion.3), channel_id=1, source_target_pairs={{1,0},{2,1},{3,2},{5,17},{6,5},{7,6},{22,18},{10,22},{11,10},{23,1... | collective-permute-start | bytes 405512 | tf_op jit(solution)/shard_map/ppermute | solution.py:56
  57.0 0.5 second_sums.1
  57.5 1.1 %collective-permute-done.10 = bf16[12,44,128]{2,0,1:T(8,128)(2,1)S(1)} collective-permute-done((bf16[12,44,128]{2,0,1:T(8,128)(2,1)S(1)}, bf16[12,44,128]{2,0,1:T(8,128)(2,1)S(1)}, u32[]{:S(2)}, u32[]{:S(2)}) %collective-permute-start.10) | collective-permute-done | bytes 135200 | tf_op jit(solution)/shard_map/ppermute | solution.py:56
  58.6 4.5 %collective-permute-done.11 = bf16[12,44,128]{2,0,1:T(8,128)(2,1)S(1)} collective-permute-done((bf16[12,44,128]{2,0,1:T(8,128)(2,1)S(1)}, bf16[12,44,128]{2,0,1:T(8,128)(2,1)S(1)}, u32[]{:S(2)}, u32[]{:S(2)}) %collective-permute-start.11) | collective-permute-done | bytes 135200 | tf_op jit(solution)/shard_map/ppermute | solution.py:56
  63.1 3.8 %backward.1 = (bf16[32,48,128]{2,1,0:T(8,128)(2,1)}, bf16[3,28,32,128]{3,2,1,0:T(8,128)(2,1)S(1)}, bf16[24,24,128]{2,1,0:T(8,128)(2,1)S(1)}) custom-call(bf16[24,32,128]{2,1,0:T(8,128)(2,1)S(1)} %get-tuple-element.44.grad_pre, bf16[24,32,128]{2,1,0:T(8,128)(2,1)S(1)} %get-tuple-element.45.grad_tile, bf16[12,24,128]{2,1,0:T(8,128)(2,1)S(1)} %collective-permute-done.8.above, ...), custom_call_target="tpu_custom_call" | custom-call | flops 528482304 | bytes 4222976 | tf_op jit(solution)/shard_map/backward/pallas_call | solution.py:404
  67.0 3.4 %all-to-all-start = ((bf16[32,48,128]{2,1,0:T(8,128)(2,1)}), bf16[32,48,128]{2,1,0:T(8,128)(2,1)S(1)}, u32[]{:S(2)}, u32[]{:S(2)}) async-start(bf16[32,48,128]{2,1,0:T(8,128)(2,1)} %get-tuple-element.59), calls=%async_computation | async-start | bytes 786432 | tf_op jit(solution)/shard_map/all_to_all | solution.py:545
  70.4 0.9 input.1
  71.3 0.7 collective-permute-start.12
  72.0 0.0 collective-permute-done.12
  72.0 13.2 %all-to-all-done.parts = bf16[32,48,128]{2,1,0:T(8,128)(2,1)S(1)} async-done(((bf16[32,48,128]{2,1,0:T(8,128)(2,1)}), bf16[32,48,128]{2,1,0:T(8,128)(2,1)S(1)}, u32[]{:S(2)}, u32[]{:S(2)}) %all-to-all-start) | async-done | bytes 393248 | tf_op jit(solution)/shard_map/all_to_all | solution.py:545
  85.2 0.7 total.1
  86.0 4.2 %all-to-all-start.1 = ((bf16[16,40,128]{2,1,0:T(8,128)(2,1)}), bf16[16,40,128]{2,1,0:T(8,128)(2,1)S(1)}, u32[]{:S(2)}, u32[]{:S(2)}) async-start(bf16[16,40,128]{2,1,0:T(8,128)(2,1)} %get-tuple-element.65), calls=%async_computation.1 | async-start | bytes 327680 | tf_op jit(solution)/shard_map/all_to_all | solution.py:564
  90.2 9.2 %all-to-all-done.1 = bf16[16,40,128]{2,1,0:T(8,128)(2,1)S(1)} async-done(((bf16[16,40,128]{2,1,0:T(8,128)(2,1)}), bf16[16,40,128]{2,1,0:T(8,128)(2,1)S(1)}, u32[]{:S(2)}, u32[]{:S(2)}) %all-to-all-start.1) | async-done | bytes 163872 | tf_op jit(solution)/shard_map/all_to_all | solution.py:564
  99.4 0.7 outputs.1
  100.2 0.7 copy.10
  (16 shorter events, 0.3 us)
Async XLA Ops:
  0.6 5.2 %collective-permute-start = (bf16[24,24,128]{2,1,0:T(8,128)(2,1)}, bf16[24,24,128]{2,1,0:T(8,128)(2,1)S(1)}, u32[]{:S(2)}, u32[]{:S(2)}) collective-permute-start(bf16[24,24,128]{2,1,0:T(8,128)(2,1)} %bitcast.39), channel_id=1, source_target_pairs={{0,0},{1,1},{2,2},{3,3},{4,17},{5,5},{6,6},{7,7},{8,18},{9,22},{10... | collective-permute-start | bytes 442376 | tf_op jit(solution)/shard_map/ppermute | solution.py:56
  2.2 20.9 %collective-permute-start.5 = (bf16[24,24,128]{2,1,0:T(8,128)(2,1)}, bf16[24,24,128]{2,1,0:T(8,128)(2,1)S(1)}, u32[]{:S(2)}, u32[]{:S(2)}) collective-permute-start(bf16[24,24,128]{2,1,0:T(8,128)(2,1)} %bitcast.40), channel_id=1, source_target_pairs={{0,0},{1,1},{2,2},{3,3},{4,17},{5,5},{6,6},{7,7},{8,18},{9,22},{10... | collective-permute-start | bytes 442376 | tf_op jit(solution)/shard_map/ppermute | solution.py:56
  3.8 0.7 copy-start
  5.4 17.4 %collective-permute-start.6 = (bf16[656,128]{1,0:T(8,128)(2,1)S(1)}, bf16[656,128]{1,0:T(8,128)(2,1)S(1)}, u32[]{:S(2)}, u32[]{:S(2)}) collective-permute-start(bf16[656,128]{1,0:T(8,128)(2,1)S(1)} %fusion.1.mine), channel_id=1, source_target_pairs={{0,16},{16,0},{1,17},{17,1},{2,18},{18,2},{3,19},{19,3},{4,20},{20... | collective-permute-start | bytes 503816 | tf_op jit(solution)/shard_map/ppermute | solution.py:437
  5.9 12.3 %collective-permute-start.2 = (bf16[10,24,128]{2,1,0:T(8,128)(2,1)S(1)}, bf16[10,24,128]{2,1,0:T(8,128)(2,1)S(1)}, u32[]{:S(2)}, u32[]{:S(2)}) collective-permute-start(bf16[10,24,128]{2,1,0:T(8,128)(2,1)S(1)} %get-tuple-element.76), channel_id=1, source_target_pairs={{17,0},{5,1},{6,2},{7,3},{18,17},{22,5},{10,6},{11,7},{19,18},{23,... | collective-permute-start | bytes 184328 | tf_op jit(solution)/shard_map/ppermute | solution.py:56
  7.2 10.8 %collective-permute-start.1 = (bf16[10,24,128]{2,1,0:T(8,128)(2,1)S(1)}, bf16[10,24,128]{2,1,0:T(8,128)(2,1)S(1)}, u32[]{:S(2)}, u32[]{:S(2)}) collective-permute-start(bf16[10,24,128]{2,1,0:T(8,128)(2,1)S(1)} %get-tuple-element.77), channel_id=1, source_target_pairs={{0,17},{1,5},{2,6},{3,7},{17,18},{5,22},{6,10},{7,11},{18,19},{22,... | collective-permute-start | bytes 184328 | tf_op jit(solution)/shard_map/ppermute | solution.py:56
  18.3 6.1 %collective-permute-start.3 = (bf16[10,44,128]{2,0,1:T(8,128)(2,1)S(1)}, bf16[10,44,128]{2,0,1:T(8,128)(2,1)S(1)}, u32[]{:S(2)}, u32[]{:S(2)}) collective-permute-start(bf16[10,44,128]{2,0,1:T(8,128)(2,1)S(1)} %maximum_bitcast_fusion), channel_id=1, source_target_pairs={{0,1},{1,2},{2,3},{17,5},{5,6},{6,7},{18,22},{22,10},{10,11},{19,2... | collective-permute-start | bytes 337928 | tf_op jit(solution)/shard_map/ppermute | solution.py:56
  21.4 7.8 %collective-permute-start.4 = (bf16[10,44,128]{2,0,1:T(8,128)(2,1)S(1)}, bf16[10,44,128]{2,0,1:T(8,128)(2,1)S(1)}, u32[]{:S(2)}, u32[]{:S(2)}) collective-permute-start(bf16[10,44,128]{2,0,1:T(8,128)(2,1)S(1)} %maximum_bitcast_fusion.1), channel_id=1, source_target_pairs={{1,0},{2,1},{3,2},{5,17},{6,5},{7,6},{22,18},{10,22},{11,10},{23,1... | collective-permute-start | bytes 337928 | tf_op jit(solution)/shard_map/ppermute | solution.py:56
  32.8 0.7 collective-permute-start.7
  35.6 10.3 %collective-permute-start.8 = (bf16[12,24,128]{2,1,0:T(8,128)(2,1)S(1)}, bf16[12,24,128]{2,1,0:T(8,128)(2,1)S(1)}, u32[]{:S(2)}, u32[]{:S(2)}) collective-permute-start(bf16[12,24,128]{2,1,0:T(8,128)(2,1)S(1)} %get-tuple-element.46), channel_id=1, source_target_pairs={{0,17},{1,5},{2,6},{3,7},{17,18},{5,22},{6,10},{7,11},{18,19},{22,... | collective-permute-start | bytes 221192 | tf_op jit(solution)/shard_map/ppermute | solution.py:56
  44.0 5.8 %collective-permute-start.9 = (bf16[12,24,128]{2,1,0:T(8,128)(2,1)S(1)}, bf16[12,24,128]{2,1,0:T(8,128)(2,1)S(1)}, u32[]{:S(2)}, u32[]{:S(2)}) collective-permute-start(bf16[12,24,128]{2,1,0:T(8,128)(2,1)S(1)} %get-tuple-element.47), channel_id=1, source_target_pairs={{17,0},{5,1},{6,2},{7,3},{18,17},{22,5},{10,6},{11,7},{19,18},{23,... | collective-permute-start | bytes 221192 | tf_op jit(solution)/shard_map/ppermute | solution.py:56
  49.9 8.7 %collective-permute-start.10 = (bf16[12,44,128]{2,0,1:T(8,128)(2,1)S(1)}, bf16[12,44,128]{2,0,1:T(8,128)(2,1)S(1)}, u32[]{:S(2)}, u32[]{:S(2)}) collective-permute-start(bf16[12,44,128]{2,0,1:T(8,128)(2,1)S(1)} %maximum_bitcast_fusion.2), channel_id=1, source_target_pairs={{0,1},{1,2},{2,3},{17,5},{5,6},{6,7},{18,22},{22,10},{10,11},{19,2... | collective-permute-start | bytes 405512 | tf_op jit(solution)/shard_map/ppermute | solution.py:56
  55.7 7.4 %collective-permute-start.11 = (bf16[12,44,128]{2,0,1:T(8,128)(2,1)S(1)}, bf16[12,44,128]{2,0,1:T(8,128)(2,1)S(1)}, u32[]{:S(2)}, u32[]{:S(2)}) collective-permute-start(bf16[12,44,128]{2,0,1:T(8,128)(2,1)S(1)} %maximum_bitcast_fusion.3), channel_id=1, source_target_pairs={{1,0},{2,1},{3,2},{5,17},{6,5},{7,6},{22,18},{10,22},{11,10},{23,1... | collective-permute-start | bytes 405512 | tf_op jit(solution)/shard_map/ppermute | solution.py:56
  67.0 18.3 %all-to-all-start = ((bf16[32,48,128]{2,1,0:T(8,128)(2,1)}), bf16[32,48,128]{2,1,0:T(8,128)(2,1)S(1)}, u32[]{:S(2)}, u32[]{:S(2)}) async-start(bf16[32,48,128]{2,1,0:T(8,128)(2,1)} %get-tuple-element.59), calls=%async_computation | async-start | bytes 786432 | tf_op jit(solution)/shard_map/all_to_all | solution.py:545
  71.3 0.7 collective-permute-start.12
  86.0 13.5 %all-to-all-start.1 = ((bf16[16,40,128]{2,1,0:T(8,128)(2,1)}), bf16[16,40,128]{2,1,0:T(8,128)(2,1)S(1)}, u32[]{:S(2)}, u32[]{:S(2)}) async-start(bf16[16,40,128]{2,1,0:T(8,128)(2,1)} %get-tuple-element.65), calls=%async_computation.1 | async-start | bytes 327680 | tf_op jit(solution)/shard_map/all_to_all | solution.py:564

commit v10 on v9

--- a/solution.py
+++ b/solution.py
@@ -61,8 +61,14 @@
     return (batch * number + r) * number + c
 
 
-def bring(x):
-    return permute(x, lambda m, r, c: (stored(m, r, c), home(m, r, c)))
+def bring(x, down=0):
+    number = lax.axis_size("row")
+
+    def pair(batch, r, c):
+        if 0 <= r + down < number:
+            return stored(batch, r, c), home(batch, r + down, c)
+
+    return permute(x, pair)
 
 
 def take_back(x):
@@ -291,7 +297,7 @@
 def backward_kernel(
     grad_pre, grad_tile, above, below, left, right, left_branch, right_branch, gate_second, gate_first, near_hidden,
     bottle_first, v_second, p_first, rows_second, ends_second,
-    parts, windows, grad_first,
+    keep, away, windows, grad_first,
     area, shifted, branch, grads, rows, ends,
 ):
     side, channels = grad_first.shape[0], grad_first.shape[2]
@@ -343,25 +349,35 @@
         windows[b + 1] = grads[:, at : at + small].astype(BF16)
     part = branch[first : first + side, first : first + small]
     grad_first[...] = part[:, :side].astype(BF16)
-    keep = lax.broadcasted_iota(jnp.int32, part.shape, 1) < side
-    part = jnp.where(keep, part, 0).astype(BF16)
-    grad = jnp.where(keep, grads[first : first + side, first : first + small], 0)
+    real = lax.broadcasted_iota(jnp.int32, part.shape, 1) < side
+    part = jnp.where(real, part, 0).astype(BF16)
+    grad = jnp.where(real, grads[first : first + side, first : first + small], 0)
 
     def hidden(a, b):
         return near_hidden[b, first * a : first * a + side]
 
     weight_sums(rows, ends, grad, hidden, bottle_first, part)
 
-    devices, share = parts.shape[0] // 2, parts.shape[1] - 8
+    first_core = lax.axis_index("segment") == 0
     count = rows.shape[0]
-    for section, (table, end) in enumerate(((rows, ends), (rows_second, ends_second))):
-        for j in range(devices):
-            at = section * devices + j
-            low, high = min(j * share, count), min((j + 1) * share, count)
-            pieces = [table[low:high]] if low < high else []
-            if high - low < share:
-                pieces.append(jnp.zeros((share - (high - low), channels), F32))
-            parts[at] = jnp.concatenate(pieces + [end[...]]).astype(BF16)
+    for here, one, two in (
+        (slice(0, count), rows[...], rows_second[...]),
+        (slice(count, count + ends.shape[0]), ends[...], ends_second[...]),
+    ):
+        keep[here] = jnp.where(first_core, one, two)
+        away[here] = jnp.where(first_core, two, one).astype(BF16)
+
+
+def pair_kernel(keep, other, parts):
+    devices, share = parts.shape[0], parts.shape[1] - 8
+    total = keep[...] + other[...].astype(F32)
+    count = keep.shape[0] - 16
+    for j in range(devices):
+        low, high = min(j * share, count), min((j + 1) * share, count)
+        pieces = [total[low:high]] if low < high else []
+        if high - low < share:
+            pieces.append(jnp.zeros((share - (high - low), keep.shape[1]), F32))
+        parts[j] = jnp.concatenate(pieces + [total[count : count + 8]]).astype(BF16)
 
 
 def input_kernel(windows, grad_first, tile, v_first, out):
@@ -419,8 +435,8 @@
     wide, small = up16(span), up16(near)
     tile = bring(activations[0])
 
-    above = send(tile[side - HALO :], lambda r, c: (r + 1, c))
-    below = send(tile[:HALO], lambda r, c: (r - 1, c))
+    above = bring(activations[0, side - HALO :], 1)
+    below = bring(activations[0, :HALO], -1)
 
     def columns(low, high):
         strip = jnp.concatenate([above[:, low:high], tile[:, low:high], below[:, low:high]])
@@ -430,6 +446,7 @@
     right = send(columns(0, HALO), lambda r, c: (r, c - 1))
     late = bring(cotangent[0])
 
+    _, conv_bias = lax.optimization_barrier((above, conv_bias))
     bias_rows = jnp.pad(conv_bias, ((0, 15), (0, channels - inner)))
     packed = jnp.concatenate(
         [jnp.swapaxes(conv_weight[0], 1, 2).reshape(9 * inner, channels), out_weight[0], bias_rows]
@@ -501,7 +518,7 @@
     rows_second, ends_second = call(
         second_sums_kernel,
         "second_sums",
-        [((10 * inner, channels), F32), ((8, channels), F32)],
+        [((10 * inner, channels), F32), ((16, channels), F32)],
         [],
         20 * side * small * channels * inner,
         *(grad_pre, hidden_pairs, hidden_last, bottle_second, grad_tile),
@@ -520,11 +537,12 @@
 
     devices = number * number
     share = -(-10 * inner // (8 * devices)) * 8
-    parts, windows, grad_first = call(
+    keep, away, windows, grad_first = call(
         backward_kernel,
         "backward",
         [
-            ((2 * devices, share + 8, channels), BF16),
+            ((10 * inner + 16, channels), F32),
+            ((10 * inner + 16, channels), BF16),
             ((3, near, small, channels), BF16),
             ((side, side, channels), BF16),
         ],
@@ -534,7 +552,7 @@
             ((near, small + 16, channels), F32),
             ((near, small + 16, channels), F32),
             ((10 * inner, channels), F32),
-            ((8, channels), F32),
+            ((16, channels), F32),
         ],
         36 * near * small * channels * channels,
         *(grad_pre, grad_tile, above, below, left[:, :HALO], right[:, :HALO]),
@@ -542,7 +560,15 @@
         *(gate_second, gate_first, near_hidden, bottle_first, v_second, p_back, rows_second, ends_second),
     )
 
-    parts = lax.all_to_all(parts, ALL, 0, 0, tiled=True)
+    (parts,) = call(
+        pair_kernel,
+        "pair",
+        [((devices, share + 8, channels), BF16)],
+        [],
+        keep.size,
+        *(keep, lax.ppermute(away, "segment", [(0, 1), (1, 0)])),
+    )
+    parts = lax.all_to_all(parts, GRID, 0, 0, tiled=True)
     (input_gradient,) = call(
         input_kernel,
         "input",
@@ -551,7 +577,7 @@
         18 * side * small * channels * channels,
         *(windows, grad_first, tile, v_first),
     )
-    parts, input_gradient = lax.optimization_barrier((parts, take_back(input_gradient)))
+    input_gradient = take_back(input_gradient)
     cells = lax.axis_size("segment") * (side * number) * (side * number)
     rows, ends = call(
         functools.partial(total_kernel, float(cells) ** -0.5),
@@ -561,6 +587,7 @@
         parts.size,
         parts,
     )
+    rows, _ = lax.optimization_barrier((rows, input_gradient))
     rows = lax.all_to_all(rows, GRID, 0, 0, tiled=True).reshape(devices * share, channels)
     conv_gradient, bias_gradient, out_gradient = call(
         outputs_kernel,

time: 101 us -> 99.2 us (0.982)
  waiting for transfers between devices: 40.8 us -> 36.1 us
  starting transfers between devices: 43.7 us -> 46.2 us
    all_to_all x1, waiting for transfers between devices: 13.2 us -> 7.85 us  [local(): parts = lax.all_to_all(parts, GRID, 0, 0, tiled=True)]
    ppermute x0 -> x1, waiting for transfers between devices: none -> 1.39 us  [local(): lax.ppermute(away, 'segment', [(0, 1), (1, 0)])]
    ppermute x12, starting transfers between devices: 35.6 us -> 36.8 us  [permute(): return lax.ppermute(x, ALL, [found for found in pairs if found is not None])]
    pallas_call x8 -> x9, Pallas kernels: 12.7 us -> 12.6 us  [call(): pl.pallas_call(kernel, name=name, out_shape=outs, scratch_shapes=[pltpu.V...]
  transfers between devices with their start and end apart: 15 -> 16, of which waited for: 10 -> 10; matrix products, arithmetic and copies ran while one was open for 1% -> 0% of each run, Pallas kernels for 2% -> 3%
where the time goes in v10:
time: 99.2 us; the launch traced here: 98.5 us
  starting transfers between devices  46.2 us (47%)
  waiting for transfers between devices  36.1 us (36%)
  Pallas kernels  12.6 us (13%)
  local copies, waits for them, and re-layouts  2.44 us (2%)
    ppermute x12, starting transfers between devices, permute(): return lax.ppermute(x, ALL, [found for found in pairs if found is not None])  36.8 us
    ppermute x12, waiting for transfers between devices, permute(): return lax.ppermute(x, ALL, [found for found in pairs if found is not None])  17.8 us
    pallas_call x9, Pallas kernels, call(): pl.pallas_call(kernel, name=name, out_shape=outs, scratch_shapes=[pltpu.V...  12.6 us
    all_to_all x1, waiting for transfers between devices, local(): lax.all_to_all(rows, GRID, 0, 0, tiled=True)  9.04 us
    all_to_all x1, waiting for transfers between devices, local(): parts = lax.all_to_all(parts, GRID, 0, 0, tiled=True)  7.85 us
    all_to_all x1, starting transfers between devices, local(): lax.all_to_all(rows, GRID, 0, 0, tiled=True)  5.17 us
    all_to_all x1, starting transfers between devices, local(): parts = lax.all_to_all(parts, GRID, 0, 0, tiled=True)  4.03 us
  transfers between devices with their start and end apart: 16, of which 10 were waited for; matrix products, arithmetic and copies ran while one was open for 0% of the time, Pallas kernels for 3%

profile of v10, /device:TPU:0, one launch (start us, length us, event | category | flops | bytes accessed | tf_op | source)
XLA Modules:
  0.0 98.5 jit_solution(792729976869903105)
XLA Ops:
  0.6 0.0 copy-start
  0.7 0.9 slice_bitcast_fusion
  1.6 4.4 %collective-permute-start.1 = (bf16[10,24,128]{2,1,0:T(8,128)(2,1)S(1)}, bf16[10,24,128]{2,1,0:T(8,128)(2,1)S(1)}, u32[]{:S(2)}, u32[]{:S(2)}) collective-permute-start(bf16[10,24,128]{2,1,0:T(8,128)(2,1)S(1)} %get-tuple-element.79), channel_id=1, source_target_pairs={{0,17},{1,5},{2,6},{3,7},{4,18},{5,22},{6,10},{7,11},{8,19},{9,23}... | collective-permute-start | bytes 184328 | tf_op jit(solution)/shard_map/ppermute | solution.py:56
  5.9 1.3 %collective-permute-start.2 = (bf16[10,24,128]{2,1,0:T(8,128)(2,1)S(1)}, bf16[10,24,128]{2,1,0:T(8,128)(2,1)S(1)}, u32[]{:S(2)}, u32[]{:S(2)}) collective-permute-start(bf16[10,24,128]{2,1,0:T(8,128)(2,1)S(1)} %get-tuple-element.78), channel_id=1, source_target_pairs={{4,0},{5,1},{6,2},{7,3},{8,17},{9,5},{10,6},{11,7},{12,18},{13,22}... | collective-permute-start | bytes 184328 | tf_op jit(solution)/shard_map/ppermute | solution.py:56
  7.2 1.6 %collective-permute-start.5 = (bf16[24,24,128]{2,1,0:T(8,128)(2,1)}, bf16[24,24,128]{2,1,0:T(8,128)(2,1)S(1)}, u32[]{:S(2)}, u32[]{:S(2)}) collective-permute-start(bf16[24,24,128]{2,1,0:T(8,128)(2,1)} %bitcast.44), channel_id=1, source_target_pairs={{0,0},{1,1},{2,2},{3,3},{4,17},{5,5},{6,6},{7,7},{8,18},{9,22},{10... | collective-permute-start | bytes 442376 | tf_op jit(solution)/shard_map/ppermute | solution.py:56
  8.8 1.6 %collective-permute-start = (bf16[24,24,128]{2,1,0:T(8,128)(2,1)}, bf16[24,24,128]{2,1,0:T(8,128)(2,1)S(1)}, u32[]{:S(2)}, u32[]{:S(2)}) collective-permute-start(bf16[24,24,128]{2,1,0:T(8,128)(2,1)} %bitcast.41), channel_id=1, source_target_pairs={{0,0},{1,1},{2,2},{3,3},{4,17},{5,5},{6,6},{7,7},{8,18},{9,22},{10... | collective-permute-start | bytes 442376 | tf_op jit(solution)/shard_map/ppermute | solution.py:56
  10.4 0.0 collective-permute-done.1.above
  10.4 0.0 copy-done.1
  10.4 0.6 copy-done.2
  11.0 0.1 collective-permute-start.6
  11.2 1.4 %collective-permute-done.2.below = bf16[10,24,128]{2,1,0:T(8,128)(2,1)S(1)} collective-permute-done((bf16[10,24,128]{2,1,0:T(8,128)(2,1)S(1)}, bf16[10,24,128]{2,1,0:T(8,128)(2,1)S(1)}, u32[]{:S(2)}, u32[]{:S(2)}) %collective-permute-start.2) | collective-permute-done | bytes 61472 | tf_op jit(solution)/shard_map/ppermute | solution.py:56
  12.5 0.0 collective-permute-done.tile
  12.6 6.0 %collective-permute-start.3 = (bf16[10,44,128]{2,0,1:T(8,128)(2,1)S(1)}, bf16[10,44,128]{2,0,1:T(8,128)(2,1)S(1)}, u32[]{:S(2)}, u32[]{:S(2)}) collective-permute-start(bf16[10,44,128]{2,0,1:T(8,128)(2,1)S(1)} %maximum_bitcast_fusion), channel_id=1, source_target_pairs={{0,1},{1,2},{2,3},{17,5},{5,6},{6,7},{18,22},{22,10},{10,11},{19,2... | collective-permute-start | bytes 337928 | tf_op jit(solution)/shard_map/ppermute | solution.py:56
  18.6 1.3 %collective-permute-start.4 = (bf16[10,44,128]{2,0,1:T(8,128)(2,1)S(1)}, bf16[10,44,128]{2,0,1:T(8,128)(2,1)S(1)}, u32[]{:S(2)}, u32[]{:S(2)}) collective-permute-start(bf16[10,44,128]{2,0,1:T(8,128)(2,1)S(1)} %maximum_bitcast_fusion.1), channel_id=1, source_target_pairs={{1,0},{2,1},{3,2},{5,17},{6,5},{7,6},{22,18},{10,22},{11,10},{23,1... | collective-permute-start | bytes 337928 | tf_op jit(solution)/shard_map/ppermute | solution.py:56
  19.9 0.0 collective-permute-done.6.theirs
  20.0 0.4 weights.1
  20.3 0.0 collective-permute-done.5.late
  20.3 1.2 %collective-permute-done.3 = bf16[10,44,128]{2,0,1:T(8,128)(2,1)S(1)} collective-permute-done((bf16[10,44,128]{2,0,1:T(8,128)(2,1)S(1)}, bf16[10,44,128]{2,0,1:T(8,128)(2,1)S(1)}, u32[]{:S(2)}, u32[]{:S(2)}) %collective-permute-start.3) | collective-permute-done | bytes 112672 | tf_op jit(solution)/shard_map/ppermute | solution.py:56
  21.6 5.0 %collective-permute-done.4 = bf16[10,44,128]{2,0,1:T(8,128)(2,1)S(1)} collective-permute-done((bf16[10,44,128]{2,0,1:T(8,128)(2,1)S(1)}, bf16[10,44,128]{2,0,1:T(8,128)(2,1)S(1)}, u32[]{:S(2)}, u32[]{:S(2)}) %collective-permute-start.4) | collective-permute-done | bytes 112672 | tf_op jit(solution)/shard_map/ppermute | solution.py:56
  26.6 3.5 %own_branch.1 = (bf16[64,40,128]{2,1,0:T(8,128)(2,1)S(1)}, bf16[28,32,128]{2,1,0:T(8,128)(2,1)S(1)}, bf16[24,32,64]{2,1,0:T(8,128)(2,1)S(1)}, bf16[3,28,32,128]{3,2,1,0:T(8,128)(2,1)S(1)}) custom-call(bf16[24,24,128]{2,1,0:T(8,128)(2,1)S(1)} %collective-permute-done.tile, bf16[10,24,128]{2,1,0:T(8,128)(2,1)S(1)} %collective-permute-done.1.above, ...), custom_call_target="tpu_custom_call" | custom-call | flops 314572800 | bytes 2478336 | tf_op jit(solution)/shard_map/own_branch/pallas_call | solution.py:420
  30.1 0.7 collective-permute-start.7
  30.8 0.0 collective-permute-done.7.other
  30.9 2.0 %middle.1 = (bf16[28,32,128]{2,1,0:T(8,128)(2,1)S(1)}, bf16[40,32,256]{2,1,0:T(8,128)(2,1)S(1)}, bf16[48,32,256]{2,1,0:T(8,128)(2,1)S(1)}, bf16[24,32,64]{2,1,0:...) custom-call(bf16[64,40,128]{2,1,0:T(8,128)(2,1)S(1)} %get-tuple-elem, ...), custom_call_target="tpu_custom_call" | custom-call | flops 301989888 | bytes 3949056 | tf_op jit(solution)/shard_map/middle/pallas_call | solution.py:420
  32.9 12.6 %collective-permute-start.8 = (bf16[12,24,128]{2,1,0:T(8,128)(2,1)S(1)}, bf16[12,24,128]{2,1,0:T(8,128)(2,1)S(1)}, u32[]{:S(2)}, u32[]{:S(2)}) collective-permute-start(bf16[12,24,128]{2,1,0:T(8,128)(2,1)S(1)} %get-tuple-element.48), channel_id=1, source_target_pairs={{0,17},{1,5},{2,6},{3,7},{17,18},{5,22},{6,10},{7,11},{18,19},{22,... | collective-permute-start | bytes 221192 | tf_op jit(solution)/shard_map/ppermute | solution.py:56
  45.6 1.3 %collective-permute-start.9 = (bf16[12,24,128]{2,1,0:T(8,128)(2,1)S(1)}, bf16[12,24,128]{2,1,0:T(8,128)(2,1)S(1)}, u32[]{:S(2)}, u32[]{:S(2)}) collective-permute-start(bf16[12,24,128]{2,1,0:T(8,128)(2,1)S(1)} %get-tuple-element.49), channel_id=1, source_target_pairs={{17,0},{5,1},{6,2},{7,3},{18,17},{22,5},{10,6},{11,7},{19,18},{23,... | collective-permute-start | bytes 221192 | tf_op jit(solution)/shard_map/ppermute | solution.py:56
  46.9 0.6 collective-permute-done.8.above
  47.5 4.0 %collective-permute-done.9.below = bf16[12,24,128]{2,1,0:T(8,128)(2,1)S(1)} collective-permute-done((bf16[12,24,128]{2,1,0:T(8,128)(2,1)S(1)}, bf16[12,24,128]{2,1,0:T(8,128)(2,1)S(1)}, u32[]{:S(2)}, u32[]{:S(2)}) %collective-permute-start.9) | collective-permute-done | bytes 73760 | tf_op jit(solution)/shard_map/ppermute | solution.py:56
  51.6 0.1 maximum_bitcast_fusion.2
  51.6 4.2 %collective-permute-start.10 = (bf16[12,44,128]{2,0,1:T(8,128)(2,1)S(1)}, bf16[12,44,128]{2,0,1:T(8,128)(2,1)S(1)}, u32[]{:S(2)}, u32[]{:S(2)}) collective-permute-start(bf16[12,44,128]{2,0,1:T(8,128)(2,1)S(1)} %maximum_bitcast_fusion.2), channel_id=1, source_target_pairs={{0,1},{1,2},{2,3},{17,5},{5,6},{6,7},{18,22},{22,10},{10,11},{19,2... | collective-permute-start | bytes 405512 | tf_op jit(solution)/shard_map/ppermute | solution.py:56
  55.9 0.1 maximum_bitcast_fusion.3
  56.0 1.3 %collective-permute-start.11 = (bf16[12,44,128]{2,0,1:T(8,128)(2,1)S(1)}, bf16[12,44,128]{2,0,1:T(8,128)(2,1)S(1)}, u32[]{:S(2)}, u32[]{:S(2)}) collective-permute-start(bf16[12,44,128]{2,0,1:T(8,128)(2,1)S(1)} %maximum_bitcast_fusion.3), channel_id=1, source_target_pairs={{1,0},{2,1},{3,2},{5,17},{6,5},{7,6},{22,18},{10,22},{11,10},{23,1... | collective-permute-start | bytes 405512 | tf_op jit(solution)/shard_map/ppermute | solution.py:56
  57.3 0.5 second_sums.1
  57.8 1.1 %collective-permute-done.10 = bf16[12,44,128]{2,0,1:T(8,128)(2,1)S(1)} collective-permute-done((bf16[12,44,128]{2,0,1:T(8,128)(2,1)S(1)}, bf16[12,44,128]{2,0,1:T(8,128)(2,1)S(1)}, u32[]{:S(2)}, u32[]{:S(2)}) %collective-permute-start.10) | collective-permute-done | bytes 135200 | tf_op jit(solution)/shard_map/ppermute | solution.py:56
  58.9 4.5 %collective-permute-done.11 = bf16[12,44,128]{2,0,1:T(8,128)(2,1)S(1)} collective-permute-done((bf16[12,44,128]{2,0,1:T(8,128)(2,1)S(1)}, bf16[12,44,128]{2,0,1:T(8,128)(2,1)S(1)}, u32[]{:S(2)}, u32[]{:S(2)}) %collective-permute-start.11) | collective-permute-done | bytes 135200 | tf_op jit(solution)/shard_map/ppermute | solution.py:56
  63.4 3.1 %backward.1 = (f32[656,128]{1,0:T(8,128)S(1)}, bf16[656,128]{1,0:T(8,128)(2,1)S(1)}, bf16[3,28,32,128]{3,2,1,0:T(8,128)(2,1)S(1)}, bf16[24,24,128]{2,1,0:T(8,128)(2,1)S(1)}) custom-call(bf16[24,32,128]{2,1,0:T(8,128)(2,1)S(1)} %get-tuple-element.46.grad_pre, bf16[24,32,128]{2,1,0:T(8,128)(2,1)S(1)} %get-tuple-element.47.grad_tile, ...), custom_call_target="tpu_custom_call" | custom-call | flops 528482304 | bytes 4337664 | tf_op jit(solution)/shard_map/backward/pallas_call | solution.py:420
  66.5 0.1 collective-permute-start.13
  66.6 1.4 %collective-permute-done.13.other = bf16[656,128]{1,0:T(8,128)(2,1)S(1)} collective-permute-done((bf16[656,128]{1,0:T(8,128)(2,1)S(1)}, bf16[656,128]{1,0:T(8,128)(2,1)S(1)}, u32[]{:S(2)}, u32[]{:S(2)}) %collective-permute-start.13) | collective-permute-done | bytes 167968 | tf_op jit(solution)/shard_map/ppermute | solution.py:569
  68.0 0.7 pair.1
  68.7 4.0 %all-to-all-start = ((bf16[16,48,128]{2,1,0:T(8,128)(2,1)}), bf16[16,48,128]{2,1,0:T(8,128)(2,1)S(1)}, u32[]{:S(2)}, u32[]{:S(2)}) async-start(bf16[16,48,128]{2,1,0:T(8,128)(2,1)} %pair.1), calls=%async_computation | async-start | bytes 393216 | tf_op jit(solution)/shard_map/all_to_all | solution.py:571
  72.7 0.9 input.1
  73.7 0.7 collective-permute-start.12
  74.4 7.9 %all-to-all-done.parts = bf16[16,48,128]{2,1,0:T(8,128)(2,1)S(1)} async-done(((bf16[16,48,128]{2,1,0:T(8,128)(2,1)}), bf16[16,48,128]{2,1,0:T(8,128)(2,1)S(1)}, u32[]{:S(2)}, u32[]{:S(2)}) %all-to-all-start) | async-done | bytes 196640 | tf_op jit(solution)/shard_map/all_to_all | solution.py:571
  82.2 0.7 total.1
  82.9 0.0 collective-permute-done.12
  82.9 5.2 %all-to-all-start.1 = ((bf16[16,40,128]{2,1,0:T(8,128)(2,1)}), bf16[16,40,128]{2,1,0:T(8,128)(2,1)S(1)}, u32[]{:S(2)}, u32[]{:S(2)}) async-start(bf16[16,40,128]{2,1,0:T(8,128)(2,1)} %get-tuple-element.67), calls=%async_computation.1 | async-start | bytes 327680 | tf_op jit(solution)/shard_map/all_to_all | solution.py:591
  88.1 9.0 %all-to-all-done.1 = bf16[16,40,128]{2,1,0:T(8,128)(2,1)S(1)} async-done(((bf16[16,40,128]{2,1,0:T(8,128)(2,1)}), bf16[16,40,128]{2,1,0:T(8,128)(2,1)S(1)}, u32[]{:S(2)}, u32[]{:S(2)}) %all-to-all-start.1) | async-done | bytes 163872 | tf_op jit(solution)/shard_map/all_to_all | solution.py:591
  97.1 0.7 outputs.1
  97.9 0.7 copy.10
  (19 shorter events, 0.3 us)
Async XLA Ops:
  0.6 9.7 %copy-start = (bf16[1,9,128,64]{2,3,1,0:T(8,128)(2,1)S(1)}, bf16[1,9,128,64]{2,3,1,0:T(8,128)(2,1)}, u32[]{:S(2)}) copy-start(bf16[1,9,128,64]{2,3,1,0:T(8,128)(2,1)} %param.7) | copy-start | bytes 442372
  0.6 9.7 %copy-start.1 = (bf16[1,64,128]{2,1,0:T(8,128)(2,1)S(1)}, bf16[1,64,128]{2,1,0:T(8,128)(2,1)}, u32[]{:S(2)}) copy-start(bf16[1,64,128]{2,1,0:T(8,128)(2,1)} %param.9) | copy-start | bytes 49156
  1.6 8.8 %collective-permute-start.1 = (bf16[10,24,128]{2,1,0:T(8,128)(2,1)S(1)}, bf16[10,24,128]{2,1,0:T(8,128)(2,1)S(1)}, u32[]{:S(2)}, u32[]{:S(2)}) collective-permute-start(bf16[10,24,128]{2,1,0:T(8,128)(2,1)S(1)} %get-tuple-element.79), channel_id=1, source_target_pairs={{0,17},{1,5},{2,6},{3,7},{4,18},{5,22},{6,10},{7,11},{8,19},{9,23}... | collective-permute-start | bytes 184328 | tf_op jit(solution)/shard_map/ppermute | solution.py:56
  5.9 6.6 %collective-permute-start.2 = (bf16[10,24,128]{2,1,0:T(8,128)(2,1)S(1)}, bf16[10,24,128]{2,1,0:T(8,128)(2,1)S(1)}, u32[]{:S(2)}, u32[]{:S(2)}) collective-permute-start(bf16[10,24,128]{2,1,0:T(8,128)(2,1)S(1)} %get-tuple-element.78), channel_id=1, source_target_pairs={{4,0},{5,1},{6,2},{7,3},{8,17},{9,5},{10,6},{11,7},{12,18},{13,22}... | collective-permute-start | bytes 184328 | tf_op jit(solution)/shard_map/ppermute | solution.py:56
  7.2 13.1 %collective-permute-start.5 = (bf16[24,24,128]{2,1,0:T(8,128)(2,1)}, bf16[24,24,128]{2,1,0:T(8,128)(2,1)S(1)}, u32[]{:S(2)}, u32[]{:S(2)}) collective-permute-start(bf16[24,24,128]{2,1,0:T(8,128)(2,1)} %bitcast.44), channel_id=1, source_target_pairs={{0,0},{1,1},{2,2},{3,3},{4,17},{5,5},{6,6},{7,7},{8,18},{9,22},{10... | collective-permute-start | bytes 442376 | tf_op jit(solution)/shard_map/ppermute | solution.py:56
  8.8 3.7 %collective-permute-start = (bf16[24,24,128]{2,1,0:T(8,128)(2,1)}, bf16[24,24,128]{2,1,0:T(8,128)(2,1)S(1)}, u32[]{:S(2)}, u32[]{:S(2)}) collective-permute-start(bf16[24,24,128]{2,1,0:T(8,128)(2,1)} %bitcast.41), channel_id=1, source_target_pairs={{0,0},{1,1},{2,2},{3,3},{4,17},{5,5},{6,6},{7,7},{8,18},{9,22},{10... | collective-permute-start | bytes 442376 | tf_op jit(solution)/shard_map/ppermute | solution.py:56
  10.4 0.7 copy-start.2
  11.0 8.9 %collective-permute-start.6 = (bf16[656,128]{1,0:T(8,128)(2,1)S(1)}, bf16[656,128]{1,0:T(8,128)(2,1)S(1)}, u32[]{:S(2)}, u32[]{:S(2)}) collective-permute-start(bf16[656,128]{1,0:T(8,128)(2,1)S(1)} %fusion.1.mine), channel_id=1, source_target_pairs={{0,16},{16,0},{1,17},{17,1},{2,18},{18,2},{3,19},{19,3},{4,20},{20... | collective-permute-start | bytes 503816 | tf_op jit(solution)/shard_map/ppermute | solution.py:454
  12.6 8.9 %collective-permute-start.3 = (bf16[10,44,128]{2,0,1:T(8,128)(2,1)S(1)}, bf16[10,44,128]{2,0,1:T(8,128)(2,1)S(1)}, u32[]{:S(2)}, u32[]{:S(2)}) collective-permute-start(bf16[10,44,128]{2,0,1:T(8,128)(2,1)S(1)} %maximum_bitcast_fusion), channel_id=1, source_target_pairs={{0,1},{1,2},{2,3},{17,5},{5,6},{6,7},{18,22},{22,10},{10,11},{19,2... | collective-permute-start | bytes 337928 | tf_op jit(solution)/shard_map/ppermute | solution.py:56
  18.6 8.0 %collective-permute-start.4 = (bf16[10,44,128]{2,0,1:T(8,128)(2,1)S(1)}, bf16[10,44,128]{2,0,1:T(8,128)(2,1)S(1)}, u32[]{:S(2)}, u32[]{:S(2)}) collective-permute-start(bf16[10,44,128]{2,0,1:T(8,128)(2,1)S(1)} %maximum_bitcast_fusion.1), channel_id=1, source_target_pairs={{1,0},{2,1},{3,2},{5,17},{6,5},{7,6},{22,18},{10,22},{11,10},{23,1... | collective-permute-start | bytes 337928 | tf_op jit(solution)/shard_map/ppermute | solution.py:56
  30.1 0.7 collective-permute-start.7
  32.9 14.6 %collective-permute-start.8 = (bf16[12,24,128]{2,1,0:T(8,128)(2,1)S(1)}, bf16[12,24,128]{2,1,0:T(8,128)(2,1)S(1)}, u32[]{:S(2)}, u32[]{:S(2)}) collective-permute-start(bf16[12,24,128]{2,1,0:T(8,128)(2,1)S(1)} %get-tuple-element.48), channel_id=1, source_target_pairs={{0,17},{1,5},{2,6},{3,7},{17,18},{5,22},{6,10},{7,11},{18,19},{22,... | collective-permute-start | bytes 221192 | tf_op jit(solution)/shard_map/ppermute | solution.py:56
  45.6 5.9 %collective-permute-start.9 = (bf16[12,24,128]{2,1,0:T(8,128)(2,1)S(1)}, bf16[12,24,128]{2,1,0:T(8,128)(2,1)S(1)}, u32[]{:S(2)}, u32[]{:S(2)}) collective-permute-start(bf16[12,24,128]{2,1,0:T(8,128)(2,1)S(1)} %get-tuple-element.49), channel_id=1, source_target_pairs={{17,0},{5,1},{6,2},{7,3},{18,17},{22,5},{10,6},{11,7},{19,18},{23,... | collective-permute-start | bytes 221192 | tf_op jit(solution)/shard_map/ppermute | solution.py:56
  51.6 7.2 %collective-permute-start.10 = (bf16[12,44,128]{2,0,1:T(8,128)(2,1)S(1)}, bf16[12,44,128]{2,0,1:T(8,128)(2,1)S(1)}, u32[]{:S(2)}, u32[]{:S(2)}) collective-permute-start(bf16[12,44,128]{2,0,1:T(8,128)(2,1)S(1)} %maximum_bitcast_fusion.2), channel_id=1, source_target_pairs={{0,1},{1,2},{2,3},{17,5},{5,6},{6,7},{18,22},{22,10},{10,11},{19,2... | collective-permute-start | bytes 405512 | tf_op jit(solution)/shard_map/ppermute | solution.py:56
  56.0 7.4 %collective-permute-start.11 = (bf16[12,44,128]{2,0,1:T(8,128)(2,1)S(1)}, bf16[12,44,128]{2,0,1:T(8,128)(2,1)S(1)}, u32[]{:S(2)}, u32[]{:S(2)}) collective-permute-start(bf16[12,44,128]{2,0,1:T(8,128)(2,1)S(1)} %maximum_bitcast_fusion.3), channel_id=1, source_target_pairs={{1,0},{2,1},{3,2},{5,17},{6,5},{7,6},{22,18},{10,22},{11,10},{23,1... | collective-permute-start | bytes 405512 | tf_op jit(solution)/shard_map/ppermute | solution.py:56
  66.5 1.5 %collective-permute-start.13 = (bf16[656,128]{1,0:T(8,128)(2,1)S(1)}, bf16[656,128]{1,0:T(8,128)(2,1)S(1)}, u32[]{:S(2)}, u32[]{:S(2)}) collective-permute-start(bf16[656,128]{1,0:T(8,128)(2,1)S(1)} %get-tuple-element.65), channel_id=1, source_target_pairs={{0,16},{16,0},{1,17},{17,1},{2,18},{18,2},{3,19},{19,3},{4,20},{20... | collective-permute-start | bytes 503816 | tf_op jit(solution)/shard_map/ppermute | solution.py:569
  68.7 13.5 %all-to-all-start = ((bf16[16,48,128]{2,1,0:T(8,128)(2,1)}), bf16[16,48,128]{2,1,0:T(8,128)(2,1)S(1)}, u32[]{:S(2)}, u32[]{:S(2)}) async-start(bf16[16,48,128]{2,1,0:T(8,128)(2,1)} %pair.1), calls=%async_computation | async-start | bytes 393216 | tf_op jit(solution)/shard_map/all_to_all | solution.py:571
  73.7 9.2 %collective-permute-start.12 = (bf16[24,24,128]{2,1,0:T(8,128)(2,1)S(1)}, bf16[24,24,128]{2,1,0:T(8,128)(2,1)S(1)}, u32[]{:S(2)}, u32[]{:S(2)}) collective-permute-start(bf16[24,24,128]{2,1,0:T(8,128)(2,1)S(1)} %input.1), channel_id=1, source_target_pairs={{0,0},{1,1},{2,2},{3,3},{17,4},{5,5},{6,6},{7,7},{18,8},{22,9},{10... | collective-permute-start | bytes 442376 | tf_op jit(solution)/shard_map/ppermute | solution.py:56
  82.9 14.2 %all-to-all-start.1 = ((bf16[16,40,128]{2,1,0:T(8,128)(2,1)}), bf16[16,40,128]{2,1,0:T(8,128)(2,1)S(1)}, u32[]{:S(2)}, u32[]{:S(2)}) async-start(bf16[16,40,128]{2,1,0:T(8,128)(2,1)} %get-tuple-element.67), calls=%async_computation.1 | async-start | bytes 327680 | tf_op jit(solution)/shard_map/all_to_all | solution.py:591

commit v11 on v10

--- a/solution.py
+++ b/solution.py
@@ -165,21 +165,21 @@
 
 
 def own_kernel(
-    tile, above, below, left, right, late, weights, bias, proj,
+    brought, above, below, left, right, weights, bias, proj,
     swapped, gate_first, bottle_first, near_hidden,
     area, pairs, last, pre,
 ):
-    side, first, second, inner = tile.shape[0], FIRST_DILATION, SECOND_DILATION, bias.shape[1]
+    side, first, second, inner = brought.shape[1], FIRST_DILATION, SECOND_DILATION, bias.shape[1]
     near, small = gate_first.shape[:2]
     span = side + 2 * second
-    assemble(area, tile[...].astype(F32), above, below, left, right)
+    assemble(area, brought[:side].astype(F32), above, below, left, right)
 
     def store(top, pre_act, branch):
         pre[pl.ds(top, 8)] = pre_act
         swapped[pl.ds(top, 8)] = branch[:, :span].astype(BF16)
 
     first_branch(area, pairs, last, weights, bias, proj, store)
-    swapped[span:, :side] = late[...]
+    swapped[span:, :side] = brought[side:]
     for b in (-1, 0, 1):
         at = LEAD + first * b
         near_hidden[b + 1] = positive(area[HALO - first : HALO + side + first, at : at + small]).astype(BF16)
@@ -380,8 +380,8 @@
         parts[j] = jnp.concatenate(pieces + [total[count : count + 8]]).astype(BF16)
 
 
-def input_kernel(windows, grad_first, tile, v_first, out):
-    side, channels = tile.shape[0], tile.shape[2]
+def input_kernel(windows, grad_first, brought, v_first, out):
+    side, channels = out.shape[0], out.shape[2]
     small = windows.shape[2]
     first = FIRST_DILATION
 
@@ -393,7 +393,7 @@
             total = total + dot(window, v_first[tap(a, b)])
         here = pl.ds(top, 8)
         total = total.reshape(8, small, channels)[:, :side]
-        total = jnp.where(tile[here].astype(F32) > 0, total, 0)
+        total = jnp.where(brought[here].astype(F32) > 0, total, 0)
         out[here] = (grad_first[here].astype(F32) + total).astype(BF16)
         return 0
 
@@ -433,20 +433,21 @@
     first, second = FIRST_DILATION, SECOND_DILATION
     full, span, near = side + 2 * HALO, side + 2 * second, side + 2 * first
     wide, small = up16(span), up16(near)
-    tile = bring(activations[0])
-
+
+    brought = bring(jnp.concatenate([activations[0], cotangent[0]]))
+    tile = brought[:side]
     above = bring(activations[0, side - HALO :], 1)
     below = bring(activations[0, :HALO], -1)
 
     def columns(low, high):
-        strip = jnp.concatenate([above[:, low:high], tile[:, low:high], below[:, low:high]])
-        return jnp.swapaxes(strip, 0, 1)
+        strip = jnp.pad(jnp.swapaxes(tile[:, low:high], 0, 1), ((0, 0), (HALO, HALO), (0, 0)))
+        strip = lax.optimization_barrier(strip)
+        strip = lax.dynamic_update_slice(strip, jnp.swapaxes(above[:, low:high], 0, 1), (0, 0, 0))
+        return lax.dynamic_update_slice(strip, jnp.swapaxes(below[:, low:high], 0, 1), (0, HALO + side, 0))
 
     left = send(columns(side - HALO, side), lambda r, c: (r, c + 1))
     right = send(columns(0, HALO), lambda r, c: (r, c - 1))
-    late = bring(cotangent[0])
-
-    _, conv_bias = lax.optimization_barrier((above, conv_bias))
+
     bias_rows = jnp.pad(conv_bias, ((0, 15), (0, channels - inner)))
     packed = jnp.concatenate(
         [jnp.swapaxes(conv_weight[0], 1, 2).reshape(9 * inner, channels), out_weight[0], bias_rows]
@@ -487,7 +488,7 @@
             ((span, wide, inner), F32),
         ],
         span * wide * channels * inner * 20,
-        *(tile, above, below, jnp.swapaxes(left, 0, 1), jnp.swapaxes(right, 0, 1), late),
+        *(brought, above, below, jnp.swapaxes(left, 0, 1), jnp.swapaxes(right, 0, 1)),
         *(w_first, b_first, p_first),
     )
     other = send(kept, lambda r, c: (c, r))
@@ -560,23 +561,25 @@
         *(gate_second, gate_first, near_hidden, bottle_first, v_second, p_back, rows_second, ends_second),
     )
 
+    (input_gradient,) = call(
+        input_kernel,
+        "input",
+        [((side, side, channels), BF16)],
+        [],
+        18 * side * small * channels * channels,
+        *(windows, grad_first, brought, v_first),
+    )
+    other = lax.ppermute(away, "segment", [(0, 1), (1, 0)])
+    other, input_gradient = lax.optimization_barrier((other, input_gradient))
     (parts,) = call(
         pair_kernel,
         "pair",
         [((devices, share + 8, channels), BF16)],
         [],
         keep.size,
-        *(keep, lax.ppermute(away, "segment", [(0, 1), (1, 0)])),
+        *(keep, other),
     )
     parts = lax.all_to_all(parts, GRID, 0, 0, tiled=True)
-    (input_gradient,) = call(
-        input_kernel,
-        "input",
-        [((side, side, channels), BF16)],
-        [],
-        18 * side * small * channels * channels,
-        *(windows, grad_first, tile, v_first),
-    )
     input_gradient = take_back(input_gradient)
     cells = lax.axis_size("segment") * (side * number) * (side * number)
     rows, ends = call(

time: 99.2 us -> 96.9 us (0.977)
  waiting for transfers between devices: 36.1 us -> 31.5 us
  starting transfers between devices: 46.2 us -> 48 us
    all_to_all x1, starting transfers between devices: 4.03 us -> 8.22 us  [local(): parts = lax.all_to_all(parts, GRID, 0, 0, tiled=True)]
    ppermute x12 -> x11, waiting for transfers between devices: 17.8 us -> 13.8 us  [permute(): return lax.ppermute(x, ALL, [found for found in pairs if found is not None])]
    ppermute x12 -> x11, starting transfers between devices: 36.8 us -> 34.4 us  [permute(): return lax.ppermute(x, ALL, [found for found in pairs if found is not None])]
    ppermute x1, waiting for transfers between devices: 1.39 us -> 0.1 us  [local(): other = lax.ppermute(away, 'segment', [(0, 1), (1, 0)])]
    concatenate x0 -> x1, other arithmetic: none -> 1.05 us  [local(): brought = bring(jnp.concatenate([activations[0], cotangent[0]]))]
  transfers between devices with their start and end apart: 16 -> 15, of which waited for: 10 -> 10; matrix products, arithmetic and copies ran while one was open for 0% -> 0% of each run, Pallas kernels for 3% -> 3%
where the time goes in v11:
time: 96.9 us; the launch traced here: 95.9 us
  starting transfers between devices  48 us (50%)
  waiting for transfers between devices  31.5 us (33%)
  Pallas kernels  12.6 us (13%)
  local copies, waits for them, and re-layouts  1.61 us (2%)
  other arithmetic  1.24 us (1%)
  between operations  0.97 us (1%)
    ppermute x11, starting transfers between devices, permute(): return lax.ppermute(x, ALL, [found for found in pairs if found is not None])  34.4 us
    ppermute x11, waiting for transfers between devices, permute(): return lax.ppermute(x, ALL, [found for found in pairs if found is not None])  13.8 us
    pallas_call x9, Pallas kernels, call(): pl.pallas_call(kernel, name=name, out_shape=outs, scratch_shapes=[pltpu.V...  12.6 us
    all_to_all x1, waiting for transfers between devices, local(): lax.all_to_all(rows, GRID, 0, 0, tiled=True)  8.81 us
    all_to_all x1, waiting for transfers between devices, local(): parts = lax.all_to_all(parts, GRID, 0, 0, tiled=True)  8.8 us
    all_to_all x1, starting transfers between devices, local(): parts = lax.all_to_all(parts, GRID, 0, 0, tiled=True)  8.22 us
    all_to_all x1, starting transfers between devices, local(): lax.all_to_all(rows, GRID, 0, 0, tiled=True)  4.45 us
  transfers between devices with their start and end apart: 15, of which 10 were waited for; matrix products, arithmetic and copies ran while one was open for 0% of the time, Pallas kernels for 3%

profile of v11, /device:TPU:0, one launch (start us, length us, event | category | flops | bytes accessed | tf_op | source)
XLA Modules:
  0.0 95.9 jit_solution(12379490281254332861)
XLA Ops:
  0.6 0.0 copy-start
  0.6 1.0 %pad_maximum_fusion = bf16[48,24,128]{2,1,0:T(8,128)(2,1)S(1)} fusion(bf16[24,24,128]{2,1,0:T(8,128)(2,1)} %bitcast.58, bf16[24,24,128]{2,1,0:T(8,128)(2,1)} %bitcast.55), kind=kLoop, calls=%fused_computation.2 | loop fusion | flops 147456 | bytes 589824 | tf_op jit(solution)/shard_map/concatenate | solution.py:437
  1.7 0.0 copy-start.1
  1.7 0.8 collective-permute-start
  2.5 0.0 copy-start.2
  2.6 1.3 %collective-permute-start.2 = (bf16[10,24,128]{2,1,0:T(8,128)(2,1)S(1)}, bf16[10,24,128]{2,1,0:T(8,128)(2,1)S(1)}, u32[]{:S(2)}, u32[]{:S(2)}) collective-permute-start(bf16[10,24,128]{2,1,0:T(8,128)(2,1)S(1)} %get-tuple-element.80), channel_id=1, source_target_pairs={{4,0},{5,1},{6,2},{7,3},{8,17},{9,5},{10,6},{11,7},{12,18},{13,22}... | collective-permute-start | bytes 184328 | tf_op jit(solution)/shard_map/ppermute | solution.py:56
  3.9 7.3 %collective-permute-start.1 = (bf16[10,24,128]{2,1,0:T(8,128)(2,1)S(1)}, bf16[10,24,128]{2,1,0:T(8,128)(2,1)S(1)}, u32[]{:S(2)}, u32[]{:S(2)}) collective-permute-start(bf16[10,24,128]{2,1,0:T(8,128)(2,1)S(1)} %get-tuple-element.81), channel_id=1, source_target_pairs={{0,17},{1,5},{2,6},{3,7},{4,18},{5,22},{6,10},{7,11},{8,19},{9,23}... | collective-permute-start | bytes 184328 | tf_op jit(solution)/shard_map/ppermute | solution.py:56
  11.1 0.0 copy-start.3
  11.2 0.6 copy-done.3
  11.8 0.1 collective-permute-start.5
  11.9 0.0 collective-permute-done.brought
  12.0 1.0 %collective-permute-done.1.above = bf16[10,24,128]{2,1,0:T(8,128)(2,1)S(1)} collective-permute-done((bf16[10,24,128]{2,1,0:T(8,128)(2,1)S(1)}, bf16[10,24,128]{2,1,0:T(8,128)(2,1)S(1)}, u32[]{:S(2)}, u32[]{:S(2)}) %collective-permute-start.1) | collective-permute-done | bytes 61472 | tf_op jit(solution)/shard_map/ppermute | solution.py:56
  13.0 0.0 collective-permute-done.2.below
  13.0 1.3 %collective-permute-start.4 = (bf16[10,44,128]{2,0,1:T(8,128)(2,1)S(1)}, bf16[10,44,128]{2,0,1:T(8,128)(2,1)S(1)}, u32[]{:S(2)}, u32[]{:S(2)}) collective-permute-start(bf16[10,44,128]{2,0,1:T(8,128)(2,1)S(1)} %get-tuple-element.90), channel_id=1, source_target_pairs={{1,0},{2,1},{3,2},{5,17},{6,5},{7,6},{22,18},{10,22},{11,10},{23,1... | collective-permute-start | bytes 337928 | tf_op jit(solution)/shard_map/ppermute | solution.py:56
  14.3 7.2 %collective-permute-start.3 = (bf16[10,44,128]{2,0,1:T(8,128)(2,1)S(1)}, bf16[10,44,128]{2,0,1:T(8,128)(2,1)S(1)}, u32[]{:S(2)}, u32[]{:S(2)}) collective-permute-start(bf16[10,44,128]{2,0,1:T(8,128)(2,1)S(1)} %get-tuple-element.91), channel_id=1, source_target_pairs={{0,1},{1,2},{2,3},{17,5},{5,6},{6,7},{18,22},{22,10},{10,11},{19,2... | collective-permute-start | bytes 337928 | tf_op jit(solution)/shard_map/ppermute | solution.py:56
  21.5 0.0 collective-permute-done.5.theirs
  21.5 0.4 weights.1
  21.9 1.1 %collective-permute-done.4 = bf16[10,44,128]{2,0,1:T(8,128)(2,1)S(1)} collective-permute-done((bf16[10,44,128]{2,0,1:T(8,128)(2,1)S(1)}, bf16[10,44,128]{2,0,1:T(8,128)(2,1)S(1)}, u32[]{:S(2)}, u32[]{:S(2)}) %collective-permute-start.4) | collective-permute-done | bytes 112672 | tf_op jit(solution)/shard_map/ppermute | solution.py:56
  23.1 1.5 %collective-permute-done.3 = bf16[10,44,128]{2,0,1:T(8,128)(2,1)S(1)} collective-permute-done((bf16[10,44,128]{2,0,1:T(8,128)(2,1)S(1)}, bf16[10,44,128]{2,0,1:T(8,128)(2,1)S(1)}, u32[]{:S(2)}, u32[]{:S(2)}) %collective-permute-start.3) | collective-permute-done | bytes 112672 | tf_op jit(solution)/shard_map/ppermute | solution.py:56
  24.5 3.5 %own_branch.1 = (bf16[64,40,128]{2,1,0:T(8,128)(2,1)S(1)}, bf16[28,32,128]{2,1,0:T(8,128)(2,1)S(1)}, bf16[24,32,64]{2,1,0:T(8,128)(2,1)S(1)}, bf16[3,28,32,128]{3,2,1,0:T(8,128)(2,1)S(1)}) custom-call(bf16[48,24,128]{2,1,0:T(8,128)(2,1)S(1)} %collective-permute-done.brought, bf16[10,24,128]{2,1,0:T(8,128)(2,1)S(1)} %collective-permute-done.1.above, ...), custom_call_target="tpu_custom_call" | custom-call | flops 314572800 | bytes 2478336 | tf_op jit(solution)/shard_map/own_branch/pallas_call | solution.py:420
  28.1 0.7 collective-permute-start.6
  28.8 0.0 collective-permute-done.6.other
  28.8 2.0 %middle.1 = (bf16[28,32,128]{2,1,0:T(8,128)(2,1)S(1)}, bf16[40,32,256]{2,1,0:T(8,128)(2,1)S(1)}, bf16[48,32,256]{2,1,0:T(8,128)(2,1)S(1)}, bf16[24,32,64]{2,1,0:...) custom-call(bf16[64,40,128]{2,1,0:T(8,128)(2,1)S(1)} %get-tuple-elem, ...), custom_call_target="tpu_custom_call" | custom-call | flops 301989888 | bytes 3949056 | tf_op jit(solution)/shard_map/middle/pallas_call | solution.py:420
  30.8 7.4 %collective-permute-start.7 = (bf16[12,24,128]{2,1,0:T(8,128)(2,1)S(1)}, bf16[12,24,128]{2,1,0:T(8,128)(2,1)S(1)}, u32[]{:S(2)}, u32[]{:S(2)}) collective-permute-start(bf16[12,24,128]{2,1,0:T(8,128)(2,1)S(1)} %get-tuple-element.48), channel_id=1, source_target_pairs={{0,17},{1,5},{2,6},{3,7},{17,18},{5,22},{6,10},{7,11},{18,19},{22,... | collective-permute-start | bytes 221192 | tf_op jit(solution)/shard_map/ppermute | solution.py:56
  38.3 1.3 %collective-permute-start.8 = (bf16[12,24,128]{2,1,0:T(8,128)(2,1)S(1)}, bf16[12,24,128]{2,1,0:T(8,128)(2,1)S(1)}, u32[]{:S(2)}, u32[]{:S(2)}) collective-permute-start(bf16[12,24,128]{2,1,0:T(8,128)(2,1)S(1)} %get-tuple-element.49), channel_id=1, source_target_pairs={{17,0},{5,1},{6,2},{7,3},{18,17},{22,5},{10,6},{11,7},{19,18},{23,... | collective-permute-start | bytes 221192 | tf_op jit(solution)/shard_map/ppermute | solution.py:56
  39.6 0.6 collective-permute-done.7.above
  40.2 3.8 %collective-permute-done.8.below = bf16[12,24,128]{2,1,0:T(8,128)(2,1)S(1)} collective-permute-done((bf16[12,24,128]{2,1,0:T(8,128)(2,1)S(1)}, bf16[12,24,128]{2,1,0:T(8,128)(2,1)S(1)}, u32[]{:S(2)}, u32[]{:S(2)}) %collective-permute-start.8) | collective-permute-done | bytes 73760 | tf_op jit(solution)/shard_map/ppermute | solution.py:56
  44.1 0.1 maximum_bitcast_fusion
  44.1 5.2 %collective-permute-start.9 = (bf16[12,44,128]{2,0,1:T(8,128)(2,1)S(1)}, bf16[12,44,128]{2,0,1:T(8,128)(2,1)S(1)}, u32[]{:S(2)}, u32[]{:S(2)}) collective-permute-start(bf16[12,44,128]{2,0,1:T(8,128)(2,1)S(1)} %maximum_bitcast_fusion), channel_id=1, source_target_pairs={{0,1},{1,2},{2,3},{17,5},{5,6},{6,7},{18,22},{22,10},{10,11},{19,2... | collective-permute-start | bytes 405512 | tf_op jit(solution)/shard_map/ppermute | solution.py:56
  49.4 0.1 maximum_bitcast_fusion.1
  49.5 1.3 %collective-permute-start.10 = (bf16[12,44,128]{2,0,1:T(8,128)(2,1)S(1)}, bf16[12,44,128]{2,0,1:T(8,128)(2,1)S(1)}, u32[]{:S(2)}, u32[]{:S(2)}) collective-permute-start(bf16[12,44,128]{2,0,1:T(8,128)(2,1)S(1)} %maximum_bitcast_fusion.1), channel_id=1, source_target_pairs={{1,0},{2,1},{3,2},{5,17},{6,5},{7,6},{22,18},{10,22},{11,10},{23,1... | collective-permute-start | bytes 405512 | tf_op jit(solution)/shard_map/ppermute | solution.py:56
  50.8 0.5 second_sums.1
  51.3 1.1 %collective-permute-done.9 = bf16[12,44,128]{2,0,1:T(8,128)(2,1)S(1)} collective-permute-done((bf16[12,44,128]{2,0,1:T(8,128)(2,1)S(1)}, bf16[12,44,128]{2,0,1:T(8,128)(2,1)S(1)}, u32[]{:S(2)}, u32[]{:S(2)}) %collective-permute-start.9) | collective-permute-done | bytes 135200 | tf_op jit(solution)/shard_map/ppermute | solution.py:56
  52.4 4.7 %collective-permute-done.10 = bf16[12,44,128]{2,0,1:T(8,128)(2,1)S(1)} collective-permute-done((bf16[12,44,128]{2,0,1:T(8,128)(2,1)S(1)}, bf16[12,44,128]{2,0,1:T(8,128)(2,1)S(1)}, u32[]{:S(2)}, u32[]{:S(2)}) %collective-permute-start.10) | collective-permute-done | bytes 135200 | tf_op jit(solution)/shard_map/ppermute | solution.py:56
  57.1 3.1 %backward.1 = (f32[656,128]{1,0:T(8,128)S(1)}, bf16[656,128]{1,0:T(8,128)(2,1)S(1)}, bf16[3,28,32,128]{3,2,1,0:T(8,128)(2,1)S(1)}, bf16[24,24,128]{2,1,0:T(8,128)(2,1)S(1)}) custom-call(bf16[24,32,128]{2,1,0:T(8,128)(2,1)S(1)} %get-tuple-element.46.grad_pre, bf16[24,32,128]{2,1,0:T(8,128)(2,1)S(1)} %get-tuple-element.47.grad_tile, ...), custom_call_target="tpu_custom_call" | custom-call | flops 528482304 | bytes 4337664 | tf_op jit(solution)/shard_map/backward/pallas_call | solution.py:420
  60.2 0.9 collective-permute-start.11
  61.1 0.9 input.1
  62.0 0.1 collective-permute-done.11.other
  62.1 0.7 pair.1
  62.9 8.2 %all-to-all-start = ((bf16[16,48,128]{2,1,0:T(8,128)(2,1)}), bf16[16,48,128]{2,1,0:T(8,128)(2,1)S(1)}, u32[]{:S(2)}, u32[]{:S(2)}) async-start(bf16[16,48,128]{2,1,0:T(8,128)(2,1)} %pair.1), calls=%async_computation | async-start | bytes 393216 | tf_op jit(solution)/shard_map/all_to_all | solution.py:582
  71.1 0.7 collective-permute-start.12
  71.8 8.8 %all-to-all-done.parts = bf16[16,48,128]{2,1,0:T(8,128)(2,1)S(1)} async-done(((bf16[16,48,128]{2,1,0:T(8,128)(2,1)}), bf16[16,48,128]{2,1,0:T(8,128)(2,1)S(1)}, u32[]{:S(2)}, u32[]{:S(2)}) %all-to-all-start) | async-done | bytes 196640 | tf_op jit(solution)/shard_map/all_to_all | solution.py:582
  80.6 0.7 total.1
  81.3 0.0 collective-permute-done.12
  81.3 4.4 %all-to-all-start.1 = ((bf16[16,40,128]{2,1,0:T(8,128)(2,1)}), bf16[16,40,128]{2,1,0:T(8,128)(2,1)S(1)}, u32[]{:S(2)}, u32[]{:S(2)}) async-start(bf16[16,40,128]{2,1,0:T(8,128)(2,1)} %get-tuple-element.69), calls=%async_computation.1 | async-start | bytes 327680 | tf_op jit(solution)/shard_map/all_to_all | solution.py:594
  85.7 8.8 %all-to-all-done.1 = bf16[16,40,128]{2,1,0:T(8,128)(2,1)S(1)} async-done(((bf16[16,40,128]{2,1,0:T(8,128)(2,1)}), bf16[16,40,128]{2,1,0:T(8,128)(2,1)S(1)}, u32[]{:S(2)}, u32[]{:S(2)}) %all-to-all-start.1) | async-done | bytes 163872 | tf_op jit(solution)/shard_map/all_to_all | solution.py:594
  94.5 0.7 outputs.1
  95.3 0.7 copy.14
  (20 shorter events, 0.4 us)
Async XLA Ops:
  0.6 1.9 %copy-start = (bf16[1,24,24,128]{3,2,1,0:T(8,128)(2,1)S(1)}, bf16[1,24,24,128]{3,2,1,0:T(8,128)(2,1)}, u32[]{:S(2)}) copy-start(bf16[1,24,24,128]{3,2,1,0:T(8,128)(2,1)} %param.5) | copy-start | bytes 442372
  1.7 9.5 %copy-start.1 = (bf16[1,9,128,64]{2,3,1,0:T(8,128)(2,1)S(1)}, bf16[1,9,128,64]{2,3,1,0:T(8,128)(2,1)}, u32[]{:S(2)}) copy-start(bf16[1,9,128,64]{2,3,1,0:T(8,128)(2,1)} %param.7) | copy-start | bytes 442372
  1.7 10.2 %collective-permute-start = (bf16[48,24,128]{2,1,0:T(8,128)(2,1)S(1)}, bf16[48,24,128]{2,1,0:T(8,128)(2,1)S(1)}, u32[]{:S(2)}, u32[]{:S(2)}) collective-permute-start(bf16[48,24,128]{2,1,0:T(8,128)(2,1)S(1)} %pad_maximum_fusion), channel_id=1, source_target_pairs={{0,0},{1,1},{2,2},{3,3},{4,17},{5,5},{6,6},{7,7},{8,18},{9,22},{10... | collective-permute-start | bytes 884744 | tf_op jit(solution)/shard_map/ppermute | solution.py:56
  2.5 8.6 %copy-start.2 = (bf16[1,64,128]{2,1,0:T(8,128)(2,1)S(1)}, bf16[1,64,128]{2,1,0:T(8,128)(2,1)}, u32[]{:S(2)}) copy-start(bf16[1,64,128]{2,1,0:T(8,128)(2,1)} %param.9) | copy-start | bytes 49156
  2.6 10.4 %collective-permute-start.2 = (bf16[10,24,128]{2,1,0:T(8,128)(2,1)S(1)}, bf16[10,24,128]{2,1,0:T(8,128)(2,1)S(1)}, u32[]{:S(2)}, u32[]{:S(2)}) collective-permute-start(bf16[10,24,128]{2,1,0:T(8,128)(2,1)S(1)} %get-tuple-element.80), channel_id=1, source_target_pairs={{4,0},{5,1},{6,2},{7,3},{8,17},{9,5},{10,6},{11,7},{12,18},{13,22}... | collective-permute-start | bytes 184328 | tf_op jit(solution)/shard_map/ppermute | solution.py:56
  3.9 9.1 %collective-permute-start.1 = (bf16[10,24,128]{2,1,0:T(8,128)(2,1)S(1)}, bf16[10,24,128]{2,1,0:T(8,128)(2,1)S(1)}, u32[]{:S(2)}, u32[]{:S(2)}) collective-permute-start(bf16[10,24,128]{2,1,0:T(8,128)(2,1)S(1)} %get-tuple-element.81), channel_id=1, source_target_pairs={{0,17},{1,5},{2,6},{3,7},{4,18},{5,22},{6,10},{7,11},{8,19},{9,23}... | collective-permute-start | bytes 184328 | tf_op jit(solution)/shard_map/ppermute | solution.py:56
  11.1 0.7 copy-start.3
  11.8 9.7 %collective-permute-start.5 = (bf16[656,128]{1,0:T(8,128)(2,1)S(1)}, bf16[656,128]{1,0:T(8,128)(2,1)S(1)}, u32[]{:S(2)}, u32[]{:S(2)}) collective-permute-start(bf16[656,128]{1,0:T(8,128)(2,1)S(1)} %fusion.1.mine), channel_id=1, source_target_pairs={{0,16},{16,0},{1,17},{17,1},{2,18},{18,2},{3,19},{19,3},{4,20},{20... | collective-permute-start | bytes 503816 | tf_op jit(solution)/shard_map/ppermute | solution.py:455
  13.0 10.0 %collective-permute-start.4 = (bf16[10,44,128]{2,0,1:T(8,128)(2,1)S(1)}, bf16[10,44,128]{2,0,1:T(8,128)(2,1)S(1)}, u32[]{:S(2)}, u32[]{:S(2)}) collective-permute-start(bf16[10,44,128]{2,0,1:T(8,128)(2,1)S(1)} %get-tuple-element.90), channel_id=1, source_target_pairs={{1,0},{2,1},{3,2},{5,17},{6,5},{7,6},{22,18},{10,22},{11,10},{23,1... | collective-permute-start | bytes 337928 | tf_op jit(solution)/shard_map/ppermute | solution.py:56
  14.3 10.2 %collective-permute-start.3 = (bf16[10,44,128]{2,0,1:T(8,128)(2,1)S(1)}, bf16[10,44,128]{2,0,1:T(8,128)(2,1)S(1)}, u32[]{:S(2)}, u32[]{:S(2)}) collective-permute-start(bf16[10,44,128]{2,0,1:T(8,128)(2,1)S(1)} %get-tuple-element.91), channel_id=1, source_target_pairs={{0,1},{1,2},{2,3},{17,5},{5,6},{6,7},{18,22},{22,10},{10,11},{19,2... | collective-permute-start | bytes 337928 | tf_op jit(solution)/shard_map/ppermute | solution.py:56
  28.1 0.7 collective-permute-start.6
  30.8 9.4 %collective-permute-start.7 = (bf16[12,24,128]{2,1,0:T(8,128)(2,1)S(1)}, bf16[12,24,128]{2,1,0:T(8,128)(2,1)S(1)}, u32[]{:S(2)}, u32[]{:S(2)}) collective-permute-start(bf16[12,24,128]{2,1,0:T(8,128)(2,1)S(1)} %get-tuple-element.48), channel_id=1, source_target_pairs={{0,17},{1,5},{2,6},{3,7},{17,18},{5,22},{6,10},{7,11},{18,19},{22,... | collective-permute-start | bytes 221192 | tf_op jit(solution)/shard_map/ppermute | solution.py:56
  38.3 5.7 %collective-permute-start.8 = (bf16[12,24,128]{2,1,0:T(8,128)(2,1)S(1)}, bf16[12,24,128]{2,1,0:T(8,128)(2,1)S(1)}, u32[]{:S(2)}, u32[]{:S(2)}) collective-permute-start(bf16[12,24,128]{2,1,0:T(8,128)(2,1)S(1)} %get-tuple-element.49), channel_id=1, source_target_pairs={{17,0},{5,1},{6,2},{7,3},{18,17},{22,5},{10,6},{11,7},{19,18},{23,... | collective-permute-start | bytes 221192 | tf_op jit(solution)/shard_map/ppermute | solution.py:56
  44.1 8.2 %collective-permute-start.9 = (bf16[12,44,128]{2,0,1:T(8,128)(2,1)S(1)}, bf16[12,44,128]{2,0,1:T(8,128)(2,1)S(1)}, u32[]{:S(2)}, u32[]{:S(2)}) collective-permute-start(bf16[12,44,128]{2,0,1:T(8,128)(2,1)S(1)} %maximum_bitcast_fusion), channel_id=1, source_target_pairs={{0,1},{1,2},{2,3},{17,5},{5,6},{6,7},{18,22},{22,10},{10,11},{19,2... | collective-permute-start | bytes 405512 | tf_op jit(solution)/shard_map/ppermute | solution.py:56
  49.5 7.6 %collective-permute-start.10 = (bf16[12,44,128]{2,0,1:T(8,128)(2,1)S(1)}, bf16[12,44,128]{2,0,1:T(8,128)(2,1)S(1)}, u32[]{:S(2)}, u32[]{:S(2)}) collective-permute-start(bf16[12,44,128]{2,0,1:T(8,128)(2,1)S(1)} %maximum_bitcast_fusion.1), channel_id=1, source_target_pairs={{1,0},{2,1},{3,2},{5,17},{6,5},{7,6},{22,18},{10,22},{11,10},{23,1... | collective-permute-start | bytes 405512 | tf_op jit(solution)/shard_map/ppermute | solution.py:56
  60.2 1.9 %collective-permute-start.11 = (bf16[656,128]{1,0:T(8,128)(2,1)S(1)}, bf16[656,128]{1,0:T(8,128)(2,1)S(1)}, u32[]{:S(2)}, u32[]{:S(2)}) collective-permute-start(bf16[656,128]{1,0:T(8,128)(2,1)S(1)} %get-tuple-element.61), channel_id=1, source_target_pairs={{0,16},{16,0},{1,17},{17,1},{2,18},{18,2},{3,19},{19,3},{4,20},{20... | collective-permute-start | bytes 503816 | tf_op jit(solution)/shard_map/ppermute | solution.py:572
  62.9 17.7 %all-to-all-start = ((bf16[16,48,128]{2,1,0:T(8,128)(2,1)}), bf16[16,48,128]{2,1,0:T(8,128)(2,1)S(1)}, u32[]{:S(2)}, u32[]{:S(2)}) async-start(bf16[16,48,128]{2,1,0:T(8,128)(2,1)} %pair.1), calls=%async_computation | async-start | bytes 393216 | tf_op jit(solution)/shard_map/all_to_all | solution.py:582
  71.1 10.2 %collective-permute-start.12 = (bf16[24,24,128]{2,1,0:T(8,128)(2,1)S(1)}, bf16[24,24,128]{2,1,0:T(8,128)(2,1)S(1)}, u32[]{:S(2)}, u32[]{:S(2)}) collective-permute-start(bf16[24,24,128]{2,1,0:T(8,128)(2,1)S(1)} %input.1), channel_id=1, source_target_pairs={{0,0},{1,1},{2,2},{3,3},{17,4},{5,5},{6,6},{7,7},{18,8},{22,9},{10... | collective-permute-start | bytes 442376 | tf_op jit(solution)/shard_map/ppermute | solution.py:56
  81.3 13.3 %all-to-all-start.1 = ((bf16[16,40,128]{2,1,0:T(8,128)(2,1)}), bf16[16,40,128]{2,1,0:T(8,128)(2,1)S(1)}, u32[]{:S(2)}, u32[]{:S(2)}) async-start(bf16[16,40,128]{2,1,0:T(8,128)(2,1)} %get-tuple-element.69), calls=%async_computation.1 | async-start | bytes 327680 | tf_op jit(solution)/shard_map/all_to_all | solution.py:594

commit v12 on v11

--- a/solution.py
+++ b/solution.py
@@ -165,21 +165,21 @@
 
 
 def own_kernel(
-    brought, above, below, left, right, weights, bias, proj,
+    tile, above, below, left, right, weights, bias, proj,
     swapped, gate_first, bottle_first, near_hidden,
     area, pairs, last, pre,
 ):
-    side, first, second, inner = brought.shape[1], FIRST_DILATION, SECOND_DILATION, bias.shape[1]
+    side, first, second, inner = tile.shape[0], FIRST_DILATION, SECOND_DILATION, bias.shape[1]
     near, small = gate_first.shape[:2]
     span = side + 2 * second
-    assemble(area, brought[:side].astype(F32), above, below, left, right)
+    assemble(area, tile[...].astype(F32), above, below, left, right)
 
     def store(top, pre_act, branch):
         pre[pl.ds(top, 8)] = pre_act
         swapped[pl.ds(top, 8)] = branch[:, :span].astype(BF16)
 
     first_branch(area, pairs, last, weights, bias, proj, store)
-    swapped[span:, :side] = brought[side:]
+    swapped[span:] = jnp.zeros((side, span, swapped.shape[2]), BF16)
     for b in (-1, 0, 1):
         at = LEAD + first * b
         near_hidden[b + 1] = positive(area[HALO - first : HALO + side + first, at : at + small]).astype(BF16)
@@ -380,7 +380,7 @@
         parts[j] = jnp.concatenate(pieces + [total[count : count + 8]]).astype(BF16)
 
 
-def input_kernel(windows, grad_first, brought, v_first, out):
+def input_kernel(windows, grad_first, tile, v_first, out):
     side, channels = out.shape[0], out.shape[2]
     small = windows.shape[2]
     first = FIRST_DILATION
@@ -393,7 +393,7 @@
             total = total + dot(window, v_first[tap(a, b)])
         here = pl.ds(top, 8)
         total = total.reshape(8, small, channels)[:, :side]
-        total = jnp.where(brought[here].astype(F32) > 0, total, 0)
+        total = jnp.where(tile[here].astype(F32) > 0, total, 0)
         out[here] = (grad_first[here].astype(F32) + total).astype(BF16)
         return 0
 
@@ -407,11 +407,12 @@
     ends[...] = total[share:]
 
 
-def outputs_kernel(rows, ends, conv_gradient, bias_gradient, out_gradient):
+def outputs_kernel(rows, ends, moved, conv_gradient, bias_gradient, out_gradient, input_gradient):
     count, inner = conv_gradient.shape[0], out_gradient.shape[0]
     conv_gradient[...] = rows[:count].astype(F32)
     out_gradient[...] = rows[count : count + inner].astype(F32)
     bias_gradient[...] = ends[:1, :inner]
+    input_gradient[...] = moved[...]
 
 
 def call(kernel, name, outs, scratch, flops, *operands):
@@ -434,8 +435,7 @@
     full, span, near = side + 2 * HALO, side + 2 * second, side + 2 * first
     wide, small = up16(span), up16(near)
 
-    brought = bring(jnp.concatenate([activations[0], cotangent[0]]))
-    tile = brought[:side]
+    tile = bring(activations[0])
     above = bring(activations[0, side - HALO :], 1)
     below = bring(activations[0, :HALO], -1)
 
@@ -447,6 +447,7 @@
 
     left = send(columns(side - HALO, side), lambda r, c: (r, c + 1))
     right = send(columns(0, HALO), lambda r, c: (r, c - 1))
+    late = bring(cotangent[0])
 
     bias_rows = jnp.pad(conv_bias, ((0, 15), (0, channels - inner)))
     packed = jnp.concatenate(
@@ -488,9 +489,10 @@
             ((span, wide, inner), F32),
         ],
         span * wide * channels * inner * 20,
-        *(brought, above, below, jnp.swapaxes(left, 0, 1), jnp.swapaxes(right, 0, 1)),
+        *(tile, above, below, jnp.swapaxes(left, 0, 1), jnp.swapaxes(right, 0, 1)),
         *(w_first, b_first, p_first),
     )
+    kept = lax.dynamic_update_slice(kept, late, (span, 0, 0))
     other = send(kept, lambda r, c: (c, r))
     gate_second, hidden_pairs, hidden_last, bottle_second, grad_tile, grad_pre, strip_above, strip_below = call(
         middle_kernel,
@@ -567,7 +569,7 @@
         [((side, side, channels), BF16)],
         [],
         18 * side * small * channels * channels,
-        *(windows, grad_first, brought, v_first),
+        *(windows, grad_first, tile, v_first),
     )
     other = lax.ppermute(away, "segment", [(0, 1), (1, 0)])
     other, input_gradient = lax.optimization_barrier((other, input_gradient))
@@ -592,13 +594,18 @@
     )
     rows, _ = lax.optimization_barrier((rows, input_gradient))
     rows = lax.all_to_all(rows, GRID, 0, 0, tiled=True).reshape(devices * share, channels)
-    conv_gradient, bias_gradient, out_gradient = call(
+    conv_gradient, bias_gradient, out_gradient, input_gradient = call(
         outputs_kernel,
         "outputs",
-        [((9 * inner, channels), F32), ((1, inner), F32), ((inner, channels), F32)],
+        [
+            ((9 * inner, channels), F32),
+            ((1, inner), F32),
+            ((inner, channels), F32),
+            ((side, side, channels), BF16),
+        ],
         [],
         rows.size,
-        *(rows, ends),
+        *(rows, ends, input_gradient),
     )
     conv_gradient = jnp.swapaxes(conv_gradient.reshape(1, 9, inner, channels), 2, 3)
     return (input_gradient[None], conv_gradient, bias_gradient, out_gradient[None])

time: 96.9 us -> 97.7 us (level)
  blocking collectives: 0 us -> 13.7 us
  waiting for transfers between devices: 31.5 us -> 24.3 us
  starting transfers between devices: 48 us -> 43.8 us
  other arithmetic: 1.24 us -> 0.19 us
    all_to_all x0 -> x1, blocking collectives: none -> 13.7 us  [local(): lax.all_to_all(rows, GRID, 0, 0, tiled=True)]
    all_to_all x1 -> x0, waiting for transfers between devices: 8.81 us -> none  [local(): lax.all_to_all(rows, GRID, 0, 0, tiled=True)]
    all_to_all x1 -> x0, starting transfers between devices: 4.45 us -> none  [local(): lax.all_to_all(rows, GRID, 0, 0, tiled=True)]
    ppermute x11 -> x12, starting transfers between devices: 34.4 us -> 36.1 us  [permute(): return lax.ppermute(x, ALL, [found for found in pairs if found is not None])]
    ppermute x11 -> x12, waiting for transfers between devices: 13.8 us -> 15.1 us  [permute(): return lax.ppermute(x, ALL, [found for found in pairs if found is not None])]
    concatenate x1 -> x0, other arithmetic: 1.05 us -> none  [local(): brought = bring(jnp.concatenate([activations[0], cotangent[0]]))]
  transfers between devices with their start and end apart: 15 -> 15, of which waited for: 10 -> 7; matrix products, arithmetic and copies ran while one was open for 0% -> 1% of each run, Pallas kernels for 3% -> 6%
where the time goes in v12:
time: 97.7 us; the launch traced here: 96.8 us
  starting transfers between devices  43.8 us (45%)
  waiting for transfers between devices  24.3 us (25%)
  blocking collectives  13.7 us (14%)
  Pallas kernels  12 us (12%)
  local copies, waits for them, and re-layouts  1.86 us (2%)
    ppermute x12, starting transfers between devices, permute(): return lax.ppermute(x, ALL, [found for found in pairs if found is not None])  36.1 us
    ppermute x12, waiting for transfers between devices, permute(): return lax.ppermute(x, ALL, [found for found in pairs if found is not None])  15.1 us
    all_to_all x1, blocking collectives, local(): lax.all_to_all(rows, GRID, 0, 0, tiled=True)  13.7 us
    pallas_call x9, Pallas kernels, call(): pl.pallas_call(kernel, name=name, out_shape=outs, scratch_shapes=[pltpu.V...  12 us
    all_to_all x1, waiting for transfers between devices, local(): parts = lax.all_to_all(parts, GRID, 0, 0, tiled=True)  8.8 us
    all_to_all x1, starting transfers between devices, local(): parts = lax.all_to_all(parts, GRID, 0, 0, tiled=True)  7.61 us
  transfers between devices with their start and end apart: 15, of which 7 were waited for; matrix products, arithmetic and copies ran while one was open for 1% of the time, Pallas kernels for 6%

profile of v12, /device:TPU:0, one launch (start us, length us, event | category | flops | bytes accessed | tf_op | source)
XLA Modules:
  0.0 96.8 jit_solution(18421643250616394962)
XLA Ops:
  0.6 0.0 copy-start
  0.6 1.7 %collective-permute-start = (bf16[24,24,128]{2,1,0:T(8,128)(2,1)}, bf16[24,24,128]{2,1,0:T(8,128)(2,1)S(1)}, u32[]{:S(2)}, u32[]{:S(2)}) collective-permute-start(bf16[24,24,128]{2,1,0:T(8,128)(2,1)} %bitcast.56), channel_id=1, source_target_pairs={{0,0},{1,1},{2,2},{3,3},{4,17},{5,5},{6,6},{7,7},{8,18},{9,22},{10... | collective-permute-start | bytes 442376 | tf_op jit(solution)/shard_map/ppermute | solution.py:56
  2.3 0.0 copy-start.1
  2.3 0.9 slice_bitcast_fusion.2
  3.2 1.3 %collective-permute-start.2 = (bf16[10,24,128]{2,1,0:T(8,128)(2,1)S(1)}, bf16[10,24,128]{2,1,0:T(8,128)(2,1)S(1)}, u32[]{:S(2)}, u32[]{:S(2)}) collective-permute-start(bf16[10,24,128]{2,1,0:T(8,128)(2,1)S(1)} %get-tuple-element.82), channel_id=1, source_target_pairs={{4,0},{5,1},{6,2},{7,3},{8,17},{9,5},{10,6},{11,7},{12,18},{13,22}... | collective-permute-start | bytes 184328 | tf_op jit(solution)/shard_map/ppermute | solution.py:56
  4.5 6.4 %collective-permute-start.1 = (bf16[10,24,128]{2,1,0:T(8,128)(2,1)S(1)}, bf16[10,24,128]{2,1,0:T(8,128)(2,1)S(1)}, u32[]{:S(2)}, u32[]{:S(2)}) collective-permute-start(bf16[10,24,128]{2,1,0:T(8,128)(2,1)S(1)} %get-tuple-element.83), channel_id=1, source_target_pairs={{0,17},{1,5},{2,6},{3,7},{4,18},{5,22},{6,10},{7,11},{8,19},{9,23}... | collective-permute-start | bytes 184328 | tf_op jit(solution)/shard_map/ppermute | solution.py:56
  10.9 1.6 %collective-permute-start.6 = (bf16[24,24,128]{2,1,0:T(8,128)(2,1)}, bf16[24,24,128]{2,1,0:T(8,128)(2,1)S(1)}, u32[]{:S(2)}, u32[]{:S(2)}) collective-permute-start(bf16[24,24,128]{2,1,0:T(8,128)(2,1)} %bitcast.59), channel_id=1, source_target_pairs={{0,0},{1,1},{2,2},{3,3},{4,17},{5,5},{6,6},{7,7},{8,18},{9,22},{10... | collective-permute-start | bytes 442376 | tf_op jit(solution)/shard_map/ppermute | solution.py:56
  12.5 0.0 copy-start.2
  12.5 0.0 copy-done
  12.5 0.0 copy-done.1
  12.5 0.6 copy-done.2
  13.2 0.1 collective-permute-start.5
  13.2 0.0 collective-permute-done.tile
  13.4 0.0 collective-permute-done.1.above
  13.4 0.0 collective-permute-done.2.below
  13.4 1.3 %collective-permute-start.4 = (bf16[10,44,128]{2,0,1:T(8,128)(2,1)S(1)}, bf16[10,44,128]{2,0,1:T(8,128)(2,1)S(1)}, u32[]{:S(2)}, u32[]{:S(2)}) collective-permute-start(bf16[10,44,128]{2,0,1:T(8,128)(2,1)S(1)} %get-tuple-element.92), channel_id=1, source_target_pairs={{1,0},{2,1},{3,2},{5,17},{6,5},{7,6},{22,18},{10,22},{11,10},{23,1... | collective-permute-start | bytes 337928 | tf_op jit(solution)/shard_map/ppermute | solution.py:56
  14.7 6.8 %collective-permute-start.3 = (bf16[10,44,128]{2,0,1:T(8,128)(2,1)S(1)}, bf16[10,44,128]{2,0,1:T(8,128)(2,1)S(1)}, u32[]{:S(2)}, u32[]{:S(2)}) collective-permute-start(bf16[10,44,128]{2,0,1:T(8,128)(2,1)S(1)} %get-tuple-element.93), channel_id=1, source_target_pairs={{0,1},{1,2},{2,3},{17,5},{5,6},{6,7},{18,22},{22,10},{10,11},{19,2... | collective-permute-start | bytes 337928 | tf_op jit(solution)/shard_map/ppermute | solution.py:56
  21.6 0.0 collective-permute-done.5.theirs
  21.6 0.4 weights.1
  22.0 3.1 %collective-permute-done.4 = bf16[10,44,128]{2,0,1:T(8,128)(2,1)S(1)} collective-permute-done((bf16[10,44,128]{2,0,1:T(8,128)(2,1)S(1)}, bf16[10,44,128]{2,0,1:T(8,128)(2,1)S(1)}, u32[]{:S(2)}, u32[]{:S(2)}) %collective-permute-start.4) | collective-permute-done | bytes 112672 | tf_op jit(solution)/shard_map/ppermute | solution.py:56
  25.0 0.0 collective-permute-done.3
  25.0 3.5 %own_branch.1 = (bf16[64,40,128]{2,1,0:T(8,128)(2,1)S(1)}, bf16[28,32,128]{2,1,0:T(8,128)(2,1)S(1)}, bf16[24,32,64]{2,1,0:T(8,128)(2,1)S(1)}, bf16[3,28,32,128]{3,2,1,0:T(8,128)(2,1)S(1)}) custom-call(bf16[24,24,128]{2,1,0:T(8,128)(2,1)S(1)} %collective-permute-done.tile, bf16[10,24,128]{2,1,0:T(8,128)(2,1)S(1)} %collective-permute-done.1.above, ...), custom_call_target="tpu_custom_call" | custom-call | flops 314572800 | bytes 2330880 | tf_op jit(solution)/shard_map/own_branch/pallas_call | solution.py:421
  28.6 0.0 collective-permute-done.6
  28.6 0.7 collective-permute-start.7
  29.3 0.0 collective-permute-done.7.other
  29.3 2.0 %middle.1 = (bf16[28,32,128]{2,1,0:T(8,128)(2,1)S(1)}, bf16[40,32,256]{2,1,0:T(8,128)(2,1)S(1)}, bf16[48,32,256]{2,1,0:T(8,128)(2,1)S(1)}, bf16[24,32,64]{2,1,0:...) custom-call(bf16[64,40,128]{2,1,0:T(8,128)(2,1)S(1)} %constant_dynam, ...), custom_call_target="tpu_custom_call" | custom-call | flops 301989888 | bytes 3949056 | tf_op jit(solution)/shard_map/middle/pallas_call | solution.py:421
  31.3 7.1 %collective-permute-start.8 = (bf16[12,24,128]{2,1,0:T(8,128)(2,1)S(1)}, bf16[12,24,128]{2,1,0:T(8,128)(2,1)S(1)}, u32[]{:S(2)}, u32[]{:S(2)}) collective-permute-start(bf16[12,24,128]{2,1,0:T(8,128)(2,1)S(1)} %get-tuple-element.49), channel_id=1, source_target_pairs={{0,17},{1,5},{2,6},{3,7},{17,18},{5,22},{6,10},{7,11},{18,19},{22,... | collective-permute-start | bytes 221192 | tf_op jit(solution)/shard_map/ppermute | solution.py:56
  38.5 1.3 %collective-permute-start.9 = (bf16[12,24,128]{2,1,0:T(8,128)(2,1)S(1)}, bf16[12,24,128]{2,1,0:T(8,128)(2,1)S(1)}, u32[]{:S(2)}, u32[]{:S(2)}) collective-permute-start(bf16[12,24,128]{2,1,0:T(8,128)(2,1)S(1)} %get-tuple-element.50), channel_id=1, source_target_pairs={{17,0},{5,1},{6,2},{7,3},{18,17},{22,5},{10,6},{11,7},{19,18},{23,... | collective-permute-start | bytes 221192 | tf_op jit(solution)/shard_map/ppermute | solution.py:56
  39.8 0.6 collective-permute-done.8.above
  40.4 5.6 %collective-permute-done.9.below = bf16[12,24,128]{2,1,0:T(8,128)(2,1)S(1)} collective-permute-done((bf16[12,24,128]{2,1,0:T(8,128)(2,1)S(1)}, bf16[12,24,128]{2,1,0:T(8,128)(2,1)S(1)}, u32[]{:S(2)}, u32[]{:S(2)}) %collective-permute-start.9) | collective-permute-done | bytes 73760 | tf_op jit(solution)/shard_map/ppermute | solution.py:56
  46.1 0.1 maximum_bitcast_fusion
  46.2 5.9 %collective-permute-start.10 = (bf16[12,44,128]{2,0,1:T(8,128)(2,1)S(1)}, bf16[12,44,128]{2,0,1:T(8,128)(2,1)S(1)}, u32[]{:S(2)}, u32[]{:S(2)}) collective-permute-start(bf16[12,44,128]{2,0,1:T(8,128)(2,1)S(1)} %maximum_bitcast_fusion), channel_id=1, source_target_pairs={{0,1},{1,2},{2,3},{17,5},{5,6},{6,7},{18,22},{22,10},{10,11},{19,2... | collective-permute-start | bytes 405512 | tf_op jit(solution)/shard_map/ppermute | solution.py:56
  52.1 0.1 maximum_bitcast_fusion.1
  52.2 1.3 %collective-permute-start.11 = (bf16[12,44,128]{2,0,1:T(8,128)(2,1)S(1)}, bf16[12,44,128]{2,0,1:T(8,128)(2,1)S(1)}, u32[]{:S(2)}, u32[]{:S(2)}) collective-permute-start(bf16[12,44,128]{2,0,1:T(8,128)(2,1)S(1)} %maximum_bitcast_fusion.1), channel_id=1, source_target_pairs={{1,0},{2,1},{3,2},{5,17},{6,5},{7,6},{22,18},{10,22},{11,10},{23,1... | collective-permute-start | bytes 405512 | tf_op jit(solution)/shard_map/ppermute | solution.py:56
  53.5 0.5 second_sums.1
  54.0 1.1 %collective-permute-done.10 = bf16[12,44,128]{2,0,1:T(8,128)(2,1)S(1)} collective-permute-done((bf16[12,44,128]{2,0,1:T(8,128)(2,1)S(1)}, bf16[12,44,128]{2,0,1:T(8,128)(2,1)S(1)}, u32[]{:S(2)}, u32[]{:S(2)}) %collective-permute-start.10) | collective-permute-done | bytes 135200 | tf_op jit(solution)/shard_map/ppermute | solution.py:56
  55.1 4.7 %collective-permute-done.11 = bf16[12,44,128]{2,0,1:T(8,128)(2,1)S(1)} collective-permute-done((bf16[12,44,128]{2,0,1:T(8,128)(2,1)S(1)}, bf16[12,44,128]{2,0,1:T(8,128)(2,1)S(1)}, u32[]{:S(2)}, u32[]{:S(2)}) %collective-permute-start.11) | collective-permute-done | bytes 135200 | tf_op jit(solution)/shard_map/ppermute | solution.py:56
  59.9 3.1 %backward.1 = (f32[656,128]{1,0:T(8,128)S(1)}, bf16[656,128]{1,0:T(8,128)(2,1)S(1)}, bf16[3,28,32,128]{3,2,1,0:T(8,128)(2,1)S(1)}, bf16[24,24,128]{2,1,0:T(8,128)(2,1)S(1)}) custom-call(bf16[24,32,128]{2,1,0:T(8,128)(2,1)S(1)} %get-tuple-element.47.grad_pre, bf16[24,32,128]{2,1,0:T(8,128)(2,1)S(1)} %get-tuple-element.48.grad_tile, ...), custom_call_target="tpu_custom_call" | custom-call | flops 528482304 | bytes 4337664 | tf_op jit(solution)/shard_map/backward/pallas_call | solution.py:421
  63.0 0.1 collective-permute-start.12
  63.0 0.9 input.1
  64.0 0.4 collective-permute-done.12.other
  64.4 0.7 pair.1
  65.2 7.6 %all-to-all-start = ((bf16[16,48,128]{2,1,0:T(8,128)(2,1)}), bf16[16,48,128]{2,1,0:T(8,128)(2,1)S(1)}, u32[]{:S(2)}, u32[]{:S(2)}) async-start(bf16[16,48,128]{2,1,0:T(8,128)(2,1)} %pair.1), calls=%async_computation | async-start | bytes 393216 | tf_op jit(solution)/shard_map/all_to_all | solution.py:584
  72.8 0.7 collective-permute-start.13
  73.4 8.8 %all-to-all-done.parts = bf16[16,48,128]{2,1,0:T(8,128)(2,1)S(1)} async-done(((bf16[16,48,128]{2,1,0:T(8,128)(2,1)}), bf16[16,48,128]{2,1,0:T(8,128)(2,1)S(1)}, u32[]{:S(2)}, u32[]{:S(2)}) %all-to-all-start) | async-done | bytes 196640 | tf_op jit(solution)/shard_map/all_to_all | solution.py:584
  82.3 0.0 collective-permute-done.13.moved
  82.3 13.7 %all_to_all.10 = bf16[16,40,128]{2,1,0:T(8,128)(2,1)S(1)} all-to-all(bf16[16,40,128]{2,1,0:T(8,128)(2,1)S(1)} %get-tuple-element.70), channel_id=1, replica_groups=mesh['segment'=2,'row'=4,'col'=4] {'row','col'}, dimensions={0} | all-to-all | bytes 327680 | tf_op jit(solution)/shard_map/all_to_all | solution.py:596
  96.0 0.8 outputs.1
  (18 shorter events, 0.4 us)
Async XLA Ops:
  0.6 11.9 %copy-start = (bf16[1,9,128,64]{2,3,1,0:T(8,128)(2,1)S(1)}, bf16[1,9,128,64]{2,3,1,0:T(8,128)(2,1)}, u32[]{:S(2)}) copy-start(bf16[1,9,128,64]{2,3,1,0:T(8,128)(2,1)} %param.7) | copy-start | bytes 442372
  0.6 12.6 %collective-permute-start = (bf16[24,24,128]{2,1,0:T(8,128)(2,1)}, bf16[24,24,128]{2,1,0:T(8,128)(2,1)S(1)}, u32[]{:S(2)}, u32[]{:S(2)}) collective-permute-start(bf16[24,24,128]{2,1,0:T(8,128)(2,1)} %bitcast.56), channel_id=1, source_target_pairs={{0,0},{1,1},{2,2},{3,3},{4,17},{5,5},{6,6},{7,7},{8,18},{9,22},{10... | collective-permute-start | bytes 442376 | tf_op jit(solution)/shard_map/ppermute | solution.py:56
  2.3 10.2 %copy-start.1 = (bf16[1,64,128]{2,1,0:T(8,128)(2,1)S(1)}, bf16[1,64,128]{2,1,0:T(8,128)(2,1)}, u32[]{:S(2)}) copy-start(bf16[1,64,128]{2,1,0:T(8,128)(2,1)} %param.9) | copy-start | bytes 49156
  3.2 10.2 %collective-permute-start.2 = (bf16[10,24,128]{2,1,0:T(8,128)(2,1)S(1)}, bf16[10,24,128]{2,1,0:T(8,128)(2,1)S(1)}, u32[]{:S(2)}, u32[]{:S(2)}) collective-permute-start(bf16[10,24,128]{2,1,0:T(8,128)(2,1)S(1)} %get-tuple-element.82), channel_id=1, source_target_pairs={{4,0},{5,1},{6,2},{7,3},{8,17},{9,5},{10,6},{11,7},{12,18},{13,22}... | collective-permute-start | bytes 184328 | tf_op jit(solution)/shard_map/ppermute | solution.py:56
  4.5 8.8 %collective-permute-start.1 = (bf16[10,24,128]{2,1,0:T(8,128)(2,1)S(1)}, bf16[10,24,128]{2,1,0:T(8,128)(2,1)S(1)}, u32[]{:S(2)}, u32[]{:S(2)}) collective-permute-start(bf16[10,24,128]{2,1,0:T(8,128)(2,1)S(1)} %get-tuple-element.83), channel_id=1, source_target_pairs={{0,17},{1,5},{2,6},{3,7},{4,18},{5,22},{6,10},{7,11},{8,19},{9,23}... | collective-permute-start | bytes 184328 | tf_op jit(solution)/shard_map/ppermute | solution.py:56
  10.9 17.7 %collective-permute-start.6 = (bf16[24,24,128]{2,1,0:T(8,128)(2,1)}, bf16[24,24,128]{2,1,0:T(8,128)(2,1)S(1)}, u32[]{:S(2)}, u32[]{:S(2)}) collective-permute-start(bf16[24,24,128]{2,1,0:T(8,128)(2,1)} %bitcast.59), channel_id=1, source_target_pairs={{0,0},{1,1},{2,2},{3,3},{4,17},{5,5},{6,6},{7,7},{8,18},{9,22},{10... | collective-permute-start | bytes 442376 | tf_op jit(solution)/shard_map/ppermute | solution.py:56
  12.5 0.7 copy-start.2
  13.2 8.4 %collective-permute-start.5 = (bf16[656,128]{1,0:T(8,128)(2,1)S(1)}, bf16[656,128]{1,0:T(8,128)(2,1)S(1)}, u32[]{:S(2)}, u32[]{:S(2)}) collective-permute-start(bf16[656,128]{1,0:T(8,128)(2,1)S(1)} %fusion.1.mine), channel_id=1, source_target_pairs={{0,16},{16,0},{1,17},{17,1},{2,18},{18,2},{3,19},{19,3},{4,20},{20... | collective-permute-start | bytes 503816 | tf_op jit(solution)/shard_map/ppermute | solution.py:456
  13.4 11.6 %collective-permute-start.4 = (bf16[10,44,128]{2,0,1:T(8,128)(2,1)S(1)}, bf16[10,44,128]{2,0,1:T(8,128)(2,1)S(1)}, u32[]{:S(2)}, u32[]{:S(2)}) collective-permute-start(bf16[10,44,128]{2,0,1:T(8,128)(2,1)S(1)} %get-tuple-element.92), channel_id=1, source_target_pairs={{1,0},{2,1},{3,2},{5,17},{6,5},{7,6},{22,18},{10,22},{11,10},{23,1... | collective-permute-start | bytes 337928 | tf_op jit(solution)/shard_map/ppermute | solution.py:56
  14.7 10.3 %collective-permute-start.3 = (bf16[10,44,128]{2,0,1:T(8,128)(2,1)S(1)}, bf16[10,44,128]{2,0,1:T(8,128)(2,1)S(1)}, u32[]{:S(2)}, u32[]{:S(2)}) collective-permute-start(bf16[10,44,128]{2,0,1:T(8,128)(2,1)S(1)} %get-tuple-element.93), channel_id=1, source_target_pairs={{0,1},{1,2},{2,3},{17,5},{5,6},{6,7},{18,22},{22,10},{10,11},{19,2... | collective-permute-start | bytes 337928 | tf_op jit(solution)/shard_map/ppermute | solution.py:56
  28.6 0.7 collective-permute-start.7
  31.3 9.1 %collective-permute-start.8 = (bf16[12,24,128]{2,1,0:T(8,128)(2,1)S(1)}, bf16[12,24,128]{2,1,0:T(8,128)(2,1)S(1)}, u32[]{:S(2)}, u32[]{:S(2)}) collective-permute-start(bf16[12,24,128]{2,1,0:T(8,128)(2,1)S(1)} %get-tuple-element.49), channel_id=1, source_target_pairs={{0,17},{1,5},{2,6},{3,7},{17,18},{5,22},{6,10},{7,11},{18,19},{22,... | collective-permute-start | bytes 221192 | tf_op jit(solution)/shard_map/ppermute | solution.py:56
  38.5 7.5 %collective-permute-start.9 = (bf16[12,24,128]{2,1,0:T(8,128)(2,1)S(1)}, bf16[12,24,128]{2,1,0:T(8,128)(2,1)S(1)}, u32[]{:S(2)}, u32[]{:S(2)}) collective-permute-start(bf16[12,24,128]{2,1,0:T(8,128)(2,1)S(1)} %get-tuple-element.50), channel_id=1, source_target_pairs={{17,0},{5,1},{6,2},{7,3},{18,17},{22,5},{10,6},{11,7},{19,18},{23,... | collective-permute-start | bytes 221192 | tf_op jit(solution)/shard_map/ppermute | solution.py:56
  46.2 8.9 %collective-permute-start.10 = (bf16[12,44,128]{2,0,1:T(8,128)(2,1)S(1)}, bf16[12,44,128]{2,0,1:T(8,128)(2,1)S(1)}, u32[]{:S(2)}, u32[]{:S(2)}) collective-permute-start(bf16[12,44,128]{2,0,1:T(8,128)(2,1)S(1)} %maximum_bitcast_fusion), channel_id=1, source_target_pairs={{0,1},{1,2},{2,3},{17,5},{5,6},{6,7},{18,22},{22,10},{10,11},{19,2... | collective-permute-start | bytes 405512 | tf_op jit(solution)/shard_map/ppermute | solution.py:56
  52.2 7.6 %collective-permute-start.11 = (bf16[12,44,128]{2,0,1:T(8,128)(2,1)S(1)}, bf16[12,44,128]{2,0,1:T(8,128)(2,1)S(1)}, u32[]{:S(2)}, u32[]{:S(2)}) collective-permute-start(bf16[12,44,128]{2,0,1:T(8,128)(2,1)S(1)} %maximum_bitcast_fusion.1), channel_id=1, source_target_pairs={{1,0},{2,1},{3,2},{5,17},{6,5},{7,6},{22,18},{10,22},{11,10},{23,1... | collective-permute-start | bytes 405512 | tf_op jit(solution)/shard_map/ppermute | solution.py:56
  63.0 1.5 %collective-permute-start.12 = (bf16[656,128]{1,0:T(8,128)(2,1)S(1)}, bf16[656,128]{1,0:T(8,128)(2,1)S(1)}, u32[]{:S(2)}, u32[]{:S(2)}) collective-permute-start(bf16[656,128]{1,0:T(8,128)(2,1)S(1)} %get-tuple-element.63), channel_id=1, source_target_pairs={{0,16},{16,0},{1,17},{17,1},{2,18},{18,2},{3,19},{19,3},{4,20},{20... | collective-permute-start | bytes 503816 | tf_op jit(solution)/shard_map/ppermute | solution.py:574
  65.2 17.1 %all-to-all-start = ((bf16[16,48,128]{2,1,0:T(8,128)(2,1)}), bf16[16,48,128]{2,1,0:T(8,128)(2,1)S(1)}, u32[]{:S(2)}, u32[]{:S(2)}) async-start(bf16[16,48,128]{2,1,0:T(8,128)(2,1)} %pair.1), calls=%async_computation | async-start | bytes 393216 | tf_op jit(solution)/shard_map/all_to_all | solution.py:584
  72.8 9.5 %collective-permute-start.13 = (bf16[24,24,128]{2,1,0:T(8,128)(2,1)S(1)}, bf16[24,24,128]{2,1,0:T(8,128)(2,1)S(1)}, u32[]{:S(2)}, u32[]{:S(2)}) collective-permute-start(bf16[24,24,128]{2,1,0:T(8,128)(2,1)S(1)} %input.1), channel_id=1, source_target_pairs={{0,0},{1,1},{2,2},{3,3},{17,4},{5,5},{6,6},{7,7},{18,8},{22,9},{10... | collective-permute-start | bytes 442376 | tf_op jit(solution)/shard_map/ppermute | solution.py:56

commit v13 on v12

--- a/solution.py
+++ b/solution.py
@@ -445,9 +445,10 @@
         strip = lax.dynamic_update_slice(strip, jnp.swapaxes(above[:, low:high], 0, 1), (0, 0, 0))
         return lax.dynamic_update_slice(strip, jnp.swapaxes(below[:, low:high], 0, 1), (0, HALO + side, 0))
 
-    left = send(columns(side - HALO, side), lambda r, c: (r, c + 1))
-    right = send(columns(0, HALO), lambda r, c: (r, c - 1))
-    late = bring(cotangent[0])
+    strips = (columns(side - HALO, side), columns(0, HALO))
+    strips, late = lax.optimization_barrier((strips, cotangent[0]))
+    left, right = send(strips[0], lambda r, c: (r, c + 1)), send(strips[1], lambda r, c: (r, c - 1))
+    late = bring(late)
 
     bias_rows = jnp.pad(conv_bias, ((0, 15), (0, channels - inner)))
     packed = jnp.concatenate(
@@ -488,7 +489,7 @@
             ((full + first, wide, 2 * channels), BF16),
             ((span, wide, inner), F32),
         ],
-        span * wide * channels * inner * 20,
+        span * wide * channels * inner * 400,
         *(tile, above, below, jnp.swapaxes(left, 0, 1), jnp.swapaxes(right, 0, 1)),
         *(w_first, b_first, p_first),
     )

time: 97.7 us -> 97.6 us (level)
    ppermute x12, starting transfers between devices: 36.1 us -> 34 us  [permute(): return lax.ppermute(x, ALL, [found for found in pairs if found is not None])]
    ppermute x1, starting transfers between devices: 0.07 us -> 1.93 us  [local(): other = lax.ppermute(away, 'segment', [(0, 1), (1, 0)])]
    ppermute x12, waiting for transfers between devices: 15.1 us -> 16 us  [permute(): return lax.ppermute(x, ALL, [found for found in pairs if found is not None])]
  transfers between devices with their start and end apart: 15 -> 15, of which waited for: 7 -> 9; matrix products, arithmetic and copies ran while one was open for 1% -> 1% of each run, Pallas kernels for 6% -> 6%
where the time goes in v13:
time: 97.6 us; the launch traced here: 96.7 us
  starting transfers between devices  43.1 us (44%)
  waiting for transfers between devices  24.9 us (26%)
  blocking collectives  13.7 us (14%)
  Pallas kernels  12 us (12%)
  local copies, waits for them, and re-layouts  1.84 us (2%)
    ppermute x12, starting transfers between devices, permute(): return lax.ppermute(x, ALL, [found for found in pairs if found is not None])  34 us
    ppermute x12, waiting for transfers between devices, permute(): return lax.ppermute(x, ALL, [found for found in pairs if found is not None])  16 us
    all_to_all x1, blocking collectives, local(): lax.all_to_all(rows, GRID, 0, 0, tiled=True)  13.7 us
    pallas_call x9, Pallas kernels, call(): pl.pallas_call(kernel, name=name, out_shape=outs, scratch_shapes=[pltpu.V...  12 us
    all_to_all x1, waiting for transfers between devices, local(): parts = lax.all_to_all(parts, GRID, 0, 0, tiled=True)  8.8 us
    all_to_all x1, starting transfers between devices, local(): parts = lax.all_to_all(parts, GRID, 0, 0, tiled=True)  7.11 us
  transfers between devices with their start and end apart: 15, of which 9 were waited for; matrix products, arithmetic and copies ran while one was open for 1% of the time, Pallas kernels for 6%

profile of v13, /device:TPU:0, one launch (start us, length us, event | category | flops | bytes accessed | tf_op | source)
XLA Modules:
  0.0 96.7 jit_solution(1029030887200270095)
XLA Ops:
  0.6 0.0 copy-start
  0.6 1.7 %collective-permute-start = (bf16[24,24,128]{2,1,0:T(8,128)(2,1)}, bf16[24,24,128]{2,1,0:T(8,128)(2,1)S(1)}, u32[]{:S(2)}, u32[]{:S(2)}) collective-permute-start(bf16[24,24,128]{2,1,0:T(8,128)(2,1)} %bitcast.56), channel_id=1, source_target_pairs={{0,0},{1,1},{2,2},{3,3},{4,17},{5,5},{6,6},{7,7},{8,18},{9,22},{10... | collective-permute-start | bytes 442376 | tf_op jit(solution)/shard_map/ppermute | solution.py:56
  2.3 0.9 slice_bitcast_fusion.2
  3.2 1.3 %collective-permute-start.2 = (bf16[10,24,128]{2,1,0:T(8,128)(2,1)S(1)}, bf16[10,24,128]{2,1,0:T(8,128)(2,1)S(1)}, u32[]{:S(2)}, u32[]{:S(2)}) collective-permute-start(bf16[10,24,128]{2,1,0:T(8,128)(2,1)S(1)} %get-tuple-element.88), channel_id=1, source_target_pairs={{4,0},{5,1},{6,2},{7,3},{8,17},{9,5},{10,6},{11,7},{12,18},{13,22}... | collective-permute-start | bytes 184328 | tf_op jit(solution)/shard_map/ppermute | solution.py:56
  4.5 6.4 %collective-permute-start.1 = (bf16[10,24,128]{2,1,0:T(8,128)(2,1)S(1)}, bf16[10,24,128]{2,1,0:T(8,128)(2,1)S(1)}, u32[]{:S(2)}, u32[]{:S(2)}) collective-permute-start(bf16[10,24,128]{2,1,0:T(8,128)(2,1)S(1)} %get-tuple-element.89), channel_id=1, source_target_pairs={{0,17},{1,5},{2,6},{3,7},{4,18},{5,22},{6,10},{7,11},{8,19},{9,23}... | collective-permute-start | bytes 184328 | tf_op jit(solution)/shard_map/ppermute | solution.py:56
  10.9 0.0 copy-start.2
  10.9 0.0 copy-done
  10.9 0.0 copy-done.1
  11.0 0.6 copy-done.2
  11.6 0.1 collective-permute-start.5
  11.7 0.0 collective-permute-done.tile
  11.8 0.0 copy-start.3
  11.8 1.0 collective-permute-done.1.above
  12.8 0.0 collective-permute-done.2.below
  12.8 3.3 %collective-permute-start.3 = (bf16[10,44,128]{2,0,1:T(8,128)(2,1)S(1)}, bf16[10,44,128]{2,0,1:T(8,128)(2,1)S(1)}, u32[]{:S(2)}, u32[]{:S(2)}) collective-permute-start(bf16[10,44,128]{2,0,1:T(8,128)(2,1)S(1)} %get-tuple-element.43), channel_id=1, source_target_pairs={{0,1},{1,2},{2,3},{17,5},{5,6},{6,7},{18,22},{22,10},{10,11},{19,2... | collective-permute-start | bytes 337928 | tf_op jit(solution)/shard_map/ppermute | solution.py:56
  16.2 1.3 %collective-permute-start.4 = (bf16[10,44,128]{2,0,1:T(8,128)(2,1)S(1)}, bf16[10,44,128]{2,0,1:T(8,128)(2,1)S(1)}, u32[]{:S(2)}, u32[]{:S(2)}) collective-permute-start(bf16[10,44,128]{2,0,1:T(8,128)(2,1)S(1)} %get-tuple-element.44), channel_id=1, source_target_pairs={{1,0},{2,1},{3,2},{5,17},{6,5},{7,6},{22,18},{10,22},{11,10},{23,1... | collective-permute-start | bytes 337928 | tf_op jit(solution)/shard_map/ppermute | solution.py:56
  17.5 0.7 collective-permute-start.6
  18.1 0.0 collective-permute-done.5.theirs
  18.2 0.4 weights.1
  18.5 0.6 collective-permute-done.3
  19.1 4.5 %collective-permute-done.4 = bf16[10,44,128]{2,0,1:T(8,128)(2,1)S(1)} collective-permute-done((bf16[10,44,128]{2,0,1:T(8,128)(2,1)S(1)}, bf16[10,44,128]{2,0,1:T(8,128)(2,1)S(1)}, u32[]{:S(2)}, u32[]{:S(2)}) %collective-permute-start.4) | collective-permute-done | bytes 112672 | tf_op jit(solution)/shard_map/ppermute | solution.py:56
  23.7 3.5 %own_branch.1 = (bf16[64,40,128]{2,1,0:T(8,128)(2,1)S(1)}, bf16[28,32,128]{2,1,0:T(8,128)(2,1)S(1)}, bf16[24,32,64]{2,1,0:T(8,128)(2,1)S(1)}, bf16[3,28,32,128]{3,2,1,0:T(8,128)(2,1)S(1)}) custom-call(bf16[24,24,128]{2,1,0:T(8,128)(2,1)S(1)} %collective-permute-done.tile, bf16[10,24,128]{2,1,0:T(8,128)(2,1)S(1)} %collective-permute-done.1.above, ...), custom_call_target="tpu_custom_call" | custom-call | flops 6291456000 | bytes 2330880 | tf_op jit(solution)/shard_map/own_branch/pallas_call | solution.py:421
  27.2 0.0 collective-permute-done.6
  27.3 0.7 collective-permute-start.7
  28.0 0.0 collective-permute-done.7.other
  28.0 2.0 %middle.1 = (bf16[28,32,128]{2,1,0:T(8,128)(2,1)S(1)}, bf16[40,32,256]{2,1,0:T(8,128)(2,1)S(1)}, bf16[48,32,256]{2,1,0:T(8,128)(2,1)S(1)}, bf16[24,32,64]{2,1,0:...) custom-call(bf16[64,40,128]{2,1,0:T(8,128)(2,1)S(1)} %constant_dynam, ...), custom_call_target="tpu_custom_call" | custom-call | flops 301989888 | bytes 3949056 | tf_op jit(solution)/shard_map/middle/pallas_call | solution.py:421
  30.0 11.8 %collective-permute-start.8 = (bf16[12,24,128]{2,1,0:T(8,128)(2,1)S(1)}, bf16[12,24,128]{2,1,0:T(8,128)(2,1)S(1)}, u32[]{:S(2)}, u32[]{:S(2)}) collective-permute-start(bf16[12,24,128]{2,1,0:T(8,128)(2,1)S(1)} %get-tuple-element.55), channel_id=1, source_target_pairs={{0,17},{1,5},{2,6},{3,7},{17,18},{5,22},{6,10},{7,11},{18,19},{22,... | collective-permute-start | bytes 221192 | tf_op jit(solution)/shard_map/ppermute | solution.py:56
  41.9 1.3 %collective-permute-start.9 = (bf16[12,24,128]{2,1,0:T(8,128)(2,1)S(1)}, bf16[12,24,128]{2,1,0:T(8,128)(2,1)S(1)}, u32[]{:S(2)}, u32[]{:S(2)}) collective-permute-start(bf16[12,24,128]{2,1,0:T(8,128)(2,1)S(1)} %get-tuple-element.56), channel_id=1, source_target_pairs={{17,0},{5,1},{6,2},{7,3},{18,17},{22,5},{10,6},{11,7},{19,18},{23,... | collective-permute-start | bytes 221192 | tf_op jit(solution)/shard_map/ppermute | solution.py:56
  43.2 0.6 collective-permute-done.8.above
  43.8 3.8 %collective-permute-done.9.below = bf16[12,24,128]{2,1,0:T(8,128)(2,1)S(1)} collective-permute-done((bf16[12,24,128]{2,1,0:T(8,128)(2,1)S(1)}, bf16[12,24,128]{2,1,0:T(8,128)(2,1)S(1)}, u32[]{:S(2)}, u32[]{:S(2)}) %collective-permute-start.9) | collective-permute-done | bytes 73760 | tf_op jit(solution)/shard_map/ppermute | solution.py:56
  47.6 0.1 maximum_bitcast_fusion
  47.7 3.5 %collective-permute-start.10 = (bf16[12,44,128]{2,0,1:T(8,128)(2,1)S(1)}, bf16[12,44,128]{2,0,1:T(8,128)(2,1)S(1)}, u32[]{:S(2)}, u32[]{:S(2)}) collective-permute-start(bf16[12,44,128]{2,0,1:T(8,128)(2,1)S(1)} %maximum_bitcast_fusion), channel_id=1, source_target_pairs={{0,1},{1,2},{2,3},{17,5},{5,6},{6,7},{18,22},{22,10},{10,11},{19,2... | collective-permute-start | bytes 405512 | tf_op jit(solution)/shard_map/ppermute | solution.py:56
  51.3 0.1 maximum_bitcast_fusion.1
  51.4 1.3 %collective-permute-start.11 = (bf16[12,44,128]{2,0,1:T(8,128)(2,1)S(1)}, bf16[12,44,128]{2,0,1:T(8,128)(2,1)S(1)}, u32[]{:S(2)}, u32[]{:S(2)}) collective-permute-start(bf16[12,44,128]{2,0,1:T(8,128)(2,1)S(1)} %maximum_bitcast_fusion.1), channel_id=1, source_target_pairs={{1,0},{2,1},{3,2},{5,17},{6,5},{7,6},{22,18},{10,22},{11,10},{23,1... | collective-permute-start | bytes 405512 | tf_op jit(solution)/shard_map/ppermute | solution.py:56
  52.7 0.5 second_sums.1
  53.2 1.1 %collective-permute-done.10 = bf16[12,44,128]{2,0,1:T(8,128)(2,1)S(1)} collective-permute-done((bf16[12,44,128]{2,0,1:T(8,128)(2,1)S(1)}, bf16[12,44,128]{2,0,1:T(8,128)(2,1)S(1)}, u32[]{:S(2)}, u32[]{:S(2)}) %collective-permute-start.10) | collective-permute-done | bytes 135200 | tf_op jit(solution)/shard_map/ppermute | solution.py:56
  54.3 4.5 %collective-permute-done.11 = bf16[12,44,128]{2,0,1:T(8,128)(2,1)S(1)} collective-permute-done((bf16[12,44,128]{2,0,1:T(8,128)(2,1)S(1)}, bf16[12,44,128]{2,0,1:T(8,128)(2,1)S(1)}, u32[]{:S(2)}, u32[]{:S(2)}) %collective-permute-start.11) | collective-permute-done | bytes 135200 | tf_op jit(solution)/shard_map/ppermute | solution.py:56
  58.8 3.1 %backward.1 = (f32[656,128]{1,0:T(8,128)S(1)}, bf16[656,128]{1,0:T(8,128)(2,1)S(1)}, bf16[3,28,32,128]{3,2,1,0:T(8,128)(2,1)S(1)}, bf16[24,24,128]{2,1,0:T(8,128)(2,1)S(1)}) custom-call(bf16[24,32,128]{2,1,0:T(8,128)(2,1)S(1)} %get-tuple-element.53.grad_pre, bf16[24,32,128]{2,1,0:T(8,128)(2,1)S(1)} %get-tuple-element.54.grad_tile, ...), custom_call_target="tpu_custom_call" | custom-call | flops 528482304 | bytes 4337664 | tf_op jit(solution)/shard_map/backward/pallas_call | solution.py:421
  61.9 1.9 %collective-permute-start.12 = (bf16[656,128]{1,0:T(8,128)(2,1)S(1)}, bf16[656,128]{1,0:T(8,128)(2,1)S(1)}, u32[]{:S(2)}, u32[]{:S(2)}) collective-permute-start(bf16[656,128]{1,0:T(8,128)(2,1)S(1)} %get-tuple-element.69), channel_id=1, source_target_pairs={{0,16},{16,0},{1,17},{17,1},{2,18},{18,2},{3,19},{19,3},{4,20},{20... | collective-permute-start | bytes 503816 | tf_op jit(solution)/shard_map/ppermute | solution.py:575
  63.8 0.9 input.1
  64.7 0.1 collective-permute-done.12.other
  64.8 0.7 pair.1
  65.5 7.1 %all-to-all-start = ((bf16[16,48,128]{2,1,0:T(8,128)(2,1)}), bf16[16,48,128]{2,1,0:T(8,128)(2,1)S(1)}, u32[]{:S(2)}, u32[]{:S(2)}) async-start(bf16[16,48,128]{2,1,0:T(8,128)(2,1)} %pair.1), calls=%async_computation | async-start | bytes 393216 | tf_op jit(solution)/shard_map/all_to_all | solution.py:585
  72.7 0.7 collective-permute-start.13
  73.3 8.8 %all-to-all-done.parts = bf16[16,48,128]{2,1,0:T(8,128)(2,1)S(1)} async-done(((bf16[16,48,128]{2,1,0:T(8,128)(2,1)}), bf16[16,48,128]{2,1,0:T(8,128)(2,1)S(1)}, u32[]{:S(2)}, u32[]{:S(2)}) %all-to-all-start) | async-done | bytes 196640 | tf_op jit(solution)/shard_map/all_to_all | solution.py:585
  82.2 0.0 collective-permute-done.13.moved
  82.2 13.7 %all_to_all.10 = bf16[16,40,128]{2,1,0:T(8,128)(2,1)S(1)} all-to-all(bf16[16,40,128]{2,1,0:T(8,128)(2,1)S(1)} %get-tuple-element.76), channel_id=1, replica_groups=mesh['segment'=2,'row'=4,'col'=4] {'row','col'}, dimensions={0} | all-to-all | bytes 327680 | tf_op jit(solution)/shard_map/all_to_all | solution.py:597
  95.9 0.8 outputs.1
  (20 shorter events, 0.4 us)
Async XLA Ops:
  0.6 10.3 %copy-start = (bf16[1,9,128,64]{2,3,1,0:T(8,128)(2,1)S(1)}, bf16[1,9,128,64]{2,3,1,0:T(8,128)(2,1)}, u32[]{:S(2)}) copy-start(bf16[1,9,128,64]{2,3,1,0:T(8,128)(2,1)} %param.7) | copy-start | bytes 442372
  0.6 11.0 %collective-permute-start = (bf16[24,24,128]{2,1,0:T(8,128)(2,1)}, bf16[24,24,128]{2,1,0:T(8,128)(2,1)S(1)}, u32[]{:S(2)}, u32[]{:S(2)}) collective-permute-start(bf16[24,24,128]{2,1,0:T(8,128)(2,1)} %bitcast.56), channel_id=1, source_target_pairs={{0,0},{1,1},{2,2},{3,3},{4,17},{5,5},{6,6},{7,7},{8,18},{9,22},{10... | collective-permute-start | bytes 442376 | tf_op jit(solution)/shard_map/ppermute | solution.py:56
  2.3 8.6 %copy-start.1 = (bf16[1,64,128]{2,1,0:T(8,128)(2,1)S(1)}, bf16[1,64,128]{2,1,0:T(8,128)(2,1)}, u32[]{:S(2)}) copy-start(bf16[1,64,128]{2,1,0:T(8,128)(2,1)} %param.9) | copy-start | bytes 49156
  3.2 9.6 %collective-permute-start.2 = (bf16[10,24,128]{2,1,0:T(8,128)(2,1)S(1)}, bf16[10,24,128]{2,1,0:T(8,128)(2,1)S(1)}, u32[]{:S(2)}, u32[]{:S(2)}) collective-permute-start(bf16[10,24,128]{2,1,0:T(8,128)(2,1)S(1)} %get-tuple-element.88), channel_id=1, source_target_pairs={{4,0},{5,1},{6,2},{7,3},{8,17},{9,5},{10,6},{11,7},{12,18},{13,22}... | collective-permute-start | bytes 184328 | tf_op jit(solution)/shard_map/ppermute | solution.py:56
  4.5 8.2 %collective-permute-start.1 = (bf16[10,24,128]{2,1,0:T(8,128)(2,1)S(1)}, bf16[10,24,128]{2,1,0:T(8,128)(2,1)S(1)}, u32[]{:S(2)}, u32[]{:S(2)}) collective-permute-start(bf16[10,24,128]{2,1,0:T(8,128)(2,1)S(1)} %get-tuple-element.89), channel_id=1, source_target_pairs={{0,17},{1,5},{2,6},{3,7},{4,18},{5,22},{6,10},{7,11},{8,19},{9,23}... | collective-permute-start | bytes 184328 | tf_op jit(solution)/shard_map/ppermute | solution.py:56
  10.9 0.7 copy-start.2
  11.6 6.6 %collective-permute-start.5 = (bf16[656,128]{1,0:T(8,128)(2,1)S(1)}, bf16[656,128]{1,0:T(8,128)(2,1)S(1)}, u32[]{:S(2)}, u32[]{:S(2)}) collective-permute-start(bf16[656,128]{1,0:T(8,128)(2,1)S(1)} %fusion.1.mine), channel_id=1, source_target_pairs={{0,16},{16,0},{1,17},{17,1},{2,18},{18,2},{3,19},{19,3},{4,20},{20... | collective-permute-start | bytes 503816 | tf_op jit(solution)/shard_map/ppermute | solution.py:457
  11.8 5.7 %copy-start.3 = (bf16[1,24,24,128]{3,2,1,0:T(8,128)(2,1)S(1)}, bf16[1,24,24,128]{3,2,1,0:T(8,128)(2,1)}, u32[]{:S(2)}) copy-start(bf16[1,24,24,128]{3,2,1,0:T(8,128)(2,1)} %param.6) | copy-start | bytes 442372
  12.8 6.3 %collective-permute-start.3 = (bf16[10,44,128]{2,0,1:T(8,128)(2,1)S(1)}, bf16[10,44,128]{2,0,1:T(8,128)(2,1)S(1)}, u32[]{:S(2)}, u32[]{:S(2)}) collective-permute-start(bf16[10,44,128]{2,0,1:T(8,128)(2,1)S(1)} %get-tuple-element.43), channel_id=1, source_target_pairs={{0,1},{1,2},{2,3},{17,5},{5,6},{6,7},{18,22},{22,10},{10,11},{19,2... | collective-permute-start | bytes 337928 | tf_op jit(solution)/shard_map/ppermute | solution.py:56
  16.2 7.5 %collective-permute-start.4 = (bf16[10,44,128]{2,0,1:T(8,128)(2,1)S(1)}, bf16[10,44,128]{2,0,1:T(8,128)(2,1)S(1)}, u32[]{:S(2)}, u32[]{:S(2)}) collective-permute-start(bf16[10,44,128]{2,0,1:T(8,128)(2,1)S(1)} %get-tuple-element.44), channel_id=1, source_target_pairs={{1,0},{2,1},{3,2},{5,17},{6,5},{7,6},{22,18},{10,22},{11,10},{23,1... | collective-permute-start | bytes 337928 | tf_op jit(solution)/shard_map/ppermute | solution.py:56
  17.5 9.7 %collective-permute-start.6 = (bf16[24,24,128]{2,1,0:T(8,128)(2,1)S(1)}, bf16[24,24,128]{2,1,0:T(8,128)(2,1)S(1)}, u32[]{:S(2)}, u32[]{:S(2)}) collective-permute-start(bf16[24,24,128]{2,1,0:T(8,128)(2,1)S(1)} %bitcast.59), channel_id=1, source_target_pairs={{0,0},{1,1},{2,2},{3,3},{4,17},{5,5},{6,6},{7,7},{8,18},{9,22},{10... | collective-permute-start | bytes 442376 | tf_op jit(solution)/shard_map/ppermute | solution.py:56
  27.3 0.7 collective-permute-start.7
  30.0 13.8 %collective-permute-start.8 = (bf16[12,24,128]{2,1,0:T(8,128)(2,1)S(1)}, bf16[12,24,128]{2,1,0:T(8,128)(2,1)S(1)}, u32[]{:S(2)}, u32[]{:S(2)}) collective-permute-start(bf16[12,24,128]{2,1,0:T(8,128)(2,1)S(1)} %get-tuple-element.55), channel_id=1, source_target_pairs={{0,17},{1,5},{2,6},{3,7},{17,18},{5,22},{6,10},{7,11},{18,19},{22,... | collective-permute-start | bytes 221192 | tf_op jit(solution)/shard_map/ppermute | solution.py:56
  41.9 5.7 %collective-permute-start.9 = (bf16[12,24,128]{2,1,0:T(8,128)(2,1)S(1)}, bf16[12,24,128]{2,1,0:T(8,128)(2,1)S(1)}, u32[]{:S(2)}, u32[]{:S(2)}) collective-permute-start(bf16[12,24,128]{2,1,0:T(8,128)(2,1)S(1)} %get-tuple-element.56), channel_id=1, source_target_pairs={{17,0},{5,1},{6,2},{7,3},{18,17},{22,5},{10,6},{11,7},{19,18},{23,... | collective-permute-start | bytes 221192 | tf_op jit(solution)/shard_map/ppermute | solution.py:56
  47.7 6.5 %collective-permute-start.10 = (bf16[12,44,128]{2,0,1:T(8,128)(2,1)S(1)}, bf16[12,44,128]{2,0,1:T(8,128)(2,1)S(1)}, u32[]{:S(2)}, u32[]{:S(2)}) collective-permute-start(bf16[12,44,128]{2,0,1:T(8,128)(2,1)S(1)} %maximum_bitcast_fusion), channel_id=1, source_target_pairs={{0,1},{1,2},{2,3},{17,5},{5,6},{6,7},{18,22},{22,10},{10,11},{19,2... | collective-permute-start | bytes 405512 | tf_op jit(solution)/shard_map/ppermute | solution.py:56
  51.4 7.4 %collective-permute-start.11 = (bf16[12,44,128]{2,0,1:T(8,128)(2,1)S(1)}, bf16[12,44,128]{2,0,1:T(8,128)(2,1)S(1)}, u32[]{:S(2)}, u32[]{:S(2)}) collective-permute-start(bf16[12,44,128]{2,0,1:T(8,128)(2,1)S(1)} %maximum_bitcast_fusion.1), channel_id=1, source_target_pairs={{1,0},{2,1},{3,2},{5,17},{6,5},{7,6},{22,18},{10,22},{11,10},{23,1... | collective-permute-start | bytes 405512 | tf_op jit(solution)/shard_map/ppermute | solution.py:56
  61.9 3.0 %collective-permute-start.12 = (bf16[656,128]{1,0:T(8,128)(2,1)S(1)}, bf16[656,128]{1,0:T(8,128)(2,1)S(1)}, u32[]{:S(2)}, u32[]{:S(2)}) collective-permute-start(bf16[656,128]{1,0:T(8,128)(2,1)S(1)} %get-tuple-element.69), channel_id=1, source_target_pairs={{0,16},{16,0},{1,17},{17,1},{2,18},{18,2},{3,19},{19,3},{4,20},{20... | collective-permute-start | bytes 503816 | tf_op jit(solution)/shard_map/ppermute | solution.py:575
  65.5 16.6 %all-to-all-start = ((bf16[16,48,128]{2,1,0:T(8,128)(2,1)}), bf16[16,48,128]{2,1,0:T(8,128)(2,1)S(1)}, u32[]{:S(2)}, u32[]{:S(2)}) async-start(bf16[16,48,128]{2,1,0:T(8,128)(2,1)} %pair.1), calls=%async_computation | async-start | bytes 393216 | tf_op jit(solution)/shard_map/all_to_all | solution.py:585
  72.7 9.5 %collective-permute-start.13 = (bf16[24,24,128]{2,1,0:T(8,128)(2,1)S(1)}, bf16[24,24,128]{2,1,0:T(8,128)(2,1)S(1)}, u32[]{:S(2)}, u32[]{:S(2)}) collective-permute-start(bf16[24,24,128]{2,1,0:T(8,128)(2,1)S(1)} %input.1), channel_id=1, source_target_pairs={{0,0},{1,1},{2,2},{3,3},{17,4},{5,5},{6,6},{7,7},{18,8},{22,9},{10... | collective-permute-start | bytes 442376 | tf_op jit(solution)/shard_map/ppermute | solution.py:56

commit v14 on v11

--- a/solution.py
+++ b/solution.py
@@ -61,12 +61,11 @@
     return (batch * number + r) * number + c
 
 
-def bring(x, down=0):
-    number = lax.axis_size("row")
-
+def bring(x, turn=None):
     def pair(batch, r, c):
-        if 0 <= r + down < number:
-            return stored(batch, r, c), home(batch, r + down, c)
+        row = r if turn is None else partner(r, turn)
+        if row is not None:
+            return stored(batch, r, c), home(batch, row, c)
 
     return permute(x, pair)
 
@@ -75,15 +74,31 @@
     return permute(x, lambda m, r, c: (home(m, r, c), stored(m, r, c)))
 
 
-def send(x, to):
-    number = lax.axis_size("row")
-
+def swap(x):
+    return permute(x, lambda m, r, c: (home(m, r, c), home(m, c, r)))
+
+
+def partner(index, turn):
+    other = index + 1 if (index + turn) % 2 == 0 else index - 1
+    return other if 0 <= other < lax.axis_size("row") else None
+
+
+def exchange(x, axis, turn):
     def pair(batch, r, c):
-        row, col = to(r, c)
-        if 0 <= row < number and 0 <= col < number:
-            return home(batch, r, c), home(batch, row, col)
+        other = partner(c if axis else r, turn)
+        if other is not None:
+            return home(batch, r, c), home(batch, r, other) if axis else home(batch, other, c)
 
     return permute(x, pair)
+
+
+def sends_last(axis, turn):
+    return lax.rem(place()[axis] + turn, 2) == 0
+
+
+def around(axis, got):
+    even = sends_last(axis, 0)
+    return jnp.where(even, got[1], got[0]), jnp.where(even, got[0], got[1])
 
 
 def inside(shape, side, width, top):
@@ -193,10 +208,10 @@
 
 def middle_kernel(
     kept, other, w_second, b_second, p_second,
-    gate_second, hidden_pairs, hidden_last, bottle_second, grad_tile, grad_pre, above, below,
+    gate_second, hidden_pairs, hidden_last, bottle_second, grad_tile, grad_pre, first_turn, second_turn,
     current, padded, pre_second,
 ):
-    side, channels, span = above.shape[1], kept.shape[2], kept.shape[1]
+    side, channels, span = first_turn.shape[1], kept.shape[2], kept.shape[1]
     first, second, inner = FIRST_DILATION, SECOND_DILATION, bottle_second.shape[2]
     near, small = gate_second.shape[:2]
     turned = jnp.swapaxes(other[:span].astype(F32), 0, 1)
@@ -225,9 +240,11 @@
     grad = dot(branch.reshape(side * small, channels), p_second[...]).reshape(side, small, 2 * inner)
     grad = jnp.where(pre_second[...] > 0, grad, 0)
     grad_pre[...] = grad.astype(BF16)
-    grad, branch = grad[:, :side].astype(BF16), padded[:, :side].astype(BF16)
-    above[:HALO], above[HALO:] = grad[:HALO], branch[:first]
-    below[:HALO], below[HALO:] = grad[side - HALO :], branch[side - first :]
+    even = sends_last(0, 0)
+    for rows, value, width in ((slice(0, HALO), grad, HALO), (slice(HALO, HALO + first), padded[...], first)):
+        head, tail = value[:width, :side], value[side - width :, :side]
+        first_turn[rows] = jnp.where(even, tail, head).astype(BF16)
+        second_turn[rows] = jnp.where(even, head, tail).astype(BF16)
 
 
 def weight_sums(rows, ends, grad_pre, hidden, bottle, grad_tile):
@@ -407,11 +424,12 @@
     ends[...] = total[share:]
 
 
-def outputs_kernel(rows, ends, conv_gradient, bias_gradient, out_gradient):
+def outputs_kernel(rows, ends, moved, conv_gradient, bias_gradient, out_gradient, input_gradient):
     count, inner = conv_gradient.shape[0], out_gradient.shape[0]
     conv_gradient[...] = rows[:count].astype(F32)
     out_gradient[...] = rows[count : count + inner].astype(F32)
     bias_gradient[...] = ends[:1, :inner]
+    input_gradient[...] = moved[...]
 
 
 def call(kernel, name, outs, scratch, flops, *operands):
@@ -436,17 +454,23 @@
 
     brought = bring(jnp.concatenate([activations[0], cotangent[0]]))
     tile = brought[:side]
-    above = bring(activations[0, side - HALO :], 1)
-    below = bring(activations[0, :HALO], -1)
-
-    def columns(low, high):
-        strip = jnp.pad(jnp.swapaxes(tile[:, low:high], 0, 1), ((0, 0), (HALO, HALO), (0, 0)))
+    stored_even = lax.rem(lax.axis_index("row"), 2) == 0
+    ends = (activations[0, side - HALO :], activations[0, :HALO])
+    got = [bring(jnp.where(stored_even, *ends), 0), bring(jnp.where(stored_even, *ends[::-1]), 1)]
+    above, below = around(0, got)
+
+    def columns(turn):
+        def chosen(x):
+            return jnp.swapaxes(jnp.where(sends_last(1, turn), x[:, side - HALO :], x[:, :HALO]), 0, 1)
+
+        strip = jnp.pad(chosen(tile), ((0, 0), (HALO, HALO), (0, 0)))
         strip = lax.optimization_barrier(strip)
-        strip = lax.dynamic_update_slice(strip, jnp.swapaxes(above[:, low:high], 0, 1), (0, 0, 0))
-        return lax.dynamic_update_slice(strip, jnp.swapaxes(below[:, low:high], 0, 1), (0, HALO + side, 0))
-
-    left = send(columns(side - HALO, side), lambda r, c: (r, c + 1))
-    right = send(columns(0, HALO), lambda r, c: (r, c - 1))
+        for row_turn in (0, 1):
+            at = jnp.where(sends_last(0, row_turn), HALO + side, 0)
+            strip = lax.dynamic_update_slice(strip, chosen(got[row_turn]), (0, at, 0))
+        return strip
+
+    left, right = around(1, [exchange(columns(turn), 1, turn) for turn in (0, 1)])
 
     bias_rows = jnp.pad(conv_bias, ((0, 15), (0, channels - inner)))
     packed = jnp.concatenate(
@@ -491,8 +515,8 @@
         *(brought, above, below, jnp.swapaxes(left, 0, 1), jnp.swapaxes(right, 0, 1)),
         *(w_first, b_first, p_first),
     )
-    other = send(kept, lambda r, c: (c, r))
-    gate_second, hidden_pairs, hidden_last, bottle_second, grad_tile, grad_pre, strip_above, strip_below = call(
+    other = swap(kept)
+    gate_second, hidden_pairs, hidden_last, bottle_second, grad_tile, grad_pre, *strips = call(
         middle_kernel,
         "middle",
         [
@@ -514,8 +538,7 @@
         *(kept, other, w_second, b_second, p_second),
     )
 
-    above = send(strip_below, lambda r, c: (r + 1, c))
-    below = send(strip_above, lambda r, c: (r - 1, c))
+    above, below = around(0, [exchange(strips[turn], 0, turn) for turn in (0, 1)])
     rows_second, ends_second = call(
         second_sums_kernel,
         "second_sums",
@@ -525,15 +548,16 @@
         *(grad_pre, hidden_pairs, hidden_last, bottle_second, grad_tile),
     )
 
-    def columns(low, high, low_branch, high_branch):
-        grads = jnp.concatenate([above[:HALO, low:high], grad_pre[:, low:high], below[:HALO, low:high]])
-        here = slice(low_branch, high_branch)
-        branches = jnp.concatenate([above[HALO:, here], grad_tile[:, here], below[HALO:, here]])
+    def columns(turn):
+        def chosen(x, width):
+            return jnp.where(sends_last(1, turn), x[:, side - width : side], x[:, :width])
+
+        grads = jnp.concatenate([chosen(x, HALO) for x in (above[:HALO], grad_pre, below[:HALO])])
+        branches = jnp.concatenate([chosen(x, first) for x in (above[HALO:], grad_tile, below[HALO:])])
         branches = jnp.pad(branches, ((second, second), (0, 0), (0, 0)))
         return jnp.swapaxes(jnp.concatenate([grads, branches], axis=1), 0, 1)
 
-    left = send(columns(side - HALO, side, side - first, side), lambda r, c: (r, c + 1))
-    right = send(columns(0, HALO, 0, first), lambda r, c: (r, c - 1))
+    left, right = around(1, [exchange(columns(turn), 1, turn) for turn in (0, 1)])
     left, right = jnp.swapaxes(left, 0, 1), jnp.swapaxes(right, 0, 1)
 
     devices = number * number
@@ -592,13 +616,18 @@
     )
     rows, _ = lax.optimization_barrier((rows, input_gradient))
     rows = lax.all_to_all(rows, GRID, 0, 0, tiled=True).reshape(devices * share, channels)
-    conv_gradient, bias_gradient, out_gradient = call(
+    conv_gradient, bias_gradient, out_gradient, input_gradient = call(
         outputs_kernel,
         "outputs",
-        [((9 * inner, channels), F32), ((1, inner), F32), ((inner, channels), F32)],
+        [
+            ((9 * inner, channels), F32),
+            ((1, inner), F32),
+            ((inner, channels), F32),
+            ((side, side, channels), BF16),
+        ],
         [],
         rows.size,
-        *(rows, ends),
+        *(rows, ends, input_gradient),
     )
     conv_gradient = jnp.swapaxes(conv_gradient.reshape(1, 9, inner, channels), 2, 3)
     return (input_gradient[None], conv_gradient, bias_gradient, out_gradient[None])

time: 96.9 us -> 88.3 us (0.911)
  blocking collectives: 0 us -> 13.7 us
  starting transfers between devices: 48 us -> 35.5 us
  waiting for transfers between devices: 31.5 us -> 23 us
    all_to_all x0 -> x1, blocking collectives: none -> 13.7 us  [local(): lax.all_to_all(rows, GRID, 0, 0, tiled=True)]
    all_to_all x1 -> x0, waiting for transfers between devices: 8.81 us -> none  [local(): lax.all_to_all(rows, GRID, 0, 0, tiled=True)]
    ppermute x11, starting transfers between devices: 34.4 us -> 28.9 us  [permute(): return lax.ppermute(x, ALL, [found for found in pairs if found is not None])]
    all_to_all x1 -> x0, starting transfers between devices: 4.45 us -> none  [local(): lax.all_to_all(rows, GRID, 0, 0, tiled=True)]
    all_to_all x1, starting transfers between devices: 8.22 us -> 5.48 us  [local(): parts = lax.all_to_all(parts, GRID, 0, 0, tiled=True)]
  transfers between devices with their start and end apart: 15 -> 14, of which waited for: 10 -> 6; matrix products, arithmetic and copies ran while one was open for 0% -> 0% of each run, Pallas kernels for 3% -> 2%
where the time goes in v14:
time: 88.3 us; the launch traced here: 87.5 us
  starting transfers between devices  35.5 us (40%)
  waiting for transfers between devices  23 us (26%)
  blocking collectives  13.7 us (16%)
  Pallas kernels  12 us (14%)
  other arithmetic  1.57 us (2%)
  between operations  1.02 us (1%)
    ppermute x11, starting transfers between devices, permute(): return lax.ppermute(x, ALL, [found for found in pairs if found is not None])  28.9 us
    ppermute x11, waiting for transfers between devices, permute(): return lax.ppermute(x, ALL, [found for found in pairs if found is not None])  14.1 us
    all_to_all x1, blocking collectives, local(): lax.all_to_all(rows, GRID, 0, 0, tiled=True)  13.7 us
    pallas_call x9, Pallas kernels, call(): pl.pallas_call(kernel, name=name, out_shape=outs, scratch_shapes=[pltpu.V...  12 us
    all_to_all x1, waiting for transfers between devices, local(): parts = lax.all_to_all(parts, GRID, 0, 0, tiled=True)  8.8 us
    all_to_all x1, starting transfers between devices, local(): parts = lax.all_to_all(parts, GRID, 0, 0, tiled=True)  5.48 us
  transfers between devices with their start and end apart: 14, of which 6 were waited for; matrix products, arithmetic and copies ran while one was open for 0% of the time, Pallas kernels for 2%

profile of v14, /device:TPU:0, one launch (start us, length us, event | category | flops | bytes accessed | tf_op | source)
XLA Modules:
  0.0 87.5 jit_solution(5906329557287240623)
XLA Ops:
  0.6 0.0 copy-start
  0.6 1.0 %pad_maximum_fusion = bf16[48,24,128]{2,1,0:T(8,128)(2,1)S(1)} fusion(bf16[24,24,128]{2,1,0:T(8,128)(2,1)} %bitcast.49, bf16[24,24,128]{2,1,0:T(8,128)(2,1)} %bitcast.47), kind=kLoop, calls=%fused_computation.2 | loop fusion | flops 147456 | bytes 589824 | tf_op jit(solution)/shard_map/concatenate | solution.py:455
  1.7 0.0 copy-start.1
  1.7 0.8 collective-permute-start
  2.5 0.0 copy-done
  2.5 0.0 copy-start.2
  2.6 5.4 %collective-permute-start.2 = (bf16[10,24,128]{2,1,0:T(8,128)(2,1)S(1)}, bf16[10,24,128]{2,1,0:T(8,128)(2,1)S(1)}, u32[]{:S(2)}, u32[]{:S(2)}) collective-permute-start(bf16[10,24,128]{2,1,0:T(8,128)(2,1)S(1)} %get-tuple-element.88), channel_id=1, source_target_pairs={{0,17},{1,5},{2,6},{3,7},{4,0},{5,1},{6,2},{7,3},{8,19},{9,23},{10... | collective-permute-start | bytes 184328 | tf_op jit(solution)/shard_map/ppermute | solution.py:56
  8.0 0.7 collective-permute-start.1
  8.6 0.0 copy-start.3
  8.7 0.0 copy-done.1
  8.7 0.0 copy-done.2
  8.7 0.6 copy-done.3
  9.3 0.1 collective-permute-start.5
  9.4 0.0 collective-permute-done.brought
  9.6 0.4 collective-permute-done.2
  10.0 0.0 collective-permute-done.1
  10.1 0.6 collective-permute-start.4
  10.7 0.7 collective-permute-start.3
  11.4 0.0 collective-permute-done.5.theirs
  11.4 0.4 weights.1
  11.8 8.7 %collective-permute-done.4 = bf16[10,44,128]{2,0,1:T(8,128)(2,1)S(1)} collective-permute-done((bf16[10,44,128]{2,0,1:T(8,128)(2,1)S(1)}, bf16[10,44,128]{2,0,1:T(8,128)(2,1)S(1)}, u32[]{:S(2)}, u32[]{:S(2)}) %collective-permute-start.4) | collective-permute-done | bytes 112672 | tf_op jit(solution)/shard_map/ppermute | solution.py:56
  20.5 0.0 collective-permute-done.3
  20.5 3.5 %own_branch.1 = (bf16[64,40,128]{2,1,0:T(8,128)(2,1)S(1)}, bf16[28,32,128]{2,1,0:T(8,128)(2,1)S(1)}, bf16[24,32,64]{2,1,0:T(8,128)(2,1)S(1)}, bf16[3,28,32,128]{3,2,1,0:T(8,128)(2,1)S(1)}) custom-call(bf16[48,24,128]{2,1,0:T(8,128)(2,1)S(1)} %collective-permute-done.brought, bf16[10,24,128]{2,1,0:T(8,128)(2,1)S(1)} %get-tuple-element.91.above, ...), custom_call_target="tpu_custom_call" | custom-call | flops 314572800 | bytes 2478336 | tf_op jit(solution)/shard_map/own_branch/pallas_call | solution.py:438
  24.1 0.7 collective-permute-start.6
  24.8 0.0 collective-permute-done.6.other
  24.8 2.0 %middle.1 = (bf16[28,32,128]{2,1,0:T(8,128)(2,1)S(1)}, bf16[40,32,256]{2,1,0:T(8,128)(2,1)S(1)}, bf16[48,32,256]{2,1,0:T(8,128)(2,1)S(1)}, bf16[24,32,64]{2,1,0:...) custom-call(bf16[64,40,128]{2,1,0:T(8,128)(2,1)S(1)} %get-tuple-elem, ...), custom_call_target="tpu_custom_call" | custom-call | flops 301989888 | bytes 3949056 | tf_op jit(solution)/shard_map/middle/pallas_call | solution.py:438
  26.8 0.7 collective-permute-start.7
  27.5 10.3 %collective-permute-start.8 = (bf16[12,24,128]{2,1,0:T(8,128)(2,1)S(1)}, bf16[12,24,128]{2,1,0:T(8,128)(2,1)S(1)}, u32[]{:S(2)}, u32[]{:S(2)}) collective-permute-start(bf16[12,24,128]{2,1,0:T(8,128)(2,1)S(1)} %get-tuple-element.50), channel_id=1, source_target_pairs={{0,17},{1,5},{2,6},{3,7},{17,0},{5,1},{6,2},{7,3},{18,19},{22,23},... | collective-permute-start | bytes 221192 | tf_op jit(solution)/shard_map/ppermute | solution.py:56
  37.9 0.0 collective-permute-done.7
  37.9 1.9 %collective-permute-done.8 = bf16[12,24,128]{2,1,0:T(8,128)(2,1)S(1)} collective-permute-done((bf16[12,24,128]{2,1,0:T(8,128)(2,1)S(1)}, bf16[12,24,128]{2,1,0:T(8,128)(2,1)S(1)}, u32[]{:S(2)}, u32[]{:S(2)}) %collective-permute-start.8) | collective-permute-done | bytes 73760 | tf_op jit(solution)/shard_map/ppermute | solution.py:56
  40.0 0.1 maximum_bitcast_fusion
  40.1 0.7 collective-permute-start.9
  40.8 0.1 maximum_bitcast_fusion.1
  40.8 7.7 %collective-permute-start.10 = (bf16[12,44,128]{2,0,1:T(8,128)(2,1)S(1)}, bf16[12,44,128]{2,0,1:T(8,128)(2,1)S(1)}, u32[]{:S(2)}, u32[]{:S(2)}) collective-permute-start(bf16[12,44,128]{2,0,1:T(8,128)(2,1)S(1)} %maximum_bitcast_fusion.1), channel_id=1, source_target_pairs={{0,1},{1,0},{2,3},{3,2},{17,5},{5,17},{6,7},{7,6},{18,22},{22,18},... | collective-permute-start | bytes 405512 | tf_op jit(solution)/shard_map/ppermute | solution.py:56
  48.6 0.5 second_sums.1
  49.1 0.0 collective-permute-done.9
  49.1 3.0 %collective-permute-done.10 = bf16[12,44,128]{2,0,1:T(8,128)(2,1)S(1)} collective-permute-done((bf16[12,44,128]{2,0,1:T(8,128)(2,1)S(1)}, bf16[12,44,128]{2,0,1:T(8,128)(2,1)S(1)}, u32[]{:S(2)}, u32[]{:S(2)}) %collective-permute-start.10) | collective-permute-done | bytes 135200 | tf_op jit(solution)/shard_map/ppermute | solution.py:56
  52.1 3.1 %backward.1 = (f32[656,128]{1,0:T(8,128)S(1)}, bf16[656,128]{1,0:T(8,128)(2,1)S(1)}, bf16[3,28,32,128]{3,2,1,0:T(8,128)(2,1)S(1)}, bf16[24,24,128]{2,1,0:T(8,128)(2,1)S(1)}) custom-call(bf16[24,32,128]{2,1,0:T(8,128)(2,1)S(1)} %get-tuple-element.47.grad_pre, bf16[24,32,128]{2,1,0:T(8,128)(2,1)S(1)} %get-tuple-element.48.grad_tile, ...), custom_call_target="tpu_custom_call" | custom-call | flops 528482304 | bytes 4337664 | tf_op jit(solution)/shard_map/backward/pallas_call | solution.py:438
  55.2 1.0 %collective-permute-start.11 = (bf16[656,128]{1,0:T(8,128)(2,1)S(1)}, bf16[656,128]{1,0:T(8,128)(2,1)S(1)}, u32[]{:S(2)}, u32[]{:S(2)}) collective-permute-start(bf16[656,128]{1,0:T(8,128)(2,1)S(1)} %get-tuple-element.63), channel_id=1, source_target_pairs={{0,16},{16,0},{1,17},{17,1},{2,18},{18,2},{3,19},{19,3},{4,20},{20... | collective-permute-start | bytes 503816 | tf_op jit(solution)/shard_map/ppermute | solution.py:596
  56.2 0.9 %input.1 = bf16[24,24,128]{2,1,0:T(8,128)(2,1)S(1)} custom-call(bf16[3,28,32,128]{3,2,1,0:T(8,128)(2,1)S(1)} %get-tuple-element.64.windows, bf16[24,24,128]{2,1,0:T(8,128)(2,1)S(1)} %get-tuple-element.65.grad_first, bf16[48,24,128]{2,1,0:T(8,128)(2,1)S(1)} %collective-permute-done.brought, bf16[9,128,128]{2,1,0:T(8,128)(2,1)S(1)} %get-tuple-element.66.v_first), custom_call_target="tpu_custom_call" | custom-call | flops 226492416 | bytes 1572864 | tf_op jit(solution)/shard_map/input/pallas_call | solution.py:438
  57.2 0.1 collective-permute-done.11.other
  57.3 0.7 pair.1
  58.0 5.5 %all-to-all-start = ((bf16[16,48,128]{2,1,0:T(8,128)(2,1)}), bf16[16,48,128]{2,1,0:T(8,128)(2,1)S(1)}, u32[]{:S(2)}, u32[]{:S(2)}) async-start(bf16[16,48,128]{2,1,0:T(8,128)(2,1)} %pair.1), calls=%async_computation | async-start | bytes 393216 | tf_op jit(solution)/shard_map/all_to_all | solution.py:606
  63.5 0.7 collective-permute-start.12
  64.1 8.8 %all-to-all-done.parts = bf16[16,48,128]{2,1,0:T(8,128)(2,1)S(1)} async-done(((bf16[16,48,128]{2,1,0:T(8,128)(2,1)}), bf16[16,48,128]{2,1,0:T(8,128)(2,1)S(1)}, u32[]{:S(2)}, u32[]{:S(2)}) %all-to-all-start) | async-done | bytes 196640 | tf_op jit(solution)/shard_map/all_to_all | solution.py:606
  73.0 0.0 collective-permute-done.12.moved
  73.0 13.7 %all_to_all.10 = bf16[16,40,128]{2,1,0:T(8,128)(2,1)S(1)} all-to-all(bf16[16,40,128]{2,1,0:T(8,128)(2,1)S(1)} %get-tuple-element.70), channel_id=1, replica_groups=mesh['segment'=2,'row'=4,'col'=4] {'row','col'}, dimensions={0} | all-to-all | bytes 327680 | tf_op jit(solution)/shard_map/all_to_all | solution.py:618
  86.7 0.8 outputs.1
  (20 shorter events, 0.5 us)
Async XLA Ops:
  0.6 1.9 %copy-start = (bf16[1,24,24,128]{3,2,1,0:T(8,128)(2,1)S(1)}, bf16[1,24,24,128]{3,2,1,0:T(8,128)(2,1)}, u32[]{:S(2)}) copy-start(bf16[1,24,24,128]{3,2,1,0:T(8,128)(2,1)} %param.5) | copy-start | bytes 442372
  1.7 7.0 %copy-start.1 = (bf16[1,9,128,64]{2,3,1,0:T(8,128)(2,1)S(1)}, bf16[1,9,128,64]{2,3,1,0:T(8,128)(2,1)}, u32[]{:S(2)}) copy-start(bf16[1,9,128,64]{2,3,1,0:T(8,128)(2,1)} %param.7) | copy-start | bytes 442372
  1.7 7.7 %collective-permute-start = (bf16[48,24,128]{2,1,0:T(8,128)(2,1)S(1)}, bf16[48,24,128]{2,1,0:T(8,128)(2,1)S(1)}, u32[]{:S(2)}, u32[]{:S(2)}) collective-permute-start(bf16[48,24,128]{2,1,0:T(8,128)(2,1)S(1)} %pad_maximum_fusion), channel_id=1, source_target_pairs={{0,0},{1,1},{2,2},{3,3},{4,17},{5,5},{6,6},{7,7},{8,18},{9,22},{10... | collective-permute-start | bytes 884744 | tf_op jit(solution)/shard_map/ppermute | solution.py:56
  2.5 6.1 %copy-start.2 = (bf16[1,64,128]{2,1,0:T(8,128)(2,1)S(1)}, bf16[1,64,128]{2,1,0:T(8,128)(2,1)}, u32[]{:S(2)}) copy-start(bf16[1,64,128]{2,1,0:T(8,128)(2,1)} %param.9) | copy-start | bytes 49156
  2.6 7.4 %collective-permute-start.2 = (bf16[10,24,128]{2,1,0:T(8,128)(2,1)S(1)}, bf16[10,24,128]{2,1,0:T(8,128)(2,1)S(1)}, u32[]{:S(2)}, u32[]{:S(2)}) collective-permute-start(bf16[10,24,128]{2,1,0:T(8,128)(2,1)S(1)} %get-tuple-element.88), channel_id=1, source_target_pairs={{0,17},{1,5},{2,6},{3,7},{4,0},{5,1},{6,2},{7,3},{8,19},{9,23},{10... | collective-permute-start | bytes 184328 | tf_op jit(solution)/shard_map/ppermute | solution.py:56
  8.0 2.0 %collective-permute-start.1 = (bf16[10,24,128]{2,1,0:T(8,128)(2,1)S(1)}, bf16[10,24,128]{2,1,0:T(8,128)(2,1)S(1)}, u32[]{:S(2)}, u32[]{:S(2)}) collective-permute-start(bf16[10,24,128]{2,1,0:T(8,128)(2,1)S(1)} %get-tuple-element.89), channel_id=1, source_target_pairs={{4,18},{5,22},{6,10},{7,11},{8,17},{9,5},{10,6},{11,7},{20,24},{21... | collective-permute-start | bytes 184328 | tf_op jit(solution)/shard_map/ppermute | solution.py:56
  8.6 0.7 copy-start.3
  9.3 2.1 %collective-permute-start.5 = (bf16[656,128]{1,0:T(8,128)(2,1)S(1)}, bf16[656,128]{1,0:T(8,128)(2,1)S(1)}, u32[]{:S(2)}, u32[]{:S(2)}) collective-permute-start(bf16[656,128]{1,0:T(8,128)(2,1)S(1)} %fusion.1.mine), channel_id=1, source_target_pairs={{0,16},{16,0},{1,17},{17,1},{2,18},{18,2},{3,19},{19,3},{4,20},{20... | collective-permute-start | bytes 503816 | tf_op jit(solution)/shard_map/ppermute | solution.py:479
  10.1 10.4 %collective-permute-start.4 = (bf16[10,44,128]{2,0,1:T(8,128)(2,1)S(1)}, bf16[10,44,128]{2,0,1:T(8,128)(2,1)S(1)}, u32[]{:S(2)}, u32[]{:S(2)}) collective-permute-start(bf16[10,44,128]{2,0,1:T(8,128)(2,1)S(1)} %get-tuple-element.100), channel_id=1, source_target_pairs={{0,1},{1,0},{2,3},{3,2},{17,5},{5,17},{6,7},{7,6},{18,22},{22,18},... | collective-permute-start | bytes 337928 | tf_op jit(solution)/shard_map/ppermute | solution.py:56
  10.7 9.8 %collective-permute-start.3 = (bf16[10,44,128]{2,0,1:T(8,128)(2,1)S(1)}, bf16[10,44,128]{2,0,1:T(8,128)(2,1)S(1)}, u32[]{:S(2)}, u32[]{:S(2)}) collective-permute-start(bf16[10,44,128]{2,0,1:T(8,128)(2,1)S(1)} %get-tuple-element.101), channel_id=1, source_target_pairs={{1,2},{2,1},{5,6},{6,5},{22,10},{10,22},{23,27},{27,23},{4,8},{8,4... | collective-permute-start | bytes 337928 | tf_op jit(solution)/shard_map/ppermute | solution.py:56
  24.1 0.7 collective-permute-start.6
  26.8 11.1 %collective-permute-start.7 = (bf16[12,24,128]{2,1,0:T(8,128)(2,1)S(1)}, bf16[12,24,128]{2,1,0:T(8,128)(2,1)S(1)}, u32[]{:S(2)}, u32[]{:S(2)}) collective-permute-start(bf16[12,24,128]{2,1,0:T(8,128)(2,1)S(1)} %get-tuple-element.49), channel_id=1, source_target_pairs={{17,18},{5,22},{6,10},{7,11},{18,17},{22,5},{10,6},{11,7},{20,24},... | collective-permute-start | bytes 221192 | tf_op jit(solution)/shard_map/ppermute | solution.py:56
  27.5 12.4 %collective-permute-start.8 = (bf16[12,24,128]{2,1,0:T(8,128)(2,1)S(1)}, bf16[12,24,128]{2,1,0:T(8,128)(2,1)S(1)}, u32[]{:S(2)}, u32[]{:S(2)}) collective-permute-start(bf16[12,24,128]{2,1,0:T(8,128)(2,1)S(1)} %get-tuple-element.50), channel_id=1, source_target_pairs={{0,17},{1,5},{2,6},{3,7},{17,0},{5,1},{6,2},{7,3},{18,19},{22,23},... | collective-permute-start | bytes 221192 | tf_op jit(solution)/shard_map/ppermute | solution.py:56
  40.1 9.0 %collective-permute-start.9 = (bf16[12,44,128]{2,0,1:T(8,128)(2,1)S(1)}, bf16[12,44,128]{2,0,1:T(8,128)(2,1)S(1)}, u32[]{:S(2)}, u32[]{:S(2)}) collective-permute-start(bf16[12,44,128]{2,0,1:T(8,128)(2,1)S(1)} %maximum_bitcast_fusion), channel_id=1, source_target_pairs={{1,2},{2,1},{5,6},{6,5},{22,10},{10,22},{23,27},{27,23},{4,8},{8,4... | collective-permute-start | bytes 405512 | tf_op jit(solution)/shard_map/ppermute | solution.py:56
  40.8 11.2 %collective-permute-start.10 = (bf16[12,44,128]{2,0,1:T(8,128)(2,1)S(1)}, bf16[12,44,128]{2,0,1:T(8,128)(2,1)S(1)}, u32[]{:S(2)}, u32[]{:S(2)}) collective-permute-start(bf16[12,44,128]{2,0,1:T(8,128)(2,1)S(1)} %maximum_bitcast_fusion.1), channel_id=1, source_target_pairs={{0,1},{1,0},{2,3},{3,2},{17,5},{5,17},{6,7},{7,6},{18,22},{22,18},... | collective-permute-start | bytes 405512 | tf_op jit(solution)/shard_map/ppermute | solution.py:56
  55.2 2.0 %collective-permute-start.11 = (bf16[656,128]{1,0:T(8,128)(2,1)S(1)}, bf16[656,128]{1,0:T(8,128)(2,1)S(1)}, u32[]{:S(2)}, u32[]{:S(2)}) collective-permute-start(bf16[656,128]{1,0:T(8,128)(2,1)S(1)} %get-tuple-element.63), channel_id=1, source_target_pairs={{0,16},{16,0},{1,17},{17,1},{2,18},{18,2},{3,19},{19,3},{4,20},{20... | collective-permute-start | bytes 503816 | tf_op jit(solution)/shard_map/ppermute | solution.py:596
  58.0 15.0 %all-to-all-start = ((bf16[16,48,128]{2,1,0:T(8,128)(2,1)}), bf16[16,48,128]{2,1,0:T(8,128)(2,1)S(1)}, u32[]{:S(2)}, u32[]{:S(2)}) async-start(bf16[16,48,128]{2,1,0:T(8,128)(2,1)} %pair.1), calls=%async_computation | async-start | bytes 393216 | tf_op jit(solution)/shard_map/all_to_all | solution.py:606
  63.5 9.5 %collective-permute-start.12 = (bf16[24,24,128]{2,1,0:T(8,128)(2,1)S(1)}, bf16[24,24,128]{2,1,0:T(8,128)(2,1)S(1)}, u32[]{:S(2)}, u32[]{:S(2)}) collective-permute-start(bf16[24,24,128]{2,1,0:T(8,128)(2,1)S(1)} %input.1), channel_id=1, source_target_pairs={{0,0},{1,1},{2,2},{3,3},{17,4},{5,5},{6,6},{7,7},{18,8},{22,9},{10... | collective-permute-start | bytes 442376 | tf_op jit(solution)/shard_map/ppermute | solution.py:56

commit v15 on v14

--- a/solution.py
+++ b/solution.py
@@ -180,21 +180,21 @@
 
 
 def own_kernel(
-    brought, above, below, left, right, weights, bias, proj,
+    tile, above, below, left, right, weights, bias, proj,
     swapped, gate_first, bottle_first, near_hidden,
     area, pairs, last, pre,
 ):
-    side, first, second, inner = brought.shape[1], FIRST_DILATION, SECOND_DILATION, bias.shape[1]
+    side, first, second, inner = tile.shape[0], FIRST_DILATION, SECOND_DILATION, bias.shape[1]
     near, small = gate_first.shape[:2]
     span = side + 2 * second
-    assemble(area, brought[:side].astype(F32), above, below, left, right)
+    assemble(area, tile[...].astype(F32), above, below, left, right)
 
     def store(top, pre_act, branch):
         pre[pl.ds(top, 8)] = pre_act
         swapped[pl.ds(top, 8)] = branch[:, :span].astype(BF16)
 
     first_branch(area, pairs, last, weights, bias, proj, store)
-    swapped[span:, :side] = brought[side:]
+    swapped[span:] = jnp.zeros((side, span, swapped.shape[2]), BF16)
     for b in (-1, 0, 1):
         at = LEAD + first * b
         near_hidden[b + 1] = positive(area[HALO - first : HALO + side + first, at : at + small]).astype(BF16)
@@ -397,7 +397,7 @@
         parts[j] = jnp.concatenate(pieces + [total[count : count + 8]]).astype(BF16)
 
 
-def input_kernel(windows, grad_first, brought, v_first, out):
+def input_kernel(windows, grad_first, tile, v_first, out):
     side, channels = out.shape[0], out.shape[2]
     small = windows.shape[2]
     first = FIRST_DILATION
@@ -410,7 +410,7 @@
             total = total + dot(window, v_first[tap(a, b)])
         here = pl.ds(top, 8)
         total = total.reshape(8, small, channels)[:, :side]
-        total = jnp.where(brought[here].astype(F32) > 0, total, 0)
+        total = jnp.where(tile[here].astype(F32) > 0, total, 0)
         out[here] = (grad_first[here].astype(F32) + total).astype(BF16)
         return 0
 
@@ -452,8 +452,7 @@
     full, span, near = side + 2 * HALO, side + 2 * second, side + 2 * first
     wide, small = up16(span), up16(near)
 
-    brought = bring(jnp.concatenate([activations[0], cotangent[0]]))
-    tile = brought[:side]
+    tile = bring(activations[0])
     stored_even = lax.rem(lax.axis_index("row"), 2) == 0
     ends = (activations[0, side - HALO :], activations[0, :HALO])
     got = [bring(jnp.where(stored_even, *ends), 0), bring(jnp.where(stored_even, *ends[::-1]), 1)]
@@ -470,7 +469,9 @@
             strip = lax.dynamic_update_slice(strip, chosen(got[row_turn]), (0, at, 0))
         return strip
 
-    left, right = around(1, [exchange(columns(turn), 1, turn) for turn in (0, 1)])
+    strips, late = lax.optimization_barrier(([columns(0), columns(1)], cotangent[0]))
+    left, right = around(1, [exchange(strips[turn], 1, turn) for turn in (0, 1)])
+    late = bring(late)
 
     bias_rows = jnp.pad(conv_bias, ((0, 15), (0, channels - inner)))
     packed = jnp.concatenate(
@@ -511,10 +512,11 @@
             ((full + first, wide, 2 * channels), BF16),
             ((span, wide, inner), F32),
         ],
-        span * wide * channels * inner * 20,
-        *(brought, above, below, jnp.swapaxes(left, 0, 1), jnp.swapaxes(right, 0, 1)),
+        span * wide * channels * inner * 400,
+        *(tile, above, below, jnp.swapaxes(left, 0, 1), jnp.swapaxes(right, 0, 1)),
         *(w_first, b_first, p_first),
     )
+    kept = lax.dynamic_update_slice(kept, late, (span, 0, 0))
     other = swap(kept)
     gate_second, hidden_pairs, hidden_last, bottle_second, grad_tile, grad_pre, *strips = call(
         middle_kernel,
@@ -591,7 +593,7 @@
         [((side, side, channels), BF16)],
         [],
         18 * side * small * channels * channels,
-        *(windows, grad_first, brought, v_first),
+        *(windows, grad_first, tile, v_first),
     )
     other = lax.ppermute(away, "segment", [(0, 1), (1, 0)])
     other, input_gradient = lax.optimization_barrier((other, input_gradient))

time: 88.3 us -> 85.4 us (0.967)
  waiting for transfers between devices: 23 us -> 16.6 us
  starting transfers between devices: 35.5 us -> 39.1 us
    ppermute x11 -> x12, waiting for transfers between devices: 14.1 us -> 7.75 us  [permute(): return lax.ppermute(x, ALL, [found for found in pairs if found is not None])]
    ppermute x11 -> x12, starting transfers between devices: 28.9 us -> 32.9 us  [permute(): return lax.ppermute(x, ALL, [found for found in pairs if found is not None])]
    concatenate x1 -> x0, other arithmetic: 1.05 us -> none  [local(): brought = bring(jnp.concatenate([activations[0], cotangent[0]]))]
  transfers between devices with their start and end apart: 14 -> 15, of which waited for: 6 -> 6; matrix products, arithmetic and copies ran while one was open for 0% -> 1% of each run, Pallas kernels for 2% -> 6%
where the time goes in v15:
time: 85.4 us; the launch traced here: 84.6 us
  starting transfers between devices  39.1 us (46%)
  waiting for transfers between devices  16.6 us (19%)
  blocking collectives  13.7 us (16%)
  Pallas kernels  12 us (14%)
  other arithmetic  1.39 us (2%)
  between operations  1.02 us (1%)
    ppermute x12, starting transfers between devices, permute(): return lax.ppermute(x, ALL, [found for found in pairs if found is not None])  32.9 us
    all_to_all x1, blocking collectives, local(): lax.all_to_all(rows, GRID, 0, 0, tiled=True)  13.7 us
    pallas_call x9, Pallas kernels, call(): pl.pallas_call(kernel, name=name, out_shape=outs, scratch_shapes=[pltpu.V...  12 us
    all_to_all x1, waiting for transfers between devices, local(): parts = lax.all_to_all(parts, GRID, 0, 0, tiled=True)  8.8 us
    ppermute x12, waiting for transfers between devices, permute(): return lax.ppermute(x, ALL, [found for found in pairs if found is not None])  7.75 us
    all_to_all x1, starting transfers between devices, local(): parts = lax.all_to_all(parts, GRID, 0, 0, tiled=True)  5.48 us
  transfers between devices with their start and end apart: 15, of which 6 were waited for; matrix products, arithmetic and copies ran while one was open for 1% of the time, Pallas kernels for 6%

profile of v15, /device:TPU:0, one launch (start us, length us, event | category | flops | bytes accessed | tf_op | source)
XLA Modules:
  0.0 84.6 jit_solution(11602315064024055430)
XLA Ops:
  0.6 0.0 copy-start
  0.6 1.7 %collective-permute-start = (bf16[24,24,128]{2,1,0:T(8,128)(2,1)}, bf16[24,24,128]{2,1,0:T(8,128)(2,1)S(1)}, u32[]{:S(2)}, u32[]{:S(2)}) collective-permute-start(bf16[24,24,128]{2,1,0:T(8,128)(2,1)} %bitcast.48), channel_id=1, source_target_pairs={{0,0},{1,1},{2,2},{3,3},{4,17},{5,5},{6,6},{7,7},{8,18},{9,22},{10... | collective-permute-start | bytes 442376 | tf_op jit(solution)/shard_map/ppermute | solution.py:56
  2.3 0.9 %select_bitcast_fusion.6 = (bf16[10,24,128]{2,1,0:T(8,128)(2,1)S(1)}, bf16[10,24,128]{2,1,0:T(8,128)(2,1)S(1)}) fusion(pred[]{:T(512)S(6)} %eq.14, bf16[1,24,24,128]{3,2,1,0:T(8,128)(2,1)} %param.5), kind=kLoop, calls=%fused_computation.16 | loop fusion | flops 61440 | bytes 245761 | tf_op jit(solution)/shard_map/jit(_where)/select_n | solution.py:458
  3.2 4.5 %collective-permute-start.2 = (bf16[10,24,128]{2,1,0:T(8,128)(2,1)S(1)}, bf16[10,24,128]{2,1,0:T(8,128)(2,1)S(1)}, u32[]{:S(2)}, u32[]{:S(2)}) collective-permute-start(bf16[10,24,128]{2,1,0:T(8,128)(2,1)S(1)} %get-tuple-element.94), channel_id=1, source_target_pairs={{0,17},{1,5},{2,6},{3,7},{4,0},{5,1},{6,2},{7,3},{8,19},{9,23},{10... | collective-permute-start | bytes 184328 | tf_op jit(solution)/shard_map/ppermute | solution.py:56
  7.8 0.7 collective-permute-start.1
  8.4 0.0 copy-start.2
  8.4 0.0 copy-done
  8.4 0.0 copy-done.1
  8.5 0.6 copy-done.2
  9.1 0.1 collective-permute-start.5
  9.2 0.0 collective-permute-done.tile
  9.3 0.4 collective-permute-done.2
  9.8 0.0 collective-permute-done.1
  9.9 0.0 copy-start.3
  9.9 0.8 collective-permute-start.3
  10.7 5.3 %collective-permute-start.4 = (bf16[10,44,128]{2,0,1:T(8,128)(2,1)S(1)}, bf16[10,44,128]{2,0,1:T(8,128)(2,1)S(1)}, u32[]{:S(2)}, u32[]{:S(2)}) collective-permute-start(bf16[10,44,128]{2,0,1:T(8,128)(2,1)S(1)} %get-tuple-element.44), channel_id=1, source_target_pairs={{0,1},{1,0},{2,3},{3,2},{17,5},{5,17},{6,7},{7,6},{18,22},{22,18},... | collective-permute-start | bytes 337928 | tf_op jit(solution)/shard_map/ppermute | solution.py:56
  16.1 0.7 collective-permute-start.6
  16.7 0.0 collective-permute-done.5.theirs
  16.7 0.4 weights.1
  17.1 0.0 collective-permute-done.3
  17.1 2.4 %collective-permute-done.4 = bf16[10,44,128]{2,0,1:T(8,128)(2,1)S(1)} collective-permute-done((bf16[10,44,128]{2,0,1:T(8,128)(2,1)S(1)}, bf16[10,44,128]{2,0,1:T(8,128)(2,1)S(1)}, u32[]{:S(2)}, u32[]{:S(2)}) %collective-permute-start.4) | collective-permute-done | bytes 112672 | tf_op jit(solution)/shard_map/ppermute | solution.py:56
  19.5 3.6 %own_branch.1 = (bf16[64,40,128]{2,1,0:T(8,128)(2,1)S(1)}, bf16[28,32,128]{2,1,0:T(8,128)(2,1)S(1)}, bf16[24,32,64]{2,1,0:T(8,128)(2,1)S(1)}, bf16[3,28,32,128]{3,2,1,0:T(8,128)(2,1)S(1)}) custom-call(bf16[24,24,128]{2,1,0:T(8,128)(2,1)S(1)} %collective-permute-done.tile, bf16[10,24,128]{2,1,0:T(8,128)(2,1)S(1)} %get-tuple-element.97.above, ...), custom_call_target="tpu_custom_call" | custom-call | flops 6291456000 | bytes 2330880 | tf_op jit(solution)/shard_map/own_branch/pallas_call | solution.py:438
  23.1 0.0 collective-permute-done.6
  23.1 0.7 collective-permute-start.7
  23.9 0.0 collective-permute-done.7.other
  23.9 2.0 %middle.1 = (bf16[28,32,128]{2,1,0:T(8,128)(2,1)S(1)}, bf16[40,32,256]{2,1,0:T(8,128)(2,1)S(1)}, bf16[48,32,256]{2,1,0:T(8,128)(2,1)S(1)}, bf16[24,32,64]{2,1,0:...) custom-call(bf16[64,40,128]{2,1,0:T(8,128)(2,1)S(1)} %constant_dynam, ...), custom_call_target="tpu_custom_call" | custom-call | flops 301989888 | bytes 3949056 | tf_op jit(solution)/shard_map/middle/pallas_call | solution.py:438
  25.9 0.7 collective-permute-start.8
  26.5 12.1 %collective-permute-start.9 = (bf16[12,24,128]{2,1,0:T(8,128)(2,1)S(1)}, bf16[12,24,128]{2,1,0:T(8,128)(2,1)S(1)}, u32[]{:S(2)}, u32[]{:S(2)}) collective-permute-start(bf16[12,24,128]{2,1,0:T(8,128)(2,1)S(1)} %get-tuple-element.56), channel_id=1, source_target_pairs={{0,17},{1,5},{2,6},{3,7},{17,0},{5,1},{6,2},{7,3},{18,19},{22,23},... | collective-permute-start | bytes 221192 | tf_op jit(solution)/shard_map/ppermute | solution.py:56
  38.7 0.0 collective-permute-done.8
  38.7 1.9 %collective-permute-done.9 = bf16[12,24,128]{2,1,0:T(8,128)(2,1)S(1)} collective-permute-done((bf16[12,24,128]{2,1,0:T(8,128)(2,1)S(1)}, bf16[12,24,128]{2,1,0:T(8,128)(2,1)S(1)}, u32[]{:S(2)}, u32[]{:S(2)}) %collective-permute-start.9) | collective-permute-done | bytes 73760 | tf_op jit(solution)/shard_map/ppermute | solution.py:56
  40.8 0.1 maximum_bitcast_fusion
  40.8 0.7 collective-permute-start.10
  41.5 0.1 maximum_bitcast_fusion.1
  41.6 4.4 %collective-permute-start.11 = (bf16[12,44,128]{2,0,1:T(8,128)(2,1)S(1)}, bf16[12,44,128]{2,0,1:T(8,128)(2,1)S(1)}, u32[]{:S(2)}, u32[]{:S(2)}) collective-permute-start(bf16[12,44,128]{2,0,1:T(8,128)(2,1)S(1)} %maximum_bitcast_fusion.1), channel_id=1, source_target_pairs={{0,1},{1,0},{2,3},{3,2},{17,5},{5,17},{6,7},{7,6},{18,22},{22,18},... | collective-permute-start | bytes 405512 | tf_op jit(solution)/shard_map/ppermute | solution.py:56
  46.0 0.5 second_sums.1
  46.5 0.0 collective-permute-done.10
  46.5 3.0 %collective-permute-done.11 = bf16[12,44,128]{2,0,1:T(8,128)(2,1)S(1)} collective-permute-done((bf16[12,44,128]{2,0,1:T(8,128)(2,1)S(1)}, bf16[12,44,128]{2,0,1:T(8,128)(2,1)S(1)}, u32[]{:S(2)}, u32[]{:S(2)}) %collective-permute-start.11) | collective-permute-done | bytes 135200 | tf_op jit(solution)/shard_map/ppermute | solution.py:56
  49.6 3.1 %backward.1 = (f32[656,128]{1,0:T(8,128)S(1)}, bf16[656,128]{1,0:T(8,128)(2,1)S(1)}, bf16[3,28,32,128]{3,2,1,0:T(8,128)(2,1)S(1)}, bf16[24,24,128]{2,1,0:T(8,128)(2,1)S(1)}) custom-call(bf16[24,32,128]{2,1,0:T(8,128)(2,1)S(1)} %get-tuple-element.53.grad_pre, bf16[24,32,128]{2,1,0:T(8,128)(2,1)S(1)} %get-tuple-element.54.grad_tile, ...), custom_call_target="tpu_custom_call" | custom-call | flops 528482304 | bytes 4337664 | tf_op jit(solution)/shard_map/backward/pallas_call | solution.py:438
  52.7 0.7 collective-permute-start.12
  53.3 0.9 %input.1 = bf16[24,24,128]{2,1,0:T(8,128)(2,1)S(1)} custom-call(bf16[3,28,32,128]{3,2,1,0:T(8,128)(2,1)S(1)} %get-tuple-element.70.windows, bf16[24,24,128]{2,1,0:T(8,128)(2,1)S(1)} %get-tuple-element.71.grad_first, bf16[24,24,128]{2,1,0:T(8,128)(2,1)S(1)} %collective-permute-done.tile, bf16[9,128,128]{2,1,0:T(8,128)(2,1)S(1)} %get-tuple-element.72.v_first), custom_call_target="tpu_custom_call" | custom-call | flops 226492416 | bytes 1425408 | tf_op jit(solution)/shard_map/input/pallas_call | solution.py:438
  54.3 0.1 collective-permute-done.12.other
  54.4 0.7 pair.1
  55.1 5.5 %all-to-all-start = ((bf16[16,48,128]{2,1,0:T(8,128)(2,1)}), bf16[16,48,128]{2,1,0:T(8,128)(2,1)S(1)}, u32[]{:S(2)}, u32[]{:S(2)}) async-start(bf16[16,48,128]{2,1,0:T(8,128)(2,1)} %pair.1), calls=%async_computation | async-start | bytes 393216 | tf_op jit(solution)/shard_map/all_to_all | solution.py:608
  60.6 0.7 collective-permute-start.13
  61.2 8.8 %all-to-all-done.parts = bf16[16,48,128]{2,1,0:T(8,128)(2,1)S(1)} async-done(((bf16[16,48,128]{2,1,0:T(8,128)(2,1)}), bf16[16,48,128]{2,1,0:T(8,128)(2,1)S(1)}, u32[]{:S(2)}, u32[]{:S(2)}) %all-to-all-start) | async-done | bytes 196640 | tf_op jit(solution)/shard_map/all_to_all | solution.py:608
  70.1 0.0 collective-permute-done.13.moved
  70.1 13.7 %all_to_all.10 = bf16[16,40,128]{2,1,0:T(8,128)(2,1)S(1)} all-to-all(bf16[16,40,128]{2,1,0:T(8,128)(2,1)S(1)} %get-tuple-element.76), channel_id=1, replica_groups=mesh['segment'=2,'row'=4,'col'=4] {'row','col'}, dimensions={0} | all-to-all | bytes 327680 | tf_op jit(solution)/shard_map/all_to_all | solution.py:620
  83.8 0.8 outputs.1
  (22 shorter events, 0.5 us)
Async XLA Ops:
  0.6 7.8 %copy-start = (bf16[1,9,128,64]{2,3,1,0:T(8,128)(2,1)S(1)}, bf16[1,9,128,64]{2,3,1,0:T(8,128)(2,1)}, u32[]{:S(2)}) copy-start(bf16[1,9,128,64]{2,3,1,0:T(8,128)(2,1)} %param.7) | copy-start | bytes 442372
  0.6 8.6 %collective-permute-start = (bf16[24,24,128]{2,1,0:T(8,128)(2,1)}, bf16[24,24,128]{2,1,0:T(8,128)(2,1)S(1)}, u32[]{:S(2)}, u32[]{:S(2)}) collective-permute-start(bf16[24,24,128]{2,1,0:T(8,128)(2,1)} %bitcast.48), channel_id=1, source_target_pairs={{0,0},{1,1},{2,2},{3,3},{4,17},{5,5},{6,6},{7,7},{8,18},{9,22},{10... | collective-permute-start | bytes 442376 | tf_op jit(solution)/shard_map/ppermute | solution.py:56
  2.3 6.1 %copy-start.1 = (bf16[1,64,128]{2,1,0:T(8,128)(2,1)S(1)}, bf16[1,64,128]{2,1,0:T(8,128)(2,1)}, u32[]{:S(2)}) copy-start(bf16[1,64,128]{2,1,0:T(8,128)(2,1)} %param.9) | copy-start | bytes 49156
  3.2 6.5 %collective-permute-start.2 = (bf16[10,24,128]{2,1,0:T(8,128)(2,1)S(1)}, bf16[10,24,128]{2,1,0:T(8,128)(2,1)S(1)}, u32[]{:S(2)}, u32[]{:S(2)}) collective-permute-start(bf16[10,24,128]{2,1,0:T(8,128)(2,1)S(1)} %get-tuple-element.94), channel_id=1, source_target_pairs={{0,17},{1,5},{2,6},{3,7},{4,0},{5,1},{6,2},{7,3},{8,19},{9,23},{10... | collective-permute-start | bytes 184328 | tf_op jit(solution)/shard_map/ppermute | solution.py:56
  7.8 2.0 %collective-permute-start.1 = (bf16[10,24,128]{2,1,0:T(8,128)(2,1)S(1)}, bf16[10,24,128]{2,1,0:T(8,128)(2,1)S(1)}, u32[]{:S(2)}, u32[]{:S(2)}) collective-permute-start(bf16[10,24,128]{2,1,0:T(8,128)(2,1)S(1)} %get-tuple-element.95), channel_id=1, source_target_pairs={{4,18},{5,22},{6,10},{7,11},{8,17},{9,5},{10,6},{11,7},{20,24},{21... | collective-permute-start | bytes 184328 | tf_op jit(solution)/shard_map/ppermute | solution.py:56
  8.4 0.7 copy-start.2
  9.1 7.6 %collective-permute-start.5 = (bf16[656,128]{1,0:T(8,128)(2,1)S(1)}, bf16[656,128]{1,0:T(8,128)(2,1)S(1)}, u32[]{:S(2)}, u32[]{:S(2)}) collective-permute-start(bf16[656,128]{1,0:T(8,128)(2,1)S(1)} %fusion.1.mine), channel_id=1, source_target_pairs={{0,16},{16,0},{1,17},{17,1},{2,18},{18,2},{3,19},{19,3},{4,20},{20... | collective-permute-start | bytes 503816 | tf_op jit(solution)/shard_map/ppermute | solution.py:480
  9.9 6.2 %copy-start.3 = (bf16[1,24,24,128]{3,2,1,0:T(8,128)(2,1)S(1)}, bf16[1,24,24,128]{3,2,1,0:T(8,128)(2,1)}, u32[]{:S(2)}) copy-start(bf16[1,24,24,128]{3,2,1,0:T(8,128)(2,1)} %param.6) | copy-start | bytes 442372
  9.9 7.2 %collective-permute-start.3 = (bf16[10,44,128]{2,0,1:T(8,128)(2,1)S(1)}, bf16[10,44,128]{2,0,1:T(8,128)(2,1)S(1)}, u32[]{:S(2)}, u32[]{:S(2)}) collective-permute-start(bf16[10,44,128]{2,0,1:T(8,128)(2,1)S(1)} %get-tuple-element.43), channel_id=1, source_target_pairs={{1,2},{2,1},{5,6},{6,5},{22,10},{10,22},{23,27},{27,23},{4,8},{8,4... | collective-permute-start | bytes 337928 | tf_op jit(solution)/shard_map/ppermute | solution.py:56
  10.7 8.8 %collective-permute-start.4 = (bf16[10,44,128]{2,0,1:T(8,128)(2,1)S(1)}, bf16[10,44,128]{2,0,1:T(8,128)(2,1)S(1)}, u32[]{:S(2)}, u32[]{:S(2)}) collective-permute-start(bf16[10,44,128]{2,0,1:T(8,128)(2,1)S(1)} %get-tuple-element.44), channel_id=1, source_target_pairs={{0,1},{1,0},{2,3},{3,2},{17,5},{5,17},{6,7},{7,6},{18,22},{22,18},... | collective-permute-start | bytes 337928 | tf_op jit(solution)/shard_map/ppermute | solution.py:56
  16.1 7.0 %collective-permute-start.6 = (bf16[24,24,128]{2,1,0:T(8,128)(2,1)S(1)}, bf16[24,24,128]{2,1,0:T(8,128)(2,1)S(1)}, u32[]{:S(2)}, u32[]{:S(2)}) collective-permute-start(bf16[24,24,128]{2,1,0:T(8,128)(2,1)S(1)} %bitcast.51), channel_id=1, source_target_pairs={{0,0},{1,1},{2,2},{3,3},{4,17},{5,5},{6,6},{7,7},{8,18},{9,22},{10... | collective-permute-start | bytes 442376 | tf_op jit(solution)/shard_map/ppermute | solution.py:56
  23.1 0.7 collective-permute-start.7
  25.9 12.8 %collective-permute-start.8 = (bf16[12,24,128]{2,1,0:T(8,128)(2,1)S(1)}, bf16[12,24,128]{2,1,0:T(8,128)(2,1)S(1)}, u32[]{:S(2)}, u32[]{:S(2)}) collective-permute-start(bf16[12,24,128]{2,1,0:T(8,128)(2,1)S(1)} %get-tuple-element.55), channel_id=1, source_target_pairs={{17,18},{5,22},{6,10},{7,11},{18,17},{22,5},{10,6},{11,7},{20,24},... | collective-permute-start | bytes 221192 | tf_op jit(solution)/shard_map/ppermute | solution.py:56
  26.5 14.1 %collective-permute-start.9 = (bf16[12,24,128]{2,1,0:T(8,128)(2,1)S(1)}, bf16[12,24,128]{2,1,0:T(8,128)(2,1)S(1)}, u32[]{:S(2)}, u32[]{:S(2)}) collective-permute-start(bf16[12,24,128]{2,1,0:T(8,128)(2,1)S(1)} %get-tuple-element.56), channel_id=1, source_target_pairs={{0,17},{1,5},{2,6},{3,7},{17,0},{5,1},{6,2},{7,3},{18,19},{22,23},... | collective-permute-start | bytes 221192 | tf_op jit(solution)/shard_map/ppermute | solution.py:56
  40.8 5.7 %collective-permute-start.10 = (bf16[12,44,128]{2,0,1:T(8,128)(2,1)S(1)}, bf16[12,44,128]{2,0,1:T(8,128)(2,1)S(1)}, u32[]{:S(2)}, u32[]{:S(2)}) collective-permute-start(bf16[12,44,128]{2,0,1:T(8,128)(2,1)S(1)} %maximum_bitcast_fusion), channel_id=1, source_target_pairs={{1,2},{2,1},{5,6},{6,5},{22,10},{10,22},{23,27},{27,23},{4,8},{8,4... | collective-permute-start | bytes 405512 | tf_op jit(solution)/shard_map/ppermute | solution.py:56
  41.6 7.9 %collective-permute-start.11 = (bf16[12,44,128]{2,0,1:T(8,128)(2,1)S(1)}, bf16[12,44,128]{2,0,1:T(8,128)(2,1)S(1)}, u32[]{:S(2)}, u32[]{:S(2)}) collective-permute-start(bf16[12,44,128]{2,0,1:T(8,128)(2,1)S(1)} %maximum_bitcast_fusion.1), channel_id=1, source_target_pairs={{0,1},{1,0},{2,3},{3,2},{17,5},{5,17},{6,7},{7,6},{18,22},{22,18},... | collective-permute-start | bytes 405512 | tf_op jit(solution)/shard_map/ppermute | solution.py:56
  52.7 1.7 %collective-permute-start.12 = (bf16[656,128]{1,0:T(8,128)(2,1)S(1)}, bf16[656,128]{1,0:T(8,128)(2,1)S(1)}, u32[]{:S(2)}, u32[]{:S(2)}) collective-permute-start(bf16[656,128]{1,0:T(8,128)(2,1)S(1)} %get-tuple-element.69), channel_id=1, source_target_pairs={{0,16},{16,0},{1,17},{17,1},{2,18},{18,2},{3,19},{19,3},{4,20},{20... | collective-permute-start | bytes 503816 | tf_op jit(solution)/shard_map/ppermute | solution.py:598
  55.1 15.0 %all-to-all-start = ((bf16[16,48,128]{2,1,0:T(8,128)(2,1)}), bf16[16,48,128]{2,1,0:T(8,128)(2,1)S(1)}, u32[]{:S(2)}, u32[]{:S(2)}) async-start(bf16[16,48,128]{2,1,0:T(8,128)(2,1)} %pair.1), calls=%async_computation | async-start | bytes 393216 | tf_op jit(solution)/shard_map/all_to_all | solution.py:608
  60.6 9.5 %collective-permute-start.13 = (bf16[24,24,128]{2,1,0:T(8,128)(2,1)S(1)}, bf16[24,24,128]{2,1,0:T(8,128)(2,1)S(1)}, u32[]{:S(2)}, u32[]{:S(2)}) collective-permute-start(bf16[24,24,128]{2,1,0:T(8,128)(2,1)S(1)} %input.1), channel_id=1, source_target_pairs={{0,0},{1,1},{2,2},{3,3},{17,4},{5,5},{6,6},{7,7},{18,8},{22,9},{10... | collective-permute-start | bytes 442376 | tf_op jit(solution)/shard_map/ppermute | solution.py:56

commit v16 on v15

--- a/solution.py
+++ b/solution.py
@@ -181,12 +181,10 @@
 
 def own_kernel(
     tile, above, below, left, right, weights, bias, proj,
-    swapped, gate_first, bottle_first, near_hidden,
-    area, pairs, last, pre,
+    swapped, pre,
+    area, pairs, last,
 ):
-    side, first, second, inner = tile.shape[0], FIRST_DILATION, SECOND_DILATION, bias.shape[1]
-    near, small = gate_first.shape[:2]
-    span = side + 2 * second
+    side, span = tile.shape[0], pre.shape[0]
     assemble(area, tile[...].astype(F32), above, below, left, right)
 
     def store(top, pre_act, branch):
@@ -195,9 +193,20 @@
 
     first_branch(area, pairs, last, weights, bias, proj, store)
     swapped[span:] = jnp.zeros((side, span, swapped.shape[2]), BF16)
+
+
+def near_kernel(tile, above, below, left, right, pre, hidden_pairs, hidden_last, gate_first, bottle_first, area):
+    side, channels, inner = tile.shape[0], tile.shape[2], pre.shape[2]
+    first, second = FIRST_DILATION, SECOND_DILATION
+    near, small = gate_first.shape[:2]
+    assemble(area, tile[...].astype(F32), above, below, left, right)
     for b in (-1, 0, 1):
         at = LEAD + first * b
-        near_hidden[b + 1] = positive(area[HALO - first : HALO + side + first, at : at + small]).astype(BF16)
+        window = positive(area[HALO - first : HALO + side + first, at : at + small]).astype(BF16)
+        if b < 1:
+            hidden_pairs[:, :, (b + 1) * channels : (b + 2) * channels] = window
+        else:
+            hidden_last[...] = window
     edge = second - first
     part = pre[edge : edge + near, edge : edge + small]
     alive = (part > 0) & inside(part.shape, side, first, 0)
@@ -287,8 +296,9 @@
         own, other = conv(1, k), conv(1, 3 * (k % 3) + k // 3)
         w_first[here] = turned(conv(0, k))
         w_second[here] = turned(jnp.concatenate([own, other], axis=0))
-        v_second[k, :inner, :channels], v_second[k, :inner, channels:] = own, zero
-        v_second[k, inner:, :channels], v_second[k, inner:, channels:] = zero, other
+        upper, lower = (slice((2 * k + half) * inner, (2 * k + half + 1) * inner) for half in (0, 1))
+        v_second[upper, :channels], v_second[upper, channels:] = own, zero
+        v_second[lower, :channels], v_second[lower, channels:] = zero, other
         v_first[k, :inner], v_first[k, inner:] = conv(0, k), zero
     p_first[...] = conv(0, 9)
     p_second[...] = turned(jnp.concatenate([conv(1, 9), conv(1, 9)], axis=0))
@@ -312,10 +322,10 @@
 
 
 def backward_kernel(
-    grad_pre, grad_tile, above, below, left, right, left_branch, right_branch, gate_second, gate_first, near_hidden,
-    bottle_first, v_second, p_first, rows_second, ends_second,
+    grad_pre, grad_tile, above, below, left, right, left_branch, right_branch, gate_second, gate_first, near_pairs,
+    near_last, bottle_first, v_second, p_first, rows_second, ends_second,
     keep, away, windows, grad_first,
-    area, shifted, branch, grads, rows, ends,
+    area, pairs, last, branch, grads, rows, ends,
 ):
     side, channels = grad_first.shape[0], grad_first.shape[2]
     first, second = FIRST_DILATION, SECOND_DILATION
@@ -338,16 +348,23 @@
     branch[:, first + side : near] = right_branch[...].astype(F32)
     for b in (-1, 0, 1):
         at = LEAD - HALO + second * (1 - b)
-        shifted[b + 1] = area[:, at : at + small].astype(BF16)
+        window = area[:, at : at + small].astype(BF16)
+        if b < 1:
+            pairs[:, :, (b + 1) * channels : (b + 2) * channels] = window
+        else:
+            last[...] = window
     grads[:, small:] = jnp.zeros((near, grads.shape[1] - small, channels), F32)
 
     def sections(step, _):
         top = step * 7
         size = 7 * small
-        total = jnp.zeros((size, 2 * channels), F32)
-        for a, b in TAPS:
-            window = shifted[b + 1, pl.ds(top + second * (1 - a), 7)].reshape(size, channels)
-            total = total + dot(window, v_second[tap(a, b)])
+        total = None
+        for a in (-1, 0, 1):
+            rows_of = pl.ds(top + second * (1 - a), 7)
+            at = 3 * (a + 1) * channels
+            term = dot(pairs[rows_of].reshape(size, 2 * channels), v_second[at : at + 2 * channels])
+            total = term if total is None else total + term
+            total = total + dot(last[rows_of].reshape(size, channels), v_second[at + 2 * channels : at + 3 * channels])
         here = pl.ds(top, 7)
         grad = branch[here, :small].reshape(size, channels)
         gate = gate_second[here].astype(F32).reshape(size, channels) > 0
@@ -371,7 +388,7 @@
     grad = jnp.where(real, grads[first : first + side, first : first + small], 0)
 
     def hidden(a, b):
-        return near_hidden[b, first * a : first * a + side]
+        return (near_last if b else near_pairs)[first * a : first * a + side]
 
     weight_sums(rows, ends, grad, hidden, bottle_first, part)
 
@@ -484,7 +501,7 @@
         [
             ((9 * channels, inner), BF16),
             ((9 * channels, 2 * inner), BF16),
-            ((9, 2 * inner, 2 * channels), BF16),
+            ((18 * inner, 2 * channels), BF16),
             ((9, 2 * inner, channels), BF16),
             ((inner, channels), BF16),
             ((channels, 2 * inner), BF16),
@@ -497,23 +514,15 @@
         *(packed, others),
     )
 
-    kept, gate_first, bottle_first, near_hidden = call(
+    own = (tile, above, below, jnp.swapaxes(left, 0, 1), jnp.swapaxes(right, 0, 1))
+    area = ((full, LEAD + up16(side + LEAD), channels), F32)
+    kept, pre_first = call(
         own_kernel,
         "own_branch",
-        [
-            ((span + side, span, channels), BF16),
-            ((near, small, channels), BF16),
-            ((side, small, inner), BF16),
-            ((3, near, small, channels), BF16),
-        ],
-        [
-            ((full, LEAD + up16(side + LEAD), channels), F32),
-            ((full, wide, 2 * channels), BF16),
-            ((full + first, wide, 2 * channels), BF16),
-            ((span, wide, inner), F32),
-        ],
+        [((span + side, span, channels), BF16), ((span, wide, inner), F32)],
+        [area, ((full, wide, 2 * channels), BF16), ((full + first, wide, 2 * channels), BF16)],
         span * wide * channels * inner * 400,
-        *(tile, above, below, jnp.swapaxes(left, 0, 1), jnp.swapaxes(right, 0, 1)),
+        *own,
         *(w_first, b_first, p_first),
     )
     kept = lax.dynamic_update_slice(kept, late, (span, 0, 0))
@@ -540,6 +549,21 @@
         *(kept, other, w_second, b_second, p_second),
     )
 
+    near_pairs, near_last, gate_first, bottle_first = call(
+        near_kernel,
+        "near",
+        [
+            ((near, small, 2 * channels), BF16),
+            ((near, small, channels), BF16),
+            ((near, small, channels), BF16),
+            ((side, small, inner), BF16),
+        ],
+        [area],
+        near * small * channels,
+        *own,
+        pre_first,
+    )
+
     above, below = around(0, [exchange(strips[turn], 0, turn) for turn in (0, 1)])
     rows_second, ends_second = call(
         second_sums_kernel,
@@ -575,7 +599,8 @@
         ],
         [
             ((full, LEAD + up16(side + HALO + first), channels), F32),
-            ((3, full, small, channels), BF16),
+            ((full, small, 2 * channels), BF16),
+            ((full, small, channels), BF16),
             ((near, small + 16, channels), F32),
             ((near, small + 16, channels), F32),
             ((10 * inner, channels), F32),
@@ -584,7 +609,7 @@
         36 * near * small * channels * channels,
         *(grad_pre, grad_tile, above, below, left[:, :HALO], right[:, :HALO]),
         *(left[second : second + near, HALO:], right[second : second + near, HALO:]),
-        *(gate_second, gate_first, near_hidden, bottle_first, v_second, p_back, rows_second, ends_second),
+        *(gate_second, gate_first, near_pairs, near_last, bottle_first, v_second, p_back, rows_second, ends_second),
     )
 
     (input_gradient,) = call(

time: 85.4 us -> 85.1 us (level)
    pallas_call x9 -> x10, Pallas kernels: 12 us -> 11.9 us  [call(): pl.pallas_call(kernel, name=name, out_shape=outs, scratch_shapes=[pltpu.V...]
  transfers between devices with their start and end apart: 15 -> 15, of which waited for: 6 -> 6; matrix products, arithmetic and copies ran while one was open for 1% -> 2% of each run, Pallas kernels for 6% -> 7%
where the time goes in v16:
time: 85.1 us; the launch traced here: 84.3 us
  starting transfers between devices  39.3 us (46%)
  waiting for transfers between devices  16.2 us (19%)
  blocking collectives  13.7 us (16%)
  Pallas kernels  11.9 us (14%)
  other arithmetic  1.39 us (2%)
  between operations  1.02 us (1%)
    ppermute x12, starting transfers between devices, permute(): return lax.ppermute(x, ALL, [found for found in pairs if found is not None])  33.1 us
    all_to_all x1, blocking collectives, local(): lax.all_to_all(rows, GRID, 0, 0, tiled=True)  13.7 us
    pallas_call x10, Pallas kernels, call(): pl.pallas_call(kernel, name=name, out_shape=outs, scratch_shapes=[pltpu.V...  11.9 us
    all_to_all x1, waiting for transfers between devices, local(): parts = lax.all_to_all(parts, GRID, 0, 0, tiled=True)  8.8 us
    ppermute x12, waiting for transfers between devices, permute(): return lax.ppermute(x, ALL, [found for found in pairs if found is not None])  7.32 us
    all_to_all x1, starting transfers between devices, local(): parts = lax.all_to_all(parts, GRID, 0, 0, tiled=True)  5.47 us
  transfers between devices with their start and end apart: 15, of which 6 were waited for; matrix products, arithmetic and copies ran while one was open for 2% of the time, Pallas kernels for 7%

profile of v16, /device:TPU:0, one launch (start us, length us, event | category | flops | bytes accessed | tf_op | source)
XLA Modules:
  0.0 84.3 jit_solution(8832700700820717361)
XLA Ops:
  0.6 0.0 copy-start
  0.6 1.7 %collective-permute-start = (bf16[24,24,128]{2,1,0:T(8,128)(2,1)}, bf16[24,24,128]{2,1,0:T(8,128)(2,1)S(1)}, u32[]{:S(2)}, u32[]{:S(2)}) collective-permute-start(bf16[24,24,128]{2,1,0:T(8,128)(2,1)} %bitcast.48), channel_id=1, source_target_pairs={{0,0},{1,1},{2,2},{3,3},{4,17},{5,5},{6,6},{7,7},{8,18},{9,22},{10... | collective-permute-start | bytes 442376 | tf_op jit(solution)/shard_map/ppermute | solution.py:56
  2.3 0.9 %select_bitcast_fusion.6 = (bf16[10,24,128]{2,1,0:T(8,128)(2,1)S(1)}, bf16[10,24,128]{2,1,0:T(8,128)(2,1)S(1)}) fusion(pred[]{:T(512)S(6)} %eq.14, bf16[1,24,24,128]{3,2,1,0:T(8,128)(2,1)} %param.5), kind=kLoop, calls=%fused_computation.16 | loop fusion | flops 61440 | bytes 245761 | tf_op jit(solution)/shard_map/jit(_where)/select_n | solution.py:475
  3.2 4.5 %collective-permute-start.2 = (bf16[10,24,128]{2,1,0:T(8,128)(2,1)S(1)}, bf16[10,24,128]{2,1,0:T(8,128)(2,1)S(1)}, u32[]{:S(2)}, u32[]{:S(2)}) collective-permute-start(bf16[10,24,128]{2,1,0:T(8,128)(2,1)S(1)} %get-tuple-element.98), channel_id=1, source_target_pairs={{0,17},{1,5},{2,6},{3,7},{4,0},{5,1},{6,2},{7,3},{8,19},{9,23},{10... | collective-permute-start | bytes 184328 | tf_op jit(solution)/shard_map/ppermute | solution.py:56
  7.8 0.7 collective-permute-start.1
  8.4 0.0 copy-start.2
  8.4 0.0 copy-done
  8.5 0.6 copy-done.2
  9.1 0.1 collective-permute-start.5
  9.2 0.0 collective-permute-done.tile
  9.3 0.4 collective-permute-done.2
  9.8 0.0 collective-permute-done.1
  9.9 0.0 copy-start.3
  9.9 0.8 collective-permute-start.3
  10.7 5.3 %collective-permute-start.4 = (bf16[10,44,128]{2,0,1:T(8,128)(2,1)S(1)}, bf16[10,44,128]{2,0,1:T(8,128)(2,1)S(1)}, u32[]{:S(2)}, u32[]{:S(2)}) collective-permute-start(bf16[10,44,128]{2,0,1:T(8,128)(2,1)S(1)} %get-tuple-element.46), channel_id=1, source_target_pairs={{0,1},{1,0},{2,3},{3,2},{17,5},{5,17},{6,7},{7,6},{18,22},{22,18},... | collective-permute-start | bytes 337928 | tf_op jit(solution)/shard_map/ppermute | solution.py:56
  16.1 0.7 collective-permute-start.6
  16.7 0.0 collective-permute-done.5.theirs
  16.7 0.4 weights.1
  17.1 0.0 collective-permute-done.3
  17.1 2.4 %collective-permute-done.4 = bf16[10,44,128]{2,0,1:T(8,128)(2,1)S(1)} collective-permute-done((bf16[10,44,128]{2,0,1:T(8,128)(2,1)S(1)}, bf16[10,44,128]{2,0,1:T(8,128)(2,1)S(1)}, u32[]{:S(2)}, u32[]{:S(2)}) %collective-permute-start.4) | collective-permute-done | bytes 112672 | tf_op jit(solution)/shard_map/ppermute | solution.py:56
  19.5 3.3 %own_branch.1 = (bf16[64,40,128]{2,1,0:T(8,128)(2,1)S(1)}, f32[40,48,64]{2,1,0:T(8,128)S(1)}) custom-call(bf16[24,24,128]{2,1,0:T(8,128)(2,1)S(1)} %collective-permute-done.tile, bf16[10,24,128]{2,1,0:T(8,128)(2,1)S(1)} %get-tuple-element.101.above, bf16[10,24,128]{2,1,0:T(8,128)(2,1)S(1)} %get-tuple-element.100.below, ...), custom_call_target="tpu_custom_call" | custom-call | flops 6291456000 | bytes 1806592 | tf_op jit(solution)/shard_map/own_branch/pallas_call | solution.py:455
  22.8 0.0 collective-permute-done.6
  22.9 0.7 collective-permute-start.7
  23.6 0.0 collective-permute-done.7.other
  23.6 2.0 %middle.1 = (bf16[28,32,128]{2,1,0:T(8,128)(2,1)S(1)}, bf16[40,32,256]{2,1,0:T(8,128)(2,1)S(1)}, bf16[48,32,256]{2,1,0:T(8,128)(2,1)S(1)}, bf16[24,32,64]{2,1,0:...) custom-call(bf16[64,40,128]{2,1,0:T(8,128)(2,1)S(1)} %constant_dynam, ...), custom_call_target="tpu_custom_call" | custom-call | flops 301989888 | bytes 3949056 | tf_op jit(solution)/shard_map/middle/pallas_call | solution.py:455
  25.6 0.7 collective-permute-start.8
  26.3 12.3 %collective-permute-start.9 = (bf16[12,24,128]{2,1,0:T(8,128)(2,1)S(1)}, bf16[12,24,128]{2,1,0:T(8,128)(2,1)S(1)}, u32[]{:S(2)}, u32[]{:S(2)}) collective-permute-start(bf16[12,24,128]{2,1,0:T(8,128)(2,1)S(1)} %get-tuple-element.58), channel_id=1, source_target_pairs={{0,17},{1,5},{2,6},{3,7},{17,0},{5,1},{6,2},{7,3},{18,19},{22,23},... | collective-permute-start | bytes 221192 | tf_op jit(solution)/shard_map/ppermute | solution.py:56
  38.7 0.0 collective-permute-done.8
  38.7 1.9 %collective-permute-done.9 = bf16[12,24,128]{2,1,0:T(8,128)(2,1)S(1)} collective-permute-done((bf16[12,24,128]{2,1,0:T(8,128)(2,1)S(1)}, bf16[12,24,128]{2,1,0:T(8,128)(2,1)S(1)}, u32[]{:S(2)}, u32[]{:S(2)}) %collective-permute-start.9) | collective-permute-done | bytes 73760 | tf_op jit(solution)/shard_map/ppermute | solution.py:56
  40.8 0.1 maximum_bitcast_fusion
  40.9 0.7 collective-permute-start.10
  41.6 0.1 maximum_bitcast_fusion.1
  41.6 4.4 %collective-permute-start.11 = (bf16[12,44,128]{2,0,1:T(8,128)(2,1)S(1)}, bf16[12,44,128]{2,0,1:T(8,128)(2,1)S(1)}, u32[]{:S(2)}, u32[]{:S(2)}) collective-permute-start(bf16[12,44,128]{2,0,1:T(8,128)(2,1)S(1)} %maximum_bitcast_fusion.1), channel_id=1, source_target_pairs={{0,1},{1,0},{2,3},{3,2},{17,5},{5,17},{6,7},{7,6},{18,22},{22,18},... | collective-permute-start | bytes 405512 | tf_op jit(solution)/shard_map/ppermute | solution.py:56
  46.0 0.4 near.1
  46.5 0.5 second_sums.1
  47.0 0.0 collective-permute-done.10
  47.0 2.5 %collective-permute-done.11 = bf16[12,44,128]{2,0,1:T(8,128)(2,1)S(1)} collective-permute-done((bf16[12,44,128]{2,0,1:T(8,128)(2,1)S(1)}, bf16[12,44,128]{2,0,1:T(8,128)(2,1)S(1)}, u32[]{:S(2)}, u32[]{:S(2)}) %collective-permute-start.11) | collective-permute-done | bytes 135200 | tf_op jit(solution)/shard_map/ppermute | solution.py:56
  49.6 2.8 %backward.1 = (f32[656,128]{1,0:T(8,128)S(1)}, bf16[656,128]{1,0:T(8,128)(2,1)S(1)}, bf16[3,28,32,128]{3,2,1,0:T(8,128)(2,1)S(1)}, bf16[24,24,128]{2,1,0:T(8,128)(2,1)S(1)}) custom-call(bf16[24,32,128]{2,1,0:T(8,128)(2,1)S(1)} %get-tuple-element.55.grad_pre, bf16[24,32,128]{2,1,0:T(8,128)(2,1)S(1)} %get-tuple-element.56.grad_tile, ...), custom_call_target="tpu_custom_call" | custom-call | flops 528482304 | bytes 4337664 | tf_op jit(solution)/shard_map/backward/pallas_call | solution.py:455
  52.4 0.6 collective-permute-start.12
  53.0 0.9 %input.1 = bf16[24,24,128]{2,1,0:T(8,128)(2,1)S(1)} custom-call(bf16[3,28,32,128]{3,2,1,0:T(8,128)(2,1)S(1)} %get-tuple-element.74.windows, bf16[24,24,128]{2,1,0:T(8,128)(2,1)S(1)} %get-tuple-element.75.grad_first, bf16[24,24,128]{2,1,0:T(8,128)(2,1)S(1)} %collective-permute-done.tile, bf16[9,128,128]{2,1,0:T(8,128)(2,1)S(1)} %get-tuple-element.76.v_first), custom_call_target="tpu_custom_call" | custom-call | flops 226492416 | bytes 1425408 | tf_op jit(solution)/shard_map/input/pallas_call | solution.py:455
  54.0 0.1 collective-permute-done.12.other
  54.1 0.7 pair.1
  54.8 5.5 %all-to-all-start = ((bf16[16,48,128]{2,1,0:T(8,128)(2,1)}), bf16[16,48,128]{2,1,0:T(8,128)(2,1)S(1)}, u32[]{:S(2)}, u32[]{:S(2)}) async-start(bf16[16,48,128]{2,1,0:T(8,128)(2,1)} %pair.1), calls=%async_computation | async-start | bytes 393216 | tf_op jit(solution)/shard_map/all_to_all | solution.py:633
  60.3 0.7 collective-permute-start.13
  61.0 8.8 %all-to-all-done.parts = bf16[16,48,128]{2,1,0:T(8,128)(2,1)S(1)} async-done(((bf16[16,48,128]{2,1,0:T(8,128)(2,1)}), bf16[16,48,128]{2,1,0:T(8,128)(2,1)S(1)}, u32[]{:S(2)}, u32[]{:S(2)}) %all-to-all-start) | async-done | bytes 196640 | tf_op jit(solution)/shard_map/all_to_all | solution.py:633
  69.8 0.0 collective-permute-done.13.moved
  69.8 13.7 %all_to_all.10 = bf16[16,40,128]{2,1,0:T(8,128)(2,1)S(1)} all-to-all(bf16[16,40,128]{2,1,0:T(8,128)(2,1)S(1)} %get-tuple-element.80), channel_id=1, replica_groups=mesh['segment'=2,'row'=4,'col'=4] {'row','col'}, dimensions={0} | all-to-all | bytes 327680 | tf_op jit(solution)/shard_map/all_to_all | solution.py:645
  83.5 0.8 outputs.1
  (23 shorter events, 0.5 us)
Async XLA Ops:
  0.6 7.8 %copy-start = (bf16[1,9,128,64]{2,3,1,0:T(8,128)(2,1)S(1)}, bf16[1,9,128,64]{2,3,1,0:T(8,128)(2,1)}, u32[]{:S(2)}) copy-start(bf16[1,9,128,64]{2,3,1,0:T(8,128)(2,1)} %param.7) | copy-start | bytes 442372
  0.6 8.6 %collective-permute-start = (bf16[24,24,128]{2,1,0:T(8,128)(2,1)}, bf16[24,24,128]{2,1,0:T(8,128)(2,1)S(1)}, u32[]{:S(2)}, u32[]{:S(2)}) collective-permute-start(bf16[24,24,128]{2,1,0:T(8,128)(2,1)} %bitcast.48), channel_id=1, source_target_pairs={{0,0},{1,1},{2,2},{3,3},{4,17},{5,5},{6,6},{7,7},{8,18},{9,22},{10... | collective-permute-start | bytes 442376 | tf_op jit(solution)/shard_map/ppermute | solution.py:56
  2.3 6.1 %copy-start.1 = (bf16[1,64,128]{2,1,0:T(8,128)(2,1)S(1)}, bf16[1,64,128]{2,1,0:T(8,128)(2,1)}, u32[]{:S(2)}) copy-start(bf16[1,64,128]{2,1,0:T(8,128)(2,1)} %param.9) | copy-start | bytes 49156
  3.2 6.5 %collective-permute-start.2 = (bf16[10,24,128]{2,1,0:T(8,128)(2,1)S(1)}, bf16[10,24,128]{2,1,0:T(8,128)(2,1)S(1)}, u32[]{:S(2)}, u32[]{:S(2)}) collective-permute-start(bf16[10,24,128]{2,1,0:T(8,128)(2,1)S(1)} %get-tuple-element.98), channel_id=1, source_target_pairs={{0,17},{1,5},{2,6},{3,7},{4,0},{5,1},{6,2},{7,3},{8,19},{9,23},{10... | collective-permute-start | bytes 184328 | tf_op jit(solution)/shard_map/ppermute | solution.py:56
  7.8 2.0 %collective-permute-start.1 = (bf16[10,24,128]{2,1,0:T(8,128)(2,1)S(1)}, bf16[10,24,128]{2,1,0:T(8,128)(2,1)S(1)}, u32[]{:S(2)}, u32[]{:S(2)}) collective-permute-start(bf16[10,24,128]{2,1,0:T(8,128)(2,1)S(1)} %get-tuple-element.99), channel_id=1, source_target_pairs={{4,18},{5,22},{6,10},{7,11},{8,17},{9,5},{10,6},{11,7},{20,24},{21... | collective-permute-start | bytes 184328 | tf_op jit(solution)/shard_map/ppermute | solution.py:56
  8.4 0.7 copy-start.2
  9.1 7.6 %collective-permute-start.5 = (bf16[656,128]{1,0:T(8,128)(2,1)S(1)}, bf16[656,128]{1,0:T(8,128)(2,1)S(1)}, u32[]{:S(2)}, u32[]{:S(2)}) collective-permute-start(bf16[656,128]{1,0:T(8,128)(2,1)S(1)} %fusion.1.mine), channel_id=1, source_target_pairs={{0,16},{16,0},{1,17},{17,1},{2,18},{18,2},{3,19},{19,3},{4,20},{20... | collective-permute-start | bytes 503816 | tf_op jit(solution)/shard_map/ppermute | solution.py:497
  9.9 6.2 %copy-start.3 = (bf16[1,24,24,128]{3,2,1,0:T(8,128)(2,1)S(1)}, bf16[1,24,24,128]{3,2,1,0:T(8,128)(2,1)}, u32[]{:S(2)}) copy-start(bf16[1,24,24,128]{3,2,1,0:T(8,128)(2,1)} %param.6) | copy-start | bytes 442372
  9.9 7.2 %collective-permute-start.3 = (bf16[10,44,128]{2,0,1:T(8,128)(2,1)S(1)}, bf16[10,44,128]{2,0,1:T(8,128)(2,1)S(1)}, u32[]{:S(2)}, u32[]{:S(2)}) collective-permute-start(bf16[10,44,128]{2,0,1:T(8,128)(2,1)S(1)} %get-tuple-element.45), channel_id=1, source_target_pairs={{1,2},{2,1},{5,6},{6,5},{22,10},{10,22},{23,27},{27,23},{4,8},{8,4... | collective-permute-start | bytes 337928 | tf_op jit(solution)/shard_map/ppermute | solution.py:56
  10.7 8.8 %collective-permute-start.4 = (bf16[10,44,128]{2,0,1:T(8,128)(2,1)S(1)}, bf16[10,44,128]{2,0,1:T(8,128)(2,1)S(1)}, u32[]{:S(2)}, u32[]{:S(2)}) collective-permute-start(bf16[10,44,128]{2,0,1:T(8,128)(2,1)S(1)} %get-tuple-element.46), channel_id=1, source_target_pairs={{0,1},{1,0},{2,3},{3,2},{17,5},{5,17},{6,7},{7,6},{18,22},{22,18},... | collective-permute-start | bytes 337928 | tf_op jit(solution)/shard_map/ppermute | solution.py:56
  16.1 6.8 %collective-permute-start.6 = (bf16[24,24,128]{2,1,0:T(8,128)(2,1)S(1)}, bf16[24,24,128]{2,1,0:T(8,128)(2,1)S(1)}, u32[]{:S(2)}, u32[]{:S(2)}) collective-permute-start(bf16[24,24,128]{2,1,0:T(8,128)(2,1)S(1)} %bitcast.51), channel_id=1, source_target_pairs={{0,0},{1,1},{2,2},{3,3},{4,17},{5,5},{6,6},{7,7},{8,18},{9,22},{10... | collective-permute-start | bytes 442376 | tf_op jit(solution)/shard_map/ppermute | solution.py:56
  22.9 0.7 collective-permute-start.7
  25.6 13.1 %collective-permute-start.8 = (bf16[12,24,128]{2,1,0:T(8,128)(2,1)S(1)}, bf16[12,24,128]{2,1,0:T(8,128)(2,1)S(1)}, u32[]{:S(2)}, u32[]{:S(2)}) collective-permute-start(bf16[12,24,128]{2,1,0:T(8,128)(2,1)S(1)} %get-tuple-element.57), channel_id=1, source_target_pairs={{17,18},{5,22},{6,10},{7,11},{18,17},{22,5},{10,6},{11,7},{20,24},... | collective-permute-start | bytes 221192 | tf_op jit(solution)/shard_map/ppermute | solution.py:56
  26.3 14.4 %collective-permute-start.9 = (bf16[12,24,128]{2,1,0:T(8,128)(2,1)S(1)}, bf16[12,24,128]{2,1,0:T(8,128)(2,1)S(1)}, u32[]{:S(2)}, u32[]{:S(2)}) collective-permute-start(bf16[12,24,128]{2,1,0:T(8,128)(2,1)S(1)} %get-tuple-element.58), channel_id=1, source_target_pairs={{0,17},{1,5},{2,6},{3,7},{17,0},{5,1},{6,2},{7,3},{18,19},{22,23},... | collective-permute-start | bytes 221192 | tf_op jit(solution)/shard_map/ppermute | solution.py:56
  40.9 6.1 %collective-permute-start.10 = (bf16[12,44,128]{2,0,1:T(8,128)(2,1)S(1)}, bf16[12,44,128]{2,0,1:T(8,128)(2,1)S(1)}, u32[]{:S(2)}, u32[]{:S(2)}) collective-permute-start(bf16[12,44,128]{2,0,1:T(8,128)(2,1)S(1)} %maximum_bitcast_fusion), channel_id=1, source_target_pairs={{1,2},{2,1},{5,6},{6,5},{22,10},{10,22},{23,27},{27,23},{4,8},{8,4... | collective-permute-start | bytes 405512 | tf_op jit(solution)/shard_map/ppermute | solution.py:56
  41.6 7.9 %collective-permute-start.11 = (bf16[12,44,128]{2,0,1:T(8,128)(2,1)S(1)}, bf16[12,44,128]{2,0,1:T(8,128)(2,1)S(1)}, u32[]{:S(2)}, u32[]{:S(2)}) collective-permute-start(bf16[12,44,128]{2,0,1:T(8,128)(2,1)S(1)} %maximum_bitcast_fusion.1), channel_id=1, source_target_pairs={{0,1},{1,0},{2,3},{3,2},{17,5},{5,17},{6,7},{7,6},{18,22},{22,18},... | collective-permute-start | bytes 405512 | tf_op jit(solution)/shard_map/ppermute | solution.py:56
  52.4 1.7 %collective-permute-start.12 = (bf16[656,128]{1,0:T(8,128)(2,1)S(1)}, bf16[656,128]{1,0:T(8,128)(2,1)S(1)}, u32[]{:S(2)}, u32[]{:S(2)}) collective-permute-start(bf16[656,128]{1,0:T(8,128)(2,1)S(1)} %get-tuple-element.73), channel_id=1, source_target_pairs={{0,16},{16,0},{1,17},{17,1},{2,18},{18,2},{3,19},{19,3},{4,20},{20... | collective-permute-start | bytes 503816 | tf_op jit(solution)/shard_map/ppermute | solution.py:623
  54.8 15.0 %all-to-all-start = ((bf16[16,48,128]{2,1,0:T(8,128)(2,1)}), bf16[16,48,128]{2,1,0:T(8,128)(2,1)S(1)}, u32[]{:S(2)}, u32[]{:S(2)}) async-start(bf16[16,48,128]{2,1,0:T(8,128)(2,1)} %pair.1), calls=%async_computation | async-start | bytes 393216 | tf_op jit(solution)/shard_map/all_to_all | solution.py:633
  60.3 9.5 %collective-permute-start.13 = (bf16[24,24,128]{2,1,0:T(8,128)(2,1)S(1)}, bf16[24,24,128]{2,1,0:T(8,128)(2,1)S(1)}, u32[]{:S(2)}, u32[]{:S(2)}) collective-permute-start(bf16[24,24,128]{2,1,0:T(8,128)(2,1)S(1)} %input.1), channel_id=1, source_target_pairs={{0,0},{1,1},{2,2},{3,3},{17,4},{5,5},{6,6},{7,7},{18,8},{22,9},{10... | collective-permute-start | bytes 442376 | tf_op jit(solution)/shard_map/ppermute | solution.py:56

commit v17 on v16

--- a/solution.py
+++ b/solution.py
@@ -124,7 +124,7 @@
         last[rows, :, high] = window[2]
         return 0
 
-    lax.fori_loop(0, source.shape[0] // 4, step, 0)
+    lax.fori_loop(0, source.shape[0] // 4, step, 0, unroll=True)
 
 
 def taps_sum(pairs, last, top, rows, dilation, weights):
@@ -176,7 +176,7 @@
         store(top, pre.reshape(8, wide, pre.shape[1]), branch)
         return 0
 
-    lax.fori_loop(0, (full - 2 * FIRST_DILATION) // 8, rows, 0)
+    lax.fori_loop(0, (full - 2 * FIRST_DILATION) // 8, rows, 0, unroll=True)
 
 
 def own_kernel(
@@ -238,7 +238,7 @@
         pre_second[pl.ds(top, 8)] = total.reshape(8, small, total.shape[1])
         return 0
 
-    lax.fori_loop(0, side // 8, rows, 0)
+    lax.fori_loop(0, side // 8, rows, 0, unroll=True)
     bottle_second[...] = positive(pre_second[:, :, :inner]).astype(BF16)
 
     turned = jnp.swapaxes(other[span:, :side].astype(F32), 0, 1)
@@ -377,7 +377,7 @@
         grads[here, :small] = grad.reshape(7, small, channels)
         return 0
 
-    lax.fori_loop(0, near // 7, sections, 0)
+    lax.fori_loop(0, near // 7, sections, 0, unroll=True)
     for b in (-1, 0, 1):
         at = first * (1 - b)
         windows[b + 1] = grads[:, at : at + small].astype(BF16)
@@ -431,7 +431,7 @@
         out[here] = (grad_first[here].astype(F32) + total).astype(BF16)
         return 0
 
-    lax.fori_loop(0, side // 8, rows, 0)
+    lax.fori_loop(0, side // 8, rows, 0, unroll=True)
 
 
 def total_kernel(scale, parts, rows, ends):

time: 85.1 us -> 84.2 us (0.989)
  Pallas kernels: 11.9 us -> 10.2 us
    pallas_call x10, Pallas kernels: 11.9 us -> 10.2 us  [call(): pl.pallas_call(kernel, name=name, out_shape=outs, scratch_shapes=[pltpu.V...]
  transfers between devices with their start and end apart: 15 -> 15, of which waited for: 6 -> 6; matrix products, arithmetic and copies ran while one was open for 2% -> 2% of each run, Pallas kernels for 7% -> 6%
where the time goes in v17:
time: 84.2 us; the launch traced here: 83.4 us
  starting transfers between devices  39.8 us (47%)
  waiting for transfers between devices  16.5 us (20%)
  blocking collectives  13.7 us (16%)
  Pallas kernels  10.2 us (12%)
  other arithmetic  1.39 us (2%)
  between operations  1.03 us (1%)
    ppermute x12, starting transfers between devices, permute(): return lax.ppermute(x, ALL, [found for found in pairs if found is not None])  33.6 us
    all_to_all x1, blocking collectives, local(): lax.all_to_all(rows, GRID, 0, 0, tiled=True)  13.7 us
    pallas_call x10, Pallas kernels, call(): pl.pallas_call(kernel, name=name, out_shape=outs, scratch_shapes=[pltpu.V...  10.2 us
    all_to_all x1, waiting for transfers between devices, local(): parts = lax.all_to_all(parts, GRID, 0, 0, tiled=True)  8.8 us
    ppermute x12, waiting for transfers between devices, permute(): return lax.ppermute(x, ALL, [found for found in pairs if found is not None])  7.32 us
    all_to_all x1, starting transfers between devices, local(): parts = lax.all_to_all(parts, GRID, 0, 0, tiled=True)  5.48 us
  transfers between devices with their start and end apart: 15, of which 6 were waited for; matrix products, arithmetic and copies ran while one was open for 2% of the time, Pallas kernels for 6%

profile of v17, /device:TPU:0, one launch (start us, length us, event | category | flops | bytes accessed | tf_op | source)
XLA Modules:
  0.0 83.4 jit_solution(1601524713083068749)
XLA Ops:
  0.6 0.0 copy-start
  0.6 1.7 %collective-permute-start = (bf16[24,24,128]{2,1,0:T(8,128)(2,1)}, bf16[24,24,128]{2,1,0:T(8,128)(2,1)S(1)}, u32[]{:S(2)}, u32[]{:S(2)}) collective-permute-start(bf16[24,24,128]{2,1,0:T(8,128)(2,1)} %bitcast.48), channel_id=1, source_target_pairs={{0,0},{1,1},{2,2},{3,3},{4,17},{5,5},{6,6},{7,7},{8,18},{9,22},{10... | collective-permute-start | bytes 442376 | tf_op jit(solution)/shard_map/ppermute | solution.py:56
  2.3 0.9 %select_bitcast_fusion.6 = (bf16[10,24,128]{2,1,0:T(8,128)(2,1)S(1)}, bf16[10,24,128]{2,1,0:T(8,128)(2,1)S(1)}) fusion(pred[]{:T(512)S(6)} %eq.14, bf16[1,24,24,128]{3,2,1,0:T(8,128)(2,1)} %param.5), kind=kLoop, calls=%fused_computation.16 | loop fusion | flops 61440 | bytes 245761 | tf_op jit(solution)/shard_map/jit(_where)/select_n | solution.py:475
  3.2 4.5 %collective-permute-start.2 = (bf16[10,24,128]{2,1,0:T(8,128)(2,1)S(1)}, bf16[10,24,128]{2,1,0:T(8,128)(2,1)S(1)}, u32[]{:S(2)}, u32[]{:S(2)}) collective-permute-start(bf16[10,24,128]{2,1,0:T(8,128)(2,1)S(1)} %get-tuple-element.98), channel_id=1, source_target_pairs={{0,17},{1,5},{2,6},{3,7},{4,0},{5,1},{6,2},{7,3},{8,19},{9,23},{10... | collective-permute-start | bytes 184328 | tf_op jit(solution)/shard_map/ppermute | solution.py:56
  7.8 0.7 collective-permute-start.1
  8.4 0.0 copy-start.2
  8.4 0.0 copy-done
  8.5 0.6 copy-done.2
  9.1 0.1 collective-permute-start.5
  9.2 0.0 collective-permute-done.tile
  9.3 0.4 collective-permute-done.2
  9.8 0.0 collective-permute-done.1
  9.9 0.0 copy-start.3
  9.9 0.8 collective-permute-start.3
  10.7 5.3 %collective-permute-start.4 = (bf16[10,44,128]{2,0,1:T(8,128)(2,1)S(1)}, bf16[10,44,128]{2,0,1:T(8,128)(2,1)S(1)}, u32[]{:S(2)}, u32[]{:S(2)}) collective-permute-start(bf16[10,44,128]{2,0,1:T(8,128)(2,1)S(1)} %get-tuple-element.46), channel_id=1, source_target_pairs={{0,1},{1,0},{2,3},{3,2},{17,5},{5,17},{6,7},{7,6},{18,22},{22,18},... | collective-permute-start | bytes 337928 | tf_op jit(solution)/shard_map/ppermute | solution.py:56
  16.1 0.7 collective-permute-start.6
  16.7 0.0 collective-permute-done.5.theirs
  16.7 0.4 weights.1
  17.1 0.0 collective-permute-done.3
  17.1 2.4 %collective-permute-done.4 = bf16[10,44,128]{2,0,1:T(8,128)(2,1)S(1)} collective-permute-done((bf16[10,44,128]{2,0,1:T(8,128)(2,1)S(1)}, bf16[10,44,128]{2,0,1:T(8,128)(2,1)S(1)}, u32[]{:S(2)}, u32[]{:S(2)}) %collective-permute-start.4) | collective-permute-done | bytes 112672 | tf_op jit(solution)/shard_map/ppermute | solution.py:56
  19.5 2.9 %own_branch.1 = (bf16[64,40,128]{2,1,0:T(8,128)(2,1)S(1)}, f32[40,48,64]{2,1,0:T(8,128)S(1)}) custom-call(bf16[24,24,128]{2,1,0:T(8,128)(2,1)S(1)} %collective-permute-done.tile, bf16[10,24,128]{2,1,0:T(8,128)(2,1)S(1)} %get-tuple-element.101.above, bf16[10,24,128]{2,1,0:T(8,128)(2,1)S(1)} %get-tuple-element.100.below, ...), custom_call_target="tpu_custom_call" | custom-call | flops 6291456000 | bytes 1806592 | tf_op jit(solution)/shard_map/own_branch/pallas_call | solution.py:455
  22.4 0.0 collective-permute-done.6
  22.4 0.7 collective-permute-start.7
  23.2 0.0 collective-permute-done.7.other
  23.2 1.2 %middle.1 = (bf16[28,32,128]{2,1,0:T(8,128)(2,1)S(1)}, bf16[40,32,256]{2,1,0:T(8,128)(2,1)S(1)}, bf16[48,32,256]{2,1,0:T(8,128)(2,1)S(1)}, bf16[24,32,64]{2,1,0:...) custom-call(bf16[64,40,128]{2,1,0:T(8,128)(2,1)S(1)} %constant_dynam, ...), custom_call_target="tpu_custom_call" | custom-call | flops 301989888 | bytes 3949056 | tf_op jit(solution)/shard_map/middle/pallas_call | solution.py:455
  24.4 0.7 collective-permute-start.8
  25.0 12.8 %collective-permute-start.9 = (bf16[12,24,128]{2,1,0:T(8,128)(2,1)S(1)}, bf16[12,24,128]{2,1,0:T(8,128)(2,1)S(1)}, u32[]{:S(2)}, u32[]{:S(2)}) collective-permute-start(bf16[12,24,128]{2,1,0:T(8,128)(2,1)S(1)} %get-tuple-element.58), channel_id=1, source_target_pairs={{0,17},{1,5},{2,6},{3,7},{17,0},{5,1},{6,2},{7,3},{18,19},{22,23},... | collective-permute-start | bytes 221192 | tf_op jit(solution)/shard_map/ppermute | solution.py:56
  37.9 0.0 collective-permute-done.8
  37.9 1.9 %collective-permute-done.9 = bf16[12,24,128]{2,1,0:T(8,128)(2,1)S(1)} collective-permute-done((bf16[12,24,128]{2,1,0:T(8,128)(2,1)S(1)}, bf16[12,24,128]{2,1,0:T(8,128)(2,1)S(1)}, u32[]{:S(2)}, u32[]{:S(2)}) %collective-permute-start.9) | collective-permute-done | bytes 73760 | tf_op jit(solution)/shard_map/ppermute | solution.py:56
  39.9 0.1 maximum_bitcast_fusion
  40.0 0.7 collective-permute-start.10
  40.7 0.1 maximum_bitcast_fusion.1
  40.8 4.4 %collective-permute-start.11 = (bf16[12,44,128]{2,0,1:T(8,128)(2,1)S(1)}, bf16[12,44,128]{2,0,1:T(8,128)(2,1)S(1)}, u32[]{:S(2)}, u32[]{:S(2)}) collective-permute-start(bf16[12,44,128]{2,0,1:T(8,128)(2,1)S(1)} %maximum_bitcast_fusion.1), channel_id=1, source_target_pairs={{0,1},{1,0},{2,3},{3,2},{17,5},{5,17},{6,7},{7,6},{18,22},{22,18},... | collective-permute-start | bytes 405512 | tf_op jit(solution)/shard_map/ppermute | solution.py:56
  45.2 0.4 near.1
  45.6 0.5 second_sums.1
  46.1 0.0 collective-permute-done.10
  46.1 2.5 %collective-permute-done.11 = bf16[12,44,128]{2,0,1:T(8,128)(2,1)S(1)} collective-permute-done((bf16[12,44,128]{2,0,1:T(8,128)(2,1)S(1)}, bf16[12,44,128]{2,0,1:T(8,128)(2,1)S(1)}, u32[]{:S(2)}, u32[]{:S(2)}) %collective-permute-start.11) | collective-permute-done | bytes 135200 | tf_op jit(solution)/shard_map/ppermute | solution.py:56
  48.8 2.7 %backward.1 = (f32[656,128]{1,0:T(8,128)S(1)}, bf16[656,128]{1,0:T(8,128)(2,1)S(1)}, bf16[3,28,32,128]{3,2,1,0:T(8,128)(2,1)S(1)}, bf16[24,24,128]{2,1,0:T(8,128)(2,1)S(1)}) custom-call(bf16[24,32,128]{2,1,0:T(8,128)(2,1)S(1)} %get-tuple-element.55.grad_pre, bf16[24,32,128]{2,1,0:T(8,128)(2,1)S(1)} %get-tuple-element.56.grad_tile, ...), custom_call_target="tpu_custom_call" | custom-call | flops 528482304 | bytes 4337664 | tf_op jit(solution)/shard_map/backward/pallas_call | solution.py:455
  51.5 0.7 collective-permute-start.12
  52.2 0.6 input.1
  52.8 0.4 collective-permute-done.12.other
  53.2 0.7 pair.1
  53.9 5.5 %all-to-all-start = ((bf16[16,48,128]{2,1,0:T(8,128)(2,1)}), bf16[16,48,128]{2,1,0:T(8,128)(2,1)S(1)}, u32[]{:S(2)}, u32[]{:S(2)}) async-start(bf16[16,48,128]{2,1,0:T(8,128)(2,1)} %pair.1), calls=%async_computation | async-start | bytes 393216 | tf_op jit(solution)/shard_map/all_to_all | solution.py:633
  59.4 0.7 collective-permute-start.13
  60.1 8.8 %all-to-all-done.parts = bf16[16,48,128]{2,1,0:T(8,128)(2,1)S(1)} async-done(((bf16[16,48,128]{2,1,0:T(8,128)(2,1)}), bf16[16,48,128]{2,1,0:T(8,128)(2,1)S(1)}, u32[]{:S(2)}, u32[]{:S(2)}) %all-to-all-start) | async-done | bytes 196640 | tf_op jit(solution)/shard_map/all_to_all | solution.py:633
  68.9 0.0 collective-permute-done.13.moved
  68.9 13.7 %all_to_all.10 = bf16[16,40,128]{2,1,0:T(8,128)(2,1)S(1)} all-to-all(bf16[16,40,128]{2,1,0:T(8,128)(2,1)S(1)} %get-tuple-element.80), channel_id=1, replica_groups=mesh['segment'=2,'row'=4,'col'=4] {'row','col'}, dimensions={0} | all-to-all | bytes 327680 | tf_op jit(solution)/shard_map/all_to_all | solution.py:645
  82.6 0.8 outputs.1
  (23 shorter events, 0.5 us)
Async XLA Ops:
  0.6 7.8 %copy-start = (bf16[1,9,128,64]{2,3,1,0:T(8,128)(2,1)S(1)}, bf16[1,9,128,64]{2,3,1,0:T(8,128)(2,1)}, u32[]{:S(2)}) copy-start(bf16[1,9,128,64]{2,3,1,0:T(8,128)(2,1)} %param.7) | copy-start | bytes 442372
  0.6 8.6 %collective-permute-start = (bf16[24,24,128]{2,1,0:T(8,128)(2,1)}, bf16[24,24,128]{2,1,0:T(8,128)(2,1)S(1)}, u32[]{:S(2)}, u32[]{:S(2)}) collective-permute-start(bf16[24,24,128]{2,1,0:T(8,128)(2,1)} %bitcast.48), channel_id=1, source_target_pairs={{0,0},{1,1},{2,2},{3,3},{4,17},{5,5},{6,6},{7,7},{8,18},{9,22},{10... | collective-permute-start | bytes 442376 | tf_op jit(solution)/shard_map/ppermute | solution.py:56
  2.3 6.1 %copy-start.1 = (bf16[1,64,128]{2,1,0:T(8,128)(2,1)S(1)}, bf16[1,64,128]{2,1,0:T(8,128)(2,1)}, u32[]{:S(2)}) copy-start(bf16[1,64,128]{2,1,0:T(8,128)(2,1)} %param.9) | copy-start | bytes 49156
  3.2 6.5 %collective-permute-start.2 = (bf16[10,24,128]{2,1,0:T(8,128)(2,1)S(1)}, bf16[10,24,128]{2,1,0:T(8,128)(2,1)S(1)}, u32[]{:S(2)}, u32[]{:S(2)}) collective-permute-start(bf16[10,24,128]{2,1,0:T(8,128)(2,1)S(1)} %get-tuple-element.98), channel_id=1, source_target_pairs={{0,17},{1,5},{2,6},{3,7},{4,0},{5,1},{6,2},{7,3},{8,19},{9,23},{10... | collective-permute-start | bytes 184328 | tf_op jit(solution)/shard_map/ppermute | solution.py:56
  7.8 2.0 %collective-permute-start.1 = (bf16[10,24,128]{2,1,0:T(8,128)(2,1)S(1)}, bf16[10,24,128]{2,1,0:T(8,128)(2,1)S(1)}, u32[]{:S(2)}, u32[]{:S(2)}) collective-permute-start(bf16[10,24,128]{2,1,0:T(8,128)(2,1)S(1)} %get-tuple-element.99), channel_id=1, source_target_pairs={{4,18},{5,22},{6,10},{7,11},{8,17},{9,5},{10,6},{11,7},{20,24},{21... | collective-permute-start | bytes 184328 | tf_op jit(solution)/shard_map/ppermute | solution.py:56
  8.4 0.7 copy-start.2
  9.1 7.6 %collective-permute-start.5 = (bf16[656,128]{1,0:T(8,128)(2,1)S(1)}, bf16[656,128]{1,0:T(8,128)(2,1)S(1)}, u32[]{:S(2)}, u32[]{:S(2)}) collective-permute-start(bf16[656,128]{1,0:T(8,128)(2,1)S(1)} %fusion.1.mine), channel_id=1, source_target_pairs={{0,16},{16,0},{1,17},{17,1},{2,18},{18,2},{3,19},{19,3},{4,20},{20... | collective-permute-start | bytes 503816 | tf_op jit(solution)/shard_map/ppermute | solution.py:497
  9.9 6.2 %copy-start.3 = (bf16[1,24,24,128]{3,2,1,0:T(8,128)(2,1)S(1)}, bf16[1,24,24,128]{3,2,1,0:T(8,128)(2,1)}, u32[]{:S(2)}) copy-start(bf16[1,24,24,128]{3,2,1,0:T(8,128)(2,1)} %param.6) | copy-start | bytes 442372
  9.9 7.2 %collective-permute-start.3 = (bf16[10,44,128]{2,0,1:T(8,128)(2,1)S(1)}, bf16[10,44,128]{2,0,1:T(8,128)(2,1)S(1)}, u32[]{:S(2)}, u32[]{:S(2)}) collective-permute-start(bf16[10,44,128]{2,0,1:T(8,128)(2,1)S(1)} %get-tuple-element.45), channel_id=1, source_target_pairs={{1,2},{2,1},{5,6},{6,5},{22,10},{10,22},{23,27},{27,23},{4,8},{8,4... | collective-permute-start | bytes 337928 | tf_op jit(solution)/shard_map/ppermute | solution.py:56
  10.7 8.8 %collective-permute-start.4 = (bf16[10,44,128]{2,0,1:T(8,128)(2,1)S(1)}, bf16[10,44,128]{2,0,1:T(8,128)(2,1)S(1)}, u32[]{:S(2)}, u32[]{:S(2)}) collective-permute-start(bf16[10,44,128]{2,0,1:T(8,128)(2,1)S(1)} %get-tuple-element.46), channel_id=1, source_target_pairs={{0,1},{1,0},{2,3},{3,2},{17,5},{5,17},{6,7},{7,6},{18,22},{22,18},... | collective-permute-start | bytes 337928 | tf_op jit(solution)/shard_map/ppermute | solution.py:56
  16.1 6.3 %collective-permute-start.6 = (bf16[24,24,128]{2,1,0:T(8,128)(2,1)S(1)}, bf16[24,24,128]{2,1,0:T(8,128)(2,1)S(1)}, u32[]{:S(2)}, u32[]{:S(2)}) collective-permute-start(bf16[24,24,128]{2,1,0:T(8,128)(2,1)S(1)} %bitcast.51), channel_id=1, source_target_pairs={{0,0},{1,1},{2,2},{3,3},{4,17},{5,5},{6,6},{7,7},{8,18},{9,22},{10... | collective-permute-start | bytes 442376 | tf_op jit(solution)/shard_map/ppermute | solution.py:56
  22.4 0.7 collective-permute-start.7
  24.4 13.5 %collective-permute-start.8 = (bf16[12,24,128]{2,1,0:T(8,128)(2,1)S(1)}, bf16[12,24,128]{2,1,0:T(8,128)(2,1)S(1)}, u32[]{:S(2)}, u32[]{:S(2)}) collective-permute-start(bf16[12,24,128]{2,1,0:T(8,128)(2,1)S(1)} %get-tuple-element.57), channel_id=1, source_target_pairs={{17,18},{5,22},{6,10},{7,11},{18,17},{22,5},{10,6},{11,7},{20,24},... | collective-permute-start | bytes 221192 | tf_op jit(solution)/shard_map/ppermute | solution.py:56
  25.0 14.8 %collective-permute-start.9 = (bf16[12,24,128]{2,1,0:T(8,128)(2,1)S(1)}, bf16[12,24,128]{2,1,0:T(8,128)(2,1)S(1)}, u32[]{:S(2)}, u32[]{:S(2)}) collective-permute-start(bf16[12,24,128]{2,1,0:T(8,128)(2,1)S(1)} %get-tuple-element.58), channel_id=1, source_target_pairs={{0,17},{1,5},{2,6},{3,7},{17,0},{5,1},{6,2},{7,3},{18,19},{22,23},... | collective-permute-start | bytes 221192 | tf_op jit(solution)/shard_map/ppermute | solution.py:56
  40.0 6.1 %collective-permute-start.10 = (bf16[12,44,128]{2,0,1:T(8,128)(2,1)S(1)}, bf16[12,44,128]{2,0,1:T(8,128)(2,1)S(1)}, u32[]{:S(2)}, u32[]{:S(2)}) collective-permute-start(bf16[12,44,128]{2,0,1:T(8,128)(2,1)S(1)} %maximum_bitcast_fusion), channel_id=1, source_target_pairs={{1,2},{2,1},{5,6},{6,5},{22,10},{10,22},{23,27},{27,23},{4,8},{8,4... | collective-permute-start | bytes 405512 | tf_op jit(solution)/shard_map/ppermute | solution.py:56
  40.8 7.9 %collective-permute-start.11 = (bf16[12,44,128]{2,0,1:T(8,128)(2,1)S(1)}, bf16[12,44,128]{2,0,1:T(8,128)(2,1)S(1)}, u32[]{:S(2)}, u32[]{:S(2)}) collective-permute-start(bf16[12,44,128]{2,0,1:T(8,128)(2,1)S(1)} %maximum_bitcast_fusion.1), channel_id=1, source_target_pairs={{0,1},{1,0},{2,3},{3,2},{17,5},{5,17},{6,7},{7,6},{18,22},{22,18},... | collective-permute-start | bytes 405512 | tf_op jit(solution)/shard_map/ppermute | solution.py:56
  51.5 1.7 %collective-permute-start.12 = (bf16[656,128]{1,0:T(8,128)(2,1)S(1)}, bf16[656,128]{1,0:T(8,128)(2,1)S(1)}, u32[]{:S(2)}, u32[]{:S(2)}) collective-permute-start(bf16[656,128]{1,0:T(8,128)(2,1)S(1)} %get-tuple-element.73), channel_id=1, source_target_pairs={{0,16},{16,0},{1,17},{17,1},{2,18},{18,2},{3,19},{19,3},{4,20},{20... | collective-permute-start | bytes 503816 | tf_op jit(solution)/shard_map/ppermute | solution.py:623
  53.9 15.0 %all-to-all-start = ((bf16[16,48,128]{2,1,0:T(8,128)(2,1)}), bf16[16,48,128]{2,1,0:T(8,128)(2,1)S(1)}, u32[]{:S(2)}, u32[]{:S(2)}) async-start(bf16[16,48,128]{2,1,0:T(8,128)(2,1)} %pair.1), calls=%async_computation | async-start | bytes 393216 | tf_op jit(solution)/shard_map/all_to_all | solution.py:633
  59.4 9.5 %collective-permute-start.13 = (bf16[24,24,128]{2,1,0:T(8,128)(2,1)S(1)}, bf16[24,24,128]{2,1,0:T(8,128)(2,1)S(1)}, u32[]{:S(2)}, u32[]{:S(2)}) collective-permute-start(bf16[24,24,128]{2,1,0:T(8,128)(2,1)S(1)} %input.1), channel_id=1, source_target_pairs={{0,0},{1,1},{2,2},{3,3},{17,4},{5,5},{6,6},{7,7},{18,8},{22,9},{10... | collective-permute-start | bytes 442376 | tf_op jit(solution)/shard_map/ppermute | solution.py:56

commit v18 on v17

--- a/solution.py
+++ b/solution.py
@@ -641,7 +641,6 @@
         parts.size,
         parts,
     )
-    rows, _ = lax.optimization_barrier((rows, input_gradient))
     rows = lax.all_to_all(rows, GRID, 0, 0, tiled=True).reshape(devices * share, channels)
     conv_gradient, bias_gradient, out_gradient, input_gradient = call(
         outputs_kernel,

time: 84.2 us -> 83.1 us (0.987)
  the two profiles are of different devices: /device:TPU:0 before, /device:TPU:2 now
where the time goes in v18:
time: 83.1 us; the launch traced here: 82.6 us
  starting transfers between devices  36.3 us (44%)
  waiting for transfers between devices  19 us (23%)
  blocking collectives  13.9 us (17%)
  Pallas kernels  10.2 us (12%)
  other arithmetic  1.39 us (2%)
  between operations  1.05 us (1%)
    ppermute x12, starting transfers between devices, permute(): return lax.ppermute(x, ALL, [found for found in pairs if found is not None])  30.7 us
    ppermute x12, waiting for transfers between devices, permute(): return lax.ppermute(x, ALL, [found for found in pairs if found is not None])  18.2 us
    all_to_all x1, blocking collectives, local(): parts = lax.all_to_all(parts, GRID, 0, 0, tiled=True)  13.9 us
    pallas_call x10, Pallas kernels, call(): pl.pallas_call(kernel, name=name, out_shape=outs, scratch_shapes=[pltpu.V...  10.2 us
    all_to_all x1, starting transfers between devices, local(): lax.all_to_all(rows, GRID, 0, 0, tiled=True)  5.47 us
  transfers between devices with their start and end apart: 15, of which 7 were waited for; matrix products, arithmetic and copies ran while one was open for 2% of the time, Pallas kernels for 6%

profile of v18, /device:TPU:2, one launch (start us, length us, event | category | flops | bytes accessed | tf_op | source)
XLA Modules:
  0.0 82.6 jit_solution(3522225685128365502)
XLA Ops:
  0.6 0.0 copy-start
  0.6 3.0 %collective-permute-start = (bf16[24,24,128]{2,1,0:T(8,128)(2,1)}, bf16[24,24,128]{2,1,0:T(8,128)(2,1)S(1)}, u32[]{:S(2)}, u32[]{:S(2)}) collective-permute-start(bf16[24,24,128]{2,1,0:T(8,128)(2,1)} %bitcast.48), channel_id=1, source_target_pairs={{0,0},{1,1},{2,2},{3,3},{4,17},{5,5},{6,6},{7,7},{8,18},{9,22},{10... | collective-permute-start | bytes 442376 | tf_op jit(solution)/shard_map/ppermute | solution.py:56
  3.7 0.0 copy-start.1
  3.7 0.9 %select_bitcast_fusion.6 = (bf16[10,24,128]{2,1,0:T(8,128)(2,1)S(1)}, bf16[10,24,128]{2,1,0:T(8,128)(2,1)S(1)}) fusion(pred[]{:T(512)S(6)} %eq.14, bf16[1,24,24,128]{3,2,1,0:T(8,128)(2,1)} %param.5), kind=kLoop, calls=%fused_computation.16 | loop fusion | flops 61440 | bytes 245761 | tf_op jit(solution)/shard_map/jit(_where)/select_n | solution.py:475
  4.6 0.1 collective-permute-start.2
  4.6 6.5 %collective-permute-start.1 = (bf16[10,24,128]{2,1,0:T(8,128)(2,1)S(1)}, bf16[10,24,128]{2,1,0:T(8,128)(2,1)S(1)}, u32[]{:S(2)}, u32[]{:S(2)}) collective-permute-start(bf16[10,24,128]{2,1,0:T(8,128)(2,1)S(1)} %get-tuple-element.97), channel_id=1, source_target_pairs={{4,18},{5,22},{6,10},{7,11},{8,17},{9,5},{10,6},{11,7},{20,24},{21... | collective-permute-start | bytes 184328 | tf_op jit(solution)/shard_map/ppermute | solution.py:56
  11.1 0.0 copy-start.2
  11.2 0.6 copy-done.2
  11.8 0.1 collective-permute-start.5
  11.9 0.0 collective-permute-done.tile
  12.0 0.0 collective-permute-done.2
  12.1 0.9 %collective-permute-done.1 = bf16[10,24,128]{2,1,0:T(8,128)(2,1)S(1)} collective-permute-done((bf16[10,24,128]{2,1,0:T(8,128)(2,1)S(1)}, bf16[10,24,128]{2,1,0:T(8,128)(2,1)S(1)}, u32[]{:S(2)}, u32[]{:S(2)}) %collective-permute-start.1) | collective-permute-done | bytes 61472 | tf_op jit(solution)/shard_map/ppermute | solution.py:56
  13.0 0.0 copy-start.3
  13.0 3.1 %collective-permute-start.3 = (bf16[10,44,128]{2,0,1:T(8,128)(2,1)S(1)}, bf16[10,44,128]{2,0,1:T(8,128)(2,1)S(1)}, u32[]{:S(2)}, u32[]{:S(2)}) collective-permute-start(bf16[10,44,128]{2,0,1:T(8,128)(2,1)S(1)} %get-tuple-element.44), channel_id=1, source_target_pairs={{1,2},{2,1},{5,6},{6,5},{22,10},{10,22},{23,27},{27,23},{4,8},{8,4... | collective-permute-start | bytes 337928 | tf_op jit(solution)/shard_map/ppermute | solution.py:56
  16.1 0.1 collective-permute-start.4
  16.3 4.3 %collective-permute-start.6 = (bf16[24,24,128]{2,1,0:T(8,128)(2,1)S(1)}, bf16[24,24,128]{2,1,0:T(8,128)(2,1)S(1)}, u32[]{:S(2)}, u32[]{:S(2)}) collective-permute-start(bf16[24,24,128]{2,1,0:T(8,128)(2,1)S(1)} %bitcast.51), channel_id=1, source_target_pairs={{0,0},{1,1},{2,2},{3,3},{4,17},{5,5},{6,6},{7,7},{8,18},{9,22},{10... | collective-permute-start | bytes 442376 | tf_op jit(solution)/shard_map/ppermute | solution.py:56
  20.6 0.0 collective-permute-done.5.theirs
  20.6 0.4 weights.1
  21.0 0.5 collective-permute-done.3
  21.4 0.0 collective-permute-done.4
  21.5 2.9 %own_branch.1 = (bf16[64,40,128]{2,1,0:T(8,128)(2,1)S(1)}, f32[40,48,64]{2,1,0:T(8,128)S(1)}) custom-call(bf16[24,24,128]{2,1,0:T(8,128)(2,1)S(1)} %collective-permute-done.tile, bf16[10,24,128]{2,1,0:T(8,128)(2,1)S(1)} %get-tuple-element.99.above, bf16[10,24,128]{2,1,0:T(8,128)(2,1)S(1)} %get-tuple-element.98.below, ...), custom_call_target="tpu_custom_call" | custom-call | flops 6291456000 | bytes 1806592 | tf_op jit(solution)/shard_map/own_branch/pallas_call | solution.py:455
  24.3 0.0 collective-permute-done.6
  24.4 3.0 %collective-permute-start.7 = (bf16[64,40,128]{2,1,0:T(8,128)(2,1)S(1)}, bf16[64,40,128]{2,1,0:T(8,128)(2,1)S(1)}, u32[]{:S(2)}, u32[]{:S(2)}) collective-permute-start(bf16[64,40,128]{2,1,0:T(8,128)(2,1)S(1)} %constant_dynamic-update-slice_fusion.kept), channel_id=1, source_target_pairs={{0,0},{1,17},{2,18},{3,19},{17,1},{5,5},{6,22},{7,23},{18,2},{22,6... | collective-permute-start | bytes 1966088 | tf_op jit(solution)/shard_map/ppermute | solution.py:56
  27.4 1.7 %collective-permute-done.7.other = bf16[64,40,128]{2,1,0:T(8,128)(2,1)S(1)} collective-permute-done((bf16[64,40,128]{2,1,0:T(8,128)(2,1)S(1)}, bf16[64,40,128]{2,1,0:T(8,128)(2,1)S(1)}, u32[]{:S(2)}, u32[]{:S(2)}) %collective-permute-start.7) | collective-permute-done | bytes 655392 | tf_op jit(solution)/shard_map/ppermute | solution.py:56
  29.1 1.2 %middle.1 = (bf16[28,32,128]{2,1,0:T(8,128)(2,1)S(1)}, bf16[40,32,256]{2,1,0:T(8,128)(2,1)S(1)}, bf16[48,32,256]{2,1,0:T(8,128)(2,1)S(1)}, bf16[24,32,64]{2,1,0:...) custom-call(bf16[64,40,128]{2,1,0:T(8,128)(2,1)S(1)} %constant_dynam, ...), custom_call_target="tpu_custom_call" | custom-call | flops 301989888 | bytes 3949056 | tf_op jit(solution)/shard_map/middle/pallas_call | solution.py:455
  30.3 0.7 collective-permute-start.8
  30.9 5.2 %collective-permute-start.9 = (bf16[12,24,128]{2,1,0:T(8,128)(2,1)S(1)}, bf16[12,24,128]{2,1,0:T(8,128)(2,1)S(1)}, u32[]{:S(2)}, u32[]{:S(2)}) collective-permute-start(bf16[12,24,128]{2,1,0:T(8,128)(2,1)S(1)} %get-tuple-element.57), channel_id=1, source_target_pairs={{0,17},{1,5},{2,6},{3,7},{17,0},{5,1},{6,2},{7,3},{18,19},{22,23},... | collective-permute-start | bytes 221192 | tf_op jit(solution)/shard_map/ppermute | solution.py:56
  36.2 0.0 collective-permute-done.8
  36.2 1.9 %collective-permute-done.9 = bf16[12,24,128]{2,1,0:T(8,128)(2,1)S(1)} collective-permute-done((bf16[12,24,128]{2,1,0:T(8,128)(2,1)S(1)}, bf16[12,24,128]{2,1,0:T(8,128)(2,1)S(1)}, u32[]{:S(2)}, u32[]{:S(2)}) %collective-permute-start.9) | collective-permute-done | bytes 73760 | tf_op jit(solution)/shard_map/ppermute | solution.py:56
  38.3 0.1 maximum_bitcast_fusion
  38.4 2.8 %collective-permute-start.10 = (bf16[12,44,128]{2,0,1:T(8,128)(2,1)S(1)}, bf16[12,44,128]{2,0,1:T(8,128)(2,1)S(1)}, u32[]{:S(2)}, u32[]{:S(2)}) collective-permute-start(bf16[12,44,128]{2,0,1:T(8,128)(2,1)S(1)} %maximum_bitcast_fusion), channel_id=1, source_target_pairs={{1,2},{2,1},{5,6},{6,5},{22,10},{10,22},{23,27},{27,23},{4,8},{8,4... | collective-permute-start | bytes 405512 | tf_op jit(solution)/shard_map/ppermute | solution.py:56
  41.2 0.1 maximum_bitcast_fusion.1
  41.2 0.1 collective-permute-start.11
  41.3 0.4 near.1
  41.7 0.5 second_sums.1
  42.2 4.4 %collective-permute-done.10 = bf16[12,44,128]{2,0,1:T(8,128)(2,1)S(1)} collective-permute-done((bf16[12,44,128]{2,0,1:T(8,128)(2,1)S(1)}, bf16[12,44,128]{2,0,1:T(8,128)(2,1)S(1)}, u32[]{:S(2)}, u32[]{:S(2)}) %collective-permute-start.10) | collective-permute-done | bytes 135200 | tf_op jit(solution)/shard_map/ppermute | solution.py:56
  46.7 0.0 collective-permute-done.11
  46.7 2.7 %backward.1 = (f32[656,128]{1,0:T(8,128)S(1)}, bf16[656,128]{1,0:T(8,128)(2,1)S(1)}, bf16[3,28,32,128]{3,2,1,0:T(8,128)(2,1)S(1)}, bf16[24,24,128]{2,1,0:T(8,128)(2,1)S(1)}) custom-call(bf16[24,32,128]{2,1,0:T(8,128)(2,1)S(1)} %get-tuple-element.54.grad_pre, bf16[24,32,128]{2,1,0:T(8,128)(2,1)S(1)} %get-tuple-element.55.grad_tile, ...), custom_call_target="tpu_custom_call" | custom-call | flops 528482304 | bytes 4337664 | tf_op jit(solution)/shard_map/backward/pallas_call | solution.py:455
  49.5 0.1 collective-permute-start.12
  49.6 0.6 input.1
  50.2 0.8 collective-permute-done.12.other
  51.0 13.9 %all_to_all.10.parts = bf16[16,48,128]{2,1,0:T(8,128)(2,1)S(1)} all-to-all(bf16[16,48,128]{2,1,0:T(8,128)(2,1)S(1)} %pair.1), channel_id=1, replica_groups=mesh['segment'=2,'row'=4,'col'=4] {'row','col'}, dimensions={0} | all-to-all | bytes 393216 | tf_op jit(solution)/shard_map/all_to_all | solution.py:633
  64.9 0.7 total.1
  65.6 5.5 %all-to-all-start.1 = ((bf16[16,40,128]{2,1,0:T(8,128)(2,1)}), bf16[16,40,128]{2,1,0:T(8,128)(2,1)S(1)}, u32[]{:S(2)}, u32[]{:S(2)}) async-start(bf16[16,40,128]{2,1,0:T(8,128)(2,1)} %get-tuple-element.77), calls=%async_computation.1 | async-start | bytes 327680 | tf_op jit(solution)/shard_map/all_to_all | solution.py:644
  71.1 1.9 %collective-permute-start.13 = (bf16[24,24,128]{2,1,0:T(8,128)(2,1)S(1)}, bf16[24,24,128]{2,1,0:T(8,128)(2,1)S(1)}, u32[]{:S(2)}, u32[]{:S(2)}) collective-permute-start(bf16[24,24,128]{2,1,0:T(8,128)(2,1)S(1)} %input.1), channel_id=1, source_target_pairs={{0,0},{1,1},{2,2},{3,3},{17,4},{5,5},{6,6},{7,7},{18,8},{22,9},{10... | collective-permute-start | bytes 442376 | tf_op jit(solution)/shard_map/ppermute | solution.py:56
  73.0 8.8 %collective-permute-done.13.moved = bf16[24,24,128]{2,1,0:T(8,128)(2,1)S(1)} collective-permute-done((bf16[24,24,128]{2,1,0:T(8,128)(2,1)S(1)}, bf16[24,24,128]{2,1,0:T(8,128)(2,1)S(1)}, u32[]{:S(2)}, u32[]{:S(2)}) %collective-permute-start.13) | collective-permute-done | bytes 147488 | tf_op jit(solution)/shard_map/ppermute | solution.py:56
  81.8 0.0 all-to-all-done.1
  81.8 0.8 outputs.1
  (23 shorter events, 0.5 us)
Async XLA Ops:
  0.6 10.5 %copy-start = (bf16[1,9,128,64]{2,3,1,0:T(8,128)(2,1)S(1)}, bf16[1,9,128,64]{2,3,1,0:T(8,128)(2,1)}, u32[]{:S(2)}) copy-start(bf16[1,9,128,64]{2,3,1,0:T(8,128)(2,1)} %param.7) | copy-start | bytes 442372
  0.6 11.3 %collective-permute-start = (bf16[24,24,128]{2,1,0:T(8,128)(2,1)}, bf16[24,24,128]{2,1,0:T(8,128)(2,1)S(1)}, u32[]{:S(2)}, u32[]{:S(2)}) collective-permute-start(bf16[24,24,128]{2,1,0:T(8,128)(2,1)} %bitcast.48), channel_id=1, source_target_pairs={{0,0},{1,1},{2,2},{3,3},{4,17},{5,5},{6,6},{7,7},{8,18},{9,22},{10... | collective-permute-start | bytes 442376 | tf_op jit(solution)/shard_map/ppermute | solution.py:56
  3.7 7.5 %copy-start.1 = (bf16[1,64,128]{2,1,0:T(8,128)(2,1)S(1)}, bf16[1,64,128]{2,1,0:T(8,128)(2,1)}, u32[]{:S(2)}) copy-start(bf16[1,64,128]{2,1,0:T(8,128)(2,1)} %param.9) | copy-start | bytes 49156
  4.6 7.5 %collective-permute-start.2 = (bf16[10,24,128]{2,1,0:T(8,128)(2,1)S(1)}, bf16[10,24,128]{2,1,0:T(8,128)(2,1)S(1)}, u32[]{:S(2)}, u32[]{:S(2)}) collective-permute-start(bf16[10,24,128]{2,1,0:T(8,128)(2,1)S(1)} %get-tuple-element.96), channel_id=1, source_target_pairs={{0,17},{1,5},{2,6},{3,7},{4,0},{5,1},{6,2},{7,3},{8,19},{9,23},{10... | collective-permute-start | bytes 184328 | tf_op jit(solution)/shard_map/ppermute | solution.py:56
  4.6 8.3 %collective-permute-start.1 = (bf16[10,24,128]{2,1,0:T(8,128)(2,1)S(1)}, bf16[10,24,128]{2,1,0:T(8,128)(2,1)S(1)}, u32[]{:S(2)}, u32[]{:S(2)}) collective-permute-start(bf16[10,24,128]{2,1,0:T(8,128)(2,1)S(1)} %get-tuple-element.97), channel_id=1, source_target_pairs={{4,18},{5,22},{6,10},{7,11},{8,17},{9,5},{10,6},{11,7},{20,24},{21... | collective-permute-start | bytes 184328 | tf_op jit(solution)/shard_map/ppermute | solution.py:56
  11.1 0.7 copy-start.2
  11.8 8.8 %collective-permute-start.5 = (bf16[656,128]{1,0:T(8,128)(2,1)S(1)}, bf16[656,128]{1,0:T(8,128)(2,1)S(1)}, u32[]{:S(2)}, u32[]{:S(2)}) collective-permute-start(bf16[656,128]{1,0:T(8,128)(2,1)S(1)} %fusion.1.mine), channel_id=1, source_target_pairs={{0,16},{16,0},{1,17},{17,1},{2,18},{18,2},{3,19},{19,3},{4,20},{20... | collective-permute-start | bytes 503816 | tf_op jit(solution)/shard_map/ppermute | solution.py:497
  13.0 3.2 %copy-start.3 = (bf16[1,24,24,128]{3,2,1,0:T(8,128)(2,1)S(1)}, bf16[1,24,24,128]{3,2,1,0:T(8,128)(2,1)}, u32[]{:S(2)}) copy-start(bf16[1,24,24,128]{3,2,1,0:T(8,128)(2,1)} %param.6) | copy-start | bytes 442372
  13.0 8.4 %collective-permute-start.3 = (bf16[10,44,128]{2,0,1:T(8,128)(2,1)S(1)}, bf16[10,44,128]{2,0,1:T(8,128)(2,1)S(1)}, u32[]{:S(2)}, u32[]{:S(2)}) collective-permute-start(bf16[10,44,128]{2,0,1:T(8,128)(2,1)S(1)} %get-tuple-element.44), channel_id=1, source_target_pairs={{1,2},{2,1},{5,6},{6,5},{22,10},{10,22},{23,27},{27,23},{4,8},{8,4... | collective-permute-start | bytes 337928 | tf_op jit(solution)/shard_map/ppermute | solution.py:56
  16.1 5.3 %collective-permute-start.4 = (bf16[10,44,128]{2,0,1:T(8,128)(2,1)S(1)}, bf16[10,44,128]{2,0,1:T(8,128)(2,1)S(1)}, u32[]{:S(2)}, u32[]{:S(2)}) collective-permute-start(bf16[10,44,128]{2,0,1:T(8,128)(2,1)S(1)} %get-tuple-element.45), channel_id=1, source_target_pairs={{0,1},{1,0},{2,3},{3,2},{17,5},{5,17},{6,7},{7,6},{18,22},{22,18},... | collective-permute-start | bytes 337928 | tf_op jit(solution)/shard_map/ppermute | solution.py:56
  16.3 8.1 %collective-permute-start.6 = (bf16[24,24,128]{2,1,0:T(8,128)(2,1)S(1)}, bf16[24,24,128]{2,1,0:T(8,128)(2,1)S(1)}, u32[]{:S(2)}, u32[]{:S(2)}) collective-permute-start(bf16[24,24,128]{2,1,0:T(8,128)(2,1)S(1)} %bitcast.51), channel_id=1, source_target_pairs={{0,0},{1,1},{2,2},{3,3},{4,17},{5,5},{6,6},{7,7},{8,18},{9,22},{10... | collective-permute-start | bytes 442376 | tf_op jit(solution)/shard_map/ppermute | solution.py:56
  24.4 4.7 %collective-permute-start.7 = (bf16[64,40,128]{2,1,0:T(8,128)(2,1)S(1)}, bf16[64,40,128]{2,1,0:T(8,128)(2,1)S(1)}, u32[]{:S(2)}, u32[]{:S(2)}) collective-permute-start(bf16[64,40,128]{2,1,0:T(8,128)(2,1)S(1)} %constant_dynamic-update-slice_fusion.kept), channel_id=1, source_target_pairs={{0,0},{1,17},{2,18},{3,19},{17,1},{5,5},{6,22},{7,23},{18,2},{22,6... | collective-permute-start | bytes 1966088 | tf_op jit(solution)/shard_map/ppermute | solution.py:56
  30.3 6.0 %collective-permute-start.8 = (bf16[12,24,128]{2,1,0:T(8,128)(2,1)S(1)}, bf16[12,24,128]{2,1,0:T(8,128)(2,1)S(1)}, u32[]{:S(2)}, u32[]{:S(2)}) collective-permute-start(bf16[12,24,128]{2,1,0:T(8,128)(2,1)S(1)} %get-tuple-element.56), channel_id=1, source_target_pairs={{17,18},{5,22},{6,10},{7,11},{18,17},{22,5},{10,6},{11,7},{20,24},... | collective-permute-start | bytes 221192 | tf_op jit(solution)/shard_map/ppermute | solution.py:56
  30.9 7.3 %collective-permute-start.9 = (bf16[12,24,128]{2,1,0:T(8,128)(2,1)S(1)}, bf16[12,24,128]{2,1,0:T(8,128)(2,1)S(1)}, u32[]{:S(2)}, u32[]{:S(2)}) collective-permute-start(bf16[12,24,128]{2,1,0:T(8,128)(2,1)S(1)} %get-tuple-element.57), channel_id=1, source_target_pairs={{0,17},{1,5},{2,6},{3,7},{17,0},{5,1},{6,2},{7,3},{18,19},{22,23},... | collective-permute-start | bytes 221192 | tf_op jit(solution)/shard_map/ppermute | solution.py:56
  38.4 8.3 %collective-permute-start.10 = (bf16[12,44,128]{2,0,1:T(8,128)(2,1)S(1)}, bf16[12,44,128]{2,0,1:T(8,128)(2,1)S(1)}, u32[]{:S(2)}, u32[]{:S(2)}) collective-permute-start(bf16[12,44,128]{2,0,1:T(8,128)(2,1)S(1)} %maximum_bitcast_fusion), channel_id=1, source_target_pairs={{1,2},{2,1},{5,6},{6,5},{22,10},{10,22},{23,27},{27,23},{4,8},{8,4... | collective-permute-start | bytes 405512 | tf_op jit(solution)/shard_map/ppermute | solution.py:56
  41.2 5.4 %collective-permute-start.11 = (bf16[12,44,128]{2,0,1:T(8,128)(2,1)S(1)}, bf16[12,44,128]{2,0,1:T(8,128)(2,1)S(1)}, u32[]{:S(2)}, u32[]{:S(2)}) collective-permute-start(bf16[12,44,128]{2,0,1:T(8,128)(2,1)S(1)} %maximum_bitcast_fusion.1), channel_id=1, source_target_pairs={{0,1},{1,0},{2,3},{3,2},{17,5},{5,17},{6,7},{7,6},{18,22},{22,18},... | collective-permute-start | bytes 405512 | tf_op jit(solution)/shard_map/ppermute | solution.py:56
  49.5 1.5 %collective-permute-start.12 = (bf16[656,128]{1,0:T(8,128)(2,1)S(1)}, bf16[656,128]{1,0:T(8,128)(2,1)S(1)}, u32[]{:S(2)}, u32[]{:S(2)}) collective-permute-start(bf16[656,128]{1,0:T(8,128)(2,1)S(1)} %get-tuple-element.72), channel_id=1, source_target_pairs={{0,16},{16,0},{1,17},{17,1},{2,18},{18,2},{3,19},{19,3},{4,20},{20... | collective-permute-start | bytes 503816 | tf_op jit(solution)/shard_map/ppermute | solution.py:623
  65.6 16.2 %all-to-all-start.1 = ((bf16[16,40,128]{2,1,0:T(8,128)(2,1)}), bf16[16,40,128]{2,1,0:T(8,128)(2,1)S(1)}, u32[]{:S(2)}, u32[]{:S(2)}) async-start(bf16[16,40,128]{2,1,0:T(8,128)(2,1)} %get-tuple-element.77), calls=%async_computation.1 | async-start | bytes 327680 | tf_op jit(solution)/shard_map/all_to_all | solution.py:644
  71.1 10.7 %collective-permute-start.13 = (bf16[24,24,128]{2,1,0:T(8,128)(2,1)S(1)}, bf16[24,24,128]{2,1,0:T(8,128)(2,1)S(1)}, u32[]{:S(2)}, u32[]{:S(2)}) collective-permute-start(bf16[24,24,128]{2,1,0:T(8,128)(2,1)S(1)} %input.1), channel_id=1, source_target_pairs={{0,0},{1,1},{2,2},{3,3},{17,4},{5,5},{6,6},{7,7},{18,8},{22,9},{10... | collective-permute-start | bytes 442376 | tf_op jit(solution)/shard_map/ppermute | solution.py:56

commit v19 on v18

--- a/solution.py
+++ b/solution.py
@@ -441,12 +441,15 @@
     ends[...] = total[share:]
 
 
-def outputs_kernel(rows, ends, moved, conv_gradient, bias_gradient, out_gradient, input_gradient):
+def landed_kernel(moved, input_gradient):
+    input_gradient[...] = moved[...]
+
+
+def outputs_kernel(rows, ends, conv_gradient, bias_gradient, out_gradient):
     count, inner = conv_gradient.shape[0], out_gradient.shape[0]
     conv_gradient[...] = rows[:count].astype(F32)
     out_gradient[...] = rows[count : count + inner].astype(F32)
     bias_gradient[...] = ends[:1, :inner]
-    input_gradient[...] = moved[...]
 
 
 def call(kernel, name, outs, scratch, flops, *operands):
@@ -642,18 +645,17 @@
         parts,
     )
     rows = lax.all_to_all(rows, GRID, 0, 0, tiled=True).reshape(devices * share, channels)
-    conv_gradient, bias_gradient, out_gradient, input_gradient = call(
+    (input_gradient,) = call(
+        landed_kernel, "landed", [((side, side, channels), BF16)], [], side**2 * channels * 400000, input_gradient
+    )
+    rows, input_gradient = lax.optimization_barrier((rows, input_gradient))
+    conv_gradient, bias_gradient, out_gradient = call(
         outputs_kernel,
         "outputs",
-        [
-            ((9 * inner, channels), F32),
-            ((1, inner), F32),
-            ((inner, channels), F32),
-            ((side, side, channels), BF16),
-        ],
+        [((9 * inner, channels), F32), ((1, inner), F32), ((inner, channels), F32)],
         [],
         rows.size,
-        *(rows, ends, input_gradient),
+        *(rows, ends),
     )
     conv_gradient = jnp.swapaxes(conv_gradient.reshape(1, 9, inner, channels), 2, 3)
     return (input_gradient[None], conv_gradient, bias_gradient, out_gradient[None])

time: 83.1 us -> 82 us (0.987)
  the two profiles are of different devices: /device:TPU:2 before, /device:TPU:0 now
where the time goes in v19:
time: 82 us; the launch traced here: 81.5 us
  starting transfers between devices  43.3 us (53%)
  waiting for transfers between devices  23.5 us (29%)
  Pallas kernels  11.5 us (14%)
  other arithmetic  1.39 us (2%)
  between operations  1.03 us (1%)
    ppermute x12, starting transfers between devices, permute(): return lax.ppermute(x, ALL, [found for found in pairs if found is not None])  33.6 us
    pallas_call x11, Pallas kernels, call(): pl.pallas_call(kernel, name=name, out_shape=outs, scratch_shapes=[pltpu.V...  11.5 us
    all_to_all x1, waiting for transfers between devices, local(): parts = lax.all_to_all(parts, GRID, 0, 0, tiled=True)  8.8 us
    ppermute x12, waiting for transfers between devices, permute(): return lax.ppermute(x, ALL, [found for found in pairs if found is not None])  7.32 us
    all_to_all x1, waiting for transfers between devices, local(): lax.all_to_all(rows, GRID, 0, 0, tiled=True)  6.99 us
    all_to_all x1, starting transfers between devices, local(): parts = lax.all_to_all(parts, GRID, 0, 0, tiled=True)  5.48 us
    all_to_all x1, starting transfers between devices, local(): lax.all_to_all(rows, GRID, 0, 0, tiled=True)  3.52 us
  transfers between devices with their start and end apart: 16, of which 7 were waited for; matrix products, arithmetic and copies ran while one was open for 2% of the time, Pallas kernels for 8%

profile of v19, /device:TPU:0, one launch (start us, length us, event | category | flops | bytes accessed | tf_op | source)
XLA Modules:
  0.0 81.5 jit_solution(8647512045582183879)
XLA Ops:
  0.6 1.7 %collective-permute-start = (bf16[24,24,128]{2,1,0:T(8,128)(2,1)}, bf16[24,24,128]{2,1,0:T(8,128)(2,1)S(1)}, u32[]{:S(2)}, u32[]{:S(2)}) collective-permute-start(bf16[24,24,128]{2,1,0:T(8,128)(2,1)} %bitcast.48), channel_id=1, source_target_pairs={{0,0},{1,1},{2,2},{3,3},{4,17},{5,5},{6,6},{7,7},{8,18},{9,22},{10... | collective-permute-start | bytes 442376 | tf_op jit(solution)/shard_map/ppermute | solution.py:56
  2.3 0.9 %select_bitcast_fusion.6 = (bf16[10,24,128]{2,1,0:T(8,128)(2,1)S(1)}, bf16[10,24,128]{2,1,0:T(8,128)(2,1)S(1)}) fusion(pred[]{:T(512)S(6)} %eq.14, bf16[1,24,24,128]{3,2,1,0:T(8,128)(2,1)} %param.5), kind=kLoop, calls=%fused_computation.16 | loop fusion | flops 61440 | bytes 245761 | tf_op jit(solution)/shard_map/jit(_where)/select_n | solution.py:478
  3.2 4.5 %collective-permute-start.2 = (bf16[10,24,128]{2,1,0:T(8,128)(2,1)S(1)}, bf16[10,24,128]{2,1,0:T(8,128)(2,1)S(1)}, u32[]{:S(2)}, u32[]{:S(2)}) collective-permute-start(bf16[10,24,128]{2,1,0:T(8,128)(2,1)S(1)} %get-tuple-element.98), channel_id=1, source_target_pairs={{0,17},{1,5},{2,6},{3,7},{4,0},{5,1},{6,2},{7,3},{8,19},{9,23},{10... | collective-permute-start | bytes 184328 | tf_op jit(solution)/shard_map/ppermute | solution.py:56
  7.8 0.7 collective-permute-start.1
  8.4 0.0 copy-start.2
  8.5 0.6 copy-done.2
  9.1 0.1 collective-permute-start.5
  9.2 0.0 collective-permute-done.tile
  9.3 0.4 collective-permute-done.2
  9.8 0.0 collective-permute-done.1
  9.9 0.0 copy-start.3
  9.9 0.8 collective-permute-start.3
  10.7 5.3 %collective-permute-start.4 = (bf16[10,44,128]{2,0,1:T(8,128)(2,1)S(1)}, bf16[10,44,128]{2,0,1:T(8,128)(2,1)S(1)}, u32[]{:S(2)}, u32[]{:S(2)}) collective-permute-start(bf16[10,44,128]{2,0,1:T(8,128)(2,1)S(1)} %get-tuple-element.46), channel_id=1, source_target_pairs={{0,1},{1,0},{2,3},{3,2},{17,5},{5,17},{6,7},{7,6},{18,22},{22,18},... | collective-permute-start | bytes 337928 | tf_op jit(solution)/shard_map/ppermute | solution.py:56
  16.1 0.7 collective-permute-start.6
  16.7 0.0 collective-permute-done.5.theirs
  16.7 0.4 weights.1
  17.1 0.0 collective-permute-done.3
  17.1 2.4 %collective-permute-done.4 = bf16[10,44,128]{2,0,1:T(8,128)(2,1)S(1)} collective-permute-done((bf16[10,44,128]{2,0,1:T(8,128)(2,1)S(1)}, bf16[10,44,128]{2,0,1:T(8,128)(2,1)S(1)}, u32[]{:S(2)}, u32[]{:S(2)}) %collective-permute-start.4) | collective-permute-done | bytes 112672 | tf_op jit(solution)/shard_map/ppermute | solution.py:56
  19.5 2.9 %own_branch.1 = (bf16[64,40,128]{2,1,0:T(8,128)(2,1)S(1)}, f32[40,48,64]{2,1,0:T(8,128)S(1)}) custom-call(bf16[24,24,128]{2,1,0:T(8,128)(2,1)S(1)} %collective-permute-done.tile, bf16[10,24,128]{2,1,0:T(8,128)(2,1)S(1)} %get-tuple-element.101.above, bf16[10,24,128]{2,1,0:T(8,128)(2,1)S(1)} %get-tuple-element.100.below, ...), custom_call_target="tpu_custom_call" | custom-call | flops 6291456000 | bytes 1806592 | tf_op jit(solution)/shard_map/own_branch/pallas_call | solution.py:458
  22.4 0.0 collective-permute-done.6
  22.4 0.7 collective-permute-start.7
  23.2 0.0 collective-permute-done.7.other
  23.2 1.2 %middle.1 = (bf16[28,32,128]{2,1,0:T(8,128)(2,1)S(1)}, bf16[40,32,256]{2,1,0:T(8,128)(2,1)S(1)}, bf16[48,32,256]{2,1,0:T(8,128)(2,1)S(1)}, bf16[24,32,64]{2,1,0:...) custom-call(bf16[64,40,128]{2,1,0:T(8,128)(2,1)S(1)} %constant_dynam, ...), custom_call_target="tpu_custom_call" | custom-call | flops 301989888 | bytes 3949056 | tf_op jit(solution)/shard_map/middle/pallas_call | solution.py:458
  24.4 0.7 collective-permute-start.8
  25.0 12.8 %collective-permute-start.9 = (bf16[12,24,128]{2,1,0:T(8,128)(2,1)S(1)}, bf16[12,24,128]{2,1,0:T(8,128)(2,1)S(1)}, u32[]{:S(2)}, u32[]{:S(2)}) collective-permute-start(bf16[12,24,128]{2,1,0:T(8,128)(2,1)S(1)} %get-tuple-element.58), channel_id=1, source_target_pairs={{0,17},{1,5},{2,6},{3,7},{17,0},{5,1},{6,2},{7,3},{18,19},{22,23},... | collective-permute-start | bytes 221192 | tf_op jit(solution)/shard_map/ppermute | solution.py:56
  37.9 0.0 collective-permute-done.8
  37.9 1.9 %collective-permute-done.9 = bf16[12,24,128]{2,1,0:T(8,128)(2,1)S(1)} collective-permute-done((bf16[12,24,128]{2,1,0:T(8,128)(2,1)S(1)}, bf16[12,24,128]{2,1,0:T(8,128)(2,1)S(1)}, u32[]{:S(2)}, u32[]{:S(2)}) %collective-permute-start.9) | collective-permute-done | bytes 73760 | tf_op jit(solution)/shard_map/ppermute | solution.py:56
  40.0 0.1 maximum_bitcast_fusion
  40.0 0.7 collective-permute-start.10
  40.7 0.1 maximum_bitcast_fusion.1
  40.8 4.4 %collective-permute-start.11 = (bf16[12,44,128]{2,0,1:T(8,128)(2,1)S(1)}, bf16[12,44,128]{2,0,1:T(8,128)(2,1)S(1)}, u32[]{:S(2)}, u32[]{:S(2)}) collective-permute-start(bf16[12,44,128]{2,0,1:T(8,128)(2,1)S(1)} %maximum_bitcast_fusion.1), channel_id=1, source_target_pairs={{0,1},{1,0},{2,3},{3,2},{17,5},{5,17},{6,7},{7,6},{18,22},{22,18},... | collective-permute-start | bytes 405512 | tf_op jit(solution)/shard_map/ppermute | solution.py:56
  45.2 0.4 near.1
  45.6 0.5 second_sums.1
  46.1 0.0 collective-permute-done.10
  46.1 2.5 %collective-permute-done.11 = bf16[12,44,128]{2,0,1:T(8,128)(2,1)S(1)} collective-permute-done((bf16[12,44,128]{2,0,1:T(8,128)(2,1)S(1)}, bf16[12,44,128]{2,0,1:T(8,128)(2,1)S(1)}, u32[]{:S(2)}, u32[]{:S(2)}) %collective-permute-start.11) | collective-permute-done | bytes 135200 | tf_op jit(solution)/shard_map/ppermute | solution.py:56
  48.8 2.7 %backward.1 = (f32[656,128]{1,0:T(8,128)S(1)}, bf16[656,128]{1,0:T(8,128)(2,1)S(1)}, bf16[3,28,32,128]{3,2,1,0:T(8,128)(2,1)S(1)}, bf16[24,24,128]{2,1,0:T(8,128)(2,1)S(1)}) custom-call(bf16[24,32,128]{2,1,0:T(8,128)(2,1)S(1)} %get-tuple-element.55.grad_pre, bf16[24,32,128]{2,1,0:T(8,128)(2,1)S(1)} %get-tuple-element.56.grad_tile, ...), custom_call_target="tpu_custom_call" | custom-call | flops 528482304 | bytes 4337664 | tf_op jit(solution)/shard_map/backward/pallas_call | solution.py:458
  51.5 0.7 collective-permute-start.12
  52.2 0.6 input.1
  52.8 0.4 collective-permute-done.12.other
  53.2 0.7 pair.1
  53.9 5.5 %all-to-all-start = ((bf16[16,48,128]{2,1,0:T(8,128)(2,1)}), bf16[16,48,128]{2,1,0:T(8,128)(2,1)S(1)}, u32[]{:S(2)}, u32[]{:S(2)}) async-start(bf16[16,48,128]{2,1,0:T(8,128)(2,1)} %pair.1), calls=%async_computation | async-start | bytes 393216 | tf_op jit(solution)/shard_map/all_to_all | solution.py:636
  59.4 0.7 collective-permute-start.13
  60.1 8.8 %all-to-all-done.parts = bf16[16,48,128]{2,1,0:T(8,128)(2,1)S(1)} async-done(((bf16[16,48,128]{2,1,0:T(8,128)(2,1)}), bf16[16,48,128]{2,1,0:T(8,128)(2,1)S(1)}, u32[]{:S(2)}, u32[]{:S(2)}) %all-to-all-start) | async-done | bytes 196640 | tf_op jit(solution)/shard_map/all_to_all | solution.py:636
  68.9 0.7 total.1
  69.6 3.5 %all-to-all-start.1 = ((bf16[16,40,128]{2,1,0:T(8,128)(2,1)}), bf16[16,40,128]{2,1,0:T(8,128)(2,1)S(1)}, u32[]{:S(2)}, u32[]{:S(2)}) async-start(bf16[16,40,128]{2,1,0:T(8,128)(2,1)} %get-tuple-element.78), calls=%async_computation.1 | async-start | bytes 327680 | tf_op jit(solution)/shard_map/all_to_all | solution.py:647
  73.1 0.7 landed.1
  73.8 7.0 %all-to-all-done.1 = bf16[16,40,128]{2,1,0:T(8,128)(2,1)S(1)} async-done(((bf16[16,40,128]{2,1,0:T(8,128)(2,1)}), bf16[16,40,128]{2,1,0:T(8,128)(2,1)S(1)}, u32[]{:S(2)}, u32[]{:S(2)}) %all-to-all-start.1) | async-done | bytes 163872 | tf_op jit(solution)/shard_map/all_to_all | solution.py:647
  80.8 0.7 outputs.1
  (25 shorter events, 0.5 us)
Async XLA Ops:
  0.6 7.8 %copy-start = (bf16[1,9,128,64]{2,3,1,0:T(8,128)(2,1)S(1)}, bf16[1,9,128,64]{2,3,1,0:T(8,128)(2,1)}, u32[]{:S(2)}) copy-start(bf16[1,9,128,64]{2,3,1,0:T(8,128)(2,1)} %param.7) | copy-start | bytes 442372
  0.6 8.6 %collective-permute-start = (bf16[24,24,128]{2,1,0:T(8,128)(2,1)}, bf16[24,24,128]{2,1,0:T(8,128)(2,1)S(1)}, u32[]{:S(2)}, u32[]{:S(2)}) collective-permute-start(bf16[24,24,128]{2,1,0:T(8,128)(2,1)} %bitcast.48), channel_id=1, source_target_pairs={{0,0},{1,1},{2,2},{3,3},{4,17},{5,5},{6,6},{7,7},{8,18},{9,22},{10... | collective-permute-start | bytes 442376 | tf_op jit(solution)/shard_map/ppermute | solution.py:56
  2.3 6.1 %copy-start.1 = (bf16[1,64,128]{2,1,0:T(8,128)(2,1)S(1)}, bf16[1,64,128]{2,1,0:T(8,128)(2,1)}, u32[]{:S(2)}) copy-start(bf16[1,64,128]{2,1,0:T(8,128)(2,1)} %param.9) | copy-start | bytes 49156
  3.2 6.5 %collective-permute-start.2 = (bf16[10,24,128]{2,1,0:T(8,128)(2,1)S(1)}, bf16[10,24,128]{2,1,0:T(8,128)(2,1)S(1)}, u32[]{:S(2)}, u32[]{:S(2)}) collective-permute-start(bf16[10,24,128]{2,1,0:T(8,128)(2,1)S(1)} %get-tuple-element.98), channel_id=1, source_target_pairs={{0,17},{1,5},{2,6},{3,7},{4,0},{5,1},{6,2},{7,3},{8,19},{9,23},{10... | collective-permute-start | bytes 184328 | tf_op jit(solution)/shard_map/ppermute | solution.py:56
  7.8 2.0 %collective-permute-start.1 = (bf16[10,24,128]{2,1,0:T(8,128)(2,1)S(1)}, bf16[10,24,128]{2,1,0:T(8,128)(2,1)S(1)}, u32[]{:S(2)}, u32[]{:S(2)}) collective-permute-start(bf16[10,24,128]{2,1,0:T(8,128)(2,1)S(1)} %get-tuple-element.99), channel_id=1, source_target_pairs={{4,18},{5,22},{6,10},{7,11},{8,17},{9,5},{10,6},{11,7},{20,24},{21... | collective-permute-start | bytes 184328 | tf_op jit(solution)/shard_map/ppermute | solution.py:56
  8.4 0.7 copy-start.2
  9.1 7.6 %collective-permute-start.5 = (bf16[656,128]{1,0:T(8,128)(2,1)S(1)}, bf16[656,128]{1,0:T(8,128)(2,1)S(1)}, u32[]{:S(2)}, u32[]{:S(2)}) collective-permute-start(bf16[656,128]{1,0:T(8,128)(2,1)S(1)} %fusion.1.mine), channel_id=1, source_target_pairs={{0,16},{16,0},{1,17},{17,1},{2,18},{18,2},{3,19},{19,3},{4,20},{20... | collective-permute-start | bytes 503816 | tf_op jit(solution)/shard_map/ppermute | solution.py:500
  9.9 6.2 %copy-start.3 = (bf16[1,24,24,128]{3,2,1,0:T(8,128)(2,1)S(1)}, bf16[1,24,24,128]{3,2,1,0:T(8,128)(2,1)}, u32[]{:S(2)}) copy-start(bf16[1,24,24,128]{3,2,1,0:T(8,128)(2,1)} %param.6) | copy-start | bytes 442372
  9.9 7.2 %collective-permute-start.3 = (bf16[10,44,128]{2,0,1:T(8,128)(2,1)S(1)}, bf16[10,44,128]{2,0,1:T(8,128)(2,1)S(1)}, u32[]{:S(2)}, u32[]{:S(2)}) collective-permute-start(bf16[10,44,128]{2,0,1:T(8,128)(2,1)S(1)} %get-tuple-element.45), channel_id=1, source_target_pairs={{1,2},{2,1},{5,6},{6,5},{22,10},{10,22},{23,27},{27,23},{4,8},{8,4... | collective-permute-start | bytes 337928 | tf_op jit(solution)/shard_map/ppermute | solution.py:56
  10.7 8.8 %collective-permute-start.4 = (bf16[10,44,128]{2,0,1:T(8,128)(2,1)S(1)}, bf16[10,44,128]{2,0,1:T(8,128)(2,1)S(1)}, u32[]{:S(2)}, u32[]{:S(2)}) collective-permute-start(bf16[10,44,128]{2,0,1:T(8,128)(2,1)S(1)} %get-tuple-element.46), channel_id=1, source_target_pairs={{0,1},{1,0},{2,3},{3,2},{17,5},{5,17},{6,7},{7,6},{18,22},{22,18},... | collective-permute-start | bytes 337928 | tf_op jit(solution)/shard_map/ppermute | solution.py:56
  16.1 6.3 %collective-permute-start.6 = (bf16[24,24,128]{2,1,0:T(8,128)(2,1)S(1)}, bf16[24,24,128]{2,1,0:T(8,128)(2,1)S(1)}, u32[]{:S(2)}, u32[]{:S(2)}) collective-permute-start(bf16[24,24,128]{2,1,0:T(8,128)(2,1)S(1)} %bitcast.51), channel_id=1, source_target_pairs={{0,0},{1,1},{2,2},{3,3},{4,17},{5,5},{6,6},{7,7},{8,18},{9,22},{10... | collective-permute-start | bytes 442376 | tf_op jit(solution)/shard_map/ppermute | solution.py:56
  22.4 0.7 collective-permute-start.7
  24.4 13.5 %collective-permute-start.8 = (bf16[12,24,128]{2,1,0:T(8,128)(2,1)S(1)}, bf16[12,24,128]{2,1,0:T(8,128)(2,1)S(1)}, u32[]{:S(2)}, u32[]{:S(2)}) collective-permute-start(bf16[12,24,128]{2,1,0:T(8,128)(2,1)S(1)} %get-tuple-element.57), channel_id=1, source_target_pairs={{17,18},{5,22},{6,10},{7,11},{18,17},{22,5},{10,6},{11,7},{20,24},... | collective-permute-start | bytes 221192 | tf_op jit(solution)/shard_map/ppermute | solution.py:56
  25.0 14.8 %collective-permute-start.9 = (bf16[12,24,128]{2,1,0:T(8,128)(2,1)S(1)}, bf16[12,24,128]{2,1,0:T(8,128)(2,1)S(1)}, u32[]{:S(2)}, u32[]{:S(2)}) collective-permute-start(bf16[12,24,128]{2,1,0:T(8,128)(2,1)S(1)} %get-tuple-element.58), channel_id=1, source_target_pairs={{0,17},{1,5},{2,6},{3,7},{17,0},{5,1},{6,2},{7,3},{18,19},{22,23},... | collective-permute-start | bytes 221192 | tf_op jit(solution)/shard_map/ppermute | solution.py:56
  40.0 6.1 %collective-permute-start.10 = (bf16[12,44,128]{2,0,1:T(8,128)(2,1)S(1)}, bf16[12,44,128]{2,0,1:T(8,128)(2,1)S(1)}, u32[]{:S(2)}, u32[]{:S(2)}) collective-permute-start(bf16[12,44,128]{2,0,1:T(8,128)(2,1)S(1)} %maximum_bitcast_fusion), channel_id=1, source_target_pairs={{1,2},{2,1},{5,6},{6,5},{22,10},{10,22},{23,27},{27,23},{4,8},{8,4... | collective-permute-start | bytes 405512 | tf_op jit(solution)/shard_map/ppermute | solution.py:56
  40.8 7.9 %collective-permute-start.11 = (bf16[12,44,128]{2,0,1:T(8,128)(2,1)S(1)}, bf16[12,44,128]{2,0,1:T(8,128)(2,1)S(1)}, u32[]{:S(2)}, u32[]{:S(2)}) collective-permute-start(bf16[12,44,128]{2,0,1:T(8,128)(2,1)S(1)} %maximum_bitcast_fusion.1), channel_id=1, source_target_pairs={{0,1},{1,0},{2,3},{3,2},{17,5},{5,17},{6,7},{7,6},{18,22},{22,18},... | collective-permute-start | bytes 405512 | tf_op jit(solution)/shard_map/ppermute | solution.py:56
  51.5 1.7 %collective-permute-start.12 = (bf16[656,128]{1,0:T(8,128)(2,1)S(1)}, bf16[656,128]{1,0:T(8,128)(2,1)S(1)}, u32[]{:S(2)}, u32[]{:S(2)}) collective-permute-start(bf16[656,128]{1,0:T(8,128)(2,1)S(1)} %get-tuple-element.73), channel_id=1, source_target_pairs={{0,16},{16,0},{1,17},{17,1},{2,18},{18,2},{3,19},{19,3},{4,20},{20... | collective-permute-start | bytes 503816 | tf_op jit(solution)/shard_map/ppermute | solution.py:626
  53.9 15.0 %all-to-all-start = ((bf16[16,48,128]{2,1,0:T(8,128)(2,1)}), bf16[16,48,128]{2,1,0:T(8,128)(2,1)S(1)}, u32[]{:S(2)}, u32[]{:S(2)}) async-start(bf16[16,48,128]{2,1,0:T(8,128)(2,1)} %pair.1), calls=%async_computation | async-start | bytes 393216 | tf_op jit(solution)/shard_map/all_to_all | solution.py:636
  59.4 13.7 %collective-permute-start.13 = (bf16[24,24,128]{2,1,0:T(8,128)(2,1)S(1)}, bf16[24,24,128]{2,1,0:T(8,128)(2,1)S(1)}, u32[]{:S(2)}, u32[]{:S(2)}) collective-permute-start(bf16[24,24,128]{2,1,0:T(8,128)(2,1)S(1)} %input.1), channel_id=1, source_target_pairs={{0,0},{1,1},{2,2},{3,3},{17,4},{5,5},{6,6},{7,7},{18,8},{22,9},{10... | collective-permute-start | bytes 442376 | tf_op jit(solution)/shard_map/ppermute | solution.py:56
  69.6 11.2 %all-to-all-start.1 = ((bf16[16,40,128]{2,1,0:T(8,128)(2,1)}), bf16[16,40,128]{2,1,0:T(8,128)(2,1)S(1)}, u32[]{:S(2)}, u32[]{:S(2)}) async-start(bf16[16,40,128]{2,1,0:T(8,128)(2,1)} %get-tuple-element.78), calls=%async_computation.1 | async-start | bytes 327680 | tf_op jit(solution)/shard_map/all_to_all | solution.py:647

commit v20 on v19

--- a/solution.py
+++ b/solution.py
@@ -324,8 +324,8 @@
 def backward_kernel(
     grad_pre, grad_tile, above, below, left, right, left_branch, right_branch, gate_second, gate_first, near_pairs,
     near_last, bottle_first, v_second, p_first, rows_second, ends_second,
-    keep, away, windows, grad_first,
-    area, pairs, last, branch, grads, rows, ends,
+    keep, away, grads, grad_first,
+    area, pairs, last, branch, rows, ends,
 ):
     side, channels = grad_first.shape[0], grad_first.shape[2]
     first, second = FIRST_DILATION, SECOND_DILATION
@@ -378,9 +378,6 @@
         return 0
 
     lax.fori_loop(0, near // 7, sections, 0, unroll=True)
-    for b in (-1, 0, 1):
-        at = first * (1 - b)
-        windows[b + 1] = grads[:, at : at + small].astype(BF16)
     part = branch[first : first + side, first : first + small]
     grad_first[...] = part[:, :side].astype(BF16)
     real = lax.broadcasted_iota(jnp.int32, part.shape, 1) < side
@@ -414,10 +411,13 @@
         parts[j] = jnp.concatenate(pieces + [total[count : count + 8]]).astype(BF16)
 
 
-def input_kernel(windows, grad_first, tile, v_first, out):
+def input_kernel(grads, grad_first, tile, v_first, out, windows):
     side, channels = out.shape[0], out.shape[2]
     small = windows.shape[2]
     first = FIRST_DILATION
+    for b in (-1, 0, 1):
+        at = first * (1 - b)
+        windows[b + 1] = grads[:, at : at + small].astype(BF16)
 
     def rows(step, _):
         top = step * 8
@@ -591,20 +591,19 @@
 
     devices = number * number
     share = -(-10 * inner // (8 * devices)) * 8
-    keep, away, windows, grad_first = call(
+    keep, away, grads, grad_first = call(
         backward_kernel,
         "backward",
         [
             ((10 * inner + 16, channels), F32),
             ((10 * inner + 16, channels), BF16),
-            ((3, near, small, channels), BF16),
+            ((near, small + 16, channels), F32),
             ((side, side, channels), BF16),
         ],
         [
             ((full, LEAD + up16(side + HALO + first), channels), F32),
             ((full, small, 2 * channels), BF16),
             ((full, small, channels), BF16),
-            ((near, small + 16, channels), F32),
             ((near, small + 16, channels), F32),
             ((10 * inner, channels), F32),
             ((16, channels), F32),
@@ -619,9 +618,9 @@
         input_kernel,
         "input",
         [((side, side, channels), BF16)],
-        [],
+        [((3, near, small, channels), BF16)],
         18 * side * small * channels * channels,
-        *(windows, grad_first, tile, v_first),
+        *(grads, grad_first, tile, v_first),
     )
     other = lax.ppermute(away, "segment", [(0, 1), (1, 0)])
     other, input_gradient = lax.optimization_barrier((other, input_gradient))

time: 82 us -> 82 us (level)
  no operation moved by 1% of the time
where the time goes in v20:
time: 82 us; the launch traced here: 81.5 us
  starting transfers between devices  43.3 us (53%)
  waiting for transfers between devices  23.5 us (29%)
  Pallas kernels  11.5 us (14%)
  other arithmetic  1.39 us (2%)
  between operations  1.03 us (1%)
    ppermute x12, starting transfers between devices, permute(): return lax.ppermute(x, ALL, [found for found in pairs if found is not None])  33.6 us
    pallas_call x11, Pallas kernels, call(): pl.pallas_call(kernel, name=name, out_shape=outs, scratch_shapes=[pltpu.V...  11.5 us
    all_to_all x1, waiting for transfers between devices, local(): parts = lax.all_to_all(parts, GRID, 0, 0, tiled=True)  8.8 us
    ppermute x12, waiting for transfers between devices, permute(): return lax.ppermute(x, ALL, [found for found in pairs if found is not None])  7.32 us
    all_to_all x1, waiting for transfers between devices, local(): lax.all_to_all(rows, GRID, 0, 0, tiled=True)  6.99 us
    all_to_all x1, starting transfers between devices, local(): parts = lax.all_to_all(parts, GRID, 0, 0, tiled=True)  5.48 us
    all_to_all x1, starting transfers between devices, local(): lax.all_to_all(rows, GRID, 0, 0, tiled=True)  3.52 us
  transfers between devices with their start and end apart: 16, of which 7 were waited for; matrix products, arithmetic and copies ran while one was open for 2% of the time, Pallas kernels for 8%

profile of v20, /device:TPU:0, one launch (start us, length us, event | category | flops | bytes accessed | tf_op | source)
XLA Modules:
  0.0 81.5 jit_solution(15372090529702358680)
XLA Ops:
  0.6 1.7 %collective-permute-start = (bf16[24,24,128]{2,1,0:T(8,128)(2,1)}, bf16[24,24,128]{2,1,0:T(8,128)(2,1)S(1)}, u32[]{:S(2)}, u32[]{:S(2)}) collective-permute-start(bf16[24,24,128]{2,1,0:T(8,128)(2,1)} %bitcast.48), channel_id=1, source_target_pairs={{0,0},{1,1},{2,2},{3,3},{4,17},{5,5},{6,6},{7,7},{8,18},{9,22},{10... | collective-permute-start | bytes 442376 | tf_op jit(solution)/shard_map/ppermute | solution.py:56
  2.3 0.9 %select_bitcast_fusion.6 = (bf16[10,24,128]{2,1,0:T(8,128)(2,1)S(1)}, bf16[10,24,128]{2,1,0:T(8,128)(2,1)S(1)}) fusion(pred[]{:T(512)S(6)} %eq.14, bf16[1,24,24,128]{3,2,1,0:T(8,128)(2,1)} %param.5), kind=kLoop, calls=%fused_computation.16 | loop fusion | flops 61440 | bytes 245761 | tf_op jit(solution)/shard_map/jit(_where)/select_n | solution.py:478
  3.2 4.5 %collective-permute-start.2 = (bf16[10,24,128]{2,1,0:T(8,128)(2,1)S(1)}, bf16[10,24,128]{2,1,0:T(8,128)(2,1)S(1)}, u32[]{:S(2)}, u32[]{:S(2)}) collective-permute-start(bf16[10,24,128]{2,1,0:T(8,128)(2,1)S(1)} %get-tuple-element.98), channel_id=1, source_target_pairs={{0,17},{1,5},{2,6},{3,7},{4,0},{5,1},{6,2},{7,3},{8,19},{9,23},{10... | collective-permute-start | bytes 184328 | tf_op jit(solution)/shard_map/ppermute | solution.py:56
  7.8 0.7 collective-permute-start.1
  8.4 0.0 copy-start.2
  8.5 0.6 copy-done.2
  9.1 0.1 collective-permute-start.5
  9.2 0.0 collective-permute-done.tile
  9.3 0.4 collective-permute-done.2
  9.8 0.0 collective-permute-done.1
  9.9 0.0 copy-start.3
  9.9 0.8 collective-permute-start.3
  10.7 5.3 %collective-permute-start.4 = (bf16[10,44,128]{2,0,1:T(8,128)(2,1)S(1)}, bf16[10,44,128]{2,0,1:T(8,128)(2,1)S(1)}, u32[]{:S(2)}, u32[]{:S(2)}) collective-permute-start(bf16[10,44,128]{2,0,1:T(8,128)(2,1)S(1)} %get-tuple-element.46), channel_id=1, source_target_pairs={{0,1},{1,0},{2,3},{3,2},{17,5},{5,17},{6,7},{7,6},{18,22},{22,18},... | collective-permute-start | bytes 337928 | tf_op jit(solution)/shard_map/ppermute | solution.py:56
  16.1 0.7 collective-permute-start.6
  16.7 0.0 collective-permute-done.5.theirs
  16.7 0.4 weights.1
  17.1 0.0 collective-permute-done.3
  17.1 2.4 %collective-permute-done.4 = bf16[10,44,128]{2,0,1:T(8,128)(2,1)S(1)} collective-permute-done((bf16[10,44,128]{2,0,1:T(8,128)(2,1)S(1)}, bf16[10,44,128]{2,0,1:T(8,128)(2,1)S(1)}, u32[]{:S(2)}, u32[]{:S(2)}) %collective-permute-start.4) | collective-permute-done | bytes 112672 | tf_op jit(solution)/shard_map/ppermute | solution.py:56
  19.5 2.9 %own_branch.1 = (bf16[64,40,128]{2,1,0:T(8,128)(2,1)S(1)}, f32[40,48,64]{2,1,0:T(8,128)S(1)}) custom-call(bf16[24,24,128]{2,1,0:T(8,128)(2,1)S(1)} %collective-permute-done.tile, bf16[10,24,128]{2,1,0:T(8,128)(2,1)S(1)} %get-tuple-element.101.above, bf16[10,24,128]{2,1,0:T(8,128)(2,1)S(1)} %get-tuple-element.100.below, ...), custom_call_target="tpu_custom_call" | custom-call | flops 6291456000 | bytes 1806592 | tf_op jit(solution)/shard_map/own_branch/pallas_call | solution.py:458
  22.4 0.0 collective-permute-done.6
  22.4 0.7 collective-permute-start.7
  23.2 0.0 collective-permute-done.7.other
  23.2 1.2 %middle.1 = (bf16[28,32,128]{2,1,0:T(8,128)(2,1)S(1)}, bf16[40,32,256]{2,1,0:T(8,128)(2,1)S(1)}, bf16[48,32,256]{2,1,0:T(8,128)(2,1)S(1)}, bf16[24,32,64]{2,1,0:...) custom-call(bf16[64,40,128]{2,1,0:T(8,128)(2,1)S(1)} %constant_dynam, ...), custom_call_target="tpu_custom_call" | custom-call | flops 301989888 | bytes 3949056 | tf_op jit(solution)/shard_map/middle/pallas_call | solution.py:458
  24.4 0.7 collective-permute-start.8
  25.0 12.8 %collective-permute-start.9 = (bf16[12,24,128]{2,1,0:T(8,128)(2,1)S(1)}, bf16[12,24,128]{2,1,0:T(8,128)(2,1)S(1)}, u32[]{:S(2)}, u32[]{:S(2)}) collective-permute-start(bf16[12,24,128]{2,1,0:T(8,128)(2,1)S(1)} %get-tuple-element.58), channel_id=1, source_target_pairs={{0,17},{1,5},{2,6},{3,7},{17,0},{5,1},{6,2},{7,3},{18,19},{22,23},... | collective-permute-start | bytes 221192 | tf_op jit(solution)/shard_map/ppermute | solution.py:56
  37.9 1.9 %collective-permute-done.9 = bf16[12,24,128]{2,1,0:T(8,128)(2,1)S(1)} collective-permute-done((bf16[12,24,128]{2,1,0:T(8,128)(2,1)S(1)}, bf16[12,24,128]{2,1,0:T(8,128)(2,1)S(1)}, u32[]{:S(2)}, u32[]{:S(2)}) %collective-permute-start.9) | collective-permute-done | bytes 73760 | tf_op jit(solution)/shard_map/ppermute | solution.py:56
  40.0 0.1 maximum_bitcast_fusion
  40.0 0.7 collective-permute-start.10
  40.7 0.1 maximum_bitcast_fusion.1
  40.8 4.4 %collective-permute-start.11 = (bf16[12,44,128]{2,0,1:T(8,128)(2,1)S(1)}, bf16[12,44,128]{2,0,1:T(8,128)(2,1)S(1)}, u32[]{:S(2)}, u32[]{:S(2)}) collective-permute-start(bf16[12,44,128]{2,0,1:T(8,128)(2,1)S(1)} %maximum_bitcast_fusion.1), channel_id=1, source_target_pairs={{0,1},{1,0},{2,3},{3,2},{17,5},{5,17},{6,7},{7,6},{18,22},{22,18},... | collective-permute-start | bytes 405512 | tf_op jit(solution)/shard_map/ppermute | solution.py:56
  45.2 0.4 near.1
  45.6 0.5 second_sums.1
  46.1 0.0 collective-permute-done.10
  46.1 2.5 %collective-permute-done.11 = bf16[12,44,128]{2,0,1:T(8,128)(2,1)S(1)} collective-permute-done((bf16[12,44,128]{2,0,1:T(8,128)(2,1)S(1)}, bf16[12,44,128]{2,0,1:T(8,128)(2,1)S(1)}, u32[]{:S(2)}, u32[]{:S(2)}) %collective-permute-start.11) | collective-permute-done | bytes 135200 | tf_op jit(solution)/shard_map/ppermute | solution.py:56
  48.8 2.7 %backward.1 = (f32[656,128]{1,0:T(8,128)S(1)}, bf16[656,128]{1,0:T(8,128)(2,1)S(1)}, f32[28,48,128]{2,1,0:T(8,128)S(1)}, bf16[24,24,128]{2,1,0:T(8,128)(2,1)S(1)}) custom-call(bf16[24,32,128]{2,1,0:T(8,128)(2,1)S(1)} %get-tuple-element.55.grad_pre, bf16[24,32,128]{2,1,0:T(8,128)(2,1)S(1)} %get-tuple-element.56.grad_tile, ...), custom_call_target="tpu_custom_call" | custom-call | flops 528482304 | bytes 4337664 | tf_op jit(solution)/shard_map/backward/pallas_call | solution.py:458
  51.5 0.7 collective-permute-start.12
  52.1 0.7 input.1
  52.8 0.4 collective-permute-done.12.other
  53.1 0.7 pair.1
  53.9 5.5 %all-to-all-start = ((bf16[16,48,128]{2,1,0:T(8,128)(2,1)}), bf16[16,48,128]{2,1,0:T(8,128)(2,1)S(1)}, u32[]{:S(2)}, u32[]{:S(2)}) async-start(bf16[16,48,128]{2,1,0:T(8,128)(2,1)} %pair.1), calls=%async_computation | async-start | bytes 393216 | tf_op jit(solution)/shard_map/all_to_all | solution.py:635
  59.4 0.7 collective-permute-start.13
  60.0 8.8 %all-to-all-done.parts = bf16[16,48,128]{2,1,0:T(8,128)(2,1)S(1)} async-done(((bf16[16,48,128]{2,1,0:T(8,128)(2,1)}), bf16[16,48,128]{2,1,0:T(8,128)(2,1)S(1)}, u32[]{:S(2)}, u32[]{:S(2)}) %all-to-all-start) | async-done | bytes 196640 | tf_op jit(solution)/shard_map/all_to_all | solution.py:635
  68.8 0.7 total.1
  69.5 3.5 %all-to-all-start.1 = ((bf16[16,40,128]{2,1,0:T(8,128)(2,1)}), bf16[16,40,128]{2,1,0:T(8,128)(2,1)S(1)}, u32[]{:S(2)}, u32[]{:S(2)}) async-start(bf16[16,40,128]{2,1,0:T(8,128)(2,1)} %get-tuple-element.78), calls=%async_computation.1 | async-start | bytes 327680 | tf_op jit(solution)/shard_map/all_to_all | solution.py:646
  73.1 0.0 collective-permute-done.13.moved
  73.1 0.7 landed.1
  73.7 7.0 %all-to-all-done.1 = bf16[16,40,128]{2,1,0:T(8,128)(2,1)S(1)} async-done(((bf16[16,40,128]{2,1,0:T(8,128)(2,1)}), bf16[16,40,128]{2,1,0:T(8,128)(2,1)S(1)}, u32[]{:S(2)}, u32[]{:S(2)}) %all-to-all-start.1) | async-done | bytes 163872 | tf_op jit(solution)/shard_map/all_to_all | solution.py:646
  80.7 0.7 outputs.1
  (25 shorter events, 0.5 us)
Async XLA Ops:
  0.6 7.8 %copy-start = (bf16[1,9,128,64]{2,3,1,0:T(8,128)(2,1)S(1)}, bf16[1,9,128,64]{2,3,1,0:T(8,128)(2,1)}, u32[]{:S(2)}) copy-start(bf16[1,9,128,64]{2,3,1,0:T(8,128)(2,1)} %param.7) | copy-start | bytes 442372
  0.6 8.6 %collective-permute-start = (bf16[24,24,128]{2,1,0:T(8,128)(2,1)}, bf16[24,24,128]{2,1,0:T(8,128)(2,1)S(1)}, u32[]{:S(2)}, u32[]{:S(2)}) collective-permute-start(bf16[24,24,128]{2,1,0:T(8,128)(2,1)} %bitcast.48), channel_id=1, source_target_pairs={{0,0},{1,1},{2,2},{3,3},{4,17},{5,5},{6,6},{7,7},{8,18},{9,22},{10... | collective-permute-start | bytes 442376 | tf_op jit(solution)/shard_map/ppermute | solution.py:56
  2.3 6.1 %copy-start.1 = (bf16[1,64,128]{2,1,0:T(8,128)(2,1)S(1)}, bf16[1,64,128]{2,1,0:T(8,128)(2,1)}, u32[]{:S(2)}) copy-start(bf16[1,64,128]{2,1,0:T(8,128)(2,1)} %param.9) | copy-start | bytes 49156
  3.2 6.5 %collective-permute-start.2 = (bf16[10,24,128]{2,1,0:T(8,128)(2,1)S(1)}, bf16[10,24,128]{2,1,0:T(8,128)(2,1)S(1)}, u32[]{:S(2)}, u32[]{:S(2)}) collective-permute-start(bf16[10,24,128]{2,1,0:T(8,128)(2,1)S(1)} %get-tuple-element.98), channel_id=1, source_target_pairs={{0,17},{1,5},{2,6},{3,7},{4,0},{5,1},{6,2},{7,3},{8,19},{9,23},{10... | collective-permute-start | bytes 184328 | tf_op jit(solution)/shard_map/ppermute | solution.py:56
  7.8 2.0 %collective-permute-start.1 = (bf16[10,24,128]{2,1,0:T(8,128)(2,1)S(1)}, bf16[10,24,128]{2,1,0:T(8,128)(2,1)S(1)}, u32[]{:S(2)}, u32[]{:S(2)}) collective-permute-start(bf16[10,24,128]{2,1,0:T(8,128)(2,1)S(1)} %get-tuple-element.99), channel_id=1, source_target_pairs={{4,18},{5,22},{6,10},{7,11},{8,17},{9,5},{10,6},{11,7},{20,24},{21... | collective-permute-start | bytes 184328 | tf_op jit(solution)/shard_map/ppermute | solution.py:56
  8.4 0.7 copy-start.2
  9.1 7.6 %collective-permute-start.5 = (bf16[656,128]{1,0:T(8,128)(2,1)S(1)}, bf16[656,128]{1,0:T(8,128)(2,1)S(1)}, u32[]{:S(2)}, u32[]{:S(2)}) collective-permute-start(bf16[656,128]{1,0:T(8,128)(2,1)S(1)} %fusion.1.mine), channel_id=1, source_target_pairs={{0,16},{16,0},{1,17},{17,1},{2,18},{18,2},{3,19},{19,3},{4,20},{20... | collective-permute-start | bytes 503816 | tf_op jit(solution)/shard_map/ppermute | solution.py:500
  9.9 6.2 %copy-start.3 = (bf16[1,24,24,128]{3,2,1,0:T(8,128)(2,1)S(1)}, bf16[1,24,24,128]{3,2,1,0:T(8,128)(2,1)}, u32[]{:S(2)}) copy-start(bf16[1,24,24,128]{3,2,1,0:T(8,128)(2,1)} %param.6) | copy-start | bytes 442372
  9.9 7.2 %collective-permute-start.3 = (bf16[10,44,128]{2,0,1:T(8,128)(2,1)S(1)}, bf16[10,44,128]{2,0,1:T(8,128)(2,1)S(1)}, u32[]{:S(2)}, u32[]{:S(2)}) collective-permute-start(bf16[10,44,128]{2,0,1:T(8,128)(2,1)S(1)} %get-tuple-element.45), channel_id=1, source_target_pairs={{1,2},{2,1},{5,6},{6,5},{22,10},{10,22},{23,27},{27,23},{4,8},{8,4... | collective-permute-start | bytes 337928 | tf_op jit(solution)/shard_map/ppermute | solution.py:56
  10.7 8.8 %collective-permute-start.4 = (bf16[10,44,128]{2,0,1:T(8,128)(2,1)S(1)}, bf16[10,44,128]{2,0,1:T(8,128)(2,1)S(1)}, u32[]{:S(2)}, u32[]{:S(2)}) collective-permute-start(bf16[10,44,128]{2,0,1:T(8,128)(2,1)S(1)} %get-tuple-element.46), channel_id=1, source_target_pairs={{0,1},{1,0},{2,3},{3,2},{17,5},{5,17},{6,7},{7,6},{18,22},{22,18},... | collective-permute-start | bytes 337928 | tf_op jit(solution)/shard_map/ppermute | solution.py:56
  16.1 6.3 %collective-permute-start.6 = (bf16[24,24,128]{2,1,0:T(8,128)(2,1)S(1)}, bf16[24,24,128]{2,1,0:T(8,128)(2,1)S(1)}, u32[]{:S(2)}, u32[]{:S(2)}) collective-permute-start(bf16[24,24,128]{2,1,0:T(8,128)(2,1)S(1)} %bitcast.51), channel_id=1, source_target_pairs={{0,0},{1,1},{2,2},{3,3},{4,17},{5,5},{6,6},{7,7},{8,18},{9,22},{10... | collective-permute-start | bytes 442376 | tf_op jit(solution)/shard_map/ppermute | solution.py:56
  22.4 0.7 collective-permute-start.7
  24.4 13.5 %collective-permute-start.8 = (bf16[12,24,128]{2,1,0:T(8,128)(2,1)S(1)}, bf16[12,24,128]{2,1,0:T(8,128)(2,1)S(1)}, u32[]{:S(2)}, u32[]{:S(2)}) collective-permute-start(bf16[12,24,128]{2,1,0:T(8,128)(2,1)S(1)} %get-tuple-element.57), channel_id=1, source_target_pairs={{17,18},{5,22},{6,10},{7,11},{18,17},{22,5},{10,6},{11,7},{20,24},... | collective-permute-start | bytes 221192 | tf_op jit(solution)/shard_map/ppermute | solution.py:56
  25.0 14.8 %collective-permute-start.9 = (bf16[12,24,128]{2,1,0:T(8,128)(2,1)S(1)}, bf16[12,24,128]{2,1,0:T(8,128)(2,1)S(1)}, u32[]{:S(2)}, u32[]{:S(2)}) collective-permute-start(bf16[12,24,128]{2,1,0:T(8,128)(2,1)S(1)} %get-tuple-element.58), channel_id=1, source_target_pairs={{0,17},{1,5},{2,6},{3,7},{17,0},{5,1},{6,2},{7,3},{18,19},{22,23},... | collective-permute-start | bytes 221192 | tf_op jit(solution)/shard_map/ppermute | solution.py:56
  40.0 6.1 %collective-permute-start.10 = (bf16[12,44,128]{2,0,1:T(8,128)(2,1)S(1)}, bf16[12,44,128]{2,0,1:T(8,128)(2,1)S(1)}, u32[]{:S(2)}, u32[]{:S(2)}) collective-permute-start(bf16[12,44,128]{2,0,1:T(8,128)(2,1)S(1)} %maximum_bitcast_fusion), channel_id=1, source_target_pairs={{1,2},{2,1},{5,6},{6,5},{22,10},{10,22},{23,27},{27,23},{4,8},{8,4... | collective-permute-start | bytes 405512 | tf_op jit(solution)/shard_map/ppermute | solution.py:56
  40.8 7.9 %collective-permute-start.11 = (bf16[12,44,128]{2,0,1:T(8,128)(2,1)S(1)}, bf16[12,44,128]{2,0,1:T(8,128)(2,1)S(1)}, u32[]{:S(2)}, u32[]{:S(2)}) collective-permute-start(bf16[12,44,128]{2,0,1:T(8,128)(2,1)S(1)} %maximum_bitcast_fusion.1), channel_id=1, source_target_pairs={{0,1},{1,0},{2,3},{3,2},{17,5},{5,17},{6,7},{7,6},{18,22},{22,18},... | collective-permute-start | bytes 405512 | tf_op jit(solution)/shard_map/ppermute | solution.py:56
  51.5 1.7 %collective-permute-start.12 = (bf16[656,128]{1,0:T(8,128)(2,1)S(1)}, bf16[656,128]{1,0:T(8,128)(2,1)S(1)}, u32[]{:S(2)}, u32[]{:S(2)}) collective-permute-start(bf16[656,128]{1,0:T(8,128)(2,1)S(1)} %get-tuple-element.73), channel_id=1, source_target_pairs={{0,16},{16,0},{1,17},{17,1},{2,18},{18,2},{3,19},{19,3},{4,20},{20... | collective-permute-start | bytes 503816 | tf_op jit(solution)/shard_map/ppermute | solution.py:625
  53.9 15.0 %all-to-all-start = ((bf16[16,48,128]{2,1,0:T(8,128)(2,1)}), bf16[16,48,128]{2,1,0:T(8,128)(2,1)S(1)}, u32[]{:S(2)}, u32[]{:S(2)}) async-start(bf16[16,48,128]{2,1,0:T(8,128)(2,1)} %pair.1), calls=%async_computation | async-start | bytes 393216 | tf_op jit(solution)/shard_map/all_to_all | solution.py:635
  59.4 13.7 %collective-permute-start.13 = (bf16[24,24,128]{2,1,0:T(8,128)(2,1)S(1)}, bf16[24,24,128]{2,1,0:T(8,128)(2,1)S(1)}, u32[]{:S(2)}, u32[]{:S(2)}) collective-permute-start(bf16[24,24,128]{2,1,0:T(8,128)(2,1)S(1)} %input.1), channel_id=1, source_target_pairs={{0,0},{1,1},{2,2},{3,3},{17,4},{5,5},{6,6},{7,7},{18,8},{22,9},{10... | collective-permute-start | bytes 442376 | tf_op jit(solution)/shard_map/ppermute | solution.py:56
  69.5 11.2 %all-to-all-start.1 = ((bf16[16,40,128]{2,1,0:T(8,128)(2,1)}), bf16[16,40,128]{2,1,0:T(8,128)(2,1)S(1)}, u32[]{:S(2)}, u32[]{:S(2)}) async-start(bf16[16,40,128]{2,1,0:T(8,128)(2,1)} %get-tuple-element.78), calls=%async_computation.1 | async-start | bytes 327680 | tf_op jit(solution)/shard_map/all_to_all | solution.py:646
